TPU v7x, 256 devices: a whole 4x4x8 slice. The times are simulated.
256 devices in a mesh: row: 16 (over x, y), col: 16 (over z, core).
Axes of the slice: x: 4, y: 4, z: 8, core: 2. Of those that a mesh axis runs over, the one named last changes fastest.
Arguments:
- factor: float32 [4, 2048, 4, 2048], P(None, 'row', None, 'col'), may hold values from -4 to 4, as said below
- structure: int32 [4, 64], replicated, may hold values from 0 to 1, as said below
Outputs:
- inverse: float32 [4, 2048, 4, 2048], P(None, 'row', None, 'col')
Inputs may be any that keep to these rules, and one draw needn't show every extreme that they name: structure[s, t] is 1 only for tiles t of proper ancestors of supernode s; row 3 is zero; where structure[0, t] or structure[1, t] is 1 for a tile t of supernode 3, structure[2, t] is 1 too. `factor`: the diagonal supernode blocks of F are symmetric.
All inputs are finite; a program needn't handle non-finite values.
Results may differ from a plain program's by a relative error of at most 0.000055.
Values sent between devices are 32-bit elements; how exact they have to be, the bound alone decides.
No kernel may reach another device: no remote copies, remote signals or barrier semaphores. Data moves between devices by JAX's collectives and lax.ppermute only.
A program may use at most 64 MiB of HBM per device.

v0:
```python
import jax
import jax.numpy as jnp
import numpy as np
from jax import lax
from jax.sharding import PartitionSpec as P

W = 2048
TB = 128


HIGH = lax.Precision.HIGHEST


def ordered_columns(panel, col_parts, nodes, tile):
    height = panel.shape[0]
    node_tiles = panel.shape[1] // (col_parts * nodes * tile) * col_parts
    shaped = panel.reshape(height, col_parts, nodes, node_tiles // col_parts, tile)
    shaped = shaped.transpose(0, 2, 3, 1, 4)
    return shaped.transpose(0, 3, 1, 2, 4)


def ordered_rows(panel, row_parts, nodes, tile):
    breadth = panel.shape[1]
    node_tiles = panel.shape[0] // (row_parts * nodes * tile) * row_parts
    shaped = panel.reshape(row_parts, nodes, node_tiles // row_parts, tile, breadth)
    shaped = shaped.transpose(1, 2, 0, 3, 4)
    return shaped


def fold_product(piece, lower_panel):
    nodes = lower_panel.shape[0]
    col_tiles = lower_panel.shape[1]
    tile = lower_panel.shape[3]
    unit = nodes * col_tiles * tile
    shards = piece.shape[1] // unit
    blocks = piece.reshape(piece.shape[0], shards, nodes, col_tiles, tile)
    return jnp.einsum("rknbt,nbktc->rc", blocks, lower_panel, precision=HIGH)


def scatter_term(count, ordered, right):
    term = jnp.einsum("tpnar,tnc->pnarc", ordered, right, precision=HIGH)
    return term.reshape(count, right.shape[2])


def body(factor, structure):
    row_parts = lax.axis_size("row")
    col_parts = lax.axis_size("col")
    row_place = lax.axis_index("row")
    col_place = lax.axis_index("col")
    row_count = factor.shape[0]
    tile = factor.shape[1]
    col_count = factor.shape[2]
    node_tiles = W // TB
    row_tiles = node_tiles // row_parts
    col_tiles = node_tiles // col_parts
    row_height = row_tiles * tile
    col_width = col_tiles * tile
    row_mask = lax.dynamic_index_in_dim(
        structure.reshape(4, row_count, row_parts), row_place, axis=2, keepdims=False
    )
    col_mask = lax.dynamic_index_in_dim(
        structure.reshape(4, col_count, col_parts), col_place, axis=2, keepdims=False
    )
    node_pick = (np.arange(col_count)[:, None] // col_tiles == np.arange(4)[None, :]).astype(
        np.float32
    )
    tile_mask = jnp.dot(node_pick, row_mask.astype(jnp.float32)).T
    cell_mask = jnp.broadcast_to(tile_mask[:, None, :, None], factor.shape).reshape(
        row_count * tile, col_count * tile
    )
    matrix = factor.reshape(row_count * tile, col_count * tile)
    lower = matrix * cell_mask

    def region(array, row_node, col_node, row_nodes, col_nodes):
        return array[
            row_node * row_height : (row_node + row_nodes) * row_height,
            col_node * col_width : (col_node + col_nodes) * col_width,
        ]

    root_block = region(matrix, 3, 3, 1, 1)
    lower_one = region(lower, 3, 2, 1, 1)
    column_one = lax.all_gather(lower_one, "row", axis=0, tiled=True)
    sorted_one = ordered_rows(column_one, row_parts, 1, tile)
    product_one = fold_product(
        lax.all_gather(root_block, "col", axis=1, tiled=True), lower_panel=sorted_one
    )
    image_one = -product_one * region(cell_mask, 3, 2, 1, 1)
    mirror_mask = jnp.repeat(col_mask[2, 3 * col_tiles : 4 * col_tiles], tile).astype(jnp.float32)[
        None, :
    ]
    image_panel = lax.all_gather(image_one, "col", axis=1, tiled=True)
    image_sorted = ordered_columns(image_panel, col_parts, 1, tile)
    sums_one = lax.psum_scatter(
        scatter_term(
            row_height * lax.axis_size("row"), ordered=image_sorted, right=lower_one[:, None, :]
        ),
        "row",
        scatter_dimension=0,
        tiled=True,
    )
    factor_panel = lax.all_gather(lower_one, "col", axis=1, tiled=True)
    factor_sorted = ordered_columns(factor_panel, col_parts, 1, tile)
    cross_one = lax.psum_scatter(
        scatter_term(
            row_height * lax.axis_size("row"), ordered=factor_sorted, right=root_block[:, None, :]
        ),
        "row",
        scatter_dimension=0,
        tiled=True,
    )
    inner_two = region(matrix, 2, 2, 1, 1) - sums_one
    mirror_one = -cross_one * mirror_mask
    ancestors = jnp.concatenate(
        [
            jnp.concatenate([inner_two, mirror_one], axis=1),
            jnp.concatenate([image_one, root_block], axis=1),
        ],
        axis=0,
    )
    lower_two = region(lower, 2, 0, 2, 2)
    column_two = lax.all_gather(lower_two, "row", axis=0, tiled=True)
    sorted_two = ordered_rows(column_two, row_parts, 2, tile)
    product_two = fold_product(
        lax.all_gather(ancestors, "col", axis=1, tiled=True), lower_panel=sorted_two
    )
    image_two = -product_two * region(cell_mask, 2, 0, 2, 2)
    panel_two = lax.all_gather(image_two, "col", axis=1, tiled=True)
    right_two = lower_two.reshape(2 * row_height, 2, col_width)
    sorted_cols = ordered_columns(panel_two, col_parts, 2, tile)
    sums_two = lax.psum_scatter(
        scatter_term(2 * row_height * lax.axis_size("row"), ordered=sorted_cols, right=right_two),
        "row",
        scatter_dimension=0,
        tiled=True,
    )
    sums_two = sums_two.reshape(2, row_height, col_width)
    inner_zero = region(matrix, 0, 0, 1, 1) - sums_two[0]
    inner_first = region(matrix, 1, 1, 1, 1) - sums_two[1]
    result = jnp.zeros_like(matrix)
    result = result.at[0:row_height, 0:col_width].set(inner_zero)
    result = result.at[row_height : 2 * row_height, col_width : 2 * col_width].set(inner_first)
    result = result.at[2 * row_height : 4 * row_height, 0 : 2 * col_width].set(image_two)
    result = result.at[2 * row_height : 3 * row_height, 2 * col_width : 3 * col_width].set(
        inner_two
    )
    result = result.at[3 * row_height : 4 * row_height, 2 * col_width : 3 * col_width].set(
        image_one
    )
    result = result.at[3 * row_height : 4 * row_height, 3 * col_width : 4 * col_width].set(
        root_block
    )
    return result.reshape(factor.shape)


def solution(mesh):
    return jax.shard_map(
        body,
        mesh=mesh,
        in_specs=(P(None, "row", None, "col"), P()),
        out_specs=P(None, "row", None, "col"),
        check_vma=False,
    )
```

profile of v0, /device:TPU:32, one launch (start us, length us, event | category | flops | bytes accessed | tf_op | source)
XLA Modules:
  0.0 600.3 jit_solution(13026006305057683345)
XLA Ops:
  7.5 1.3 copy.46
  11.9 1.0 copy.45
  12.9 48.5 %all-gather.8.cloned.1.call-done = f32[2048,128]{0,1:T(8,128)} async-done(((f32[128,128]{0,1:T(8,128)}), f32[2048,128]{0,1:T(8,128)}) %all-gather.8.cloned.1.call-update) | async-done | bytes 1048592 | tf_op jit(solution)/shard_map/all_gather | solution.py:82
  61.5 39.4 %all-gather.10.cloned.1.call-done = f32[128,2048]{0,1:T(8,128)} async-done(((f32[128,128]{0,1:T(8,128)}), f32[128,2048]{0,1:T(8,128)}) %all-gather.10.cloned.1.call-update) | async-done | bytes 1048592 | tf_op jit(solution)/shard_map/all_gather | solution.py:85
  100.8 3.3 fusion.8
  104.2 35.8 %all-gather.14.cloned.1.call-done = f32[128,2048]{0,1:T(8,128)} async-done(((f32[128,128]{0,1:T(8,128)}), f32[128,2048]{0,1:T(8,128)}) %all-gather.14.cloned.1.call-update) | async-done | bytes 1048592 | tf_op jit(solution)/shard_map/all_gather | solution.py:101
  140.0 2.2 fusion.10
  142.2 1.3 copy.30
  143.6 35.3 %all-gather.12.cloned.1.call-done = f32[128,2048]{0,1:T(8,128)} async-done(((f32[128,128]{0,1:T(8,128)}), f32[128,2048]{0,1:T(8,128)}) %all-gather.12.cloned.1.call-update) | async-done | bytes 1048592 | tf_op jit(solution)/shard_map/all_gather | solution.py:91
  178.9 2.2 convolution_bitcast_fusion
  181.2 1.3 copy.28
  184.7 74.7 %reduce-scatter.6.cloned.1.call-done = f32[128,128]{0,1:T(8,128)} async-done(((f32[2048,128]{0,1:T(8,128)}), f32[128,128]{0,1:T(8,128)}) %reduce-scatter.6.cloned.1.call-update) | async-done | bytes 65552 | tf_op jit(solution)/shard_map/reduce_scatter | solution.py:103
  260.3 80.3 %reduce-scatter.4.cloned.1.call-done = f32[128,128]{0,1:T(8,128)} async-done(((f32[2048,128]{0,1:T(8,128)}), f32[128,128]{0,1:T(8,128)}) %reduce-scatter.4.cloned.1.call-update) | async-done | bytes 65552 | tf_op jit(solution)/shard_map/reduce_scatter | solution.py:93
  342.5 62.6 %all-gather.18.cloned.1.call-done = f32[4096,256]{0,1:T(8,128)} async-done(((f32[256,256]{0,1:T(8,128)}), f32[4096,256]{0,1:T(8,128)}) %all-gather.18.cloned.1.call-update) | async-done | bytes 4194320 | tf_op jit(solution)/shard_map/all_gather | solution.py:121
  405.0 5.6 copy.31
  410.7 37.5 %all-gather.16.cloned.1.call-done = f32[256,4096]{0,1:T(8,128)} async-done(((f32[256,256]{0,1:T(8,128)}), f32[256,4096]{0,1:T(8,128)}) %all-gather.16.cloned.1.call-update) | async-done | bytes 4194320 | tf_op jit(solution)/shard_map/all_gather | solution.py:124
  448.2 10.9 %fusion.6 = f32[256,256]{0,1:T(8,128)} fusion(f32[256,16,2,128]{0,3,2,1:T(8,128)} %bitcast.82, f32[2,16,128,256]{3,2,0,1:T(8,128)} %bitcast.79, f32[512,512]{0,1:T(8,128)} %bitcast.88), kind=kOutput, calls=%fused_computation.6 | convolution fusion | flops 3221356544 | bytes 8912896 | tf_op jit(solution)/shard_map/rknbt,nbktc->rc/dot_general | solution.py:37
  459.2 40.8 %all-gather.20.cloned.1.call-done = f32[256,4096]{0,1:T(8,128)} async-done(((f32[256,256]{0,1:T(8,128)}), f32[256,4096]{0,1:T(8,128)}) %all-gather.20.cloned.1.call-update) | async-done | bytes 4194320 | tf_op jit(solution)/shard_map/all_gather | solution.py:127
  499.9 5.2 fusion.2
  505.2 2.4 copy.17
  507.6 3.9 reshape.261
  511.5 78.3 %reduce-scatter.8.cloned.1.call-done = f32[256,128]{0,1:T(8,128)} async-done(((f32[4096,128]{0,1:T(8,128)}), f32[256,128]{0,1:T(8,128)}) %reduce-scatter.8.cloned.1.call-update) | async-done | bytes 131088 | tf_op jit(solution)/shard_map/reduce_scatter | solution.py:130
  590.8 0.9 fusion.9
  592.1 1.3 copy.18
  (52 shorter events, 9.8 us)
Async XLA Ops:
  6.5 2.6 copy-start.4
  6.5 54.9 %all-gather.8.cloned.1.call-start = ((), (), s32[]{:S(2)}) async-start(), calls=%async_computation.3 | async-start | bytes 1114112 | tf_op jit(solution)/shard_map/all_gather | solution.py:82
  10.4 90.5 %all-gather.10.cloned.1.call-start = ((), (), s32[]{:S(2)}) async-start(), calls=%async_computation.4 | async-start | bytes 1114112 | tf_op jit(solution)/shard_map/all_gather | solution.py:85
  11.1 128.9 %all-gather.14.cloned.1.call-start = ((), (), s32[]{:S(2)}) async-start(), calls=%async_computation.7 | async-start | bytes 1114112 | tf_op jit(solution)/shard_map/all_gather | solution.py:101
  11.8 167.1 %all-gather.12.cloned.1.call-start = ((), (), s32[]{:S(2)}) async-start(), calls=%async_computation.5 | async-start | bytes 1114112 | tf_op jit(solution)/shard_map/all_gather | solution.py:91
  104.2 155.3 %reduce-scatter.6.cloned.1.call-start = ((), (), s32[]{:S(2)}) async-start(), calls=%async_computation.8 | async-start | bytes 1114112 | tf_op jit(solution)/shard_map/reduce_scatter | solution.py:103
  143.5 197.9 %copy-start.2 = (f32[128,128]{0,1:T(8,128)S(1)}, f32[128,128]{0,1:T(8,128)}, u32[]{:S(2)}) copy-start(f32[128,128]{0,1:T(8,128)} %fusion.8) | copy-start | bytes 196612
  143.5 197.9 %copy-start.3 = (f32[128,128]{0,1:T(8,128)S(1)}, f32[128,128]{0,1:T(8,128)}, u32[]{:S(2)}) copy-start(f32[128,128]{0,1:T(8,128)} %slice.179) | copy-start | bytes 196612
  143.5 197.1 %reduce-scatter.4.cloned.1.call-start = ((), (), s32[]{:S(2)}) async-start(), calls=%async_computation.6 | async-start | bytes 1114112 | tf_op jit(solution)/shard_map/reduce_scatter | solution.py:93
  182.5 222.5 %all-gather.18.cloned.1.call-start = ((), (), s32[]{:S(2)}) async-start(), calls=%async_computation.10 | async-start | bytes 4456448 | tf_op jit(solution)/shard_map/all_gather | solution.py:121
  183.3 264.8 %all-gather.16.cloned.1.call-start = ((), (), s32[]{:S(2)}) async-start(), calls=%async_computation.9 | async-start | bytes 4456448 | tf_op jit(solution)/shard_map/all_gather | solution.py:124
  342.2 157.7 %all-gather.20.cloned.1.call-start = ((), (), s32[]{:S(2)}) async-start(), calls=%async_computation.11 | async-start | bytes 4456448 | tf_op jit(solution)/shard_map/all_gather | solution.py:127
  448.1 51.8 %copy-start = (f32[256,256]{0,1:T(8,128)S(1)}, f32[256,256]{0,1:T(8,128)}, u32[]{:S(2)}) copy-start(f32[256,256]{0,1:T(8,128)} %slice.176) | copy-start | bytes 786436
  459.1 130.7 %reduce-scatter.8.cloned.1.call-start = ((), (), s32[]{:S(2)}) async-start(), calls=%async_computation.12 | async-start | bytes 2228224 | tf_op jit(solution)/shard_map/reduce_scatter | solution.py:130
  507.6 84.1 %copy-start.1 = (f32[256,256]{0,1:T(8,128)S(1)}, f32[256,256]{0,1:T(8,128)}, u32[]{:S(2)}) copy-start(f32[256,256]{0,1:T(8,128)} %fusion.6) | copy-start | bytes 786436
Sparse Core Ops, SparseCore 0:
  10.5 50.9 all-gather.7
  63.3 37.5 all-gather.9
  102.7 37.2 all-gather.13
  141.6 37.2 all-gather.11
  182.3 77.1 reduce-scatter.5
  263.2 77.3 reduce-scatter.3
  343.0 61.9 all-gather.17
  406.9 41.2 all-gather.15
  459.2 40.6 all-gather.19
  511.6 78.1 reduce-scatter.7
where the time goes:
time: 601 us; the launch traced here: 600 us
  waiting for transfers between devices  534 us (89%)
  matrix products  24 us (4%)
  local copies, waits for them, and re-layouts  23 us (4%)
  between operations  14.3 us (2%)
    reduce_scatter x2, waiting for transfers between devices, body(): lax.psum_scatter(scatter_term(row_height * lax.axis_size('row'), ordered=...  155 us
    reduce_scatter x1, waiting for transfers between devices, body(): lax.psum_scatter(scatter_term(2 * row_height * lax.axis_size('row'), orde...  78.3 us
    all_gather x1, waiting for transfers between devices, body(): column_two = lax.all_gather(lower_two, 'row', axis=0, tiled=True)  62.6 us
    all_gather x1, waiting for transfers between devices, body(): column_one = lax.all_gather(lower_one, 'row', axis=0, tiled=True)  48.5 us
    all_gather x1, waiting for transfers between devices, body(): panel_two = lax.all_gather(image_two, 'col', axis=1, tiled=True)  40.8 us
    all_gather x1, waiting for transfers between devices, body(): lax.all_gather(root_block, 'col', axis=1, tiled=True)  39.4 us
    all_gather x1, waiting for transfers between devices, body(): lax.all_gather(ancestors, 'col', axis=1, tiled=True)  37.5 us
    all_gather x1, waiting for transfers between devices, body(): factor_panel = lax.all_gather(lower_one, 'col', axis=1, tiled=True)  35.8 us
  transfers between devices with their start and end apart: 10, of which 10 were waited for; matrix products, arithmetic and copies ran while one was open for 4% of the time, Pallas kernels for 0%

commit v1 on v0

v1 whole, which is shorter than its diff:
```python
import jax
import jax.numpy as jnp
from jax import lax
from jax.sharding import PartitionSpec as P

N = 16
TB = 128
HIGH = lax.Precision.HIGH
PAIR_SWAP = [(i, i ^ 1) for i in range(N)]
SAME_PARITY = [[p + 2 * i for i in range(N // 2)] for p in range(2)]


def swap_rows(x):
    return lax.ppermute(x, "row", PAIR_SWAP)


def gather_layers_start(x):
    parts = [x]
    for d in range(1, N // 2):
        parts.append(lax.ppermute(x, "col", [((i + 2 * d) % N, i) for i in range(N)]))
    return parts


def gather_layers_end(parts, layer, core):
    mine = jnp.zeros((N // 2,) + parts[0].shape, parts[0].dtype)
    for d, part in enumerate(parts):
        mine = lax.dynamic_update_index_in_dim(mine, part, lax.rem(layer + d, N // 2), 0)
    other = lax.ppermute(mine, "col", PAIR_SWAP)
    even = jnp.where(core == 0, mine, other)
    odd = jnp.where(core == 0, other, mine)
    return jnp.stack([even, odd])


def by_parity(panel):
    return panel.reshape((N // 2, 2) + panel.shape[1:]).swapaxes(0, 1)


def times(left, right):
    return jnp.einsum("pkmab,pkbc->mac", left, right, precision=HIGH)


def spread(left, right):
    out = jnp.einsum("pkmab,mac->kpcb", left, right, precision=HIGH)
    return out.reshape(N, TB, TB)


def body(factor, structure):
    row = lax.axis_index("row")
    col = lax.axis_index("col")
    side = lax.rem(row, 2)
    layer = col // 2
    core = lax.rem(col, 2)

    def pair(own, other):
        return jnp.where(side == 0, jnp.stack([own, other]), jnp.stack([other, own]))

    def pick(zero, one):
        return jnp.where(side == 0, zero, one)

    mask = structure.reshape(4, 4, N)
    mask = lax.dynamic_index_in_dim(mask, row, axis=2, keepdims=False) == 1

    def block(r, c):
        return factor[r, :, c, :]

    def lower(r, c):
        return jnp.where(mask[c, r], block(r, c), 0.0)

    root = block(3, 3)
    lower_32 = lower(3, 2)
    lower_2 = [lower(2, 0), lower(2, 1)]
    lower_3 = [lower(3, 0), lower(3, 1)]
    diag_2 = block(2, 2)

    with jax.named_scope("swap_first"):
        lower_32_pair = pair(lower_32, swap_rows(lower_32))
    with jax.named_scope("gather_l32"):
        parts_32 = gather_layers_start(lower_32_pair)
    with jax.named_scope("gather_l2"):
        send = jnp.broadcast_to(jnp.stack(lower_2)[None], (N // 2, 2, TB, TB)).reshape(N, TB, TB)
        l2_cols = by_parity(lax.all_to_all(send, "row", 0, 0, tiled=True))
    with jax.named_scope("swap_rest"):
        rest = jnp.stack([root, diag_2, pick(lower_2[1], lower_2[0]), pick(lower_3[1], lower_3[0])])
        other = swap_rows(rest)
    l2_pair = pair(pick(lower_2[0], lower_2[1]), other[2])
    l3_pair = pair(pick(lower_3[0], lower_3[1]), other[3])
    with jax.named_scope("sc_rows"):
        packed = jnp.concatenate([pair(root, other[0]), pair(diag_2, other[1]), l2_pair])
        panels = by_parity(lax.all_gather(packed, "col", axis=0))
        root_rows, diag_rows, l2_rows = panels[:, :, 0:2], panels[:, :, 2:4], panels[:, :, 4:6]
    with jax.named_scope("sc_l32_cols"):
        l32_cols = by_parity(lax.all_gather(lower_32, "row", axis=0))
    with jax.named_scope("gather_l32"):
        l32_rows = gather_layers_end(parts_32, layer, core)
    with jax.named_scope("term_t"):
        t_pair = times(l32_rows, l2_cols) - l3_pair
    with jax.named_scope("gather_t_rows"):
        parts_t = gather_layers_start(t_pair)
    with jax.named_scope("gather_t_cols"):
        send = jnp.broadcast_to(t_pair[None], (N // 2, 2, TB, TB))
        t_cols = lax.all_to_all(send, "row", 0, 0, tiled=True, axis_index_groups=SAME_PARITY)
        t_cols = t_cols.swapaxes(0, 1)
    with jax.named_scope("term_y"):
        y_pair = times(root_rows, t_cols)
    with jax.named_scope("term_u"):
        u_pair = times(diag_rows, l2_cols)
    with jax.named_scope("term_q"):
        root_own = lax.dynamic_index_in_dim(root_rows, side, axis=2)
        l32_own = lax.dynamic_index_in_dim(l32_rows, side, axis=2)
        q = times(root_own, l32_cols)
    with jax.named_scope("gather_t_rows"):
        t_rows = gather_layers_end(parts_t, layer, core)
    with jax.named_scope("swap_y"):
        y_away = swap_rows(pick(y_pair[1], y_pair[0]))
        y_home = pick(y_pair[0], y_pair[1])
    with jax.named_scope("sums"):
        start = row - side
        x_sum = spread(l32_rows, y_pair)
        x_sum = lax.dynamic_update_slice_in_dim(
            x_sum,
            lax.dynamic_slice_in_dim(x_sum, start, 2, 0) + u_pair.swapaxes(1, 2),
            start,
            0,
        )
        z_sum = spread(
            jnp.concatenate([t_rows, l2_rows], axis=2), jnp.concatenate([y_pair, u_pair])
        )
        q_sum = spread(l32_own, q)
        send = jnp.stack([x_sum, z_sum, q_sum], axis=1)
    with jax.named_scope("scatter_sums"):
        got = lax.all_to_all(send, "row", 0, 0, tiled=True)
    with jax.named_scope("finish"):
        both = got[:, :2].reshape(N // 2, 2, 2, TB, TB).sum(axis=0)
        x_two = -both[:, 0].swapaxes(1, 2)
        inner = both[:, 1].swapaxes(1, 2)
        inner_two = diag_2 + got[:, 2].sum(axis=0).T
        y_zero = pick(y_home, y_away)
        y_one = pick(y_away, y_home)
        empty = jnp.zeros((TB, TB), factor.dtype)

        def masked(s, r, x):
            return jnp.where(mask[s, r], x, 0.0)

        tiles = [
            [block(0, 0) + inner[0], empty, empty, empty],
            [empty, block(1, 1) + inner[1], empty, empty],
            [masked(0, 2, x_two[0]), masked(1, 2, x_two[1]), inner_two, empty],
            [masked(0, 3, y_zero), masked(1, 3, y_one), masked(2, 3, -q[0]), root],
        ]
        return jnp.stack([jnp.stack(t, axis=1) for t in tiles])


def solution(mesh):
    return jax.shard_map(
        body,
        mesh=mesh,
        in_specs=(P(None, "row", None, "col"), P()),
        out_specs=P(None, "row", None, "col"),
        check_vma=False,
    )
```

time: 601 us -> 242 us (0.40)
  waiting for transfers between devices: 534 us -> 106 us
  starting transfers between devices: 0.56 us -> 52.9 us
  other arithmetic: 4.34 us -> 20.1 us
  local copies, waits for them, and re-layouts: 23 us -> 37.2 us
  matrix products: 24 us -> 10.4 us
    all_gather x7 -> x2, waiting for transfers between devices: 300 us -> 5.72 us  [the longest x1 5.72 us: body(): l32_cols = by_parity(lax.all_gather(lower_32, 'row', axis=0))]
    reduce_scatter x3 -> x0, waiting for transfers between devices: 233 us -> none  [the longest x2 155 us: body(): lax.psum_scatter(scatter_term(row_height * lax.axis_size('row'), ordered=...]
    ppermute x0 -> x19, waiting for transfers between devices: none -> 80.4 us  [the longest x3 42.2 us: swap_rows(): return lax.ppermute(x, 'row', PAIR_SWAP)]
    ppermute x0 -> x19, starting transfers between devices: none -> 35.3 us  [the longest x14 29.9 us: gather_layers_start(): lax.ppermute(x, 'col', [((i + 2 * d) % N, i) for i in range(N)])]
    all_to_all x0 -> x3, waiting for transfers between devices: none -> 19.8 us  [the longest x1 16.5 us: body(): l2_cols = by_parity(lax.all_to_all(send, 'row', 0, 0, tiled=True))]
    all_to_all x0 -> x3, starting transfers between devices: none -> 17.5 us  [the longest x1 7.5 us: body(): l2_cols = by_parity(lax.all_to_all(send, 'row', 0, 0, tiled=True))]
    dot_general x5 -> x7, matrix products: 21.8 us -> 10.4 us  [the longest x4 7.7 us: times(): return jnp.einsum('pkmab,pkbc->mac', left, right, precision=HIGH)]
    reshape x8 -> x2, local copies, waits for them, and re-layouts: 15 us -> 4.03 us  [the longest x1 3.27 us: by_parity(): return panel.reshape((N // 2, 2) + panel.shape[1:]).swapaxes(0, 1)]
  transfers between devices with their start and end apart: 10 -> 24, of which waited for: 10 -> 15; matrix products, arithmetic and copies ran while one was open for 4% -> 13% of each run, Pallas kernels for 0% -> 0%
where the time goes in v1:
time: 242 us; the launch traced here: 241 us
  waiting for transfers between devices  106 us (44%)
  starting transfers between devices  52.9 us (22%)
  local copies, waits for them, and re-layouts  37.2 us (15%)
  other arithmetic  20.1 us (8%)
  between operations  14 us (6%)
  matrix products  10.4 us (4%)
    ppermute x3, waiting for transfers between devices, swap_rows(): return lax.ppermute(x, 'row', PAIR_SWAP)  42.2 us
    ppermute x14, waiting for transfers between devices, gather_layers_start(): lax.ppermute(x, 'col', [((i + 2 * d) % N, i) for i in range(N)])  38.2 us
    ppermute x14, starting transfers between devices, gather_layers_start(): lax.ppermute(x, 'col', [((i + 2 * d) % N, i) for i in range(N)])  29.9 us
    all_to_all x1, waiting for transfers between devices, body(): l2_cols = by_parity(lax.all_to_all(send, 'row', 0, 0, tiled=True))  16.5 us
    dot_general x4, matrix products, times(): return jnp.einsum('pkmab,pkbc->mac', left, right, precision=HIGH)  7.7 us
    all_to_all x1, starting transfers between devices, body(): l2_cols = by_parity(lax.all_to_all(send, 'row', 0, 0, tiled=True))  7.5 us
    unnamed x23, local copies, waits for them, and re-layouts  6.38 us
    all_gather x1, waiting for transfers between devices, body(): l32_cols = by_parity(lax.all_gather(lower_32, 'row', axis=0))  5.72 us
  transfers between devices with their start and end apart: 24, of which 15 were waited for; matrix products, arithmetic and copies ran while one was open for 13% of the time, Pallas kernels for 0%

profile of v1, /device:TPU:32, one launch (start us, length us, event | category | flops | bytes accessed | tf_op | source)
XLA Modules:
  0.0 240.5 jit_solution(18321873699155699099)
XLA Ops:
  6.5 3.0 %fusion.43 = (f32[1,128,1,128]{3,2,1,0:T(1,128)}, f32[1,128,1,128]{3,2,1,0:T(1,128)S(1)}, f32[1,128,1,128]{3,2,1,0:T(1,128)S(1)}, f32[1,128,1,128]{3,2,1,0:T(1,1...) fusion(f32[4,128,4,128]{3,2,1,0:T(4,128)} %param.2), kind=kLoop, calls=%fused_computation.107 | loop fusion | bytes 1179648 | tf_op jit(solution)/shard_map/finish/slice | solution.py:64
  15.4 6.5 %collective-permute-done = f32[4,128,128]{2,1,0:T(8,128)S(1)} collective-permute-done((f32[4,128,128]{2,1,0:T(8,128)S(1)}, f32[4,128,128]{2,1,0:T(8,128)S(1)}, u32[]{:S(2)}, u32[]{:S(2)}) %collective-permute-start) | collective-permute-done | bytes 262176 | tf_op jit(solution)/shard_map/swap_rest/ppermute | solution.py:14
  29.4 6.3 %collective-permute-start.3 = (f32[2,128,128]{2,1,0:T(8,128)S(1)}, f32[2,128,128]{2,1,0:T(8,128)S(1)}, u32[]{:S(2)}, u32[]{:S(2)}) collective-permute-start(f32[2,128,128]{2,1,0:T(8,128)S(1)} %maximum_select_fusion.4), channel_id=1, source_target_pairs={{4,0},{5,1},{6,2},{7,3},{8,4},{9,5},{10,6},{11,7},{12,8},{13,9},{1... | collective-permute-start | bytes 393224 | tf_op jit(solution)/shard_map/gather_l32/ppermute | solution.py:20
  36.7 4.5 %collective-permute-start.5 = (f32[2,128,128]{2,1,0:T(8,128)S(1)}, f32[2,128,128]{2,1,0:T(8,128)S(1)}, u32[]{:S(2)}, u32[]{:S(2)}) collective-permute-start(f32[2,128,128]{2,1,0:T(8,128)S(1)} %maximum_select_fusion.4), channel_id=1, source_target_pairs={{8,0},{9,1},{10,2},{11,3},{12,4},{13,5},{14,6},{15,7},{0,8},{1,9},... | collective-permute-start | bytes 393224 | tf_op jit(solution)/shard_map/gather_l32/ppermute | solution.py:20
  41.9 2.9 %collective-permute-start.7 = (f32[2,128,128]{2,1,0:T(8,128)S(1)}, f32[2,128,128]{2,1,0:T(8,128)S(1)}, u32[]{:S(2)}, u32[]{:S(2)}) collective-permute-start(f32[2,128,128]{2,1,0:T(8,128)S(1)} %maximum_select_fusion.4), channel_id=1, source_target_pairs={{12,0},{13,1},{14,2},{15,3},{0,4},{1,5},{2,6},{3,7},{4,8},{5,9},{6... | collective-permute-start | bytes 393224 | tf_op jit(solution)/shard_map/gather_l32/ppermute | solution.py:20
  44.8 2.9 %collective-permute-done.3 = f32[2,128,128]{2,1,0:T(8,128)S(1)} collective-permute-done((f32[2,128,128]{2,1,0:T(8,128)S(1)}, f32[2,128,128]{2,1,0:T(8,128)S(1)}, u32[]{:S(2)}, u32[]{:S(2)}) %collective-permute-start.3) | collective-permute-done | bytes 131104 | tf_op jit(solution)/shard_map/gather_l32/ppermute | solution.py:20
  47.7 9.3 %collective-permute-done.4 = f32[2,128,128]{2,1,0:T(8,128)S(1)} collective-permute-done((f32[2,128,128]{2,1,0:T(8,128)S(1)}, f32[2,128,128]{2,1,0:T(8,128)S(1)}, u32[]{:S(2)}, u32[]{:S(2)}) %collective-permute-start.4) | collective-permute-done | bytes 131104 | tf_op jit(solution)/shard_map/gather_l32/ppermute | solution.py:20
  57.0 7.9 %collective-permute-done.5 = f32[2,128,128]{2,1,0:T(8,128)S(1)} collective-permute-done((f32[2,128,128]{2,1,0:T(8,128)S(1)}, f32[2,128,128]{2,1,0:T(8,128)S(1)}, u32[]{:S(2)}, u32[]{:S(2)}) %collective-permute-start.5) | collective-permute-done | bytes 131104 | tf_op jit(solution)/shard_map/gather_l32/ppermute | solution.py:20
  65.6 5.8 %collective-permute-done.8 = f32[2,128,128]{2,1,0:T(8,128)S(1)} collective-permute-done((f32[2,128,128]{2,1,0:T(8,128)S(1)}, f32[2,128,128]{2,1,0:T(8,128)S(1)}, u32[]{:S(2)}, u32[]{:S(2)}) %collective-permute-start.8) | collective-permute-done | bytes 131104 | tf_op jit(solution)/shard_map/gather_l32/ppermute | solution.py:20
  72.7 7.5 %all-to-all-start = ((f32[16,128,128]{2,1,0:T(8,128)}), f32[16,128,128]{2,1,0:T(8,128)S(1)}, u32[]{:S(2)}, u32[]{:S(2)}) async-start(f32[16,128,128]{2,1,0:T(8,128)} %bitcast.29), calls=%async_computation | async-start | bytes 2097152 | tf_op jit(solution)/shard_map/gather_l2/all_to_all | solution.py:81
  82.0 16.5 %all-to-all-done = f32[16,128,128]{2,1,0:T(8,128)S(1)} async-done(((f32[16,128,128]{2,1,0:T(8,128)}), f32[16,128,128]{2,1,0:T(8,128)S(1)}, u32[]{:S(2)}, u32[]{:S(2)}) %all-to-all-start) | async-done | bytes 1048608 | tf_op jit(solution)/shard_map/gather_l2/all_to_all | solution.py:81
  103.0 3.5 %collective-permute-start.11 = (f32[2,128,128]{2,1,0:T(8,128)}, f32[2,128,128]{2,1,0:T(8,128)S(1)}, u32[]{:S(2)}, u32[]{:S(2)}) collective-permute-start(f32[2,128,128]{2,1,0:T(8,128)} %get-tuple-element.47), channel_id=1, source_target_pairs={{4,0},{5,1},{6,2},{7,3},{8,4},{9,5},{10,6},{11,7},{12,8},{13,9},{1... | collective-permute-start | bytes 393224 | tf_op jit(solution)/shard_map/gather_t_rows/ppermute | solution.py:20
  108.6 4.4 %collective-permute-start.13 = (f32[2,128,128]{2,1,0:T(8,128)}, f32[2,128,128]{2,1,0:T(8,128)S(1)}, u32[]{:S(2)}, u32[]{:S(2)}) collective-permute-start(f32[2,128,128]{2,1,0:T(8,128)} %get-tuple-element.47), channel_id=1, source_target_pairs={{8,0},{9,1},{10,2},{11,3},{12,4},{13,5},{14,6},{15,7},{0,8},{1,9},... | collective-permute-start | bytes 393224 | tf_op jit(solution)/shard_map/gather_t_rows/ppermute | solution.py:20
  119.2 3.9 %collective-permute-done.12 = f32[2,128,128]{2,1,0:T(8,128)S(1)} collective-permute-done((f32[2,128,128]{2,1,0:T(8,128)}, f32[2,128,128]{2,1,0:T(8,128)S(1)}, u32[]{:S(2)}, u32[]{:S(2)}) %collective-permute-start.12) | collective-permute-done | bytes 131104 | tf_op jit(solution)/shard_map/gather_t_rows/ppermute | solution.py:20
  123.7 4.4 %collective-permute-done.13 = f32[2,128,128]{2,1,0:T(8,128)S(1)} collective-permute-done((f32[2,128,128]{2,1,0:T(8,128)}, f32[2,128,128]{2,1,0:T(8,128)S(1)}, u32[]{:S(2)}, u32[]{:S(2)}) %collective-permute-start.13) | collective-permute-done | bytes 131104 | tf_op jit(solution)/shard_map/gather_t_rows/ppermute | solution.py:20
  136.2 4.6 %all-to-all-start.1 = ((f32[8,2,128,128]{3,2,1,0:T(8,128)}), f32[8,2,128,128]{3,2,1,0:T(8,128)}, u32[]{:S(2)}, u32[]{:S(2)}) async-start(f32[8,2,128,128]{3,2,1,0:T(8,128)} %broadcast_in_dim.83), calls=%async_computation.1 | async-start | bytes 2097152 | tf_op jit(solution)/shard_map/gather_t_cols/all_to_all | solution.py:101
  140.8 3.1 %select_bitcast_fusion.1 = (f32[1,8,2,128,128]{4,3,2,1,0:T(8,128)}, f32[1,8,2,128,128]{4,3,2,1,0:T(8,128)}) fusion(f32[8,2,128,128]{3,2,1,0:T(8,128)} %bitcast_dynamic-update-slice_fusion, f32[8,2,128,128]{3,2,1,0:T(8,128)} %collective-permute-done.17, pred[]{:T(512)S(6)} %eq.12), kind=kLoop, calls=%fused_computation.33 | loop fusion | flops 524288 | bytes 4194305 | tf_op jit(solution)/shard_map/gather_t_rows/stack | solution.py:31
  143.9 3.3 %copy.194 = f32[8,2,6,128,128]{4,3,2,0,1:T(8,128)S(1)} copy(f32[8,2,6,128,128]{4,3,2,1,0:T(8,128)} %bitcast.237) | data formatting | bytes 12582912 | tf_op jit(solution)/shard_map/sc_rows/reshape | solution.py:35
  147.1 2.8 %fusion.42 = (f32[2,8,2,128,128]{4,3,2,1,0:T(8,128)}, f32[2,8,2,128,128]{4,3,2,1,0:T(8,128)}, f32[2,8,2,128,128]{4,3,2,1,0:T(8,128)}) fusion(f32[2,8,6,128,128]{4,3,2,1,0:T(8,128)S(1)} %bitcast.233), kind=kLoop, calls=%fused_computation.106 | loop fusion | bytes 12582912 | tf_op jit(solution)/shard_map/sc_rows/slice | solution.py:90
  150.0 5.7 %all-gather.7.cloned.1.call-done = f32[16,128,1,128]{3,1,2,0:T(8,128)} async-done(((f32[1,128,1,128]{3,1,2,0:T(8,128)}), f32[16,128,1,128]{3,1,2,0:T(8,128)}) %all-gather.7.cloned.1.call-update) | async-done | bytes 1048592 | tf_op jit(solution)/shard_map/sc_l32_cols/all_gather | solution.py:92
  159.6 2.8 %fusion.10 = f32[2,128,128,1,1]{2,1,0,4,3:T(8,128)S(1)} fusion(f32[2,8,2,128,128]{4,3,2,1,0:T(8,128)} %get-tuple-element.10, f32[8,2,128,128]{3,2,1,0:T(8,128)} %all-to-all-done.1), kind=kOutput, calls=%fused_computation.15 | convolution fusion | flops 402653184 | bytes 3276800 | tf_op jit(solution)/shard_map/term_y/pkmab,pkbc->mac/dot_general | solution.py:39
  175.6 5.4 %all-to-all-start.2 = ((f32[16,3,128,128]{3,2,1,0:T(8,128)}), f32[16,3,128,128]{3,2,1,0:T(8,128)S(1)}, u32[]{:S(2)}, u32[]{:S(2)}) async-start(f32[16,3,128,128]{3,2,1,0:T(8,128)} %copy.139), calls=%async_computation.2 | async-start | bytes 6291456 | tf_op jit(solution)/shard_map/scatter_sums/all_to_all | solution.py:131
  183.7 33.7 %collective-permute-done.18 = f32[128,128]{1,0:T(8,128)S(1)} collective-permute-done((f32[128,128]{1,0:T(8,128)S(1)}, f32[128,128]{1,0:T(8,128)S(1)}, u32[]{:S(2)}, u32[]{:S(2)}) %collective-permute-start.18) | collective-permute-done | bytes 65568 | tf_op jit(solution)/shard_map/swap_y/ppermute | solution.py:14
  219.4 3.4 %all-to-all-done.2 = f32[16,3,128,128]{3,2,1,0:T(8,128)S(1)} async-done(((f32[16,3,128,128]{3,2,1,0:T(8,128)}), f32[16,3,128,128]{3,2,1,0:T(8,128)S(1)}, u32[]{:S(2)}, u32[]{:S(2)}) %all-to-all-start.2) | async-done | bytes 3145760 | tf_op jit(solution)/shard_map/scatter_sums/all_to_all | solution.py:131
  (125 shorter events, 72.5 us)
Async XLA Ops:
  6.5 137.3 %all-gather.5.cloned.1.call-start = ((), (), s32[]{:S(2)}) async-start(), calls=%async_computation.3 | async-start | bytes 6684672 | tf_op jit(solution)/shard_map/sc_rows/all_gather | solution.py:89
  13.8 8.1 %collective-permute-start = (f32[4,128,128]{2,1,0:T(8,128)S(1)}, f32[4,128,128]{2,1,0:T(8,128)S(1)}, u32[]{:S(2)}, u32[]{:S(2)}) collective-permute-start(f32[4,128,128]{2,1,0:T(8,128)S(1)} %pad_maximum_fusion.4), channel_id=1, source_target_pairs={{0,16},{16,0},{32,48},{48,32},{64,80},{80,64},{96,112},{112,96},{1... | collective-permute-start | bytes 786440 | tf_op jit(solution)/shard_map/swap_rest/ppermute | solution.py:14
  24.0 4.4 %collective-permute-start.1 = (f32[128,128]{1,0:T(8,128)S(1)}, f32[128,128]{1,0:T(8,128)S(1)}, u32[]{:S(2)}, u32[]{:S(2)}) collective-permute-start(f32[128,128]{1,0:T(8,128)S(1)} %fusion.53), channel_id=1, source_target_pairs={{0,16},{16,0},{32,48},{48,32},{64,80},{80,64},{96,112},{112,96},{1... | collective-permute-start | bytes 196616 | tf_op jit(solution)/shard_map/swap_first/ppermute | solution.py:14
  28.4 13.5 %collective-permute-start.2 = (f32[2,128,128]{2,1,0:T(8,128)S(1)}, f32[2,128,128]{2,1,0:T(8,128)S(1)}, u32[]{:S(2)}, u32[]{:S(2)}) collective-permute-start(f32[2,128,128]{2,1,0:T(8,128)S(1)} %maximum_select_fusion.4), channel_id=1, source_target_pairs={{2,0},{3,1},{4,2},{5,3},{6,4},{7,5},{8,6},{9,7},{10,8},{11,9},{12,... | collective-permute-start | bytes 393224 | tf_op jit(solution)/shard_map/gather_l32/ppermute | solution.py:20
  29.4 18.3 %collective-permute-start.3 = (f32[2,128,128]{2,1,0:T(8,128)S(1)}, f32[2,128,128]{2,1,0:T(8,128)S(1)}, u32[]{:S(2)}, u32[]{:S(2)}) collective-permute-start(f32[2,128,128]{2,1,0:T(8,128)S(1)} %maximum_select_fusion.4), channel_id=1, source_target_pairs={{4,0},{5,1},{6,2},{7,3},{8,4},{9,5},{10,6},{11,7},{12,8},{13,9},{1... | collective-permute-start | bytes 393224 | tf_op jit(solution)/shard_map/gather_l32/ppermute | solution.py:20
  35.7 21.3 %collective-permute-start.4 = (f32[2,128,128]{2,1,0:T(8,128)S(1)}, f32[2,128,128]{2,1,0:T(8,128)S(1)}, u32[]{:S(2)}, u32[]{:S(2)}) collective-permute-start(f32[2,128,128]{2,1,0:T(8,128)S(1)} %maximum_select_fusion.4), channel_id=1, source_target_pairs={{6,0},{7,1},{8,2},{9,3},{10,4},{11,5},{12,6},{13,7},{14,8},{15,9},... | collective-permute-start | bytes 393224 | tf_op jit(solution)/shard_map/gather_l32/ppermute | solution.py:20
  36.7 28.3 %collective-permute-start.5 = (f32[2,128,128]{2,1,0:T(8,128)S(1)}, f32[2,128,128]{2,1,0:T(8,128)S(1)}, u32[]{:S(2)}, u32[]{:S(2)}) collective-permute-start(f32[2,128,128]{2,1,0:T(8,128)S(1)} %maximum_select_fusion.4), channel_id=1, source_target_pairs={{8,0},{9,1},{10,2},{11,3},{12,4},{13,5},{14,6},{15,7},{0,8},{1,9},... | collective-permute-start | bytes 393224 | tf_op jit(solution)/shard_map/gather_l32/ppermute | solution.py:20
  41.2 23.8 %collective-permute-start.6 = (f32[2,128,128]{2,1,0:T(8,128)S(1)}, f32[2,128,128]{2,1,0:T(8,128)S(1)}, u32[]{:S(2)}, u32[]{:S(2)}) collective-permute-start(f32[2,128,128]{2,1,0:T(8,128)S(1)} %maximum_select_fusion.4), channel_id=1, source_target_pairs={{10,0},{11,1},{12,2},{13,3},{14,4},{15,5},{0,6},{1,7},{2,8},{3,9},... | collective-permute-start | bytes 393224 | tf_op jit(solution)/shard_map/gather_l32/ppermute | solution.py:20
  41.9 23.7 %collective-permute-start.7 = (f32[2,128,128]{2,1,0:T(8,128)S(1)}, f32[2,128,128]{2,1,0:T(8,128)S(1)}, u32[]{:S(2)}, u32[]{:S(2)}) collective-permute-start(f32[2,128,128]{2,1,0:T(8,128)S(1)} %maximum_select_fusion.4), channel_id=1, source_target_pairs={{12,0},{13,1},{14,2},{15,3},{0,4},{1,5},{2,6},{3,7},{4,8},{5,9},{6... | collective-permute-start | bytes 393224 | tf_op jit(solution)/shard_map/gather_l32/ppermute | solution.py:20
  47.7 23.7 %collective-permute-start.8 = (f32[2,128,128]{2,1,0:T(8,128)S(1)}, f32[2,128,128]{2,1,0:T(8,128)S(1)}, u32[]{:S(2)}, u32[]{:S(2)}) collective-permute-start(f32[2,128,128]{2,1,0:T(8,128)S(1)} %maximum_select_fusion.4), channel_id=1, source_target_pairs={{14,0},{15,1},{0,2},{1,3},{2,4},{3,5},{4,6},{5,7},{6,8},{7,9},{8,1... | collective-permute-start | bytes 393224 | tf_op jit(solution)/shard_map/gather_l32/ppermute | solution.py:20
  71.4 8.9 %collective-permute-start.9 = (f32[8,2,128,128]{3,2,1,0:T(8,128)S(1)}, f32[8,2,128,128]{3,2,1,0:T(8,128)}, u32[]{:S(2)}, u32[]{:S(2)}) collective-permute-start(f32[8,2,128,128]{3,2,1,0:T(8,128)S(1)} %bitcast_dynamic-update-slice_fusion.8), channel_id=1, source_target_pairs={{0,1},{1,0},{2,3},{3,2},{4,5},{5,4},{6,7},{7,6},{8,9},{9,8},{10,11... | collective-permute-start | bytes 3145736 | tf_op jit(solution)/shard_map/gather_l32/ppermute | solution.py:28
  72.7 25.8 %all-to-all-start = ((f32[16,128,128]{2,1,0:T(8,128)}), f32[16,128,128]{2,1,0:T(8,128)S(1)}, u32[]{:S(2)}, u32[]{:S(2)}) async-start(f32[16,128,128]{2,1,0:T(8,128)} %bitcast.29), calls=%async_computation | async-start | bytes 2097152 | tf_op jit(solution)/shard_map/gather_l2/all_to_all | solution.py:81
  80.2 75.5 %all-gather.7.cloned.1.call-start = ((), (), s32[]{:S(2)}) async-start(), calls=%async_computation.4 | async-start | bytes 1114112 | tf_op jit(solution)/shard_map/sc_l32_cols/all_gather | solution.py:92
  101.3 12.7 %collective-permute-start.10 = (f32[2,128,128]{2,1,0:T(8,128)}, f32[2,128,128]{2,1,0:T(8,128)}, u32[]{:S(2)}, u32[]{:S(2)}) collective-permute-start(f32[2,128,128]{2,1,0:T(8,128)} %get-tuple-element.47), channel_id=1, source_target_pairs={{2,0},{3,1},{4,2},{5,3},{6,4},{7,5},{8,6},{9,7},{10,8},{11,9},{12,... | collective-permute-start | bytes 393224 | tf_op jit(solution)/shard_map/gather_t_rows/ppermute | solution.py:20
  103.0 13.2 %collective-permute-start.11 = (f32[2,128,128]{2,1,0:T(8,128)}, f32[2,128,128]{2,1,0:T(8,128)S(1)}, u32[]{:S(2)}, u32[]{:S(2)}) collective-permute-start(f32[2,128,128]{2,1,0:T(8,128)} %get-tuple-element.47), channel_id=1, source_target_pairs={{4,0},{5,1},{6,2},{7,3},{8,4},{9,5},{10,6},{11,7},{12,8},{13,9},{1... | collective-permute-start | bytes 393224 | tf_op jit(solution)/shard_map/gather_t_rows/ppermute | solution.py:20
  106.5 16.6 %collective-permute-start.12 = (f32[2,128,128]{2,1,0:T(8,128)}, f32[2,128,128]{2,1,0:T(8,128)S(1)}, u32[]{:S(2)}, u32[]{:S(2)}) collective-permute-start(f32[2,128,128]{2,1,0:T(8,128)} %get-tuple-element.47), channel_id=1, source_target_pairs={{6,0},{7,1},{8,2},{9,3},{10,4},{11,5},{12,6},{13,7},{14,8},{15,9},... | collective-permute-start | bytes 393224 | tf_op jit(solution)/shard_map/gather_t_rows/ppermute | solution.py:20
  108.6 19.5 %collective-permute-start.13 = (f32[2,128,128]{2,1,0:T(8,128)}, f32[2,128,128]{2,1,0:T(8,128)S(1)}, u32[]{:S(2)}, u32[]{:S(2)}) collective-permute-start(f32[2,128,128]{2,1,0:T(8,128)} %get-tuple-element.47), channel_id=1, source_target_pairs={{8,0},{9,1},{10,2},{11,3},{12,4},{13,5},{14,6},{15,7},{0,8},{1,9},... | collective-permute-start | bytes 393224 | tf_op jit(solution)/shard_map/gather_t_rows/ppermute | solution.py:20
  113.0 15.8 %collective-permute-start.14 = (f32[2,128,128]{2,1,0:T(8,128)}, f32[2,128,128]{2,1,0:T(8,128)S(1)}, u32[]{:S(2)}, u32[]{:S(2)}) collective-permute-start(f32[2,128,128]{2,1,0:T(8,128)} %get-tuple-element.47), channel_id=1, source_target_pairs={{10,0},{11,1},{12,2},{13,3},{14,4},{15,5},{0,6},{1,7},{2,8},{3,9},... | collective-permute-start | bytes 393224 | tf_op jit(solution)/shard_map/gather_t_rows/ppermute | solution.py:20
  114.0 17.7 %collective-permute-start.15 = (f32[2,128,128]{2,1,0:T(8,128)}, f32[2,128,128]{2,1,0:T(8,128)S(1)}, u32[]{:S(2)}, u32[]{:S(2)}) collective-permute-start(f32[2,128,128]{2,1,0:T(8,128)} %get-tuple-element.47), channel_id=1, source_target_pairs={{12,0},{13,1},{14,2},{15,3},{0,4},{1,5},{2,6},{3,7},{4,8},{5,9},{6... | collective-permute-start | bytes 393224 | tf_op jit(solution)/shard_map/gather_t_rows/ppermute | solution.py:20
  116.2 17.4 %collective-permute-start.16 = (f32[2,128,128]{2,1,0:T(8,128)}, f32[2,128,128]{2,1,0:T(8,128)S(1)}, u32[]{:S(2)}, u32[]{:S(2)}) collective-permute-start(f32[2,128,128]{2,1,0:T(8,128)} %get-tuple-element.47), channel_id=1, source_target_pairs={{14,0},{15,1},{0,2},{1,3},{2,4},{3,5},{4,6},{5,7},{6,8},{7,9},{8,1... | collective-permute-start | bytes 393224 | tf_op jit(solution)/shard_map/gather_t_rows/ppermute | solution.py:20
  134.2 6.5 %collective-permute-start.17 = (f32[8,2,128,128]{3,2,1,0:T(8,128)}, f32[8,2,128,128]{3,2,1,0:T(8,128)}, u32[]{:S(2)}, u32[]{:S(2)}) collective-permute-start(f32[8,2,128,128]{3,2,1,0:T(8,128)} %bitcast_dynamic-update-slice_fusion), channel_id=1, source_target_pairs={{0,1},{1,0},{2,3},{3,2},{4,5},{5,4},{6,7},{7,6},{8,9},{9,8},{10,11... | collective-permute-start | bytes 3145736 | tf_op jit(solution)/shard_map/gather_t_rows/ppermute | solution.py:28
  136.2 23.3 %all-to-all-start.1 = ((f32[8,2,128,128]{3,2,1,0:T(8,128)}), f32[8,2,128,128]{3,2,1,0:T(8,128)}, u32[]{:S(2)}, u32[]{:S(2)}) async-start(f32[8,2,128,128]{3,2,1,0:T(8,128)} %broadcast_in_dim.83), calls=%async_computation.1 | async-start | bytes 2097152 | tf_op jit(solution)/shard_map/gather_t_cols/all_to_all | solution.py:101
  175.6 47.2 %all-to-all-start.2 = ((f32[16,3,128,128]{3,2,1,0:T(8,128)}), f32[16,3,128,128]{3,2,1,0:T(8,128)S(1)}, u32[]{:S(2)}, u32[]{:S(2)}) async-start(f32[16,3,128,128]{3,2,1,0:T(8,128)} %copy.139), calls=%async_computation.2 | async-start | bytes 6291456 | tf_op jit(solution)/shard_map/scatter_sums/all_to_all | solution.py:131
  181.1 36.3 %collective-permute-start.18 = (f32[128,128]{1,0:T(8,128)S(1)}, f32[128,128]{1,0:T(8,128)S(1)}, u32[]{:S(2)}, u32[]{:S(2)}) collective-permute-start(f32[128,128]{1,0:T(8,128)S(1)} %select_bitcast_fusion.4), channel_id=1, source_target_pairs={{0,16},{16,0},{32,48},{48,32},{64,80},{80,64},{96,112},{112,96},{1... | collective-permute-start | bytes 196616 | tf_op jit(solution)/shard_map/swap_y/ppermute | solution.py:14
  (9 other events, 50.3 us)
Sparse Core Ops, SparseCore 0:
  23.5 69.0 all-gather.4
  103.1 52.5 all-gather.6

commit v2 on v1

v2 whole, which is shorter than its diff:
```python
import jax
import jax.numpy as jnp
from jax import lax
from jax.experimental import pallas as pl
from jax.experimental.pallas import tpu as pltpu
from jax.sharding import PartitionSpec as P

N = 16
LAYERS = 8
TB = 128
F32 = jnp.float32
BF16 = jnp.bfloat16
CORE_SWAP = [(i, i ^ 1) for i in range(N)]
LAYER_UP = [(i, (i + 2) % N) for i in range(N)]
LAYER_DOWN = [(i, (i - 2) % N) for i in range(N)]


def split(x):
    high = x.astype(BF16)
    return high, (x - high.astype(F32)).astype(BF16)


def dot3(a, b):
    a_high, a_low = a
    b_high, b_low = b

    def one(x, y):
        return jnp.dot(x, y, preferred_element_type=F32)

    return one(a_high, b_high) + (one(a_high, b_low) + one(a_low, b_high))


def lanes(*tiles):
    return jnp.concatenate(tiles, axis=1)


def rows(*tiles):
    return jnp.concatenate(tiles, axis=0)


def tile(r, c):
    return pl.ds(r * 4 * TB + c, TB, stride=4)


def call(kernel, shapes, *args, scalars=1):
    smem = pl.BlockSpec(memory_space=pltpu.SMEM)
    vmem = pl.BlockSpec(memory_space=pltpu.VMEM)
    return pl.pallas_call(
        kernel,
        out_shape=[jax.ShapeDtypeStruct(s, F32) for s in shapes],
        in_specs=[smem] * scalars + [vmem] * (len(args) - scalars),
        out_specs=[vmem] * len(shapes),
        compiler_params=pltpu.CompilerParams(vmem_limit_bytes=28 * 2**20),
    )(*args)


def prepare_kernel(mask_ref, f_ref, l32_ref, packed_ref, send_ref, l3_ref):
    def lower(r, c):
        return jnp.where(mask_ref[c, r] == 1, f_ref[tile(r, c), :], 0.0)

    l32_ref[0] = lower(3, 2)
    packed_ref[0] = f_ref[tile(3, 3), :]
    packed_ref[1] = f_ref[tile(2, 2), :]
    for s in range(2):
        x = lower(2, s)
        packed_ref[2 + s] = x
        for k in range(N):
            send_ref[k, s] = x
        l3_ref[s] = lower(3, s)


def places(place_ref, d):
    layer, core = place_ref[0] // 2, lax.rem(place_ref[0], 2)
    k = lax.rem(layer + d, LAYERS) * 2
    return k + core, k + 1 - core


def t_kernel(place_ref, mine_ref, other_ref, l2_ref, l3_ref, t_ref, send_ref):
    total = jnp.zeros((TB, 2 * TB), F32)
    for d in range(LAYERS):
        k0, k1 = places(place_ref, d)
        a = split(lanes(mine_ref[d, 0], other_ref[d, 0]))
        b = split(rows(lanes(l2_ref[k0, 0], l2_ref[k0, 1]), lanes(l2_ref[k1, 0], l2_ref[k1, 1])))
        total += dot3(a, b)
    for s in range(2):
        x = total[:, s * TB : (s + 1) * TB] - l3_ref[s]
        t_ref[s] = x
        for k in range(N):
            send_ref[k, s] = x


def uq_kernel(rows_ref, l2_ref, l32_ref, u_ref, q_ref):
    u = jnp.zeros((TB, 2 * TB), F32)
    q = jnp.zeros((TB, TB), F32)
    for k in range(0, N, 2):
        b = split(rows(lanes(l2_ref[k, 0], l2_ref[k, 1]), lanes(l2_ref[k + 1, 0], l2_ref[k + 1, 1])))
        u += dot3(split(lanes(rows_ref[k, 1], rows_ref[k + 1, 1])), b)
        b = split(rows(l32_ref[k], l32_ref[k + 1]))
        q += dot3(split(lanes(rows_ref[k, 0], rows_ref[k + 1, 0])), b)
    for s in range(2):
        u_ref[s] = u[:, s * TB : (s + 1) * TB]
    q_ref[...] = q


def y_kernel(rows_ref, t_ref, y_ref):
    y = jnp.zeros((TB, 2 * TB), F32)
    for k in range(0, N, 2):
        b = split(rows(lanes(t_ref[k, 0], t_ref[k, 1]), lanes(t_ref[k + 1, 0], t_ref[k + 1, 1])))
        y += dot3(split(lanes(rows_ref[k, 0], rows_ref[k + 1, 0])), b)
    for s in range(2):
        y_ref[s] = y[:, s * TB : (s + 1) * TB]


def sums_kernel(
    place_ref, y_ref, u_ref, q_ref, l_mine_ref, l_other_ref, t_mine_ref, t_other_ref, rows_ref, sum_ref
):
    row = place_ref[1]
    y = [y_ref[s].T for s in range(2)]
    u = [u_ref[s].T for s in range(2)]
    left = split(rows(y[0], y[1], q_ref[...].T))
    pair = [split(lanes(y[s], u[s])) for s in range(2)]
    for d in range(LAYERS):
        ks = places(place_ref, d)
        x = dot3(left, split(lanes(l_mine_ref[d, 0], l_other_ref[d, 0])))
        for i, k in enumerate(ks):
            part = x[:, i * TB : (i + 1) * TB]
            sum_ref[k, 0] = part[:TB]
            sum_ref[k, 1] = part[TB : 2 * TB]
            sum_ref[k, 4] = part[2 * TB :]
        for s in range(2):
            b = rows(
                lanes(t_mine_ref[d, s], t_other_ref[d, s]),
                lanes(rows_ref[ks[0], 2 + s], rows_ref[ks[1], 2 + s]),
            )
            z = dot3(pair[s], split(b))
            for i, k in enumerate(ks):
                sum_ref[k, 2 + s] = z[:, i * TB : (i + 1) * TB]
    for s in range(2):
        sum_ref[row, s] += u[s]


def finish_kernel(mask_ref, f_ref, got_ref, y_ref, q_ref, out_ref):
    def total(i):
        x = got_ref[0, i]
        for k in range(1, N):
            x += got_ref[k, i]
        return x.T

    def masked(s, r, x):
        return jnp.where(mask_ref[s, r] == 1, x, 0.0)

    empty = jnp.zeros((TB, TB), F32)
    for r, c in ((0, 1), (0, 2), (0, 3), (1, 0), (1, 2), (1, 3), (2, 3)):
        out_ref[tile(r, c), :] = empty
    for s in range(2):
        out_ref[tile(s, s), :] = f_ref[tile(s, s), :] + total(2 + s)
        out_ref[tile(2, s), :] = masked(s, 2, -total(s))
        out_ref[tile(3, s), :] = masked(s, 3, y_ref[s])
    out_ref[tile(2, 2), :] = f_ref[tile(2, 2), :] + total(4)
    out_ref[tile(3, 2), :] = masked(2, 3, -q_ref[...])
    out_ref[tile(3, 3), :] = f_ref[tile(3, 3), :]


def gather_layers(x):
    found = {0: x}
    up = down = x
    for step in range(1, LAYERS // 2):
        up = lax.ppermute(up, "col", LAYER_UP)
        down = lax.ppermute(down, "col", LAYER_DOWN)
        found[LAYERS - step] = up
        found[step] = down
    half = TB // 2
    found[LAYERS // 2] = jnp.concatenate(
        [
            lax.ppermute(up[:, :half], "col", LAYER_UP),
            lax.ppermute(down[:, half:], "col", LAYER_DOWN),
        ],
        axis=1,
    )
    mine = jnp.stack([found[d] for d in range(LAYERS)])
    return mine, lax.ppermute(mine, "col", CORE_SWAP)


def body(factor, structure):
    row = lax.axis_index("row")
    col = lax.axis_index("col")
    place = jnp.stack([col, row]).astype(jnp.int32)
    mask = structure.reshape(4, 4, N)
    mask = lax.dynamic_index_in_dim(mask, row, axis=2, keepdims=False)
    flat = factor.reshape(N * TB, TB)
    square = (TB, TB)

    with jax.named_scope("prepare"):
        l32, packed, send, l3 = call(
            prepare_kernel, [(1, *square), (4, *square), (N, 2, *square), (2, *square)], mask, flat
        )
    with jax.named_scope("gather_l2_cols"):
        l2_cols = lax.all_to_all(send, "row", 0, 0, tiled=True)
    with jax.named_scope("gather_l32_rows"):
        l_mine, l_other = gather_layers(l32)
    with jax.named_scope("gather_rows"):
        panels = lax.all_gather(packed, "col", axis=0)
    with jax.named_scope("gather_l32_cols"):
        l32_cols = lax.all_gather(l32[0], "row", axis=0)
    with jax.named_scope("term_t"):
        t, send = call(
            t_kernel, [(2, *square), (N, 2, *square)], place, l_mine, l_other, l2_cols, l3
        )
    with jax.named_scope("gather_t_cols"):
        t_cols = lax.all_to_all(send, "row", 0, 0, tiled=True)
    with jax.named_scope("gather_t_rows"):
        t_mine, t_other = gather_layers(t)
    with jax.named_scope("term_uq"):
        u, q = call(uq_kernel, [(2, *square), square], panels, l2_cols, l32_cols, scalars=0)
    with jax.named_scope("term_y"):
        (y,) = call(y_kernel, [(2, *square)], panels, t_cols, scalars=0)
    with jax.named_scope("sums"):
        (sums,) = call(
            sums_kernel,
            [(N, 5, *square)],
            place,
            y,
            u,
            q,
            l_mine,
            l_other,
            t_mine,
            t_other,
            panels,
        )
    with jax.named_scope("scatter_sums"):
        got = lax.all_to_all(sums, "row", 0, 0, tiled=True)
    with jax.named_scope("finish"):
        (out,) = call(finish_kernel, [(N * TB, TB)], mask, flat, got, y, q)
        return out.reshape(factor.shape)


def solution(mesh):
    return jax.shard_map(
        body,
        mesh=mesh,
        in_specs=(P(None, "row", None, "col"), P()),
        out_specs=P(None, "row", None, "col"),
        check_vma=False,
    )
```

time: 242 us -> 229 us (0.946)
  blocking collectives: 0 us -> 69.2 us
  waiting for transfers between devices: 106 us -> 77.8 us
  local copies, waits for them, and re-layouts: 37.2 us -> 17.4 us
  other arithmetic: 20.1 us -> 0.75 us
  starting transfers between devices: 52.9 us -> 37.1 us
  Pallas kernels: 0 us -> 12.5 us
  matrix products: 10.4 us -> 0 us
    all_to_all x0 -> x1, blocking collectives: none -> 69.2 us  [body(): got = lax.all_to_all(sums, 'row', 0, 0, tiled=True)]
    ppermute x19 -> x18, waiting for transfers between devices: 80.4 us -> 17.6 us  [the longest x6 9.14 us: gather_layers(): up = lax.ppermute(up, 'col', LAYER_UP)]
    all_gather x2, waiting for transfers between devices: 5.72 us -> 49.6 us  [the longest x1 44 us: body(): panels = lax.all_gather(packed, 'col', axis=0)]
    pallas_call x0 -> x6, Pallas kernels: none -> 12.5 us  [call(): pl.pallas_call(kernel, out_shape=[jax.ShapeDtypeStruct(s, F32) for s in s...]
    dot_general x7 -> x0, matrix products: 10.4 us -> none  [the longest x4 7.7 us: times(): return jnp.einsum('pkmab,pkbc->mac', left, right, precision=HIGH)]
    all_to_all x3 -> x2, waiting for transfers between devices: 19.8 us -> 9.86 us  [the longest x1 9.85 us: body(): l2_cols = lax.all_to_all(send, 'row', 0, 0, tiled=True)]
    ppermute x19 -> x18, starting transfers between devices: 35.3 us -> 25.6 us  [the longest x6 12.4 us: gather_layers(): down = lax.ppermute(down, 'col', LAYER_DOWN)]
    another operation x12 -> x1, other arithmetic: 9.55 us -> 0.08 us  [body(): place = jnp.stack([col, row]).astype(jnp.int32)]
  transfers between devices with their start and end apart: 24 -> 22, of which waited for: 15 -> 16; matrix products, arithmetic and copies ran while one was open for 13% -> 3% of each run, Pallas kernels for 0% -> 2%
where the time goes in v2:
time: 229 us; the launch traced here: 228 us
  waiting for transfers between devices  77.8 us (34%)
  blocking collectives  69.2 us (30%)
  starting transfers between devices  37.1 us (16%)
  local copies, waits for them, and re-layouts  17.4 us (8%)
  between operations  13.6 us (6%)
  Pallas kernels  12.5 us (5%)
    all_to_all x1, blocking collectives, body(): got = lax.all_to_all(sums, 'row', 0, 0, tiled=True)  69.2 us
    all_gather x1, waiting for transfers between devices, body(): panels = lax.all_gather(packed, 'col', axis=0)  44 us
    unnamed x29, local copies, waits for them, and re-layouts  15.8 us
    pallas_call x6, Pallas kernels, call(): pl.pallas_call(kernel, out_shape=[jax.ShapeDtypeStruct(s, F32) for s in s...  12.5 us
    ppermute x6, starting transfers between devices, gather_layers(): down = lax.ppermute(down, 'col', LAYER_DOWN)  12.4 us
    all_to_all x1, waiting for transfers between devices, body(): l2_cols = lax.all_to_all(send, 'row', 0, 0, tiled=True)  9.85 us
    ppermute x6, waiting for transfers between devices, gather_layers(): up = lax.ppermute(up, 'col', LAYER_UP)  9.14 us
    ppermute x6, starting transfers between devices, gather_layers(): up = lax.ppermute(up, 'col', LAYER_UP)  7.93 us
  transfers between devices with their start and end apart: 22, of which 16 were waited for; matrix products, arithmetic and copies ran while one was open for 3% of the time, Pallas kernels for 2%

profile of v2, /device:TPU:32, one launch (start us, length us, event | category | flops | bytes accessed | tf_op | source)
XLA Modules:
  0.0 228.3 jit_solution(4061716815782558763)
XLA Ops:
  12.4 2.0 collective-permute-start.3
  14.5 7.0 %all-to-all-start = ((f32[16,2,128,128]{3,2,1,0:T(8,128)}), f32[16,2,128,128]{3,2,1,0:T(8,128)S(1)}, u32[]{:S(2)}, u32[]{:S(2)}) async-start(f32[16,2,128,128]{3,2,1,0:T(8,128)} %copy-done.5), calls=%async_computation | async-start | bytes 4194304 | tf_op jit(solution)/shard_map/gather_l2_cols/all_to_all | solution.py:198
  22.4 1.9 collective-permute-start.4
  24.3 2.2 collective-permute-start.1
  26.5 2.1 collective-permute-done.4
  29.6 2.3 %collective-permute-start.2 = (f32[1,128,128]{2,1,0:T(8,128)S(1)}, f32[1,128,128]{2,1,0:T(8,128)S(1)}, u32[]{:S(2)}, u32[]{:S(2)}) collective-permute-start(f32[1,128,128]{2,1,0:T(8,128)S(1)} %collective-permute-done.1), channel_id=1, source_target_pairs={{0,14},{1,15},{2,0},{3,1},{4,2},{5,3},{6,4},{7,5},{8,6},{9,7},{10,... | collective-permute-start | bytes 196616 | tf_op jit(solution)/shard_map/gather_l32_rows/ppermute | solution.py:169
  31.9 2.2 collective-permute-done.5
  35.1 2.4 %collective-permute-start.7 = (f32[1,64,128]{2,1,0:T(8,128)S(1)}, f32[1,64,128]{2,1,0:T(8,128)S(1)}, u32[]{:S(2)}, u32[]{:S(2)}) collective-permute-start(f32[1,64,128]{2,1,0:T(8,128)S(1)} %slice.17), channel_id=1, source_target_pairs={{0,14},{1,15},{2,0},{3,1},{4,2},{5,3},{6,4},{7,5},{8,6},{9,7},{10,... | collective-permute-start | bytes 98312 | tf_op jit(solution)/shard_map/gather_l32_rows/ppermute | solution.py:176
  42.2 9.9 %all-to-all-done.l2_ref = f32[16,2,128,128]{3,2,1,0:T(8,128)S(1)} async-done(((f32[16,2,128,128]{3,2,1,0:T(8,128)}), f32[16,2,128,128]{3,2,1,0:T(8,128)S(1)}, u32[]{:S(2)}, u32[]{:S(2)}) %all-to-all-start) | async-done | bytes 2097184 | tf_op jit(solution)/shard_map/gather_l2_cols/all_to_all | solution.py:198
  54.9 2.0 collective-permute-start.12
  56.9 2.4 %collective-permute-start.9 = (f32[2,128,128]{2,1,0:T(8,128)S(1)}, f32[2,128,128]{2,1,0:T(8,128)}, u32[]{:S(2)}, u32[]{:S(2)}) collective-permute-start(f32[2,128,128]{2,1,0:T(8,128)S(1)} %get-tuple-element.20), channel_id=1, source_target_pairs={{0,14},{1,15},{2,0},{3,1},{4,2},{5,3},{6,4},{7,5},{8,6},{9,7},{10,... | collective-permute-start | bytes 393224 | tf_op jit(solution)/shard_map/gather_t_rows/ppermute | solution.py:169
  59.3 4.4 %all-to-all-start.1 = ((f32[16,2,128,128]{3,2,1,0:T(8,128)}), f32[16,2,128,128]{3,2,1,0:T(8,128)}, u32[]{:S(2)}, u32[]{:S(2)}) async-start(f32[16,2,128,128]{3,2,1,0:T(8,128)} %copy-done.6), calls=%async_computation.1 | async-start | bytes 4194304 | tf_op jit(solution)/shard_map/gather_t_cols/all_to_all | solution.py:210
  65.3 2.5 %collective-permute-start.10 = (f32[2,128,128]{2,1,0:T(8,128)}, f32[2,128,128]{2,1,0:T(8,128)S(1)}, u32[]{:S(2)}, u32[]{:S(2)}) collective-permute-start(f32[2,128,128]{2,1,0:T(8,128)} %collective-permute-done.9), channel_id=1, source_target_pairs={{0,14},{1,15},{2,0},{3,1},{4,2},{5,3},{6,4},{7,5},{8,6},{9,7},{10,... | collective-permute-start | bytes 393224 | tf_op jit(solution)/shard_map/gather_t_rows/ppermute | solution.py:169
  71.9 2.9 %collective-permute-start.11 = (f32[2,128,128]{2,1,0:T(8,128)S(1)}, f32[2,128,128]{2,1,0:T(8,128)S(1)}, u32[]{:S(2)}, u32[]{:S(2)}) collective-permute-start(f32[2,128,128]{2,1,0:T(8,128)S(1)} %collective-permute-done.10), channel_id=1, source_target_pairs={{0,14},{1,15},{2,0},{3,1},{4,2},{5,3},{6,4},{7,5},{8,6},{9,7},{10,... | collective-permute-start | bytes 393224 | tf_op jit(solution)/shard_map/gather_t_rows/ppermute | solution.py:169
  75.5 2.9 %collective-permute-done.14 = f32[2,128,128]{2,1,0:T(8,128)S(1)} collective-permute-done((f32[2,128,128]{2,1,0:T(8,128)S(1)}, f32[2,128,128]{2,1,0:T(8,128)S(1)}, u32[]{:S(2)}, u32[]{:S(2)}) %collective-permute-start.14) | collective-permute-done | bytes 131104 | tf_op jit(solution)/shard_map/gather_t_rows/ppermute | solution.py:168
  79.0 2.5 %collective-permute-start.16 = (f32[2,64,128]{2,1,0:T(8,128)S(1)}, f32[2,64,128]{2,1,0:T(8,128)S(1)}, u32[]{:S(2)}, u32[]{:S(2)}) collective-permute-start(f32[2,64,128]{2,1,0:T(8,128)S(1)} %slice.19), channel_id=1, source_target_pairs={{0,14},{1,15},{2,0},{3,1},{4,2},{5,3},{6,4},{7,5},{8,6},{9,7},{10,... | collective-permute-start | bytes 196616 | tf_op jit(solution)/shard_map/gather_t_rows/ppermute | solution.py:176
  87.1 5.6 %all-gather.4.cloned.1.call-done.l32_ref = f32[16,128,128]{2,1,0:T(8,128)} async-done(((f32[1,128,128]{2,1,0:T(8,128)}), f32[16,128,128]{2,1,0:T(8,128)}) %all-gather.4.cloned.1.call-update) | async-done | bytes 1048592 | tf_op jit(solution)/shard_map/gather_l32_cols/all_gather | solution.py:204
  92.8 44.0 %all-gather.6.cloned.1.call-done = f32[64,128,128]{2,1,0:T(8,128)} async-done(((f32[4,128,128]{2,1,0:T(8,128)}), f32[64,128,128]{2,1,0:T(8,128)}) %all-gather.6.cloned.1.call-update) | async-done | bytes 4194320 | tf_op jit(solution)/shard_map/gather_rows/all_gather | solution.py:202
  136.7 2.2 copy-done
  141.2 2.2 copy-done.1
  143.4 2.4 %term_y.1.y_ref = f32[2,128,128]{2,1,0:T(8,128)S(1)} custom-call(f32[16,4,128,128]{3,2,1,0:T(8,128)S(1)} %bitcast.43, f32[16,2,128,128]{3,2,1,0:T(8,128)} %all-to-all-done.1.t_ref), custom_call_target="tpu_custom_call" | custom-call | tf_op jit(solution)/shard_map/term_y/pallas_call | solution.py:48
  146.2 4.1 %sums.1 = f32[16,5,128,128]{3,2,1,0:T(8,128)S(1)} custom-call(s32[2]{0:T(128)S(1)} %pad_add_fusion.place_ref, f32[2,128,128]{2,1,0:T(8,128)S(1)} %term_y.1.y_ref, f32[2,128,128]{2,1,0:T(8,128)S(1)} %get-tuple-element.18.u_ref, f32[128,128]{1,0:T(8,128)S(1)} %get-tuple-element.19.q_ref, ...), custom_call_target="tpu_custom_call" | custom-call | tf_op jit(solution)/shard_map/sums/pallas_call | solution.py:48
  150.4 69.2 %all_to_all.15.got_ref = f32[16,5,128,128]{3,2,1,0:T(8,128)S(1)} all-to-all(f32[16,5,128,128]{3,2,1,0:T(8,128)S(1)} %sums.1), channel_id=1, replica_groups=mesh['row'=16,'col'=16] {'row'}, dimensions={0} | all-to-all | bytes 10485760 | tf_op jit(solution)/shard_map/scatter_sums/all_to_all | solution.py:232
  219.6 1.9 finish.1
  (69 shorter events, 31.4 us)
Async XLA Ops:
  6.5 86.2 %all-gather.4.cloned.1.call-start = ((), (), s32[]{:S(2)}) async-start(), calls=%async_computation.3 | async-start | bytes 1114112 | tf_op jit(solution)/shard_map/gather_l32_cols/all_gather | solution.py:204
  11.6 125.1 %all-gather.6.cloned.1.call-start = ((), (), s32[]{:S(2)}) async-start(), calls=%async_computation.4 | async-start | bytes 4456448 | tf_op jit(solution)/shard_map/gather_rows/all_gather | solution.py:202
  12.4 10.0 %collective-permute-start.3 = (f32[1,128,128]{2,1,0:T(8,128)}, f32[1,128,128]{2,1,0:T(8,128)S(1)}, u32[]{:S(2)}, u32[]{:S(2)}) collective-permute-start(f32[1,128,128]{2,1,0:T(8,128)} %get-tuple-element.14), channel_id=1, source_target_pairs={{0,2},{1,3},{2,4},{3,5},{4,6},{5,7},{6,8},{7,9},{8,10},{9,11},{10,... | collective-permute-start | bytes 196616 | tf_op jit(solution)/shard_map/gather_l32_rows/ppermute | solution.py:168
  14.4 9.9 %collective-permute-start = (f32[1,128,128]{2,1,0:T(8,128)}, f32[1,128,128]{2,1,0:T(8,128)S(1)}, u32[]{:S(2)}, u32[]{:S(2)}) collective-permute-start(f32[1,128,128]{2,1,0:T(8,128)} %get-tuple-element.14), channel_id=1, source_target_pairs={{0,14},{1,15},{2,0},{3,1},{4,2},{5,3},{6,4},{7,5},{8,6},{9,7},{10,... | collective-permute-start | bytes 196616 | tf_op jit(solution)/shard_map/gather_l32_rows/ppermute | solution.py:169
  14.5 37.6 %all-to-all-start = ((f32[16,2,128,128]{3,2,1,0:T(8,128)}), f32[16,2,128,128]{3,2,1,0:T(8,128)S(1)}, u32[]{:S(2)}, u32[]{:S(2)}) async-start(f32[16,2,128,128]{3,2,1,0:T(8,128)} %copy-done.5), calls=%async_computation | async-start | bytes 4194304 | tf_op jit(solution)/shard_map/gather_l2_cols/all_to_all | solution.py:198
  22.4 6.3 %collective-permute-start.4 = (f32[1,128,128]{2,1,0:T(8,128)S(1)}, f32[1,128,128]{2,1,0:T(8,128)S(1)}, u32[]{:S(2)}, u32[]{:S(2)}) collective-permute-start(f32[1,128,128]{2,1,0:T(8,128)S(1)} %collective-permute-done.3), channel_id=1, source_target_pairs={{0,2},{1,3},{2,4},{3,5},{4,6},{5,7},{6,8},{7,9},{8,10},{9,11},{10,... | collective-permute-start | bytes 196616 | tf_op jit(solution)/shard_map/gather_l32_rows/ppermute | solution.py:168
  24.3 5.3 %collective-permute-start.1 = (f32[1,128,128]{2,1,0:T(8,128)S(1)}, f32[1,128,128]{2,1,0:T(8,128)S(1)}, u32[]{:S(2)}, u32[]{:S(2)}) collective-permute-start(f32[1,128,128]{2,1,0:T(8,128)S(1)} %collective-permute-done), channel_id=1, source_target_pairs={{0,14},{1,15},{2,0},{3,1},{4,2},{5,3},{6,4},{7,5},{8,6},{9,7},{10,... | collective-permute-start | bytes 196616 | tf_op jit(solution)/shard_map/gather_l32_rows/ppermute | solution.py:169
  28.7 5.5 %collective-permute-start.5 = (f32[1,128,128]{2,1,0:T(8,128)S(1)}, f32[1,128,128]{2,1,0:T(8,128)S(1)}, u32[]{:S(2)}, u32[]{:S(2)}) collective-permute-start(f32[1,128,128]{2,1,0:T(8,128)S(1)} %collective-permute-done.4), channel_id=1, source_target_pairs={{0,2},{1,3},{2,4},{3,5},{4,6},{5,7},{6,8},{7,9},{8,10},{9,11},{10,... | collective-permute-start | bytes 196616 | tf_op jit(solution)/shard_map/gather_l32_rows/ppermute | solution.py:168
  29.6 5.5 %collective-permute-start.2 = (f32[1,128,128]{2,1,0:T(8,128)S(1)}, f32[1,128,128]{2,1,0:T(8,128)S(1)}, u32[]{:S(2)}, u32[]{:S(2)}) collective-permute-start(f32[1,128,128]{2,1,0:T(8,128)S(1)} %collective-permute-done.1), channel_id=1, source_target_pairs={{0,14},{1,15},{2,0},{3,1},{4,2},{5,3},{6,4},{7,5},{8,6},{9,7},{10,... | collective-permute-start | bytes 196616 | tf_op jit(solution)/shard_map/gather_l32_rows/ppermute | solution.py:169
  34.1 5.1 %collective-permute-start.6 = (f32[1,64,128]{2,1,0:T(8,128)S(1)}, f32[1,64,128]{2,1,0:T(8,128)S(1)}, u32[]{:S(2)}, u32[]{:S(2)}) collective-permute-start(f32[1,64,128]{2,1,0:T(8,128)S(1)} %slice.16), channel_id=1, source_target_pairs={{0,2},{1,3},{2,4},{3,5},{4,6},{5,7},{6,8},{7,9},{8,10},{9,11},{10,... | collective-permute-start | bytes 98312 | tf_op jit(solution)/shard_map/gather_l32_rows/ppermute | solution.py:175
  35.1 5.1 %collective-permute-start.7 = (f32[1,64,128]{2,1,0:T(8,128)S(1)}, f32[1,64,128]{2,1,0:T(8,128)S(1)}, u32[]{:S(2)}, u32[]{:S(2)}) collective-permute-start(f32[1,64,128]{2,1,0:T(8,128)S(1)} %slice.17), channel_id=1, source_target_pairs={{0,14},{1,15},{2,0},{3,1},{4,2},{5,3},{6,4},{7,5},{8,6},{9,7},{10,... | collective-permute-start | bytes 98312 | tf_op jit(solution)/shard_map/gather_l32_rows/ppermute | solution.py:176
  40.2 2.0 collective-permute-start.8
  54.9 9.5 %collective-permute-start.12 = (f32[2,128,128]{2,1,0:T(8,128)S(1)}, f32[2,128,128]{2,1,0:T(8,128)S(1)}, u32[]{:S(2)}, u32[]{:S(2)}) collective-permute-start(f32[2,128,128]{2,1,0:T(8,128)S(1)} %get-tuple-element.20), channel_id=1, source_target_pairs={{0,2},{1,3},{2,4},{3,5},{4,6},{5,7},{6,8},{7,9},{8,10},{9,11},{10,... | collective-permute-start | bytes 393224 | tf_op jit(solution)/shard_map/gather_t_rows/ppermute | solution.py:168
  56.9 8.4 %collective-permute-start.9 = (f32[2,128,128]{2,1,0:T(8,128)S(1)}, f32[2,128,128]{2,1,0:T(8,128)}, u32[]{:S(2)}, u32[]{:S(2)}) collective-permute-start(f32[2,128,128]{2,1,0:T(8,128)S(1)} %get-tuple-element.20), channel_id=1, source_target_pairs={{0,14},{1,15},{2,0},{3,1},{4,2},{5,3},{6,4},{7,5},{8,6},{9,7},{10,... | collective-permute-start | bytes 393224 | tf_op jit(solution)/shard_map/gather_t_rows/ppermute | solution.py:169
  59.3 81.9 %all-to-all-start.1 = ((f32[16,2,128,128]{3,2,1,0:T(8,128)}), f32[16,2,128,128]{3,2,1,0:T(8,128)}, u32[]{:S(2)}, u32[]{:S(2)}) async-start(f32[16,2,128,128]{3,2,1,0:T(8,128)} %copy-done.6), calls=%async_computation.1 | async-start | bytes 4194304 | tf_op jit(solution)/shard_map/gather_t_cols/all_to_all | solution.py:210
  64.4 6.8 %collective-permute-start.13 = (f32[2,128,128]{2,1,0:T(8,128)S(1)}, f32[2,128,128]{2,1,0:T(8,128)S(1)}, u32[]{:S(2)}, u32[]{:S(2)}) collective-permute-start(f32[2,128,128]{2,1,0:T(8,128)S(1)} %collective-permute-done.12), channel_id=1, source_target_pairs={{0,2},{1,3},{2,4},{3,5},{4,6},{5,7},{6,8},{7,9},{8,10},{9,11},{10,... | collective-permute-start | bytes 393224 | tf_op jit(solution)/shard_map/gather_t_rows/ppermute | solution.py:168
  65.3 6.6 %collective-permute-start.10 = (f32[2,128,128]{2,1,0:T(8,128)}, f32[2,128,128]{2,1,0:T(8,128)S(1)}, u32[]{:S(2)}, u32[]{:S(2)}) collective-permute-start(f32[2,128,128]{2,1,0:T(8,128)} %collective-permute-done.9), channel_id=1, source_target_pairs={{0,14},{1,15},{2,0},{3,1},{4,2},{5,3},{6,4},{7,5},{8,6},{9,7},{10,... | collective-permute-start | bytes 393224 | tf_op jit(solution)/shard_map/gather_t_rows/ppermute | solution.py:169
  71.2 7.2 %collective-permute-start.14 = (f32[2,128,128]{2,1,0:T(8,128)S(1)}, f32[2,128,128]{2,1,0:T(8,128)S(1)}, u32[]{:S(2)}, u32[]{:S(2)}) collective-permute-start(f32[2,128,128]{2,1,0:T(8,128)S(1)} %collective-permute-done.13), channel_id=1, source_target_pairs={{0,2},{1,3},{2,4},{3,5},{4,6},{5,7},{6,8},{7,9},{8,10},{9,11},{10,... | collective-permute-start | bytes 393224 | tf_op jit(solution)/shard_map/gather_t_rows/ppermute | solution.py:168
  71.9 7.1 %collective-permute-start.11 = (f32[2,128,128]{2,1,0:T(8,128)S(1)}, f32[2,128,128]{2,1,0:T(8,128)S(1)}, u32[]{:S(2)}, u32[]{:S(2)}) collective-permute-start(f32[2,128,128]{2,1,0:T(8,128)S(1)} %collective-permute-done.10), channel_id=1, source_target_pairs={{0,14},{1,15},{2,0},{3,1},{4,2},{5,3},{6,4},{7,5},{8,6},{9,7},{10,... | collective-permute-start | bytes 393224 | tf_op jit(solution)/shard_map/gather_t_rows/ppermute | solution.py:169
  78.4 5.2 %collective-permute-start.15 = (f32[2,64,128]{2,1,0:T(8,128)S(1)}, f32[2,64,128]{2,1,0:T(8,128)S(1)}, u32[]{:S(2)}, u32[]{:S(2)}) collective-permute-start(f32[2,64,128]{2,1,0:T(8,128)S(1)} %slice.18), channel_id=1, source_target_pairs={{0,2},{1,3},{2,4},{3,5},{4,6},{5,7},{6,8},{7,9},{8,10},{9,11},{10,... | collective-permute-start | bytes 196616 | tf_op jit(solution)/shard_map/gather_t_rows/ppermute | solution.py:175
  79.0 5.5 %collective-permute-start.16 = (f32[2,64,128]{2,1,0:T(8,128)S(1)}, f32[2,64,128]{2,1,0:T(8,128)S(1)}, u32[]{:S(2)}, u32[]{:S(2)}) collective-permute-start(f32[2,64,128]{2,1,0:T(8,128)S(1)} %slice.19), channel_id=1, source_target_pairs={{0,14},{1,15},{2,0},{3,1},{4,2},{5,3},{6,4},{7,5},{8,6},{9,7},{10,... | collective-permute-start | bytes 196616 | tf_op jit(solution)/shard_map/gather_t_rows/ppermute | solution.py:176
  87.1 58.7 %collective-permute-start.17 = (f32[8,2,128,128]{3,2,1,0:T(8,128)}, f32[8,2,128,128]{3,2,1,0:T(8,128)}, u32[]{:S(2)}, u32[]{:S(2)}) collective-permute-start(f32[8,2,128,128]{3,2,1,0:T(8,128)} %bitcast_dynamic-update-slice_fusion.t_mine_ref), channel_id=1, source_target_pairs={{0,1},{1,0},{2,3},{3,2},{4,5},{5,4},{6,7},{7,6},{8,9},{9,8},{10,11... | collective-permute-start | bytes 3145736 | tf_op jit(solution)/shard_map/gather_t_rows/ppermute | solution.py:181
  143.4 2.8 %copy-start.2 = (f32[64,128,128]{2,1,0:T(8,128)S(1)}, f32[64,128,128]{2,1,0:T(8,128)}, u32[]{:S(2)}) copy-start(f32[64,128,128]{2,1,0:T(8,128)} %all-gather.6.cloned.1.call-done) | copy-start | bytes 12582916
  150.4 69.2 %copy-start.4 = (f32[4,128,4,128]{3,2,1,0:T(4,128)S(1)}, f32[4,128,4,128]{3,2,1,0:T(4,128)}, u32[]{:S(2)}) copy-start(f32[4,128,4,128]{3,2,1,0:T(4,128)} %param.2) | copy-start | bytes 3145732
  (6 other events, 9.6 us)
Sparse Core Ops, SparseCore 0:
  11.8 80.9 all-gather.3
  94.6 42.0 all-gather.5

commit v3 on v2

v3 whole, which is shorter than its diff:
```python
import jax
import jax.numpy as jnp
from jax import lax
from jax.experimental import pallas as pl
from jax.experimental.pallas import tpu as pltpu
from jax.sharding import PartitionSpec as P

N = 16
LAYERS = 8
TB = 128
F32 = jnp.float32
BF16 = jnp.bfloat16
CORE_SWAP = [(i, i ^ 1) for i in range(N)]
ROW_SWAP = [(i, i ^ 1) for i in range(N)]
SAME_SIDE = [[p + 2 * i for i in range(N // 2)] for p in range(2)]
LAYER_UP = [(i, (i + 2) % N) for i in range(N)]
LAYER_DOWN = [(i, (i - 2) % N) for i in range(N)]


def split(x):
    high = x.astype(BF16)
    return high, (x - high.astype(F32)).astype(BF16)


def dot3(a, b):
    a_high, a_low = a
    b_high, b_low = b

    def one(x, y):
        return jnp.dot(x, y, preferred_element_type=F32)

    return one(a_high, b_high) + (one(a_high, b_low) + one(a_low, b_high))


def lanes(*tiles):
    return jnp.concatenate(tiles, axis=1)


def rows(*tiles):
    return jnp.concatenate(tiles, axis=0)


def tile(r, c):
    return pl.ds(r * 4 * TB + c, TB, stride=4)


def call(kernel, shapes, *args, scalars=1):
    smem = pl.BlockSpec(memory_space=pltpu.SMEM)
    vmem = pl.BlockSpec(memory_space=pltpu.VMEM)
    return pl.pallas_call(
        kernel,
        out_shape=[jax.ShapeDtypeStruct(s, F32) for s in shapes],
        in_specs=[smem] * scalars + [vmem] * (len(args) - scalars),
        out_specs=[vmem] * len(shapes),
        compiler_params=pltpu.CompilerParams(vmem_limit_bytes=28 * 2**20),
    )(*args)


def prepare_kernel(mask_ref, place_ref, f_ref, l32_ref, away_ref, home_ref, send_ref):
    side = lax.rem(place_ref[1], 2)

    def lower(r, c):
        return jnp.where(mask_ref[c, r] == 1, f_ref[tile(r, c), :], 0.0)

    x = lower(3, 2)
    l32_ref[...] = x
    l2 = [lower(2, s) for s in range(2)]
    l3 = [lower(3, s) for s in range(2)]
    for k in range(N):
        send_ref[k, 0] = l2[k % 2]
        send_ref[k, 1] = x
    root, diag = f_ref[tile(3, 3), :], f_ref[tile(2, 2), :]
    away_ref[0] = home_ref[0] = root
    away_ref[1] = home_ref[1] = diag
    even = side == 0
    home_ref[2] = jnp.where(even, l2[0], l2[1])
    away_ref[2] = jnp.where(even, l2[1], l2[0])
    home_ref[3] = jnp.where(even, l3[0], l3[1])
    away_ref[3] = jnp.where(even, l3[1], l3[0])


def pack_kernel(place_ref, home_ref, got_ref, packed_ref, l3_ref):
    side = lax.rem(place_ref[1], 2)
    for i in range(3):
        packed_ref[i, side] = home_ref[i]
        packed_ref[i, 1 - side] = got_ref[i]
    l3_ref[side] = home_ref[3]
    l3_ref[1 - side] = got_ref[3]


def places(place_ref, d):
    layer, core = place_ref[0] // 2, lax.rem(place_ref[0], 2)
    k = lax.rem(layer + d, LAYERS) * 2
    return k + core, k + 1 - core


def t_kernel(place_ref, mine_ref, other_ref, l2_ref, l3_ref, t_ref, send_ref):
    total = jnp.zeros((2 * TB, TB), F32)
    for d in range(LAYERS):
        k0, k1 = places(place_ref, d)
        a = rows(*(lanes(mine_ref[d, i], other_ref[d, i]) for i in range(2)))
        total += dot3(split(a), split(rows(l2_ref[k0, 0], l2_ref[k1, 0])))
    for i in range(2):
        x = total[i * TB : (i + 1) * TB] - l3_ref[i]
        t_ref[i] = x
        for k in range(N // 2):
            send_ref[k, i] = x


def pair_rows(rows_ref, k, i):
    return rows(*(lanes(rows_ref[k, i, j], rows_ref[k + 1, i, j]) for j in range(2)))


def uq_kernel(place_ref, rows_ref, cols_ref, u_ref, q_ref):
    side = lax.rem(place_ref[1], 2)
    u = jnp.zeros((2 * TB, TB), F32)
    q = jnp.zeros((TB, TB), F32)
    for k in range(0, N, 2):
        b = split(rows(cols_ref[k, 0], cols_ref[k + 1, 0]))
        u += dot3(split(pair_rows(rows_ref, k, 1)), b)
        b = split(rows(cols_ref[k, 1], cols_ref[k + 1, 1]))
        q += dot3(split(lanes(rows_ref[k, 0, side], rows_ref[k + 1, 0, side])), b)
    for i in range(2):
        u_ref[i] = u[i * TB : (i + 1) * TB]
    q_ref[...] = q


def y_kernel(place_ref, rows_ref, t_ref, y_ref, home_ref, away_ref):
    side = lax.rem(place_ref[1], 2)
    y = jnp.zeros((2 * TB, TB), F32)
    for k in range(0, N, 2):
        b = split(rows(t_ref[k // 2, 0], t_ref[k // 2, 1]))
        y += dot3(split(pair_rows(rows_ref, k, 0)), b)
    y_ref[...] = y
    even = side == 0
    home_ref[...] = jnp.where(even, y[:TB], y[TB:])
    away_ref[...] = jnp.where(even, y[TB:], y[:TB])


def sums_kernel(
    place_ref, y_ref, u_ref, q_ref, l_mine_ref, l_other_ref, t_mine_ref, t_other_ref, rows_ref, sum_ref
):
    row = place_ref[1]
    side = lax.rem(row, 2)
    y = y_ref[...].T
    u = [u_ref[i].T for i in range(2)]
    y_split = split(y)
    yu_split = split(lanes(y, *u))
    q_split = split(q_ref[...].T)
    for d in range(LAYERS):
        ks = places(place_ref, d)
        l32 = rows(*(lanes(l_mine_ref[d, i], l_other_ref[d, i]) for i in range(2)))
        l32_own = lanes(l_mine_ref[d, side], l_other_ref[d, side])
        low = [lanes(t_mine_ref[d, i], t_other_ref[d, i]) for i in range(2)]
        low += [lanes(rows_ref[ks[0], 2, i], rows_ref[ks[1], 2, i]) for i in range(2)]
        parts = [
            dot3(y_split, split(l32)),
            dot3(yu_split, split(rows(*low))),
            dot3(q_split, split(l32_own)),
        ]
        for j, part in enumerate(parts):
            for i, k in enumerate(ks):
                sum_ref[k, j] = part[:, i * TB : (i + 1) * TB]
    for i in range(2):
        sum_ref[row - side + i, 0] += u[i]


def finish_kernel(mask_ref, place_ref, f_ref, got_ref, home_ref, away_ref, q_ref, out_ref):
    even = lax.rem(place_ref[1], 2) == 0

    def total(i, ks):
        x = got_ref[ks[0], i]
        for k in ks[1:]:
            x += got_ref[k, i]
        return x.T

    def masked(s, r, x):
        return jnp.where(mask_ref[s, r] == 1, x, 0.0)

    empty = jnp.zeros((TB, TB), F32)
    for r, c in ((0, 1), (0, 2), (0, 3), (1, 0), (1, 2), (1, 3), (2, 3)):
        out_ref[tile(r, c), :] = empty
    home, away = home_ref[...], away_ref[...]
    y = [jnp.where(even, home, away), jnp.where(even, away, home)]
    for s in range(2):
        ks = range(s, N, 2)
        out_ref[tile(s, s), :] = f_ref[tile(s, s), :] + total(1, ks)
        out_ref[tile(2, s), :] = masked(s, 2, -total(0, ks))
        out_ref[tile(3, s), :] = masked(s, 3, y[s])
    out_ref[tile(2, 2), :] = f_ref[tile(2, 2), :] + total(2, range(N))
    out_ref[tile(3, 2), :] = masked(2, 3, -q_ref[...])
    out_ref[tile(3, 3), :] = f_ref[tile(3, 3), :]


def gather_layers(x, beside=None):
    found = {0: x}
    up = down = x
    for step in range(1, LAYERS // 2):
        up = lax.ppermute(up, "col", LAYER_UP)
        down = lax.ppermute(down, "col", LAYER_DOWN)
        found[LAYERS - step] = up
        found[step] = down
    half = TB // 2
    found[LAYERS // 2] = jnp.concatenate(
        [
            lax.ppermute(up[:, :half], "col", LAYER_UP),
            lax.ppermute(down[:, half:], "col", LAYER_DOWN),
        ],
        axis=1,
    )
    mine = jnp.stack([found[d] for d in range(LAYERS)])
    mine, beside = lax.optimization_barrier((mine, beside))
    return mine, lax.ppermute(mine, "col", CORE_SWAP), beside


def body(factor, structure):
    row = lax.axis_index("row")
    col = lax.axis_index("col")
    place = jnp.stack([col, row]).astype(jnp.int32)
    mask = structure.reshape(4, 4, N)
    mask = lax.dynamic_index_in_dim(mask, row, axis=2, keepdims=False)
    flat = factor.reshape(N * TB, TB)
    square = (TB, TB)

    with jax.named_scope("prepare"):
        l32, away, home, send = call(
            prepare_kernel,
            [square, (4, *square), (4, *square), (N, 2, *square)],
            mask,
            place,
            flat,
            scalars=2,
        )
    with jax.named_scope("swap_l32"):
        l32_away = lax.ppermute(l32, "row", ROW_SWAP)
        even = lax.rem(row, 2) == 0
        l32_pair = jnp.stack([jnp.where(even, l32, l32_away), jnp.where(even, l32_away, l32)])
        l32_pair, away = lax.optimization_barrier((l32_pair, away))
    with jax.named_scope("swap_rest"):
        packed, l3 = call(
            pack_kernel,
            [(3, 2, *square), (2, *square)],
            place,
            home,
            lax.ppermute(away, "row", ROW_SWAP),
        )
    with jax.named_scope("gather_cols"):
        cols = lax.all_to_all(send, "row", 0, 0, tiled=True)
    with jax.named_scope("gather_l32_rows"):
        l_mine, l_other, cols = gather_layers(l32_pair, cols)
    with jax.named_scope("gather_rows"):
        panels = lax.all_gather(packed, "col", axis=0)
    with jax.named_scope("term_t"):
        t, send = call(
            t_kernel, [(2, *square), (N // 2, 2, *square)], place, l_mine, l_other, cols, l3
        )
    with jax.named_scope("gather_t_cols"):
        t_cols = lax.all_to_all(
            send, "row", 0, 0, tiled=True, axis_index_groups=SAME_SIDE
        )
    with jax.named_scope("gather_t_rows"):
        t_mine, t_other, t_cols = gather_layers(t, t_cols)
    with jax.named_scope("term_uq"):
        u, q = call(uq_kernel, [(2, *square), square], place, panels, cols)
    with jax.named_scope("term_y"):
        y, y_home, y_away = call(
            y_kernel, [(2 * TB, TB), square, square], place, panels, t_cols
        )
    with jax.named_scope("swap_y"):
        y_away = lax.ppermute(y_away, "row", ROW_SWAP)
    with jax.named_scope("sums"):
        (sums,) = call(
            sums_kernel,
            [(N, 3, *square)],
            place,
            y,
            u,
            q,
            l_mine,
            l_other,
            t_mine,
            t_other,
            panels,
        )
    with jax.named_scope("scatter_sums"):
        got = lax.all_to_all(sums, "row", 0, 0, tiled=True)
    with jax.named_scope("finish"):
        (out,) = call(
            finish_kernel, [(N * TB, TB)], mask, place, flat, got, y_home, y_away, q, scalars=2
        )
        return out.reshape(factor.shape)


def solution(mesh):
    return jax.shard_map(
        body,
        mesh=mesh,
        in_specs=(P(None, "row", None, "col"), P()),
        out_specs=P(None, "row", None, "col"),
        check_vma=False,
    )
```

time: 229 us -> 184 us (0.80)
  the two profiles are of different devices: /device:TPU:32 before, /device:TPU:20 now
where the time goes in v3:
time: 184 us
  waiting for transfers between devices  82.9 us (45%)
  starting transfers between devices  56.5 us (31%)
  local copies, waits for them, and re-layouts  16.7 us (9%)
  between operations  13.6 us (7%)
  Pallas kernels  13.2 us (7%)
    ppermute x1, waiting for transfers between devices, body(): y_away = lax.ppermute(y_away, 'row', ROW_SWAP)  23.8 us
    all_to_all x1, waiting for transfers between devices, body(): got = lax.all_to_all(sums, 'row', 0, 0, tiled=True)  22 us
    ppermute x6, starting transfers between devices, gather_layers(): down = lax.ppermute(down, 'col', LAYER_DOWN)  21.8 us
    unnamed x31, local copies, waits for them, and re-layouts  15.2 us
    pallas_call x7, Pallas kernels, call(): pl.pallas_call(kernel, out_shape=[jax.ShapeDtypeStruct(s, F32) for s in s...  13.2 us
    ppermute x6, waiting for transfers between devices, gather_layers(): up = lax.ppermute(up, 'col', LAYER_UP)  12.4 us
    ppermute x6, waiting for transfers between devices, gather_layers(): down = lax.ppermute(down, 'col', LAYER_DOWN)  8.85 us
    all_to_all x1, starting transfers between devices, body(): cols = lax.all_to_all(send, 'row', 0, 0, tiled=True)  7.24 us
  transfers between devices with their start and end apart: 25, of which 16 were waited for; matrix products, arithmetic and copies ran while one was open for 3% of the time, Pallas kernels for 3%

profile of v3, /device:TPU:20, one launch (start us, length us, event | category | flops | bytes accessed | tf_op | source)
XLA Modules:
  0.0 183.6 jit_solution(11997488612164476712)
XLA Ops:
  12.3 3.0 %collective-permute-done = f32[128,128]{1,0:T(8,128)S(1)} collective-permute-done((f32[128,128]{1,0:T(8,128)S(1)}, f32[128,128]{1,0:T(8,128)S(1)}, u32[]{:S(2)}, u32[]{:S(2)}) %collective-permute-start) | collective-permute-done | bytes 65568 | tf_op jit(solution)/shard_map/swap_l32/ppermute | solution.py:235
  16.7 5.6 %collective-permute-done.1.got_ref = f32[4,128,128]{2,1,0:T(8,128)S(1)} collective-permute-done((f32[4,128,128]{2,1,0:T(8,128)S(1)}, f32[4,128,128]{2,1,0:T(8,128)S(1)}, u32[]{:S(2)}, u32[]{:S(2)}) %collective-permute-start.1) | collective-permute-done | bytes 262176 | tf_op jit(solution)/shard_map/swap_rest/ppermute | solution.py:245
  23.6 7.2 %all-to-all-start = ((f32[16,2,128,128]{3,2,1,0:T(8,128)}), f32[16,2,128,128]{3,2,1,0:T(8,128)S(1)}, u32[]{:S(2)}, u32[]{:S(2)}) async-start(f32[16,2,128,128]{3,2,1,0:T(8,128)} %copy-done.7), calls=%async_computation | async-start | bytes 4194304 | tf_op jit(solution)/shard_map/gather_cols/all_to_all | solution.py:248
  32.8 4.0 %collective-permute-start.2 = (f32[2,128,128]{2,1,0:T(8,128)S(1)}, f32[2,128,128]{2,1,0:T(8,128)S(1)}, u32[]{:S(2)}, u32[]{:S(2)}) collective-permute-start(f32[2,128,128]{2,1,0:T(8,128)S(1)} %pad_maximum_fusion), channel_id=1, source_target_pairs={{0,14},{1,15},{2,0},{3,1},{4,2},{5,3},{6,4},{7,5},{8,6},{9,7},{10,... | collective-permute-start | bytes 393224 | tf_op jit(solution)/shard_map/gather_l32_rows/ppermute | solution.py:200
  36.8 2.8 %collective-permute-done.5 = f32[2,128,128]{2,1,0:T(8,128)S(1)} collective-permute-done((f32[2,128,128]{2,1,0:T(8,128)S(1)}, f32[2,128,128]{2,1,0:T(8,128)S(1)}, u32[]{:S(2)}, u32[]{:S(2)}) %collective-permute-start.5) | collective-permute-done | bytes 131104 | tf_op jit(solution)/shard_map/gather_l32_rows/ppermute | solution.py:199
  39.7 3.2 %collective-permute-done.2 = f32[2,128,128]{2,1,0:T(8,128)S(1)} collective-permute-done((f32[2,128,128]{2,1,0:T(8,128)S(1)}, f32[2,128,128]{2,1,0:T(8,128)S(1)}, u32[]{:S(2)}, u32[]{:S(2)}) %collective-permute-start.2) | collective-permute-done | bytes 131104 | tf_op jit(solution)/shard_map/gather_l32_rows/ppermute | solution.py:200
  42.9 3.7 %collective-permute-start.3 = (f32[2,128,128]{2,1,0:T(8,128)S(1)}, f32[2,128,128]{2,1,0:T(8,128)S(1)}, u32[]{:S(2)}, u32[]{:S(2)}) collective-permute-start(f32[2,128,128]{2,1,0:T(8,128)S(1)} %collective-permute-done.2), channel_id=1, source_target_pairs={{0,14},{1,15},{2,0},{3,1},{4,2},{5,3},{6,4},{7,5},{8,6},{9,7},{10,... | collective-permute-start | bytes 393224 | tf_op jit(solution)/shard_map/gather_l32_rows/ppermute | solution.py:200
  46.6 3.5 %collective-permute-done.6 = f32[2,128,128]{2,1,0:T(8,128)S(1)} collective-permute-done((f32[2,128,128]{2,1,0:T(8,128)S(1)}, f32[2,128,128]{2,1,0:T(8,128)S(1)}, u32[]{:S(2)}, u32[]{:S(2)}) %collective-permute-start.6) | collective-permute-done | bytes 131104 | tf_op jit(solution)/shard_map/gather_l32_rows/ppermute | solution.py:199
  50.1 2.9 %collective-permute-done.3 = f32[2,128,128]{2,1,0:T(8,128)S(1)} collective-permute-done((f32[2,128,128]{2,1,0:T(8,128)S(1)}, f32[2,128,128]{2,1,0:T(8,128)S(1)}, u32[]{:S(2)}, u32[]{:S(2)}) %collective-permute-start.3) | collective-permute-done | bytes 131104 | tf_op jit(solution)/shard_map/gather_l32_rows/ppermute | solution.py:200
  53.0 3.7 %collective-permute-start.4 = (f32[2,128,128]{2,1,0:T(8,128)S(1)}, f32[2,128,128]{2,1,0:T(8,128)S(1)}, u32[]{:S(2)}, u32[]{:S(2)}) collective-permute-start(f32[2,128,128]{2,1,0:T(8,128)S(1)} %collective-permute-done.3), channel_id=1, source_target_pairs={{0,14},{1,15},{2,0},{3,1},{4,2},{5,3},{6,4},{7,5},{8,6},{9,7},{10,... | collective-permute-start | bytes 393224 | tf_op jit(solution)/shard_map/gather_l32_rows/ppermute | solution.py:200
  56.7 2.7 %collective-permute-done.7 = f32[2,128,128]{2,1,0:T(8,128)S(1)} collective-permute-done((f32[2,128,128]{2,1,0:T(8,128)S(1)}, f32[2,128,128]{2,1,0:T(8,128)S(1)}, u32[]{:S(2)}, u32[]{:S(2)}) %collective-permute-start.7) | collective-permute-done | bytes 131104 | tf_op jit(solution)/shard_map/gather_l32_rows/ppermute | solution.py:199
  59.3 2.8 %collective-permute-done.4 = f32[2,128,128]{2,1,0:T(8,128)S(1)} collective-permute-done((f32[2,128,128]{2,1,0:T(8,128)S(1)}, f32[2,128,128]{2,1,0:T(8,128)S(1)}, u32[]{:S(2)}, u32[]{:S(2)}) %collective-permute-start.4) | collective-permute-done | bytes 131104 | tf_op jit(solution)/shard_map/gather_l32_rows/ppermute | solution.py:200
  62.1 3.7 %collective-permute-start.9 = (f32[2,64,128]{2,1,0:T(8,128)S(1)}, f32[2,64,128]{2,1,0:T(8,128)S(1)}, u32[]{:S(2)}, u32[]{:S(2)}) collective-permute-start(f32[2,64,128]{2,1,0:T(8,128)S(1)} %slice.17), channel_id=1, source_target_pairs={{0,14},{1,15},{2,0},{3,1},{4,2},{5,3},{6,4},{7,5},{8,6},{9,7},{10,... | collective-permute-start | bytes 196616 | tf_op jit(solution)/shard_map/gather_l32_rows/ppermute | solution.py:207
  66.0 2.9 %collective-permute-done.9 = f32[2,64,128]{2,1,0:T(8,128)S(1)} collective-permute-done((f32[2,64,128]{2,1,0:T(8,128)S(1)}, f32[2,64,128]{2,1,0:T(8,128)S(1)}, u32[]{:S(2)}, u32[]{:S(2)}) %collective-permute-start.9) | collective-permute-done | bytes 65568 | tf_op jit(solution)/shard_map/gather_l32_rows/ppermute | solution.py:207
  74.4 3.8 %collective-permute-start.11 = (f32[2,128,128]{2,1,0:T(8,128)S(1)}, f32[2,128,128]{2,1,0:T(8,128)}, u32[]{:S(2)}, u32[]{:S(2)}) collective-permute-start(f32[2,128,128]{2,1,0:T(8,128)S(1)} %get-tuple-element.34), channel_id=1, source_target_pairs={{0,14},{1,15},{2,0},{3,1},{4,2},{5,3},{6,4},{7,5},{8,6},{9,7},{10,... | collective-permute-start | bytes 393224 | tf_op jit(solution)/shard_map/gather_t_rows/ppermute | solution.py:200
  78.1 7.2 %all-to-all-start.1 = ((f32[8,2,128,128]{3,2,1,0:T(8,128)}), f32[8,2,128,128]{3,2,1,0:T(8,128)}, u32[]{:S(2)}, u32[]{:S(2)}) async-start(f32[8,2,128,128]{3,2,1,0:T(8,128)} %copy-done.8), calls=%async_computation.1 | async-start | bytes 2097152 | tf_op jit(solution)/shard_map/gather_t_cols/all_to_all | solution.py:258
  86.0 3.2 %collective-permute-start.12 = (f32[2,128,128]{2,1,0:T(8,128)}, f32[2,128,128]{2,1,0:T(8,128)S(1)}, u32[]{:S(2)}, u32[]{:S(2)}) collective-permute-start(f32[2,128,128]{2,1,0:T(8,128)} %collective-permute-done.11), channel_id=1, source_target_pairs={{0,14},{1,15},{2,0},{3,1},{4,2},{5,3},{6,4},{7,5},{8,6},{9,7},{10,... | collective-permute-start | bytes 393224 | tf_op jit(solution)/shard_map/gather_t_rows/ppermute | solution.py:200
  92.2 3.4 %collective-permute-start.13 = (f32[2,128,128]{2,1,0:T(8,128)S(1)}, f32[2,128,128]{2,1,0:T(8,128)S(1)}, u32[]{:S(2)}, u32[]{:S(2)}) collective-permute-start(f32[2,128,128]{2,1,0:T(8,128)S(1)} %collective-permute-done.12), channel_id=1, source_target_pairs={{0,14},{1,15},{2,0},{3,1},{4,2},{5,3},{6,4},{7,5},{8,6},{9,7},{10,... | collective-permute-start | bytes 393224 | tf_op jit(solution)/shard_map/gather_t_rows/ppermute | solution.py:200
  98.4 3.4 %collective-permute-start.18 = (f32[2,64,128]{2,1,0:T(8,128)S(1)}, f32[2,64,128]{2,1,0:T(8,128)S(1)}, u32[]{:S(2)}, u32[]{:S(2)}) collective-permute-start(f32[2,64,128]{2,1,0:T(8,128)S(1)} %slice.19), channel_id=1, source_target_pairs={{0,14},{1,15},{2,0},{3,1},{4,2},{5,3},{6,4},{7,5},{8,6},{9,7},{10,... | collective-permute-start | bytes 196616 | tf_op jit(solution)/shard_map/gather_t_rows/ppermute | solution.py:207
  106.5 2.8 %copy-done = f32[48,2,128,128]{3,2,1,0:T(8,128)S(1)} copy-done((f32[48,2,128,128]{3,2,1,0:T(8,128)S(1)}, f32[48,2,128,128]{3,2,1,0:T(8,128)}, u32[]{:S(2)}) %copy-start) | copy-done | bytes 6291480
  114.4 3.5 %sums.1 = f32[16,3,128,128]{3,2,1,0:T(8,128)S(1)} custom-call(s32[2]{0:T(128)S(1)} %pad_add_fusion.place_ref, f32[256,128]{1,0:T(8,128)S(1)} %get-tuple-element.37.y_ref, f32[2,128,128]{2,1,0:T(8,128)S(1)} %get-tuple-element.38.u_ref, f32[128,128]{1,0:T(8,128)S(1)} %get-tuple-element.39.q_ref, ...), custom_call_target="tpu_custom_call" | custom-call | tf_op jit(solution)/shard_map/sums/pallas_call | solution.py:50
  119.5 7.2 %all-to-all-start.2 = ((f32[16,3,128,128]{3,2,1,0:T(8,128)}), f32[16,3,128,128]{3,2,1,0:T(8,128)S(1)}, u32[]{:S(2)}, u32[]{:S(2)}) async-start(f32[16,3,128,128]{3,2,1,0:T(8,128)} %copy-done.2), calls=%async_computation.2 | async-start | bytes 6291456 | tf_op jit(solution)/shard_map/scatter_sums/all_to_all | solution.py:286
  127.9 23.8 %collective-permute-done.20.away_ref = f32[128,128]{1,0:T(8,128)S(1)} collective-permute-done((f32[128,128]{1,0:T(8,128)S(1)}, f32[128,128]{1,0:T(8,128)S(1)}, u32[]{:S(2)}, u32[]{:S(2)}) %collective-permute-start.20) | collective-permute-done | bytes 65568 | tf_op jit(solution)/shard_map/swap_y/ppermute | solution.py:270
  151.7 22.0 %all-to-all-done.2.got_ref = f32[16,3,128,128]{3,2,1,0:T(8,128)S(1)} async-done(((f32[16,3,128,128]{3,2,1,0:T(8,128)}), f32[16,3,128,128]{3,2,1,0:T(8,128)S(1)}, u32[]{:S(2)}, u32[]{:S(2)}) %all-to-all-start.2) | async-done | bytes 3145760 | tf_op jit(solution)/shard_map/scatter_sums/all_to_all | solution.py:286
  (78 shorter events, 37.9 us)
Async XLA Ops:
  6.5 100.0 %all-gather.3.cloned.1.call-start = ((), (), s32[]{:S(2)}) async-start(), calls=%async_computation.3 | async-start | bytes 6684672 | tf_op jit(solution)/shard_map/gather_rows/all_gather | solution.py:252
  11.0 4.3 %collective-permute-start = (f32[128,128]{1,0:T(8,128)S(1)}, f32[128,128]{1,0:T(8,128)S(1)}, u32[]{:S(2)}, u32[]{:S(2)}) collective-permute-start(f32[128,128]{1,0:T(8,128)S(1)} %get-tuple-element.25), channel_id=1, source_target_pairs={{0,16},{16,0},{32,48},{48,32},{64,80},{80,64},{96,112},{112,96},{1... | collective-permute-start | bytes 196616 | tf_op jit(solution)/shard_map/swap_l32/ppermute | solution.py:235
  15.3 7.0 %collective-permute-start.1 = (f32[4,128,128]{2,1,0:T(8,128)S(1)}, f32[4,128,128]{2,1,0:T(8,128)S(1)}, u32[]{:S(2)}, u32[]{:S(2)}) collective-permute-start(f32[4,128,128]{2,1,0:T(8,128)S(1)} %get-tuple-element.27), channel_id=1, source_target_pairs={{0,16},{16,0},{32,48},{48,32},{64,80},{80,64},{96,112},{112,96},{1... | collective-permute-start | bytes 786440 | tf_op jit(solution)/shard_map/swap_rest/ppermute | solution.py:245
  23.6 45.4 %all-to-all-start = ((f32[16,2,128,128]{3,2,1,0:T(8,128)}), f32[16,2,128,128]{3,2,1,0:T(8,128)S(1)}, u32[]{:S(2)}, u32[]{:S(2)}) async-start(f32[16,2,128,128]{3,2,1,0:T(8,128)} %copy-done.7), calls=%async_computation | async-start | bytes 4194304 | tf_op jit(solution)/shard_map/gather_cols/all_to_all | solution.py:248
  30.9 8.8 %collective-permute-start.5 = (f32[2,128,128]{2,1,0:T(8,128)S(1)}, f32[2,128,128]{2,1,0:T(8,128)S(1)}, u32[]{:S(2)}, u32[]{:S(2)}) collective-permute-start(f32[2,128,128]{2,1,0:T(8,128)S(1)} %pad_maximum_fusion), channel_id=1, source_target_pairs={{0,2},{1,3},{2,4},{3,5},{4,6},{5,7},{6,8},{7,9},{8,10},{9,11},{10,... | collective-permute-start | bytes 393224 | tf_op jit(solution)/shard_map/gather_l32_rows/ppermute | solution.py:199
  32.8 10.1 %collective-permute-start.2 = (f32[2,128,128]{2,1,0:T(8,128)S(1)}, f32[2,128,128]{2,1,0:T(8,128)S(1)}, u32[]{:S(2)}, u32[]{:S(2)}) collective-permute-start(f32[2,128,128]{2,1,0:T(8,128)S(1)} %pad_maximum_fusion), channel_id=1, source_target_pairs={{0,14},{1,15},{2,0},{3,1},{4,2},{5,3},{6,4},{7,5},{8,6},{9,7},{10,... | collective-permute-start | bytes 393224 | tf_op jit(solution)/shard_map/gather_l32_rows/ppermute | solution.py:200
  39.7 10.4 %collective-permute-start.6 = (f32[2,128,128]{2,1,0:T(8,128)S(1)}, f32[2,128,128]{2,1,0:T(8,128)S(1)}, u32[]{:S(2)}, u32[]{:S(2)}) collective-permute-start(f32[2,128,128]{2,1,0:T(8,128)S(1)} %collective-permute-done.5), channel_id=1, source_target_pairs={{0,2},{1,3},{2,4},{3,5},{4,6},{5,7},{6,8},{7,9},{8,10},{9,11},{10,... | collective-permute-start | bytes 393224 | tf_op jit(solution)/shard_map/gather_l32_rows/ppermute | solution.py:199
  42.9 10.1 %collective-permute-start.3 = (f32[2,128,128]{2,1,0:T(8,128)S(1)}, f32[2,128,128]{2,1,0:T(8,128)S(1)}, u32[]{:S(2)}, u32[]{:S(2)}) collective-permute-start(f32[2,128,128]{2,1,0:T(8,128)S(1)} %collective-permute-done.2), channel_id=1, source_target_pairs={{0,14},{1,15},{2,0},{3,1},{4,2},{5,3},{6,4},{7,5},{8,6},{9,7},{10,... | collective-permute-start | bytes 393224 | tf_op jit(solution)/shard_map/gather_l32_rows/ppermute | solution.py:200
  50.1 9.2 %collective-permute-start.7 = (f32[2,128,128]{2,1,0:T(8,128)S(1)}, f32[2,128,128]{2,1,0:T(8,128)S(1)}, u32[]{:S(2)}, u32[]{:S(2)}) collective-permute-start(f32[2,128,128]{2,1,0:T(8,128)S(1)} %collective-permute-done.6), channel_id=1, source_target_pairs={{0,2},{1,3},{2,4},{3,5},{4,6},{5,7},{6,8},{7,9},{8,10},{9,11},{10,... | collective-permute-start | bytes 393224 | tf_op jit(solution)/shard_map/gather_l32_rows/ppermute | solution.py:199
  53.0 9.2 %collective-permute-start.4 = (f32[2,128,128]{2,1,0:T(8,128)S(1)}, f32[2,128,128]{2,1,0:T(8,128)S(1)}, u32[]{:S(2)}, u32[]{:S(2)}) collective-permute-start(f32[2,128,128]{2,1,0:T(8,128)S(1)} %collective-permute-done.3), channel_id=1, source_target_pairs={{0,14},{1,15},{2,0},{3,1},{4,2},{5,3},{6,4},{7,5},{8,6},{9,7},{10,... | collective-permute-start | bytes 393224 | tf_op jit(solution)/shard_map/gather_l32_rows/ppermute | solution.py:200
  59.3 6.7 %collective-permute-start.8 = (f32[2,64,128]{2,1,0:T(8,128)S(1)}, f32[2,64,128]{2,1,0:T(8,128)S(1)}, u32[]{:S(2)}, u32[]{:S(2)}) collective-permute-start(f32[2,64,128]{2,1,0:T(8,128)S(1)} %slice.16), channel_id=1, source_target_pairs={{0,2},{1,3},{2,4},{3,5},{4,6},{5,7},{6,8},{7,9},{8,10},{9,11},{10,... | collective-permute-start | bytes 196616 | tf_op jit(solution)/shard_map/gather_l32_rows/ppermute | solution.py:206
  62.1 6.9 %collective-permute-start.9 = (f32[2,64,128]{2,1,0:T(8,128)S(1)}, f32[2,64,128]{2,1,0:T(8,128)S(1)}, u32[]{:S(2)}, u32[]{:S(2)}) collective-permute-start(f32[2,64,128]{2,1,0:T(8,128)S(1)} %slice.17), channel_id=1, source_target_pairs={{0,14},{1,15},{2,0},{3,1},{4,2},{5,3},{6,4},{7,5},{8,6},{9,7},{10,... | collective-permute-start | bytes 196616 | tf_op jit(solution)/shard_map/gather_l32_rows/ppermute | solution.py:207
  74.4 11.6 %collective-permute-start.14 = (f32[2,128,128]{2,1,0:T(8,128)S(1)}, f32[2,128,128]{2,1,0:T(8,128)S(1)}, u32[]{:S(2)}, u32[]{:S(2)}) collective-permute-start(f32[2,128,128]{2,1,0:T(8,128)S(1)} %get-tuple-element.34), channel_id=1, source_target_pairs={{0,2},{1,3},{2,4},{3,5},{4,6},{5,7},{6,8},{7,9},{8,10},{9,11},{10,... | collective-permute-start | bytes 393224 | tf_op jit(solution)/shard_map/gather_t_rows/ppermute | solution.py:199
  74.4 11.6 %collective-permute-start.11 = (f32[2,128,128]{2,1,0:T(8,128)S(1)}, f32[2,128,128]{2,1,0:T(8,128)}, u32[]{:S(2)}, u32[]{:S(2)}) collective-permute-start(f32[2,128,128]{2,1,0:T(8,128)S(1)} %get-tuple-element.34), channel_id=1, source_target_pairs={{0,14},{1,15},{2,0},{3,1},{4,2},{5,3},{6,4},{7,5},{8,6},{9,7},{10,... | collective-permute-start | bytes 393224 | tf_op jit(solution)/shard_map/gather_t_rows/ppermute | solution.py:200
  78.1 28.4 %all-to-all-start.1 = ((f32[8,2,128,128]{3,2,1,0:T(8,128)}), f32[8,2,128,128]{3,2,1,0:T(8,128)}, u32[]{:S(2)}, u32[]{:S(2)}) async-start(f32[8,2,128,128]{3,2,1,0:T(8,128)} %copy-done.8), calls=%async_computation.1 | async-start | bytes 2097152 | tf_op jit(solution)/shard_map/gather_t_cols/all_to_all | solution.py:258
  86.0 6.2 %collective-permute-start.15 = (f32[2,128,128]{2,1,0:T(8,128)S(1)}, f32[2,128,128]{2,1,0:T(8,128)S(1)}, u32[]{:S(2)}, u32[]{:S(2)}) collective-permute-start(f32[2,128,128]{2,1,0:T(8,128)S(1)} %collective-permute-done.14), channel_id=1, source_target_pairs={{0,2},{1,3},{2,4},{3,5},{4,6},{5,7},{6,8},{7,9},{8,10},{9,11},{10,... | collective-permute-start | bytes 393224 | tf_op jit(solution)/shard_map/gather_t_rows/ppermute | solution.py:199
  86.0 6.2 %collective-permute-start.12 = (f32[2,128,128]{2,1,0:T(8,128)}, f32[2,128,128]{2,1,0:T(8,128)S(1)}, u32[]{:S(2)}, u32[]{:S(2)}) collective-permute-start(f32[2,128,128]{2,1,0:T(8,128)} %collective-permute-done.11), channel_id=1, source_target_pairs={{0,14},{1,15},{2,0},{3,1},{4,2},{5,3},{6,4},{7,5},{8,6},{9,7},{10,... | collective-permute-start | bytes 393224 | tf_op jit(solution)/shard_map/gather_t_rows/ppermute | solution.py:200
  92.2 6.2 %collective-permute-start.16 = (f32[2,128,128]{2,1,0:T(8,128)S(1)}, f32[2,128,128]{2,1,0:T(8,128)S(1)}, u32[]{:S(2)}, u32[]{:S(2)}) collective-permute-start(f32[2,128,128]{2,1,0:T(8,128)S(1)} %collective-permute-done.15), channel_id=1, source_target_pairs={{0,2},{1,3},{2,4},{3,5},{4,6},{5,7},{6,8},{7,9},{8,10},{9,11},{10,... | collective-permute-start | bytes 393224 | tf_op jit(solution)/shard_map/gather_t_rows/ppermute | solution.py:199
  92.2 6.2 %collective-permute-start.13 = (f32[2,128,128]{2,1,0:T(8,128)S(1)}, f32[2,128,128]{2,1,0:T(8,128)S(1)}, u32[]{:S(2)}, u32[]{:S(2)}) collective-permute-start(f32[2,128,128]{2,1,0:T(8,128)S(1)} %collective-permute-done.12), channel_id=1, source_target_pairs={{0,14},{1,15},{2,0},{3,1},{4,2},{5,3},{6,4},{7,5},{8,6},{9,7},{10,... | collective-permute-start | bytes 393224 | tf_op jit(solution)/shard_map/gather_t_rows/ppermute | solution.py:200
  98.4 5.5 %collective-permute-start.17 = (f32[2,64,128]{2,1,0:T(8,128)S(1)}, f32[2,64,128]{2,1,0:T(8,128)S(1)}, u32[]{:S(2)}, u32[]{:S(2)}) collective-permute-start(f32[2,64,128]{2,1,0:T(8,128)S(1)} %slice.18), channel_id=1, source_target_pairs={{0,2},{1,3},{2,4},{3,5},{4,6},{5,7},{6,8},{7,9},{8,10},{9,11},{10,... | collective-permute-start | bytes 196616 | tf_op jit(solution)/shard_map/gather_t_rows/ppermute | solution.py:206
  98.4 5.4 %collective-permute-start.18 = (f32[2,64,128]{2,1,0:T(8,128)S(1)}, f32[2,64,128]{2,1,0:T(8,128)S(1)}, u32[]{:S(2)}, u32[]{:S(2)}) collective-permute-start(f32[2,64,128]{2,1,0:T(8,128)S(1)} %slice.19), channel_id=1, source_target_pairs={{0,14},{1,15},{2,0},{3,1},{4,2},{5,3},{6,4},{7,5},{8,6},{9,7},{10,... | collective-permute-start | bytes 196616 | tf_op jit(solution)/shard_map/gather_t_rows/ppermute | solution.py:207
  106.5 7.9 %collective-permute-start.19 = (f32[8,2,128,128]{3,2,1,0:T(8,128)}, f32[8,2,128,128]{3,2,1,0:T(8,128)}, u32[]{:S(2)}, u32[]{:S(2)}) collective-permute-start(f32[8,2,128,128]{3,2,1,0:T(8,128)} %bitcast_dynamic-update-slice_fusion.t_mine_ref), channel_id=1, source_target_pairs={{0,1},{1,0},{2,3},{3,2},{4,5},{5,4},{6,7},{7,6},{8,9},{9,8},{10,11... | collective-permute-start | bytes 3145736 | tf_op jit(solution)/shard_map/gather_t_rows/ppermute | solution.py:213
  119.5 54.2 %all-to-all-start.2 = ((f32[16,3,128,128]{3,2,1,0:T(8,128)}), f32[16,3,128,128]{3,2,1,0:T(8,128)S(1)}, u32[]{:S(2)}, u32[]{:S(2)}) async-start(f32[16,3,128,128]{3,2,1,0:T(8,128)} %copy-done.2), calls=%async_computation.2 | async-start | bytes 6291456 | tf_op jit(solution)/shard_map/scatter_sums/all_to_all | solution.py:286
  126.8 25.0 %collective-permute-start.20 = (f32[128,128]{1,0:T(8,128)S(1)}, f32[128,128]{1,0:T(8,128)S(1)}, u32[]{:S(2)}, u32[]{:S(2)}) collective-permute-start(f32[128,128]{1,0:T(8,128)S(1)} %get-tuple-element.42), channel_id=1, source_target_pairs={{0,16},{16,0},{32,48},{48,32},{64,80},{80,64},{96,112},{112,96},{1... | collective-permute-start | bytes 196616 | tf_op jit(solution)/shard_map/swap_y/ppermute | solution.py:270
  (10 other events, 20.9 us)
Sparse Core Ops, SparseCore 0:
  23.7 55.5 all-gather.2

commit v4 on v3

--- a/solution.py
+++ b/solution.py
@@ -67,8 +67,7 @@
     l2 = [lower(2, s) for s in range(2)]
     l3 = [lower(3, s) for s in range(2)]
     for k in range(N):
-        send_ref[k, 0] = l2[k % 2]
-        send_ref[k, 1] = x
+        send_ref[k] = l2[k % 2]
     root, diag = f_ref[tile(3, 3), :], f_ref[tile(2, 2), :]
     away_ref[0] = home_ref[0] = root
     away_ref[1] = home_ref[1] = diag
@@ -99,7 +98,7 @@
     for d in range(LAYERS):
         k0, k1 = places(place_ref, d)
         a = rows(*(lanes(mine_ref[d, i], other_ref[d, i]) for i in range(2)))
-        total += dot3(split(a), split(rows(l2_ref[k0, 0], l2_ref[k1, 0])))
+        total += dot3(split(a), split(rows(l2_ref[k0], l2_ref[k1])))
     for i in range(2):
         x = total[i * TB : (i + 1) * TB] - l3_ref[i]
         t_ref[i] = x
@@ -111,14 +110,14 @@
     return rows(*(lanes(rows_ref[k, i, j], rows_ref[k + 1, i, j]) for j in range(2)))
 
 
-def uq_kernel(place_ref, rows_ref, cols_ref, u_ref, q_ref):
+def uq_kernel(place_ref, rows_ref, l2_ref, l32_ref, u_ref, q_ref):
     side = lax.rem(place_ref[1], 2)
     u = jnp.zeros((2 * TB, TB), F32)
     q = jnp.zeros((TB, TB), F32)
     for k in range(0, N, 2):
-        b = split(rows(cols_ref[k, 0], cols_ref[k + 1, 0]))
+        b = split(rows(l2_ref[k], l2_ref[k + 1]))
         u += dot3(split(pair_rows(rows_ref, k, 1)), b)
-        b = split(rows(cols_ref[k, 1], cols_ref[k + 1, 1]))
+        b = split(rows(l32_ref[k], l32_ref[k + 1]))
         q += dot3(split(lanes(rows_ref[k, 0, side], rows_ref[k + 1, 0, side])), b)
     for i in range(2):
         u_ref[i] = u[i * TB : (i + 1) * TB]
@@ -192,12 +191,16 @@
     out_ref[tile(3, 3), :] = f_ref[tile(3, 3), :]
 
 
-def gather_layers(x, beside=None):
+def gather_layers(x, ties):
     found = {0: x}
     up = down = x
+    tied = []
     for step in range(1, LAYERS // 2):
         up = lax.ppermute(up, "col", LAYER_UP)
         down = lax.ppermute(down, "col", LAYER_DOWN)
+        if step in ties:
+            up, down, other = lax.optimization_barrier((up, down, ties[step]))
+            tied.append(other)
         found[LAYERS - step] = up
         found[step] = down
     half = TB // 2
@@ -209,8 +212,10 @@
         axis=1,
     )
     mine = jnp.stack([found[d] for d in range(LAYERS)])
-    mine, beside = lax.optimization_barrier((mine, beside))
-    return mine, lax.ppermute(mine, "col", CORE_SWAP), beside
+    if LAYERS // 2 in ties:
+        mine, other = lax.optimization_barrier((mine, ties[LAYERS // 2]))
+        tied.append(other)
+    return (mine, lax.ppermute(mine, "col", CORE_SWAP), *tied)
 
 
 def body(factor, structure):
@@ -225,7 +230,7 @@
     with jax.named_scope("prepare"):
         l32, away, home, send = call(
             prepare_kernel,
-            [square, (4, *square), (4, *square), (N, 2, *square)],
+            [square, (4, *square), (4, *square), (N, *square)],
             mask,
             place,
             flat,
@@ -235,33 +240,33 @@
         l32_away = lax.ppermute(l32, "row", ROW_SWAP)
         even = lax.rem(row, 2) == 0
         l32_pair = jnp.stack([jnp.where(even, l32, l32_away), jnp.where(even, l32_away, l32)])
-        l32_pair, away = lax.optimization_barrier((l32_pair, away))
+    with jax.named_scope("gather_l2_cols"):
+        l2_cols = lax.all_to_all(send, "row", 0, 0, tiled=True)
+    with jax.named_scope("gather_l32_cols"):
+        send = jnp.broadcast_to(l32[None], (N, *square))
+        l32_cols = lax.all_to_all(send, "row", 0, 0, tiled=True)
     with jax.named_scope("swap_rest"):
-        packed, l3 = call(
-            pack_kernel,
-            [(3, 2, *square), (2, *square)],
-            place,
-            home,
-            lax.ppermute(away, "row", ROW_SWAP),
-        )
-    with jax.named_scope("gather_cols"):
-        cols = lax.all_to_all(send, "row", 0, 0, tiled=True)
+        away = lax.ppermute(away, "row", ROW_SWAP)
     with jax.named_scope("gather_l32_rows"):
-        l_mine, l_other, cols = gather_layers(l32_pair, cols)
+        l_mine, l_other, (away, l2_cols), l32_cols = gather_layers(
+            l32_pair, {2: (away, l2_cols), 4: l32_cols}
+        )
+    with jax.named_scope("pack"):
+        packed, l3 = call(pack_kernel, [(3, 2, *square), (2, *square)], place, home, away)
     with jax.named_scope("gather_rows"):
         panels = lax.all_gather(packed, "col", axis=0)
     with jax.named_scope("term_t"):
         t, send = call(
-            t_kernel, [(2, *square), (N // 2, 2, *square)], place, l_mine, l_other, cols, l3
+            t_kernel, [(2, *square), (N // 2, 2, *square)], place, l_mine, l_other, l2_cols, l3
         )
     with jax.named_scope("gather_t_cols"):
         t_cols = lax.all_to_all(
             send, "row", 0, 0, tiled=True, axis_index_groups=SAME_SIDE
         )
     with jax.named_scope("gather_t_rows"):
-        t_mine, t_other, t_cols = gather_layers(t, t_cols)
+        t_mine, t_other, t_cols = gather_layers(t, {3: t_cols})
     with jax.named_scope("term_uq"):
-        u, q = call(uq_kernel, [(2, *square), square], place, panels, cols)
+        u, q = call(uq_kernel, [(2, *square), square], place, panels, l2_cols, l32_cols)
     with jax.named_scope("term_y"):
         y, y_home, y_away = call(
             y_kernel, [(2 * TB, TB), square, square], place, panels, t_cols
@@ -283,6 +288,7 @@
             panels,
         )
     with jax.named_scope("scatter_sums"):
+        sums, y_away = lax.optimization_barrier((sums, y_away))
         got = lax.all_to_all(sums, "row", 0, 0, tiled=True)
     with jax.named_scope("finish"):
         (out,) = call(

time: 184 us -> 192 us (1.043)
  the two profiles are of different devices: /device:TPU:20 before, /device:TPU:32 now
where the time goes in v4:
time: 192 us; the launch traced here: 188 us
  waiting for transfers between devices  48.9 us (25%)
  starting transfers between devices  47 us (24%)
  blocking collectives  46.7 us (24%)
  local copies, waits for them, and re-layouts  17.1 us (9%)
  Pallas kernels  14.4 us (8%)
  between operations  13.6 us (7%)
    all_to_all x1, blocking collectives, body(): got = lax.all_to_all(sums, 'row', 0, 0, tiled=True)  46.7 us
    ppermute x6, waiting for transfers between devices, gather_layers(): down = lax.ppermute(down, 'col', LAYER_DOWN)  17.3 us
    unnamed x34, local copies, waits for them, and re-layouts  14.4 us
    pallas_call x7, Pallas kernels, call(): pl.pallas_call(kernel, out_shape=[jax.ShapeDtypeStruct(s, F32) for s in s...  14.4 us
    ppermute x6, starting transfers between devices, gather_layers(): down = lax.ppermute(down, 'col', LAYER_DOWN)  14 us
    ppermute x1, waiting for transfers between devices, body(): l32_away = lax.ppermute(l32, 'row', ROW_SWAP)  13.6 us
    ppermute x6, waiting for transfers between devices, gather_layers(): up = lax.ppermute(up, 'col', LAYER_UP)  8.85 us
    all_to_all x1, starting transfers between devices, body(): l32_cols = lax.all_to_all(send, 'row', 0, 0, tiled=True)  7.05 us
  transfers between devices with their start and end apart: 25, of which 15 were waited for; matrix products, arithmetic and copies ran while one was open for 5% of the time, Pallas kernels for 5%

profile of v4, /device:TPU:32, one launch (start us, length us, event | category | flops | bytes accessed | tf_op | source)
XLA Modules:
  0.0 188.5 jit_solution(10018279461544491011)
XLA Ops:
  10.4 7.0 %all-to-all-start = ((f32[16,128,128]{2,1,0:T(8,128)}), f32[16,128,128]{2,1,0:T(8,128)S(1)}, u32[]{:S(2)}, u32[]{:S(2)}) async-start(f32[16,128,128]{2,1,0:T(8,128)} %get-tuple-element.32), calls=%async_computation | async-start | bytes 2097152 | tf_op jit(solution)/shard_map/gather_l2_cols/all_to_all | solution.py:244
  19.5 13.6 %collective-permute-done = f32[128,128]{1,0:T(8,128)S(1)} collective-permute-done((f32[128,128]{1,0:T(8,128)S(1)}, f32[128,128]{1,0:T(8,128)S(1)}, u32[]{:S(2)}, u32[]{:S(2)}) %collective-permute-start) | collective-permute-done | bytes 65568 | tf_op jit(solution)/shard_map/swap_l32/ppermute | solution.py:240
  35.4 2.9 %collective-permute-done.3 = f32[2,128,128]{2,1,0:T(8,128)S(1)} collective-permute-done((f32[2,128,128]{2,1,0:T(8,128)S(1)}, f32[2,128,128]{2,1,0:T(8,128)S(1)}, u32[]{:S(2)}, u32[]{:S(2)}) %collective-permute-start.3) | collective-permute-done | bytes 131104 | tf_op jit(solution)/shard_map/gather_l32_rows/ppermute | solution.py:200
  38.2 3.3 %collective-permute-start.4 = (f32[2,128,128]{2,1,0:T(8,128)S(1)}, f32[2,128,128]{2,1,0:T(8,128)S(1)}, u32[]{:S(2)}, u32[]{:S(2)}) collective-permute-start(f32[2,128,128]{2,1,0:T(8,128)S(1)} %collective-permute-done.3), channel_id=1, source_target_pairs={{0,14},{1,15},{2,0},{3,1},{4,2},{5,3},{6,4},{7,5},{8,6},{9,7},{10,... | collective-permute-start | bytes 393224 | tf_op jit(solution)/shard_map/gather_l32_rows/ppermute | solution.py:200
  42.0 2.1 %collective-permute-done.4 = f32[2,128,128]{2,1,0:T(8,128)S(1)} collective-permute-done((f32[2,128,128]{2,1,0:T(8,128)S(1)}, f32[2,128,128]{2,1,0:T(8,128)S(1)}, u32[]{:S(2)}, u32[]{:S(2)}) %collective-permute-start.4) | collective-permute-done | bytes 131104 | tf_op jit(solution)/shard_map/gather_l32_rows/ppermute | solution.py:200
  44.0 4.1 %collective-permute-done.2 = f32[2,128,128]{2,1,0:T(8,128)S(1)} collective-permute-done((f32[2,128,128]{2,1,0:T(8,128)S(1)}, f32[2,128,128]{2,1,0:T(8,128)S(1)}, u32[]{:S(2)}, u32[]{:S(2)}) %collective-permute-start.2) | collective-permute-done | bytes 131104 | tf_op jit(solution)/shard_map/gather_l32_rows/ppermute | solution.py:199
  51.2 7.1 %all-to-all-start.1 = ((f32[16,128,128]{2,1,0:T(8,128)}), f32[16,128,128]{2,1,0:T(8,128)S(1)}, u32[]{:S(2)}, u32[]{:S(2)}) async-start(f32[16,128,128]{2,1,0:T(8,128)} %broadcast_in_dim.2), calls=%async_computation.1 | async-start | bytes 2097152 | tf_op jit(solution)/shard_map/gather_l32_cols/all_to_all | solution.py:247
  59.2 3.3 %collective-permute-start.6 = (f32[2,128,128]{2,1,0:T(8,128)}, f32[2,128,128]{2,1,0:T(8,128)S(1)}, u32[]{:S(2)}, u32[]{:S(2)}) collective-permute-start(f32[2,128,128]{2,1,0:T(8,128)} %copy-done.9), channel_id=1, source_target_pairs={{0,14},{1,15},{2,0},{3,1},{4,2},{5,3},{6,4},{7,5},{8,6},{9,7},{10,... | collective-permute-start | bytes 393224 | tf_op jit(solution)/shard_map/gather_l32_rows/ppermute | solution.py:200
  63.5 5.0 %collective-permute-done.6 = f32[2,128,128]{2,1,0:T(8,128)S(1)} collective-permute-done((f32[2,128,128]{2,1,0:T(8,128)}, f32[2,128,128]{2,1,0:T(8,128)S(1)}, u32[]{:S(2)}, u32[]{:S(2)}) %collective-permute-start.6) | collective-permute-done | bytes 131104 | tf_op jit(solution)/shard_map/gather_l32_rows/ppermute | solution.py:200
  68.4 2.4 %collective-permute-start.9 = (f32[2,64,128]{2,1,0:T(8,128)S(1)}, f32[2,64,128]{2,1,0:T(8,128)S(1)}, u32[]{:S(2)}, u32[]{:S(2)}) collective-permute-start(f32[2,64,128]{2,1,0:T(8,128)S(1)} %slice.17), channel_id=1, source_target_pairs={{0,14},{1,15},{2,0},{3,1},{4,2},{5,3},{6,4},{7,5},{8,6},{9,7},{10,... | collective-permute-start | bytes 196616 | tf_op jit(solution)/shard_map/gather_l32_rows/ppermute | solution.py:210
  71.2 2.9 %collective-permute-done.9 = f32[2,64,128]{2,1,0:T(8,128)S(1)} collective-permute-done((f32[2,64,128]{2,1,0:T(8,128)S(1)}, f32[2,64,128]{2,1,0:T(8,128)S(1)}, u32[]{:S(2)}, u32[]{:S(2)}) %collective-permute-start.9) | collective-permute-done | bytes 65568 | tf_op jit(solution)/shard_map/gather_l32_rows/ppermute | solution.py:210
  74.1 2.1 %collective-permute-done.8 = f32[2,64,128]{2,1,0:T(8,128)S(1)} collective-permute-done((f32[2,64,128]{2,1,0:T(8,128)S(1)}, f32[2,64,128]{2,1,0:T(8,128)S(1)}, u32[]{:S(2)}, u32[]{:S(2)}) %collective-permute-start.8) | collective-permute-done | bytes 65568 | tf_op jit(solution)/shard_map/gather_l32_rows/ppermute | solution.py:209
  77.3 2.6 %collective-permute-done.10.other_ref.l_other_ref = f32[8,2,128,128]{3,2,1,0:T(8,128)S(1)} collective-permute-done((f32[8,2,128,128]{3,2,1,0:T(8,128)S(1)}, f32[8,2,128,128]{3,2,1,0:T(8,128)S(1)}, u32[]{:S(2)}, u32[]{:S(2)}) %collective-permute-start.10) | collective-permute-done | bytes 1048608 | tf_op jit(solution)/shard_map/gather_l32_rows/ppermute | solution.py:218
  83.5 6.8 %all-to-all-start.2 = ((f32[8,2,128,128]{3,2,1,0:T(8,128)}), f32[8,2,128,128]{3,2,1,0:T(8,128)}, u32[]{:S(2)}, u32[]{:S(2)}) async-start(f32[8,2,128,128]{3,2,1,0:T(8,128)} %copy-done.6), calls=%async_computation.2 | async-start | bytes 2097152 | tf_op jit(solution)/shard_map/gather_t_cols/all_to_all | solution.py:263
  90.3 3.5 %collective-permute-start.14 = (f32[2,128,128]{2,1,0:T(8,128)S(1)}, f32[2,128,128]{2,1,0:T(8,128)S(1)}, u32[]{:S(2)}, u32[]{:S(2)}) collective-permute-start(f32[2,128,128]{2,1,0:T(8,128)S(1)} %get-tuple-element.40), channel_id=1, source_target_pairs={{0,14},{1,15},{2,0},{3,1},{4,2},{5,3},{6,4},{7,5},{8,6},{9,7},{10,... | collective-permute-start | bytes 393224 | tf_op jit(solution)/shard_map/gather_t_rows/ppermute | solution.py:200
  94.5 3.5 %collective-permute-done.14 = f32[2,128,128]{2,1,0:T(8,128)S(1)} collective-permute-done((f32[2,128,128]{2,1,0:T(8,128)S(1)}, f32[2,128,128]{2,1,0:T(8,128)S(1)}, u32[]{:S(2)}, u32[]{:S(2)}) %collective-permute-start.14) | collective-permute-done | bytes 131104 | tf_op jit(solution)/shard_map/gather_t_rows/ppermute | solution.py:200
  100.8 2.3 %collective-permute-done.15 = f32[2,128,128]{2,1,0:T(8,128)S(1)} collective-permute-done((f32[2,128,128]{2,1,0:T(8,128)S(1)}, f32[2,128,128]{2,1,0:T(8,128)S(1)}, u32[]{:S(2)}, u32[]{:S(2)}) %collective-permute-start.15) | collective-permute-done | bytes 131104 | tf_op jit(solution)/shard_map/gather_t_rows/ppermute | solution.py:200
  103.0 2.2 %collective-permute-start.16 = (f32[2,128,128]{2,1,0:T(8,128)S(1)}, f32[2,128,128]{2,1,0:T(8,128)S(1)}, u32[]{:S(2)}, u32[]{:S(2)}) collective-permute-start(f32[2,128,128]{2,1,0:T(8,128)S(1)} %collective-permute-done.15), channel_id=1, source_target_pairs={{0,14},{1,15},{2,0},{3,1},{4,2},{5,3},{6,4},{7,5},{8,6},{9,7},{10,... | collective-permute-start | bytes 393224 | tf_op jit(solution)/shard_map/gather_t_rows/ppermute | solution.py:200
  108.0 3.9 %collective-permute-done.13 = f32[2,128,128]{2,1,0:T(8,128)S(1)} collective-permute-done((f32[2,128,128]{2,1,0:T(8,128)S(1)}, f32[2,128,128]{2,1,0:T(8,128)S(1)}, u32[]{:S(2)}, u32[]{:S(2)}) %collective-permute-start.13) | collective-permute-done | bytes 131104 | tf_op jit(solution)/shard_map/gather_t_rows/ppermute | solution.py:199
  112.0 3.3 %collective-permute-start.18 = (f32[2,64,128]{2,1,0:T(8,128)S(1)}, f32[2,64,128]{2,1,0:T(8,128)S(1)}, u32[]{:S(2)}, u32[]{:S(2)}) collective-permute-start(f32[2,64,128]{2,1,0:T(8,128)S(1)} %slice.15), channel_id=1, source_target_pairs={{0,14},{1,15},{2,0},{3,1},{4,2},{5,3},{6,4},{7,5},{8,6},{9,7},{10,... | collective-permute-start | bytes 196616 | tf_op jit(solution)/shard_map/gather_t_rows/ppermute | solution.py:210
  121.1 2.8 %copy-done = f32[48,2,128,128]{3,2,1,0:T(8,128)S(1)} copy-done((f32[48,2,128,128]{3,2,1,0:T(8,128)S(1)}, f32[48,2,128,128]{3,2,1,0:T(8,128)}, u32[]{:S(2)}) %copy-start) | copy-done | bytes 6291480
  123.8 2.4 %term_y.1 = (f32[256,128]{1,0:T(8,128)S(1)}, f32[128,128]{1,0:T(8,128)S(1)}, f32[128,128]{1,0:T(8,128)S(1)}) custom-call(s32[2]{0:T(128)S(1)} %pad_add_fusion.place_ref, f32[16,3,2,128,128]{4,3,2,1,0:T(8,128)S(1)} %bitcast.46, f32[8,2,128,128]{3,2,1,0:T(8,128)} %all-to-all-done.2.t_ref), custom_call_target="tpu_custom_call" | custom-call | tf_op jit(solution)/shard_map/term_y/pallas_call | solution.py:50
  129.5 3.6 %sums.1 = f32[16,3,128,128]{3,2,1,0:T(8,128)S(1)} custom-call(s32[2]{0:T(128)S(1)} %pad_add_fusion.place_ref, f32[256,128]{1,0:T(8,128)S(1)} %get-tuple-element.43.y_ref, f32[2,128,128]{2,1,0:T(8,128)S(1)} %get-tuple-element.45.u_ref, f32[128,128]{1,0:T(8,128)S(1)} %get-tuple-element.46.q_ref, ...), custom_call_target="tpu_custom_call" | custom-call | tf_op jit(solution)/shard_map/sums/pallas_call | solution.py:50
  133.2 46.7 %all_to_all.20.got_ref = f32[16,3,128,128]{3,2,1,0:T(8,128)S(1)} all-to-all(f32[16,3,128,128]{3,2,1,0:T(8,128)S(1)} %sums.1), channel_id=1, replica_groups=mesh['row'=16,'col'=16] {'row'}, dimensions={0} | all-to-all | bytes 6291456 | tf_op jit(solution)/shard_map/scatter_sums/all_to_all | solution.py:292
  (84 shorter events, 35.4 us)
Async XLA Ops:
  10.4 37.7 %all-to-all-start = ((f32[16,128,128]{2,1,0:T(8,128)}), f32[16,128,128]{2,1,0:T(8,128)S(1)}, u32[]{:S(2)}, u32[]{:S(2)}) async-start(f32[16,128,128]{2,1,0:T(8,128)} %get-tuple-element.32), calls=%async_computation | async-start | bytes 2097152 | tf_op jit(solution)/shard_map/gather_l2_cols/all_to_all | solution.py:244
  17.5 103.6 %all-gather.3.cloned.1.call-start = ((), (), s32[]{:S(2)}) async-start(), calls=%async_computation.4 | async-start | bytes 6684672 | tf_op jit(solution)/shard_map/gather_rows/all_gather | solution.py:257
  17.5 15.6 %collective-permute-start = (f32[128,128]{1,0:T(8,128)S(1)}, f32[128,128]{1,0:T(8,128)S(1)}, u32[]{:S(2)}, u32[]{:S(2)}) collective-permute-start(f32[128,128]{1,0:T(8,128)S(1)} %get-tuple-element.30), channel_id=1, source_target_pairs={{0,16},{16,0},{32,48},{48,32},{64,80},{80,64},{96,112},{112,96},{1... | collective-permute-start | bytes 196616 | tf_op jit(solution)/shard_map/swap_l32/ppermute | solution.py:240
  33.2 5.0 %collective-permute-start.3 = (f32[2,128,128]{2,1,0:T(8,128)S(1)}, f32[2,128,128]{2,1,0:T(8,128)S(1)}, u32[]{:S(2)}, u32[]{:S(2)}) collective-permute-start(f32[2,128,128]{2,1,0:T(8,128)S(1)} %pad_maximum_fusion), channel_id=1, source_target_pairs={{0,14},{1,15},{2,0},{3,1},{4,2},{5,3},{6,4},{7,5},{8,6},{9,7},{10,... | collective-permute-start | bytes 393224 | tf_op jit(solution)/shard_map/gather_l32_rows/ppermute | solution.py:200
  33.3 8.7 %collective-permute-start.5 = (f32[4,128,128]{2,1,0:T(8,128)S(1)}, f32[4,128,128]{2,1,0:T(8,128)S(1)}, u32[]{:S(2)}, u32[]{:S(2)}) collective-permute-start(f32[4,128,128]{2,1,0:T(8,128)S(1)} %get-tuple-element.31), channel_id=1, source_target_pairs={{0,16},{16,0},{32,48},{48,32},{64,80},{80,64},{96,112},{112,96},{1... | collective-permute-start | bytes 786440 | tf_op jit(solution)/shard_map/swap_rest/ppermute | solution.py:249
  33.4 8.6 %collective-permute-start.1 = (f32[2,128,128]{2,1,0:T(8,128)S(1)}, f32[2,128,128]{2,1,0:T(8,128)S(1)}, u32[]{:S(2)}, u32[]{:S(2)}) collective-permute-start(f32[2,128,128]{2,1,0:T(8,128)S(1)} %pad_maximum_fusion), channel_id=1, source_target_pairs={{0,2},{1,3},{2,4},{3,5},{4,6},{5,7},{6,8},{7,9},{8,10},{9,11},{10,... | collective-permute-start | bytes 393224 | tf_op jit(solution)/shard_map/gather_l32_rows/ppermute | solution.py:199
  38.2 5.8 %collective-permute-start.4 = (f32[2,128,128]{2,1,0:T(8,128)S(1)}, f32[2,128,128]{2,1,0:T(8,128)S(1)}, u32[]{:S(2)}, u32[]{:S(2)}) collective-permute-start(f32[2,128,128]{2,1,0:T(8,128)S(1)} %collective-permute-done.3), channel_id=1, source_target_pairs={{0,14},{1,15},{2,0},{3,1},{4,2},{5,3},{6,4},{7,5},{8,6},{9,7},{10,... | collective-permute-start | bytes 393224 | tf_op jit(solution)/shard_map/gather_l32_rows/ppermute | solution.py:200
  41.9 6.2 %collective-permute-start.2 = (f32[2,128,128]{2,1,0:T(8,128)S(1)}, f32[2,128,128]{2,1,0:T(8,128)S(1)}, u32[]{:S(2)}, u32[]{:S(2)}) collective-permute-start(f32[2,128,128]{2,1,0:T(8,128)S(1)} %collective-permute-done.1), channel_id=1, source_target_pairs={{0,2},{1,3},{2,4},{3,5},{4,6},{5,7},{6,8},{7,9},{8,10},{9,11},{10,... | collective-permute-start | bytes 393224 | tf_op jit(solution)/shard_map/gather_l32_rows/ppermute | solution.py:199
  51.2 26.0 %all-to-all-start.1 = ((f32[16,128,128]{2,1,0:T(8,128)}), f32[16,128,128]{2,1,0:T(8,128)S(1)}, u32[]{:S(2)}, u32[]{:S(2)}) async-start(f32[16,128,128]{2,1,0:T(8,128)} %broadcast_in_dim.2), calls=%async_computation.1 | async-start | bytes 2097152 | tf_op jit(solution)/shard_map/gather_l32_cols/all_to_all | solution.py:247
  59.2 9.2 %collective-permute-start.6 = (f32[2,128,128]{2,1,0:T(8,128)}, f32[2,128,128]{2,1,0:T(8,128)S(1)}, u32[]{:S(2)}, u32[]{:S(2)}) collective-permute-start(f32[2,128,128]{2,1,0:T(8,128)} %copy-done.9), channel_id=1, source_target_pairs={{0,14},{1,15},{2,0},{3,1},{4,2},{5,3},{6,4},{7,5},{8,6},{9,7},{10,... | collective-permute-start | bytes 393224 | tf_op jit(solution)/shard_map/gather_l32_rows/ppermute | solution.py:200
  62.5 8.3 %collective-permute-start.7 = (f32[2,128,128]{2,1,0:T(8,128)}, f32[2,128,128]{2,1,0:T(8,128)S(1)}, u32[]{:S(2)}, u32[]{:S(2)}) collective-permute-start(f32[2,128,128]{2,1,0:T(8,128)} %copy-done.7), channel_id=1, source_target_pairs={{0,2},{1,3},{2,4},{3,5},{4,6},{5,7},{6,8},{7,9},{8,10},{9,11},{10,... | collective-permute-start | bytes 393224 | tf_op jit(solution)/shard_map/gather_l32_rows/ppermute | solution.py:199
  68.4 5.6 %collective-permute-start.9 = (f32[2,64,128]{2,1,0:T(8,128)S(1)}, f32[2,64,128]{2,1,0:T(8,128)S(1)}, u32[]{:S(2)}, u32[]{:S(2)}) collective-permute-start(f32[2,64,128]{2,1,0:T(8,128)S(1)} %slice.17), channel_id=1, source_target_pairs={{0,14},{1,15},{2,0},{3,1},{4,2},{5,3},{6,4},{7,5},{8,6},{9,7},{10,... | collective-permute-start | bytes 196616 | tf_op jit(solution)/shard_map/gather_l32_rows/ppermute | solution.py:210
  70.8 5.4 %collective-permute-start.8 = (f32[2,64,128]{2,1,0:T(8,128)S(1)}, f32[2,64,128]{2,1,0:T(8,128)S(1)}, u32[]{:S(2)}, u32[]{:S(2)}) collective-permute-start(f32[2,64,128]{2,1,0:T(8,128)S(1)} %slice.16), channel_id=1, source_target_pairs={{0,2},{1,3},{2,4},{3,5},{4,6},{5,7},{6,8},{7,9},{8,10},{9,11},{10,... | collective-permute-start | bytes 196616 | tf_op jit(solution)/shard_map/gather_l32_rows/ppermute | solution.py:209
  83.5 28.4 %all-to-all-start.2 = ((f32[8,2,128,128]{3,2,1,0:T(8,128)}), f32[8,2,128,128]{3,2,1,0:T(8,128)}, u32[]{:S(2)}, u32[]{:S(2)}) async-start(f32[8,2,128,128]{3,2,1,0:T(8,128)} %copy-done.6), calls=%async_computation.2 | async-start | bytes 2097152 | tf_op jit(solution)/shard_map/gather_t_cols/all_to_all | solution.py:263
  90.3 7.7 %collective-permute-start.14 = (f32[2,128,128]{2,1,0:T(8,128)S(1)}, f32[2,128,128]{2,1,0:T(8,128)S(1)}, u32[]{:S(2)}, u32[]{:S(2)}) collective-permute-start(f32[2,128,128]{2,1,0:T(8,128)S(1)} %get-tuple-element.40), channel_id=1, source_target_pairs={{0,14},{1,15},{2,0},{3,1},{4,2},{5,3},{6,4},{7,5},{8,6},{9,7},{10,... | collective-permute-start | bytes 393224 | tf_op jit(solution)/shard_map/gather_t_rows/ppermute | solution.py:200
  93.9 5.8 %collective-permute-start.11 = (f32[2,128,128]{2,1,0:T(8,128)S(1)}, f32[2,128,128]{2,1,0:T(8,128)S(1)}, u32[]{:S(2)}, u32[]{:S(2)}) collective-permute-start(f32[2,128,128]{2,1,0:T(8,128)S(1)} %get-tuple-element.40), channel_id=1, source_target_pairs={{0,2},{1,3},{2,4},{3,5},{4,6},{5,7},{6,8},{7,9},{8,10},{9,11},{10,... | collective-permute-start | bytes 393224 | tf_op jit(solution)/shard_map/gather_t_rows/ppermute | solution.py:199
  98.1 5.0 %collective-permute-start.15 = (f32[2,128,128]{2,1,0:T(8,128)S(1)}, f32[2,128,128]{2,1,0:T(8,128)S(1)}, u32[]{:S(2)}, u32[]{:S(2)}) collective-permute-start(f32[2,128,128]{2,1,0:T(8,128)S(1)} %collective-permute-done.14), channel_id=1, source_target_pairs={{0,14},{1,15},{2,0},{3,1},{4,2},{5,3},{6,4},{7,5},{8,6},{9,7},{10,... | collective-permute-start | bytes 393224 | tf_op jit(solution)/shard_map/gather_t_rows/ppermute | solution.py:200
  99.6 6.1 %collective-permute-start.12 = (f32[2,128,128]{2,1,0:T(8,128)S(1)}, f32[2,128,128]{2,1,0:T(8,128)S(1)}, u32[]{:S(2)}, u32[]{:S(2)}) collective-permute-start(f32[2,128,128]{2,1,0:T(8,128)S(1)} %collective-permute-done.11), channel_id=1, source_target_pairs={{0,2},{1,3},{2,4},{3,5},{4,6},{5,7},{6,8},{7,9},{8,10},{9,11},{10,... | collective-permute-start | bytes 393224 | tf_op jit(solution)/shard_map/gather_t_rows/ppermute | solution.py:199
  103.0 5.0 %collective-permute-start.16 = (f32[2,128,128]{2,1,0:T(8,128)S(1)}, f32[2,128,128]{2,1,0:T(8,128)S(1)}, u32[]{:S(2)}, u32[]{:S(2)}) collective-permute-start(f32[2,128,128]{2,1,0:T(8,128)S(1)} %collective-permute-done.15), channel_id=1, source_target_pairs={{0,14},{1,15},{2,0},{3,1},{4,2},{5,3},{6,4},{7,5},{8,6},{9,7},{10,... | collective-permute-start | bytes 393224 | tf_op jit(solution)/shard_map/gather_t_rows/ppermute | solution.py:200
  105.7 6.2 %collective-permute-start.13 = (f32[2,128,128]{2,1,0:T(8,128)S(1)}, f32[2,128,128]{2,1,0:T(8,128)S(1)}, u32[]{:S(2)}, u32[]{:S(2)}) collective-permute-start(f32[2,128,128]{2,1,0:T(8,128)S(1)} %collective-permute-done.12), channel_id=1, source_target_pairs={{0,2},{1,3},{2,4},{3,5},{4,6},{5,7},{6,8},{7,9},{8,10},{9,11},{10,... | collective-permute-start | bytes 393224 | tf_op jit(solution)/shard_map/gather_t_rows/ppermute | solution.py:199
  111.9 5.6 %collective-permute-start.17 = (f32[2,64,128]{2,1,0:T(8,128)S(1)}, f32[2,64,128]{2,1,0:T(8,128)S(1)}, u32[]{:S(2)}, u32[]{:S(2)}) collective-permute-start(f32[2,64,128]{2,1,0:T(8,128)S(1)} %slice.14), channel_id=1, source_target_pairs={{0,2},{1,3},{2,4},{3,5},{4,6},{5,7},{6,8},{7,9},{8,10},{9,11},{10,... | collective-permute-start | bytes 196616 | tf_op jit(solution)/shard_map/gather_t_rows/ppermute | solution.py:209
  112.0 5.5 %collective-permute-start.18 = (f32[2,64,128]{2,1,0:T(8,128)S(1)}, f32[2,64,128]{2,1,0:T(8,128)S(1)}, u32[]{:S(2)}, u32[]{:S(2)}) collective-permute-start(f32[2,64,128]{2,1,0:T(8,128)S(1)} %slice.15), channel_id=1, source_target_pairs={{0,14},{1,15},{2,0},{3,1},{4,2},{5,3},{6,4},{7,5},{8,6},{9,7},{10,... | collective-permute-start | bytes 196616 | tf_op jit(solution)/shard_map/gather_t_rows/ppermute | solution.py:210
  121.0 8.4 %collective-permute-start.19 = (f32[8,2,128,128]{3,2,1,0:T(8,128)}, f32[8,2,128,128]{3,2,1,0:T(8,128)}, u32[]{:S(2)}, u32[]{:S(2)}) collective-permute-start(f32[8,2,128,128]{3,2,1,0:T(8,128)} %bitcast_dynamic-update-slice_fusion.t_mine_ref), channel_id=1, source_target_pairs={{0,1},{1,0},{2,3},{3,2},{4,5},{5,4},{6,7},{7,6},{8,9},{9,8},{10,11... | collective-permute-start | bytes 3145736 | tf_op jit(solution)/shard_map/gather_t_rows/ppermute | solution.py:218
  126.2 6.9 %collective-permute-start.20 = (f32[128,128]{1,0:T(8,128)S(1)}, f32[128,128]{1,0:T(8,128)S(1)}, u32[]{:S(2)}, u32[]{:S(2)}) collective-permute-start(f32[128,128]{1,0:T(8,128)S(1)} %get-tuple-element.49), channel_id=1, source_target_pairs={{0,16},{16,0},{32,48},{48,32},{64,80},{80,64},{96,112},{112,96},{1... | collective-permute-start | bytes 196616 | tf_op jit(solution)/shard_map/swap_y/ppermute | solution.py:275
  (12 other events, 79.3 us)
Sparse Core Ops, SparseCore 0:
  50.3 49.4 all-gather.2

commit v5 on v4

--- a/solution.py
+++ b/solution.py
@@ -56,7 +56,7 @@
     )(*args)
 
 
-def prepare_kernel(mask_ref, place_ref, f_ref, l32_ref, away_ref, home_ref, send_ref):
+def prepare_kernel(mask_ref, place_ref, f_ref, l32_ref, away_ref, home_ref, send_ref, wide_ref):
     side = lax.rem(place_ref[1], 2)
 
     def lower(r, c):
@@ -68,6 +68,8 @@
     l3 = [lower(3, s) for s in range(2)]
     for k in range(N):
         send_ref[k] = l2[k % 2]
+    for k in range(N // 2):
+        wide_ref[k] = x
     root, diag = f_ref[tile(3, 3), :], f_ref[tile(2, 2), :]
     away_ref[0] = home_ref[0] = root
     away_ref[1] = home_ref[1] = diag
@@ -106,22 +108,26 @@
             send_ref[k, i] = x
 
 
-def pair_rows(rows_ref, k, i):
-    return rows(*(lanes(rows_ref[k, i, j], rows_ref[k + 1, i, j]) for j in range(2)))
-
-
-def uq_kernel(place_ref, rows_ref, l2_ref, l32_ref, u_ref, q_ref):
+def pair_rows(rows_ref, k0, k1, i):
+    return rows(*(lanes(rows_ref[k0, i, j], rows_ref[k1, i, j]) for j in range(2)))
+
+
+def uq_kernel(place_ref, rows_ref, l2_ref, l32_ref, u_ref, home_ref, away_ref):
     side = lax.rem(place_ref[1], 2)
     u = jnp.zeros((2 * TB, TB), F32)
-    q = jnp.zeros((TB, TB), F32)
+    q = jnp.zeros((2 * TB, TB), F32)
     for k in range(0, N, 2):
         b = split(rows(l2_ref[k], l2_ref[k + 1]))
-        u += dot3(split(pair_rows(rows_ref, k, 1)), b)
-        b = split(rows(l32_ref[k], l32_ref[k + 1]))
-        q += dot3(split(lanes(rows_ref[k, 0, side], rows_ref[k + 1, 0, side])), b)
+        u += dot3(split(pair_rows(rows_ref, k, k + 1, 1)), b)
+    for i in range(0, N // 2, 2):
+        k = 2 * i + side
+        b = split(rows(l32_ref[i], l32_ref[i + 1]))
+        q += dot3(split(pair_rows(rows_ref, k, k + 2, 0)), b)
     for i in range(2):
         u_ref[i] = u[i * TB : (i + 1) * TB]
-    q_ref[...] = q
+    even = side == 0
+    home_ref[...] = jnp.where(even, q[:TB], q[TB:])
+    away_ref[...] = jnp.where(even, q[TB:], q[:TB])
 
 
 def y_kernel(place_ref, rows_ref, t_ref, y_ref, home_ref, away_ref):
@@ -129,7 +135,7 @@
     y = jnp.zeros((2 * TB, TB), F32)
     for k in range(0, N, 2):
         b = split(rows(t_ref[k // 2, 0], t_ref[k // 2, 1]))
-        y += dot3(split(pair_rows(rows_ref, k, 0)), b)
+        y += dot3(split(pair_rows(rows_ref, k, k + 1, 0)), b)
     y_ref[...] = y
     even = side == 0
     home_ref[...] = jnp.where(even, y[:TB], y[TB:])
@@ -137,7 +143,7 @@
 
 
 def sums_kernel(
-    place_ref, y_ref, u_ref, q_ref, l_mine_ref, l_other_ref, t_mine_ref, t_other_ref, rows_ref, sum_ref
+    place_ref, y_ref, u_ref, q_home_ref, q_away_ref, l_mine_ref, l_other_ref, t_mine_ref, t_other_ref, rows_ref, sum_ref
 ):
     row = place_ref[1]
     side = lax.rem(row, 2)
@@ -145,7 +151,7 @@
     u = [u_ref[i].T for i in range(2)]
     y_split = split(y)
     yu_split = split(lanes(y, *u))
-    q_split = split(q_ref[...].T)
+    q_split = split((q_home_ref[...] + q_away_ref[...]).T)
     for d in range(LAYERS):
         ks = places(place_ref, d)
         l32 = rows(*(lanes(l_mine_ref[d, i], l_other_ref[d, i]) for i in range(2)))
@@ -164,7 +170,7 @@
         sum_ref[row - side + i, 0] += u[i]
 
 
-def finish_kernel(mask_ref, place_ref, f_ref, got_ref, home_ref, away_ref, q_ref, out_ref):
+def finish_kernel(mask_ref, place_ref, f_ref, got_ref, home_ref, away_ref, q_home_ref, q_away_ref, out_ref):
     even = lax.rem(place_ref[1], 2) == 0
 
     def total(i, ks):
@@ -187,7 +193,7 @@
         out_ref[tile(2, s), :] = masked(s, 2, -total(0, ks))
         out_ref[tile(3, s), :] = masked(s, 3, y[s])
     out_ref[tile(2, 2), :] = f_ref[tile(2, 2), :] + total(2, range(N))
-    out_ref[tile(3, 2), :] = masked(2, 3, -q_ref[...])
+    out_ref[tile(3, 2), :] = masked(2, 3, -(q_home_ref[...] + q_away_ref[...]))
     out_ref[tile(3, 3), :] = f_ref[tile(3, 3), :]
 
 
@@ -228,9 +234,9 @@
     square = (TB, TB)
 
     with jax.named_scope("prepare"):
-        l32, away, home, send = call(
+        l32, away, home, send, wide = call(
             prepare_kernel,
-            [square, (4, *square), (4, *square), (N, *square)],
+            [square, (4, *square), (4, *square), (N, *square), (N // 2, *square)],
             mask,
             place,
             flat,
@@ -240,16 +246,17 @@
         l32_away = lax.ppermute(l32, "row", ROW_SWAP)
         even = lax.rem(row, 2) == 0
         l32_pair = jnp.stack([jnp.where(even, l32, l32_away), jnp.where(even, l32_away, l32)])
+    with jax.named_scope("swap_rest"):
+        l32_pair, away = lax.optimization_barrier((l32_pair, away))
+        away = lax.ppermute(away, "row", ROW_SWAP)
     with jax.named_scope("gather_l2_cols"):
+        send, wide, away = lax.optimization_barrier((send, wide, away))
         l2_cols = lax.all_to_all(send, "row", 0, 0, tiled=True)
     with jax.named_scope("gather_l32_cols"):
-        send = jnp.broadcast_to(l32[None], (N, *square))
-        l32_cols = lax.all_to_all(send, "row", 0, 0, tiled=True)
-    with jax.named_scope("swap_rest"):
-        away = lax.ppermute(away, "row", ROW_SWAP)
+        l32_cols = lax.all_to_all(wide, "row", 0, 0, tiled=True, axis_index_groups=SAME_SIDE)
     with jax.named_scope("gather_l32_rows"):
-        l_mine, l_other, (away, l2_cols), l32_cols = gather_layers(
-            l32_pair, {2: (away, l2_cols), 4: l32_cols}
+        l_mine, l_other, away, l2_cols, l32_cols = gather_layers(
+            l32_pair, {1: away, 3: l2_cols, 4: l32_cols}
         )
     with jax.named_scope("pack"):
         packed, l3 = call(pack_kernel, [(3, 2, *square), (2, *square)], place, home, away)
@@ -260,13 +267,18 @@
             t_kernel, [(2, *square), (N // 2, 2, *square)], place, l_mine, l_other, l2_cols, l3
         )
     with jax.named_scope("gather_t_cols"):
-        t_cols = lax.all_to_all(
-            send, "row", 0, 0, tiled=True, axis_index_groups=SAME_SIDE
-        )
+        t_cols = lax.all_to_all(send, "row", 0, 0, tiled=True, axis_index_groups=SAME_SIDE)
+    with jax.named_scope("term_uq"):
+        u, q_home, q_away = call(
+            uq_kernel, [(2, *square), square, square], place, panels, l2_cols, l32_cols
+        )
+    with jax.named_scope("swap_q"):
+        t_cols, q_away = lax.optimization_barrier((t_cols, q_away))
+        q_away = lax.ppermute(q_away, "row", ROW_SWAP)
     with jax.named_scope("gather_t_rows"):
-        t_mine, t_other, t_cols = gather_layers(t, {3: t_cols})
-    with jax.named_scope("term_uq"):
-        u, q = call(uq_kernel, [(2, *square), square], place, panels, l2_cols, l32_cols)
+        t_mine, t_other, (t_cols, u, q_home), q_away = gather_layers(
+            t, {3: (t_cols, u, q_home), 4: q_away}
+        )
     with jax.named_scope("term_y"):
         y, y_home, y_away = call(
             y_kernel, [(2 * TB, TB), square, square], place, panels, t_cols
@@ -280,7 +292,8 @@
             place,
             y,
             u,
-            q,
+            q_home,
+            q_away,
             l_mine,
             l_other,
             t_mine,
@@ -292,7 +305,17 @@
         got = lax.all_to_all(sums, "row", 0, 0, tiled=True)
     with jax.named_scope("finish"):
         (out,) = call(
-            finish_kernel, [(N * TB, TB)], mask, place, flat, got, y_home, y_away, q, scalars=2
+            finish_kernel,
+            [(N * TB, TB)],
+            mask,
+            place,
+            flat,
+            got,
+            y_home,
+            y_away,
+            q_home,
+            q_away,
+            scalars=2,
         )
         return out.reshape(factor.shape)
 

time: 192 us -> 177 us (0.922)
  waiting for transfers between devices: 48.9 us -> 32.8 us
  local copies, waits for them, and re-layouts: 17.1 us -> 19.8 us
    ppermute x1, waiting for transfers between devices: 13.6 us -> 2.69 us  [body(): l32_away = lax.ppermute(l32, 'row', ROW_SWAP)]
    ppermute x6, waiting for transfers between devices: 17.3 us -> 9.7 us  [gather_layers(): down = lax.ppermute(down, 'col', LAYER_DOWN)]
    ppermute x6, waiting for transfers between devices: 8.85 us -> 5.44 us  [gather_layers(): up = lax.ppermute(up, 'col', LAYER_UP)]
    ppermute x1, waiting for transfers between devices: 0.01 us -> 3.29 us  [body(): away = lax.ppermute(away, 'row', ROW_SWAP)]
    ppermute x2, waiting for transfers between devices: 2.88 us -> 0.01 us  [gather_layers(): lax.ppermute(down[:, half:], 'col', LAYER_DOWN)]
    ppermute x6, starting transfers between devices: 14 us -> 16.8 us  [gather_layers(): down = lax.ppermute(down, 'col', LAYER_DOWN)]
    all_to_all x1, waiting for transfers between devices: 0.01 us -> 2.55 us  [body(): lax.all_to_all(wide, 'row', 0, 0, tiled=True, axis_index_groups=SAME_SIDE)]
    all_to_all x1, starting transfers between devices: 7.05 us -> 4.57 us  [body(): lax.all_to_all(wide, 'row', 0, 0, tiled=True, axis_index_groups=SAME_SIDE)]
  transfers between devices with their start and end apart: 25 -> 26, of which waited for: 15 -> 14; matrix products, arithmetic and copies ran while one was open for 5% -> 6% of each run, Pallas kernels for 5% -> 5%
where the time goes in v5:
time: 177 us; the launch traced here: 174 us
  blocking collectives  46.9 us (26%)
  starting transfers between devices  46.2 us (26%)
  waiting for transfers between devices  32.8 us (19%)
  local copies, waits for them, and re-layouts  19.8 us (11%)
  Pallas kernels  14.2 us (8%)
  between operations  13.6 us (8%)
    all_to_all x1, blocking collectives, body(): got = lax.all_to_all(sums, 'row', 0, 0, tiled=True)  46.9 us
    ppermute x6, starting transfers between devices, gather_layers(): down = lax.ppermute(down, 'col', LAYER_DOWN)  16.8 us
    unnamed x31, local copies, waits for them, and re-layouts  16.6 us
    pallas_call x7, Pallas kernels, call(): pl.pallas_call(kernel, out_shape=[jax.ShapeDtypeStruct(s, F32) for s in s...  14.2 us
    ppermute x6, waiting for transfers between devices, gather_layers(): down = lax.ppermute(down, 'col', LAYER_DOWN)  9.7 us
    all_to_all x1, starting transfers between devices, body(): l2_cols = lax.all_to_all(send, 'row', 0, 0, tiled=True)  6.75 us
    ppermute x6, waiting for transfers between devices, gather_layers(): up = lax.ppermute(up, 'col', LAYER_UP)  5.44 us
    ppermute x2, starting transfers between devices, gather_layers(): lax.ppermute(down[:, half:], 'col', LAYER_DOWN)  5.42 us
  transfers between devices with their start and end apart: 26, of which 14 were waited for; matrix products, arithmetic and copies ran while one was open for 6% of the time, Pallas kernels for 5%

profile of v5, /device:TPU:32, one launch (start us, length us, event | category | flops | bytes accessed | tf_op | source)
XLA Modules:
  0.0 174.3 jit_solution(757621044086192839)
XLA Ops:
  12.2 2.7 %collective-permute-done = f32[128,128]{1,0:T(8,128)S(1)} collective-permute-done((f32[128,128]{1,0:T(8,128)S(1)}, f32[128,128]{1,0:T(8,128)S(1)}, u32[]{:S(2)}, u32[]{:S(2)}) %collective-permute-start) | collective-permute-done | bytes 65568 | tf_op jit(solution)/shard_map/swap_l32/ppermute | solution.py:246
  18.6 3.3 %collective-permute-done.3.got_ref = f32[4,128,128]{2,1,0:T(8,128)S(1)} collective-permute-done((f32[4,128,128]{2,1,0:T(8,128)S(1)}, f32[4,128,128]{2,1,0:T(8,128)S(1)}, u32[]{:S(2)}, u32[]{:S(2)}) %collective-permute-start.3) | collective-permute-done | bytes 262176 | tf_op jit(solution)/shard_map/swap_rest/ppermute | solution.py:251
  21.9 3.6 %collective-permute-done.1 = f32[2,128,128]{2,1,0:T(8,128)S(1)} collective-permute-done((f32[2,128,128]{2,1,0:T(8,128)S(1)}, f32[2,128,128]{2,1,0:T(8,128)S(1)}, u32[]{:S(2)}, u32[]{:S(2)}) %collective-permute-start.1) | collective-permute-done | bytes 131104 | tf_op jit(solution)/shard_map/gather_l32_rows/ppermute | solution.py:205
  26.8 6.8 %all-to-all-start = ((f32[16,128,128]{2,1,0:T(8,128)}), f32[16,128,128]{2,1,0:T(8,128)S(1)}, u32[]{:S(2)}, u32[]{:S(2)}) async-start(f32[16,128,128]{2,1,0:T(8,128)} %get-tuple-element.56), calls=%async_computation | async-start | bytes 2097152 | tf_op jit(solution)/shard_map/gather_l2_cols/all_to_all | solution.py:254
  33.6 3.3 %collective-permute-start.4 = (f32[2,128,128]{2,1,0:T(8,128)S(1)}, f32[2,128,128]{2,1,0:T(8,128)S(1)}, u32[]{:S(2)}, u32[]{:S(2)}) collective-permute-start(f32[2,128,128]{2,1,0:T(8,128)S(1)} %collective-permute-done.2), channel_id=1, source_target_pairs={{0,14},{1,15},{2,0},{3,1},{4,2},{5,3},{6,4},{7,5},{8,6},{9,7},{10,... | collective-permute-start | bytes 393224 | tf_op jit(solution)/shard_map/gather_l32_rows/ppermute | solution.py:206
  36.9 6.2 %collective-permute-done.4 = f32[2,128,128]{2,1,0:T(8,128)S(1)} collective-permute-done((f32[2,128,128]{2,1,0:T(8,128)S(1)}, f32[2,128,128]{2,1,0:T(8,128)S(1)}, u32[]{:S(2)}, u32[]{:S(2)}) %collective-permute-start.4) | collective-permute-done | bytes 131104 | tf_op jit(solution)/shard_map/gather_l32_rows/ppermute | solution.py:206
  43.1 2.5 %collective-permute-start.7 = (f32[2,128,128]{2,1,0:T(8,128)S(1)}, f32[2,128,128]{2,1,0:T(8,128)S(1)}, u32[]{:S(2)}, u32[]{:S(2)}) collective-permute-start(f32[2,128,128]{2,1,0:T(8,128)S(1)} %collective-permute-done.4), channel_id=1, source_target_pairs={{0,14},{1,15},{2,0},{3,1},{4,2},{5,3},{6,4},{7,5},{8,6},{9,7},{10,... | collective-permute-start | bytes 393224 | tf_op jit(solution)/shard_map/gather_l32_rows/ppermute | solution.py:206
  45.9 2.2 %all-to-all-done.l2_ref = f32[16,128,128]{2,1,0:T(8,128)S(1)} async-done(((f32[16,128,128]{2,1,0:T(8,128)}), f32[16,128,128]{2,1,0:T(8,128)S(1)}, u32[]{:S(2)}, u32[]{:S(2)}) %all-to-all-start) | async-done | bytes 1048608 | tf_op jit(solution)/shard_map/gather_l2_cols/all_to_all | solution.py:254
  48.1 4.6 %all-to-all-start.1 = ((f32[8,128,128]{2,1,0:T(8,128)}), f32[8,128,128]{2,1,0:T(8,128)S(1)}, u32[]{:S(2)}, u32[]{:S(2)}) async-start(f32[8,128,128]{2,1,0:T(8,128)} %get-tuple-element.59), calls=%async_computation.1 | async-start | bytes 1048576 | tf_op jit(solution)/shard_map/gather_l32_cols/all_to_all | solution.py:256
  54.2 2.1 %collective-permute-start.9 = (f32[2,64,128]{2,1,0:T(8,128)S(1)}, f32[2,64,128]{2,1,0:T(8,128)S(1)}, u32[]{:S(2)}, u32[]{:S(2)}) collective-permute-start(f32[2,64,128]{2,1,0:T(8,128)S(1)} %slice.13), channel_id=1, source_target_pairs={{0,14},{1,15},{2,0},{3,1},{4,2},{5,3},{6,4},{7,5},{8,6},{9,7},{10,... | collective-permute-start | bytes 196616 | tf_op jit(solution)/shard_map/gather_l32_rows/ppermute | solution.py:216
  56.2 3.5 %collective-permute-done.8 = f32[2,64,128]{2,1,0:T(8,128)S(1)} collective-permute-done((f32[2,64,128]{2,1,0:T(8,128)S(1)}, f32[2,64,128]{2,1,0:T(8,128)S(1)}, u32[]{:S(2)}, u32[]{:S(2)}) %collective-permute-start.8) | collective-permute-done | bytes 65568 | tf_op jit(solution)/shard_map/gather_l32_rows/ppermute | solution.py:215
  59.8 2.5 %all-to-all-done.1.l32_ref = f32[8,128,128]{2,1,0:T(8,128)S(1)} async-done(((f32[8,128,128]{2,1,0:T(8,128)}), f32[8,128,128]{2,1,0:T(8,128)S(1)}, u32[]{:S(2)}, u32[]{:S(2)}) %all-to-all-start.1) | async-done | bytes 524320 | tf_op jit(solution)/shard_map/gather_l32_cols/all_to_all | solution.py:256
  63.2 2.8 %collective-permute-done.10.other_ref.l_other_ref = f32[8,2,128,128]{3,2,1,0:T(8,128)S(1)} collective-permute-done((f32[8,2,128,128]{3,2,1,0:T(8,128)S(1)}, f32[8,2,128,128]{3,2,1,0:T(8,128)S(1)}, u32[]{:S(2)}, u32[]{:S(2)}) %collective-permute-start.10) | collective-permute-done | bytes 1048608 | tf_op jit(solution)/shard_map/gather_l32_rows/ppermute | solution.py:224
  68.6 5.0 %all-to-all-start.2 = ((f32[8,2,128,128]{3,2,1,0:T(8,128)}), f32[8,2,128,128]{3,2,1,0:T(8,128)}, u32[]{:S(2)}, u32[]{:S(2)}) async-start(f32[8,2,128,128]{3,2,1,0:T(8,128)} %copy-done.7), calls=%async_computation.2 | async-start | bytes 2097152 | tf_op jit(solution)/shard_map/gather_t_cols/all_to_all | solution.py:270
  73.6 3.4 %collective-permute-start.14 = (f32[2,128,128]{2,1,0:T(8,128)S(1)}, f32[2,128,128]{2,1,0:T(8,128)S(1)}, u32[]{:S(2)}, u32[]{:S(2)}) collective-permute-start(f32[2,128,128]{2,1,0:T(8,128)S(1)} %get-tuple-element.63), channel_id=1, source_target_pairs={{0,14},{1,15},{2,0},{3,1},{4,2},{5,3},{6,4},{7,5},{8,6},{9,7},{10,... | collective-permute-start | bytes 393224 | tf_op jit(solution)/shard_map/gather_t_rows/ppermute | solution.py:206
  77.7 2.1 %collective-permute-done.14 = f32[2,128,128]{2,1,0:T(8,128)S(1)} collective-permute-done((f32[2,128,128]{2,1,0:T(8,128)S(1)}, f32[2,128,128]{2,1,0:T(8,128)S(1)}, u32[]{:S(2)}, u32[]{:S(2)}) %collective-permute-start.14) | collective-permute-done | bytes 131104 | tf_op jit(solution)/shard_map/gather_t_rows/ppermute | solution.py:206
  79.8 3.1 %collective-permute-start.15 = (f32[2,128,128]{2,1,0:T(8,128)S(1)}, f32[2,128,128]{2,1,0:T(8,128)}, u32[]{:S(2)}, u32[]{:S(2)}) collective-permute-start(f32[2,128,128]{2,1,0:T(8,128)S(1)} %collective-permute-done.14), channel_id=1, source_target_pairs={{0,14},{1,15},{2,0},{3,1},{4,2},{5,3},{6,4},{7,5},{8,6},{9,7},{10,... | collective-permute-start | bytes 393224 | tf_op jit(solution)/shard_map/gather_t_rows/ppermute | solution.py:206
  85.4 3.7 %collective-permute-start.16 = (f32[2,128,128]{2,1,0:T(8,128)}, f32[2,128,128]{2,1,0:T(8,128)}, u32[]{:S(2)}, u32[]{:S(2)}) collective-permute-start(f32[2,128,128]{2,1,0:T(8,128)} %collective-permute-done.15), channel_id=1, source_target_pairs={{0,14},{1,15},{2,0},{3,1},{4,2},{5,3},{6,4},{7,5},{8,6},{9,7},{10,... | collective-permute-start | bytes 393224 | tf_op jit(solution)/shard_map/gather_t_rows/ppermute | solution.py:206
  91.2 2.8 %copy-done = f32[48,2,128,128]{3,2,1,0:T(8,128)S(1)} copy-done((f32[48,2,128,128]{3,2,1,0:T(8,128)S(1)}, f32[48,2,128,128]{3,2,1,0:T(8,128)}, u32[]{:S(2)}) %copy-start) | copy-done | bytes 6291480
  98.7 3.3 %collective-permute-start.18 = (f32[2,64,128]{2,1,0:T(8,128)S(1)}, f32[2,64,128]{2,1,0:T(8,128)S(1)}, u32[]{:S(2)}, u32[]{:S(2)}) collective-permute-start(f32[2,64,128]{2,1,0:T(8,128)S(1)} %slice.15), channel_id=1, source_target_pairs={{0,14},{1,15},{2,0},{3,1},{4,2},{5,3},{6,4},{7,5},{8,6},{9,7},{10,... | collective-permute-start | bytes 196616 | tf_op jit(solution)/shard_map/gather_t_rows/ppermute | solution.py:216
  108.7 2.8 %copy-done.1 = f32[48,2,128,128]{3,2,1,0:T(8,128)S(1)} copy-done((f32[48,2,128,128]{3,2,1,0:T(8,128)S(1)}, f32[48,2,128,128]{3,2,1,0:T(8,128)}, u32[]{:S(2)}) %copy-start.1) | copy-done | bytes 6291480
  111.4 2.4 %term_y.1 = (f32[256,128]{1,0:T(8,128)S(1)}, f32[128,128]{1,0:T(8,128)S(1)}, f32[128,128]{1,0:T(8,128)S(1)}) custom-call(s32[2]{0:T(128)S(1)} %pad_add_fusion.place_ref, f32[16,3,2,128,128]{4,3,2,1,0:T(8,128)S(1)} %bitcast.47, f32[8,2,128,128]{3,2,1,0:T(8,128)} %all-to-all-done.2.t_ref), custom_call_target="tpu_custom_call" | custom-call | tf_op jit(solution)/shard_map/term_y/pallas_call | solution.py:50
  115.4 3.4 %sums.1 = f32[16,3,128,128]{3,2,1,0:T(8,128)S(1)} custom-call(s32[2]{0:T(128)S(1)} %pad_add_fusion.place_ref, f32[256,128]{1,0:T(8,128)S(1)} %get-tuple-element.71.y_ref, f32[2,128,128]{2,1,0:T(8,128)S(1)} %get-tuple-element.72.u_ref, f32[128,128]{1,0:T(8,128)S(1)} %get-tuple-element.73.q_home_ref, f32[128,128]{1,0:T(8,128)S(1)} %collective-permute-done.19.q_away_ref, ...), custom_call_target="tpu_custom_call" | custom-call | tf_op jit(solution)/shard_map/sums/pallas_call | solution.py:50
  118.8 46.9 %all_to_all.20.got_ref = f32[16,3,128,128]{3,2,1,0:T(8,128)S(1)} all-to-all(f32[16,3,128,128]{3,2,1,0:T(8,128)S(1)} %sums.1), channel_id=1, replica_groups=mesh['row'=16,'col'=16] {'row'}, dimensions={0} | all-to-all | bytes 6291456 | tf_op jit(solution)/shard_map/scatter_sums/all_to_all | solution.py:305
  (81 shorter events, 35.7 us)
Async XLA Ops:
  6.5 84.7 %all-gather.3.cloned.1.call-start = ((), (), s32[]{:S(2)}) async-start(), calls=%async_computation.4 | async-start | bytes 6684672 | tf_op jit(solution)/shard_map/gather_rows/all_gather | solution.py:264
  14.9 7.0 %collective-permute-start.3 = (f32[4,128,128]{2,1,0:T(8,128)S(1)}, f32[4,128,128]{2,1,0:T(8,128)S(1)}, u32[]{:S(2)}, u32[]{:S(2)}) collective-permute-start(f32[4,128,128]{2,1,0:T(8,128)S(1)} %get-tuple-element.50), channel_id=1, source_target_pairs={{0,16},{16,0},{32,48},{48,32},{64,80},{80,64},{96,112},{112,96},{1... | collective-permute-start | bytes 786440 | tf_op jit(solution)/shard_map/swap_rest/ppermute | solution.py:251
  16.5 5.3 %collective-permute-start.2 = (f32[2,128,128]{2,1,0:T(8,128)S(1)}, f32[2,128,128]{2,1,0:T(8,128)S(1)}, u32[]{:S(2)}, u32[]{:S(2)}) collective-permute-start(f32[2,128,128]{2,1,0:T(8,128)S(1)} %pad_maximum_fusion), channel_id=1, source_target_pairs={{0,14},{1,15},{2,0},{3,1},{4,2},{5,3},{6,4},{7,5},{8,6},{9,7},{10,... | collective-permute-start | bytes 393224 | tf_op jit(solution)/shard_map/gather_l32_rows/ppermute | solution.py:206
  17.4 8.1 %collective-permute-start.1 = (f32[2,128,128]{2,1,0:T(8,128)S(1)}, f32[2,128,128]{2,1,0:T(8,128)S(1)}, u32[]{:S(2)}, u32[]{:S(2)}) collective-permute-start(f32[2,128,128]{2,1,0:T(8,128)S(1)} %pad_maximum_fusion), channel_id=1, source_target_pairs={{0,2},{1,3},{2,4},{3,5},{4,6},{5,7},{6,8},{7,9},{8,10},{9,11},{10,... | collective-permute-start | bytes 393224 | tf_op jit(solution)/shard_map/gather_l32_rows/ppermute | solution.py:205
  26.8 21.3 %all-to-all-start = ((f32[16,128,128]{2,1,0:T(8,128)}), f32[16,128,128]{2,1,0:T(8,128)S(1)}, u32[]{:S(2)}, u32[]{:S(2)}) async-start(f32[16,128,128]{2,1,0:T(8,128)} %get-tuple-element.56), calls=%async_computation | async-start | bytes 2097152 | tf_op jit(solution)/shard_map/gather_l2_cols/all_to_all | solution.py:254
  33.6 9.6 %collective-permute-start.4 = (f32[2,128,128]{2,1,0:T(8,128)S(1)}, f32[2,128,128]{2,1,0:T(8,128)S(1)}, u32[]{:S(2)}, u32[]{:S(2)}) collective-permute-start(f32[2,128,128]{2,1,0:T(8,128)S(1)} %collective-permute-done.2), channel_id=1, source_target_pairs={{0,14},{1,15},{2,0},{3,1},{4,2},{5,3},{6,4},{7,5},{8,6},{9,7},{10,... | collective-permute-start | bytes 393224 | tf_op jit(solution)/shard_map/gather_l32_rows/ppermute | solution.py:206
  36.9 8.7 %collective-permute-start.5 = (f32[2,128,128]{2,1,0:T(8,128)S(1)}, f32[2,128,128]{2,1,0:T(8,128)S(1)}, u32[]{:S(2)}, u32[]{:S(2)}) collective-permute-start(f32[2,128,128]{2,1,0:T(8,128)S(1)} %collective-permute-done.1), channel_id=1, source_target_pairs={{0,2},{1,3},{2,4},{3,5},{4,6},{5,7},{6,8},{7,9},{8,10},{9,11},{10,... | collective-permute-start | bytes 393224 | tf_op jit(solution)/shard_map/gather_l32_rows/ppermute | solution.py:205
  43.1 9.5 %collective-permute-start.7 = (f32[2,128,128]{2,1,0:T(8,128)S(1)}, f32[2,128,128]{2,1,0:T(8,128)S(1)}, u32[]{:S(2)}, u32[]{:S(2)}) collective-permute-start(f32[2,128,128]{2,1,0:T(8,128)S(1)} %collective-permute-done.4), channel_id=1, source_target_pairs={{0,14},{1,15},{2,0},{3,1},{4,2},{5,3},{6,4},{7,5},{8,6},{9,7},{10,... | collective-permute-start | bytes 393224 | tf_op jit(solution)/shard_map/gather_l32_rows/ppermute | solution.py:206
  45.6 7.9 %collective-permute-start.6 = (f32[2,128,128]{2,1,0:T(8,128)S(1)}, f32[2,128,128]{2,1,0:T(8,128)S(1)}, u32[]{:S(2)}, u32[]{:S(2)}) collective-permute-start(f32[2,128,128]{2,1,0:T(8,128)S(1)} %collective-permute-done.5), channel_id=1, source_target_pairs={{0,2},{1,3},{2,4},{3,5},{4,6},{5,7},{6,8},{7,9},{8,10},{9,11},{10,... | collective-permute-start | bytes 393224 | tf_op jit(solution)/shard_map/gather_l32_rows/ppermute | solution.py:205
  48.1 14.3 %all-to-all-start.1 = ((f32[8,128,128]{2,1,0:T(8,128)}), f32[8,128,128]{2,1,0:T(8,128)S(1)}, u32[]{:S(2)}, u32[]{:S(2)}) async-start(f32[8,128,128]{2,1,0:T(8,128)} %get-tuple-element.59), calls=%async_computation.1 | async-start | bytes 1048576 | tf_op jit(solution)/shard_map/gather_l32_cols/all_to_all | solution.py:256
  53.6 6.2 %collective-permute-start.8 = (f32[2,64,128]{2,1,0:T(8,128)S(1)}, f32[2,64,128]{2,1,0:T(8,128)S(1)}, u32[]{:S(2)}, u32[]{:S(2)}) collective-permute-start(f32[2,64,128]{2,1,0:T(8,128)S(1)} %slice.12), channel_id=1, source_target_pairs={{0,2},{1,3},{2,4},{3,5},{4,6},{5,7},{6,8},{7,9},{8,10},{9,11},{10,... | collective-permute-start | bytes 196616 | tf_op jit(solution)/shard_map/gather_l32_rows/ppermute | solution.py:215
  54.2 5.6 %collective-permute-start.9 = (f32[2,64,128]{2,1,0:T(8,128)S(1)}, f32[2,64,128]{2,1,0:T(8,128)S(1)}, u32[]{:S(2)}, u32[]{:S(2)}) collective-permute-start(f32[2,64,128]{2,1,0:T(8,128)S(1)} %slice.13), channel_id=1, source_target_pairs={{0,14},{1,15},{2,0},{3,1},{4,2},{5,3},{6,4},{7,5},{8,6},{9,7},{10,... | collective-permute-start | bytes 196616 | tf_op jit(solution)/shard_map/gather_l32_rows/ppermute | solution.py:216
  68.6 28.5 %all-to-all-start.2 = ((f32[8,2,128,128]{3,2,1,0:T(8,128)}), f32[8,2,128,128]{3,2,1,0:T(8,128)}, u32[]{:S(2)}, u32[]{:S(2)}) async-start(f32[8,2,128,128]{3,2,1,0:T(8,128)} %copy-done.7), calls=%async_computation.2 | async-start | bytes 2097152 | tf_op jit(solution)/shard_map/gather_t_cols/all_to_all | solution.py:270
  73.6 6.2 %collective-permute-start.14 = (f32[2,128,128]{2,1,0:T(8,128)S(1)}, f32[2,128,128]{2,1,0:T(8,128)S(1)}, u32[]{:S(2)}, u32[]{:S(2)}) collective-permute-start(f32[2,128,128]{2,1,0:T(8,128)S(1)} %get-tuple-element.63), channel_id=1, source_target_pairs={{0,14},{1,15},{2,0},{3,1},{4,2},{5,3},{6,4},{7,5},{8,6},{9,7},{10,... | collective-permute-start | bytes 393224 | tf_op jit(solution)/shard_map/gather_t_rows/ppermute | solution.py:206
  77.0 6.3 %collective-permute-start.11 = (f32[2,128,128]{2,1,0:T(8,128)S(1)}, f32[2,128,128]{2,1,0:T(8,128)S(1)}, u32[]{:S(2)}, u32[]{:S(2)}) collective-permute-start(f32[2,128,128]{2,1,0:T(8,128)S(1)} %get-tuple-element.63), channel_id=1, source_target_pairs={{0,2},{1,3},{2,4},{3,5},{4,6},{5,7},{6,8},{7,9},{8,10},{9,11},{10,... | collective-permute-start | bytes 393224 | tf_op jit(solution)/shard_map/gather_t_rows/ppermute | solution.py:205
  79.8 5.6 %collective-permute-start.15 = (f32[2,128,128]{2,1,0:T(8,128)S(1)}, f32[2,128,128]{2,1,0:T(8,128)}, u32[]{:S(2)}, u32[]{:S(2)}) collective-permute-start(f32[2,128,128]{2,1,0:T(8,128)S(1)} %collective-permute-done.14), channel_id=1, source_target_pairs={{0,14},{1,15},{2,0},{3,1},{4,2},{5,3},{6,4},{7,5},{8,6},{9,7},{10,... | collective-permute-start | bytes 393224 | tf_op jit(solution)/shard_map/gather_t_rows/ppermute | solution.py:206
  83.4 6.3 %collective-permute-start.12 = (f32[2,128,128]{2,1,0:T(8,128)S(1)}, f32[2,128,128]{2,1,0:T(8,128)}, u32[]{:S(2)}, u32[]{:S(2)}) collective-permute-start(f32[2,128,128]{2,1,0:T(8,128)S(1)} %collective-permute-done.11), channel_id=1, source_target_pairs={{0,2},{1,3},{2,4},{3,5},{4,6},{5,7},{6,8},{7,9},{8,10},{9,11},{10,... | collective-permute-start | bytes 393224 | tf_op jit(solution)/shard_map/gather_t_rows/ppermute | solution.py:205
  85.4 12.3 %collective-permute-start.16 = (f32[2,128,128]{2,1,0:T(8,128)}, f32[2,128,128]{2,1,0:T(8,128)}, u32[]{:S(2)}, u32[]{:S(2)}) collective-permute-start(f32[2,128,128]{2,1,0:T(8,128)} %collective-permute-done.15), channel_id=1, source_target_pairs={{0,14},{1,15},{2,0},{3,1},{4,2},{5,3},{6,4},{7,5},{8,6},{9,7},{10,... | collective-permute-start | bytes 393224 | tf_op jit(solution)/shard_map/gather_t_rows/ppermute | solution.py:206
  89.6 8.1 %collective-permute-start.13 = (f32[2,128,128]{2,1,0:T(8,128)}, f32[2,128,128]{2,1,0:T(8,128)S(1)}, u32[]{:S(2)}, u32[]{:S(2)}) collective-permute-start(f32[2,128,128]{2,1,0:T(8,128)} %collective-permute-done.12), channel_id=1, source_target_pairs={{0,2},{1,3},{2,4},{3,5},{4,6},{5,7},{6,8},{7,9},{8,10},{9,11},{10,... | collective-permute-start | bytes 393224 | tf_op jit(solution)/shard_map/gather_t_rows/ppermute | solution.py:205
  97.1 11.6 %collective-permute-start.19 = (f32[128,128]{1,0:T(8,128)S(1)}, f32[128,128]{1,0:T(8,128)S(1)}, u32[]{:S(2)}, u32[]{:S(2)}) collective-permute-start(f32[128,128]{1,0:T(8,128)S(1)} %get-tuple-element.76), channel_id=1, source_target_pairs={{0,16},{16,0},{32,48},{48,32},{64,80},{80,64},{96,112},{112,96},{1... | collective-permute-start | bytes 196616 | tf_op jit(solution)/shard_map/swap_q/ppermute | solution.py:277
  98.6 5.6 %collective-permute-start.17 = (f32[2,64,128]{2,1,0:T(8,128)S(1)}, f32[2,64,128]{2,1,0:T(8,128)S(1)}, u32[]{:S(2)}, u32[]{:S(2)}) collective-permute-start(f32[2,64,128]{2,1,0:T(8,128)S(1)} %slice.14), channel_id=1, source_target_pairs={{0,2},{1,3},{2,4},{3,5},{4,6},{5,7},{6,8},{7,9},{8,10},{9,11},{10,... | collective-permute-start | bytes 196616 | tf_op jit(solution)/shard_map/gather_t_rows/ppermute | solution.py:215
  98.7 5.5 %collective-permute-start.18 = (f32[2,64,128]{2,1,0:T(8,128)S(1)}, f32[2,64,128]{2,1,0:T(8,128)S(1)}, u32[]{:S(2)}, u32[]{:S(2)}) collective-permute-start(f32[2,64,128]{2,1,0:T(8,128)S(1)} %slice.15), channel_id=1, source_target_pairs={{0,14},{1,15},{2,0},{3,1},{4,2},{5,3},{6,4},{7,5},{8,6},{9,7},{10,... | collective-permute-start | bytes 196616 | tf_op jit(solution)/shard_map/gather_t_rows/ppermute | solution.py:216
  108.6 6.7 %collective-permute-start.20 = (f32[8,2,128,128]{3,2,1,0:T(8,128)}, f32[8,2,128,128]{3,2,1,0:T(8,128)S(1)}, u32[]{:S(2)}, u32[]{:S(2)}) collective-permute-start(f32[8,2,128,128]{3,2,1,0:T(8,128)} %bitcast_dynamic-update-slice_fusion.t_mine_ref), channel_id=1, source_target_pairs={{0,1},{1,0},{2,3},{3,2},{4,5},{5,4},{6,7},{7,6},{8,9},{9,8},{10,11... | collective-permute-start | bytes 3145736 | tf_op jit(solution)/shard_map/gather_t_rows/ppermute | solution.py:224
  113.8 4.9 %collective-permute-start.21 = (f32[128,128]{1,0:T(8,128)S(1)}, f32[128,128]{1,0:T(8,128)S(1)}, u32[]{:S(2)}, u32[]{:S(2)}) collective-permute-start(f32[128,128]{1,0:T(8,128)S(1)} %get-tuple-element.79), channel_id=1, source_target_pairs={{0,16},{16,0},{32,48},{48,32},{64,80},{80,64},{96,112},{112,96},{1... | collective-permute-start | bytes 196616 | tf_op jit(solution)/shard_map/swap_y/ppermute | solution.py:287
  (11 other events, 75.4 us)
Sparse Core Ops, SparseCore 0:
  26.9 49.7 all-gather.2

commit v6 on v5

--- a/solution.py
+++ b/solution.py
@@ -95,11 +95,13 @@
     return k + core, k + 1 - core
 
 
-def t_kernel(place_ref, mine_ref, other_ref, l2_ref, l3_ref, t_ref, send_ref):
+def t_kernel(place_ref, *refs):
+    mine, other = refs[:LAYERS], refs[LAYERS : 2 * LAYERS]
+    l2_ref, l3_ref, t_ref, send_ref = refs[2 * LAYERS :]
     total = jnp.zeros((2 * TB, TB), F32)
     for d in range(LAYERS):
         k0, k1 = places(place_ref, d)
-        a = rows(*(lanes(mine_ref[d, i], other_ref[d, i]) for i in range(2)))
+        a = rows(*(lanes(mine[d][i], other[d][i]) for i in range(2)))
         total += dot3(split(a), split(rows(l2_ref[k0], l2_ref[k1])))
     for i in range(2):
         x = total[i * TB : (i + 1) * TB] - l3_ref[i]
@@ -142,9 +144,9 @@
     away_ref[...] = jnp.where(even, y[TB:], y[:TB])
 
 
-def sums_kernel(
-    place_ref, y_ref, u_ref, q_home_ref, q_away_ref, l_mine_ref, l_other_ref, t_mine_ref, t_other_ref, rows_ref, sum_ref
-):
+def sums_kernel(place_ref, *refs):
+    l_mine, l_other, t_mine, t_other = (refs[i * LAYERS : (i + 1) * LAYERS] for i in range(4))
+    y_ref, u_ref, q_home_ref, q_away_ref, rows_ref, sum_ref = refs[4 * LAYERS :]
     row = place_ref[1]
     side = lax.rem(row, 2)
     y = y_ref[...].T
@@ -154,9 +156,9 @@
     q_split = split((q_home_ref[...] + q_away_ref[...]).T)
     for d in range(LAYERS):
         ks = places(place_ref, d)
-        l32 = rows(*(lanes(l_mine_ref[d, i], l_other_ref[d, i]) for i in range(2)))
-        l32_own = lanes(l_mine_ref[d, side], l_other_ref[d, side])
-        low = [lanes(t_mine_ref[d, i], t_other_ref[d, i]) for i in range(2)]
+        l32 = rows(*(lanes(l_mine[d][i], l_other[d][i]) for i in range(2)))
+        l32_own = lanes(l_mine[d][side], l_other[d][side])
+        low = [lanes(t_mine[d][i], t_other[d][i]) for i in range(2)]
         low += [lanes(rows_ref[ks[0], 2, i], rows_ref[ks[1], 2, i]) for i in range(2)]
         parts = [
             dot3(y_split, split(l32)),
@@ -197,31 +199,35 @@
     out_ref[tile(3, 3), :] = f_ref[tile(3, 3), :]
 
 
+def swap_cores(x):
+    return lax.ppermute(x, "col", CORE_SWAP)
+
+
 def gather_layers(x, ties):
-    found = {0: x}
+    mine = {0: x}
+    other = {}
+    late = [0]
     up = down = x
     tied = []
-    for step in range(1, LAYERS // 2):
+    last = LAYERS // 2
+    for step in range(1, last + 1):
+        swapped = [swap_cores(mine[d]) for d in late]
         up = lax.ppermute(up, "col", LAYER_UP)
-        down = lax.ppermute(down, "col", LAYER_DOWN)
-        if step in ties:
-            up, down, other = lax.optimization_barrier((up, down, ties[step]))
-            tied.append(other)
-        found[LAYERS - step] = up
-        found[step] = down
-    half = TB // 2
-    found[LAYERS // 2] = jnp.concatenate(
-        [
-            lax.ppermute(up[:, :half], "col", LAYER_UP),
-            lax.ppermute(down[:, half:], "col", LAYER_DOWN),
-        ],
-        axis=1,
-    )
-    mine = jnp.stack([found[d] for d in range(LAYERS)])
-    if LAYERS // 2 in ties:
-        mine, other = lax.optimization_barrier((mine, ties[LAYERS // 2]))
-        tied.append(other)
-    return (mine, lax.ppermute(mine, "col", CORE_SWAP), *tied)
+        if step < last:
+            down = lax.ppermute(down, "col", LAYER_DOWN)
+        up, down, swapped, more = lax.optimization_barrier((up, down, swapped, ties.get(step)))
+        tied.append(more)
+        other.update(zip(late, swapped))
+        mine[LAYERS - step] = up
+        late = [LAYERS - step]
+        if step < last:
+            mine[step] = down
+            late.append(step)
+    swapped, more = lax.optimization_barrier((swap_cores(up), ties.get(last + 1)))
+    tied.append(more)
+    other[last] = swapped
+    order = range(LAYERS)
+    return [mine[d] for d in order], [other[d] for d in order], [t for t in tied if t is not None]
 
 
 def body(factor, structure):
@@ -255,8 +261,8 @@
     with jax.named_scope("gather_l32_cols"):
         l32_cols = lax.all_to_all(wide, "row", 0, 0, tiled=True, axis_index_groups=SAME_SIDE)
     with jax.named_scope("gather_l32_rows"):
-        l_mine, l_other, away, l2_cols, l32_cols = gather_layers(
-            l32_pair, {1: away, 3: l2_cols, 4: l32_cols}
+        l_mine, l_other, (away, l2_cols, l32_cols) = gather_layers(
+            l32_pair, {1: away, 3: l2_cols, 5: l32_cols}
         )
     with jax.named_scope("pack"):
         packed, l3 = call(pack_kernel, [(3, 2, *square), (2, *square)], place, home, away)
@@ -264,7 +270,7 @@
         panels = lax.all_gather(packed, "col", axis=0)
     with jax.named_scope("term_t"):
         t, send = call(
-            t_kernel, [(2, *square), (N // 2, 2, *square)], place, l_mine, l_other, l2_cols, l3
+            t_kernel, [(2, *square), (N // 2, 2, *square)], place, *l_mine, *l_other, l2_cols, l3
         )
     with jax.named_scope("gather_t_cols"):
         t_cols = lax.all_to_all(send, "row", 0, 0, tiled=True, axis_index_groups=SAME_SIDE)
@@ -273,11 +279,10 @@
             uq_kernel, [(2, *square), square, square], place, panels, l2_cols, l32_cols
         )
     with jax.named_scope("swap_q"):
-        t_cols, q_away = lax.optimization_barrier((t_cols, q_away))
         q_away = lax.ppermute(q_away, "row", ROW_SWAP)
     with jax.named_scope("gather_t_rows"):
-        t_mine, t_other, (t_cols, u, q_home), q_away = gather_layers(
-            t, {3: (t_cols, u, q_home), 4: q_away}
+        t_mine, t_other, ((u, q_home), (t_cols, q_away)) = gather_layers(
+            t, {3: (u, q_home), 4: (t_cols, q_away)}
         )
     with jax.named_scope("term_y"):
         y, y_home, y_away = call(
@@ -290,14 +295,14 @@
             sums_kernel,
             [(N, 3, *square)],
             place,
+            *l_mine,
+            *l_other,
+            *t_mine,
+            *t_other,
             y,
             u,
             q_home,
             q_away,
-            l_mine,
-            l_other,
-            t_mine,
-            t_other,
             panels,
         )
     with jax.named_scope("scatter_sums"):

time: 177 us -> 198 us (1.12)
  waiting for transfers between devices: 32.8 us -> 55.7 us
  starting transfers between devices: 46.2 us -> 40 us
  local copies, waits for them, and re-layouts: 19.8 us -> 24.5 us
    ppermute x6 -> x8, waiting for transfers between devices: 5.44 us -> 17.6 us  [gather_layers(): up = lax.ppermute(up, 'col', LAYER_UP)]
    all_to_all x1, waiting for transfers between devices: 2.23 us -> 14.2 us  [body(): l2_cols = lax.all_to_all(send, 'row', 0, 0, tiled=True)]
    unnamed x31 -> x85, local copies, waits for them, and re-layouts: 16.6 us -> 23.6 us
    ppermute x6 -> x16, waiting for transfers between devices: 6.9 us -> 2.12 us  [swap_cores(): return lax.ppermute(x, 'col', CORE_SWAP)]
    ppermute x6 -> x16, starting transfers between devices: 6.1 us -> 2.06 us  [swap_cores(): return lax.ppermute(x, 'col', CORE_SWAP)]
    ppermute x1, waiting for transfers between devices: 0.01 us -> 3.91 us  [body(): q_away = lax.ppermute(q_away, 'row', ROW_SWAP)]
    ppermute x6, starting transfers between devices: 16.8 us -> 13 us  [gather_layers(): down = lax.ppermute(down, 'col', LAYER_DOWN)]
    all_to_all x1, waiting for transfers between devices: 2.55 us -> 0.01 us  [body(): lax.all_to_all(wide, 'row', 0, 0, tiled=True, axis_index_groups=SAME_SIDE)]
  transfers between devices with their start and end apart: 26 -> 38, of which waited for: 14 -> 17; matrix products, arithmetic and copies ran while one was open for 6% -> 0% of each run, Pallas kernels for 5% -> 5%
where the time goes in v6:
time: 198 us; the launch traced here: 196 us
  waiting for transfers between devices  55.7 us (28%)
  blocking collectives  47.5 us (24%)
  starting transfers between devices  40 us (20%)
  local copies, waits for them, and re-layouts  24.5 us (12%)
  Pallas kernels  14.2 us (7%)
  between operations  13.7 us (7%)
    all_to_all x1, blocking collectives, body(): got = lax.all_to_all(sums, 'row', 0, 0, tiled=True)  47.5 us
    unnamed x85, local copies, waits for them, and re-layouts  23.6 us
    ppermute x8, waiting for transfers between devices, gather_layers(): up = lax.ppermute(up, 'col', LAYER_UP)  17.6 us
    all_to_all x1, waiting for transfers between devices, body(): l2_cols = lax.all_to_all(send, 'row', 0, 0, tiled=True)  14.2 us
    pallas_call x7, Pallas kernels, call(): pl.pallas_call(kernel, out_shape=[jax.ShapeDtypeStruct(s, F32) for s in s...  14.2 us
    ppermute x6, starting transfers between devices, gather_layers(): down = lax.ppermute(down, 'col', LAYER_DOWN)  13 us
    ppermute x6, waiting for transfers between devices, gather_layers(): down = lax.ppermute(down, 'col', LAYER_DOWN)  11.9 us
    all_to_all x1, starting transfers between devices, body(): lax.all_to_all(send, 'row', 0, 0, tiled=True, axis_index_groups=SAME_SIDE)  7.04 us
  transfers between devices with their start and end apart: 38, of which 17 were waited for; matrix products, arithmetic and copies ran while one was open for 0% of the time, Pallas kernels for 5%

profile of v6, /device:TPU:32, one launch (start us, length us, event | category | flops | bytes accessed | tf_op | source)
XLA Modules:
  0.0 195.8 jit_solution(7340980652241623765)
XLA Ops:
  8.8 1.8 prepare.1
  12.2 2.7 %collective-permute-done = f32[128,128]{1,0:T(8,128)S(1)} collective-permute-done((f32[128,128]{1,0:T(8,128)S(1)}, f32[128,128]{1,0:T(8,128)S(1)}, u32[]{:S(2)}, u32[]{:S(2)}) %collective-permute-start) | collective-permute-done | bytes 65568 | tf_op jit(solution)/shard_map/swap_l32/ppermute | solution.py:252
  18.6 3.3 %collective-permute-done.4.got_ref = f32[4,128,128]{2,1,0:T(8,128)S(1)} collective-permute-done((f32[4,128,128]{2,1,0:T(8,128)S(1)}, f32[4,128,128]{2,1,0:T(8,128)S(1)}, u32[]{:S(2)}, u32[]{:S(2)}) %collective-permute-start.4) | collective-permute-done | bytes 262176 | tf_op jit(solution)/shard_map/swap_rest/ppermute | solution.py:257
  22.6 3.8 %collective-permute-done.1.refs_7_ = f32[2,128,128]{2,1,0:T(8,128)S(1)} collective-permute-done((f32[2,128,128]{2,1,0:T(8,128)S(1)}, f32[2,128,128]{2,1,0:T(8,128)S(1)}, u32[]{:S(2)}, u32[]{:S(2)}) %collective-permute-start.1) | collective-permute-done | bytes 131104 | tf_op jit(solution)/shard_map/gather_l32_rows/ppermute | solution.py:215
  27.8 6.8 %all-to-all-start = ((f32[16,128,128]{2,1,0:T(8,128)}), f32[16,128,128]{2,1,0:T(8,128)S(1)}, u32[]{:S(2)}, u32[]{:S(2)}) async-start(f32[16,128,128]{2,1,0:T(8,128)} %get-tuple-element.74), calls=%async_computation | async-start | bytes 2097152 | tf_op jit(solution)/shard_map/gather_l2_cols/all_to_all | solution.py:260
  34.7 3.0 %collective-permute-start.6 = (f32[2,128,128]{2,1,0:T(8,128)S(1)}, f32[2,128,128]{2,1,0:T(8,128)S(1)}, u32[]{:S(2)}, u32[]{:S(2)}) collective-permute-start(f32[2,128,128]{2,1,0:T(8,128)S(1)} %collective-permute-done.2.refs_1_), channel_id=1, source_target_pairs={{0,14},{1,15},{2,0},{3,1},{4,2},{5,3},{6,4},{7,5},{8,6},{9,7},{10,... | collective-permute-start | bytes 393224 | tf_op jit(solution)/shard_map/gather_l32_rows/ppermute | solution.py:217
  37.9 14.2 %all-to-all-done.refs_16_.l2_ref = f32[16,128,128]{2,1,0:T(8,128)S(1)} async-done(((f32[16,128,128]{2,1,0:T(8,128)}), f32[16,128,128]{2,1,0:T(8,128)S(1)}, u32[]{:S(2)}, u32[]{:S(2)}) %all-to-all-start) | async-done | bytes 1048608 | tf_op jit(solution)/shard_map/gather_l2_cols/all_to_all | solution.py:260
  52.1 3.5 %all-to-all-start.1 = ((f32[8,128,128]{2,1,0:T(8,128)}), f32[8,128,128]{2,1,0:T(8,128)S(1)}, u32[]{:S(2)}, u32[]{:S(2)}) async-start(f32[8,128,128]{2,1,0:T(8,128)} %get-tuple-element.82), calls=%async_computation.1 | async-start | bytes 1048576 | tf_op jit(solution)/shard_map/gather_l32_cols/all_to_all | solution.py:262
  55.7 2.6 %collective-permute-start.10 = (f32[2,128,128]{2,1,0:T(8,128)S(1)}, f32[2,128,128]{2,1,0:T(8,128)S(1)}, u32[]{:S(2)}, u32[]{:S(2)}) collective-permute-start(f32[2,128,128]{2,1,0:T(8,128)S(1)} %collective-permute-done.6.refs_2_), channel_id=1, source_target_pairs={{0,14},{1,15},{2,0},{3,1},{4,2},{5,3},{6,4},{7,5},{8,6},{9,7},{10,... | collective-permute-start | bytes 393224 | tf_op jit(solution)/shard_map/gather_l32_rows/ppermute | solution.py:217
  58.5 6.3 %collective-permute-done.10.refs_3_ = f32[2,128,128]{2,1,0:T(8,128)S(1)} collective-permute-done((f32[2,128,128]{2,1,0:T(8,128)S(1)}, f32[2,128,128]{2,1,0:T(8,128)S(1)}, u32[]{:S(2)}, u32[]{:S(2)}) %collective-permute-start.10) | collective-permute-done | bytes 131104 | tf_op jit(solution)/shard_map/gather_l32_rows/ppermute | solution.py:217
  64.8 2.2 %collective-permute-done.9.refs_5_ = f32[2,128,128]{2,1,0:T(8,128)S(1)} collective-permute-done((f32[2,128,128]{2,1,0:T(8,128)S(1)}, f32[2,128,128]{2,1,0:T(8,128)S(1)}, u32[]{:S(2)}, u32[]{:S(2)}) %collective-permute-start.9) | collective-permute-done | bytes 131104 | tf_op jit(solution)/shard_map/gather_l32_rows/ppermute | solution.py:215
  68.6 8.0 %collective-permute-done.13.refs_4_ = f32[2,128,128]{2,1,0:T(8,128)S(1)} collective-permute-done((f32[2,128,128]{2,1,0:T(8,128)S(1)}, f32[2,128,128]{2,1,0:T(8,128)S(1)}, u32[]{:S(2)}, u32[]{:S(2)}) %collective-permute-start.13) | collective-permute-done | bytes 131104 | tf_op jit(solution)/shard_map/gather_l32_rows/ppermute | solution.py:215
  79.0 1.9 term_t.1
  82.6 7.0 %all-to-all-start.2 = ((f32[8,2,128,128]{3,2,1,0:T(8,128)}), f32[8,2,128,128]{3,2,1,0:T(8,128)S(1)}, u32[]{:S(2)}, u32[]{:S(2)}) async-start(f32[8,2,128,128]{3,2,1,0:T(8,128)} %copy-done.5), calls=%async_computation.2 | async-start | bytes 2097152 | tf_op jit(solution)/shard_map/gather_t_cols/all_to_all | solution.py:276
  89.7 3.5 %collective-permute-start.18 = (f32[2,128,128]{2,1,0:T(8,128)}, f32[2,128,128]{2,1,0:T(8,128)S(1)}, u32[]{:S(2)}, u32[]{:S(2)}) collective-permute-start(f32[2,128,128]{2,1,0:T(8,128)} %copy-done.24), channel_id=1, source_target_pairs={{0,14},{1,15},{2,0},{3,1},{4,2},{5,3},{6,4},{7,5},{8,6},{9,7},{10,... | collective-permute-start | bytes 393224 | tf_op jit(solution)/shard_map/gather_t_rows/ppermute | solution.py:217
  93.8 3.0 %collective-permute-done.18.refs_17_ = f32[2,128,128]{2,1,0:T(8,128)S(1)} collective-permute-done((f32[2,128,128]{2,1,0:T(8,128)}, f32[2,128,128]{2,1,0:T(8,128)S(1)}, u32[]{:S(2)}, u32[]{:S(2)}) %collective-permute-start.18) | collective-permute-done | bytes 131104 | tf_op jit(solution)/shard_map/gather_t_rows/ppermute | solution.py:217
  96.8 2.1 %collective-permute-done.17.refs_23_ = f32[2,128,128]{2,1,0:T(8,128)S(1)} collective-permute-done((f32[2,128,128]{2,1,0:T(8,128)}, f32[2,128,128]{2,1,0:T(8,128)S(1)}, u32[]{:S(2)}, u32[]{:S(2)}) %collective-permute-start.17) | collective-permute-done | bytes 131104 | tf_op jit(solution)/shard_map/gather_t_rows/ppermute | solution.py:215
  109.3 2.8 %copy-done = f32[48,2,128,128]{3,2,1,0:T(8,128)S(1)} copy-done((f32[48,2,128,128]{3,2,1,0:T(8,128)S(1)}, f32[48,2,128,128]{3,2,1,0:T(8,128)}, u32[]{:S(2)}) %copy-start) | copy-done | bytes 6291480
  112.1 2.6 %term_uq.1 = (f32[2,128,128]{2,1,0:T(8,128)S(1)}, f32[128,128]{1,0:T(8,128)S(1)}, f32[128,128]{1,0:T(8,128)}) custom-call(s32[2]{0:T(128)S(1)} %pad_add_fusion.place_ref, f32[16,3,2,128,128]{4,3,2,1,0:T(8,128)S(1)} %bitcast.10, f32[16,128,128]{2,1,0:T(8,128)S(1)} %all-to-all-done.refs_16_.l2_ref, f32[8,128,128]{2,1,0:T(8,128)S(1)} %all-to-all-done.1.l32_ref), custom_call_target="tpu_custom_call" | custom-call | tf_op jit(solution)/shard_map/term_uq/pallas_call | solution.py:50
  117.7 3.9 %collective-permute-done.31.refs_35_.q_away_ref = f32[128,128]{1,0:T(8,128)S(1)} collective-permute-done((f32[128,128]{1,0:T(8,128)}, f32[128,128]{1,0:T(8,128)S(1)}, u32[]{:S(2)}, u32[]{:S(2)}) %collective-permute-start.31) | collective-permute-done | bytes 65568 | tf_op jit(solution)/shard_map/swap_q/ppermute | solution.py:282
  122.4 2.8 %copy-done.1 = f32[48,2,128,128]{3,2,1,0:T(8,128)S(1)} copy-done((f32[48,2,128,128]{3,2,1,0:T(8,128)S(1)}, f32[48,2,128,128]{3,2,1,0:T(8,128)}, u32[]{:S(2)}) %copy-start.1) | copy-done | bytes 6291480
  136.3 3.2 %sums.1 = f32[16,3,128,128]{3,2,1,0:T(8,128)S(1)} custom-call(s32[2]{0:T(128)S(1)} %pad_add_fusion.place_ref, f32[2,128,128]{2,1,0:T(8,128)S(1)} %pad_maximum_fusion.refs_0_, f32[2,128,128]{2,1,0:T(8,128)S(1)} %collective-permute-done.2.refs_1_, f32[2,128,128]{2,1,0:T(8,128)S(1)} %collective-permute-done.6.refs_2_, f32[2,128,128]{2,1,0:T(8,128)S(1)} %copy-done.11, ...), custom_call_target="tpu_custom_call" | custom-call | tf_op jit(solution)/shard_map/sums/pallas_call | solution.py:50
  139.6 47.5 %all_to_all.20.got_ref = f32[16,3,128,128]{3,2,1,0:T(8,128)S(1)} all-to-all(f32[16,3,128,128]{3,2,1,0:T(8,128)S(1)} %sums.1), channel_id=1, replica_groups=mesh['row'=16,'col'=16] {'row'}, dimensions={0} | all-to-all | bytes 6291456 | tf_op jit(solution)/shard_map/scatter_sums/all_to_all | solution.py:310
  187.1 1.8 finish.1
  (151 shorter events, 41.9 us)
Async XLA Ops:
  6.5 102.8 %all-gather.3.cloned.1.call-start = ((), (), s32[]{:S(2)}) async-start(), calls=%async_computation.4 | async-start | bytes 6684672 | tf_op jit(solution)/shard_map/gather_rows/all_gather | solution.py:270
  14.9 7.0 %collective-permute-start.4 = (f32[4,128,128]{2,1,0:T(8,128)S(1)}, f32[4,128,128]{2,1,0:T(8,128)S(1)}, u32[]{:S(2)}, u32[]{:S(2)}) collective-permute-start(f32[4,128,128]{2,1,0:T(8,128)S(1)} %get-tuple-element.68), channel_id=1, source_target_pairs={{0,16},{16,0},{32,48},{48,32},{64,80},{80,64},{96,112},{112,96},{1... | collective-permute-start | bytes 786440 | tf_op jit(solution)/shard_map/swap_rest/ppermute | solution.py:257
  16.6 6.1 %collective-permute-start.2 = (f32[2,128,128]{2,1,0:T(8,128)S(1)}, f32[2,128,128]{2,1,0:T(8,128)S(1)}, u32[]{:S(2)}, u32[]{:S(2)}) collective-permute-start(f32[2,128,128]{2,1,0:T(8,128)S(1)} %pad_maximum_fusion.refs_0_), channel_id=1, source_target_pairs={{0,14},{1,15},{2,0},{3,1},{4,2},{5,3},{6,4},{7,5},{8,6},{9,7},{10,... | collective-permute-start | bytes 393224 | tf_op jit(solution)/shard_map/gather_l32_rows/ppermute | solution.py:217
  17.5 8.9 %collective-permute-start.1 = (f32[2,128,128]{2,1,0:T(8,128)S(1)}, f32[2,128,128]{2,1,0:T(8,128)S(1)}, u32[]{:S(2)}, u32[]{:S(2)}) collective-permute-start(f32[2,128,128]{2,1,0:T(8,128)S(1)} %pad_maximum_fusion.refs_0_), channel_id=1, source_target_pairs={{0,2},{1,3},{2,4},{3,5},{4,6},{5,7},{6,8},{7,9},{8,10},{9,11},{10,... | collective-permute-start | bytes 393224 | tf_op jit(solution)/shard_map/gather_l32_rows/ppermute | solution.py:215
  27.8 24.3 %all-to-all-start = ((f32[16,128,128]{2,1,0:T(8,128)}), f32[16,128,128]{2,1,0:T(8,128)S(1)}, u32[]{:S(2)}, u32[]{:S(2)}) async-start(f32[16,128,128]{2,1,0:T(8,128)} %get-tuple-element.74), calls=%async_computation | async-start | bytes 2097152 | tf_op jit(solution)/shard_map/gather_l2_cols/all_to_all | solution.py:260
  34.6 21.0 %collective-permute-start.8 = (f32[2,128,128]{2,1,0:T(8,128)S(1)}, f32[2,128,128]{2,1,0:T(8,128)S(1)}, u32[]{:S(2)}, u32[]{:S(2)}) collective-permute-start(f32[2,128,128]{2,1,0:T(8,128)S(1)} %collective-permute-done.2.refs_1_), channel_id=1, source_target_pairs={{0,1},{1,0},{2,3},{3,2},{4,5},{5,4},{6,7},{7,6},{8,9},{9,8},{10,11... | collective-permute-start | bytes 393224 | tf_op jit(solution)/shard_map/gather_l32_rows/ppermute | solution.py:203
  34.7 20.9 %collective-permute-start.6 = (f32[2,128,128]{2,1,0:T(8,128)S(1)}, f32[2,128,128]{2,1,0:T(8,128)S(1)}, u32[]{:S(2)}, u32[]{:S(2)}) collective-permute-start(f32[2,128,128]{2,1,0:T(8,128)S(1)} %collective-permute-done.2.refs_1_), channel_id=1, source_target_pairs={{0,14},{1,15},{2,0},{3,1},{4,2},{5,3},{6,4},{7,5},{8,6},{9,7},{10,... | collective-permute-start | bytes 393224 | tf_op jit(solution)/shard_map/gather_l32_rows/ppermute | solution.py:217
  37.7 17.9 %collective-permute-start.7 = (f32[2,128,128]{2,1,0:T(8,128)S(1)}, f32[2,128,128]{2,1,0:T(8,128)S(1)}, u32[]{:S(2)}, u32[]{:S(2)}) collective-permute-start(f32[2,128,128]{2,1,0:T(8,128)S(1)} %collective-permute-done.1.refs_7_), channel_id=1, source_target_pairs={{0,1},{1,0},{2,3},{3,2},{4,5},{5,4},{6,7},{7,6},{8,9},{9,8},{10,11... | collective-permute-start | bytes 393224 | tf_op jit(solution)/shard_map/gather_l32_rows/ppermute | solution.py:203
  37.9 17.8 %collective-permute-start.5 = (f32[2,128,128]{2,1,0:T(8,128)S(1)}, f32[2,128,128]{2,1,0:T(8,128)S(1)}, u32[]{:S(2)}, u32[]{:S(2)}) collective-permute-start(f32[2,128,128]{2,1,0:T(8,128)S(1)} %collective-permute-done.1.refs_7_), channel_id=1, source_target_pairs={{0,2},{1,3},{2,4},{3,5},{4,6},{5,7},{6,8},{7,9},{8,10},{9,11},{10,... | collective-permute-start | bytes 393224 | tf_op jit(solution)/shard_map/gather_l32_rows/ppermute | solution.py:215
  52.1 24.5 %all-to-all-start.1 = ((f32[8,128,128]{2,1,0:T(8,128)}), f32[8,128,128]{2,1,0:T(8,128)S(1)}, u32[]{:S(2)}, u32[]{:S(2)}) async-start(f32[8,128,128]{2,1,0:T(8,128)} %get-tuple-element.82), calls=%async_computation.1 | async-start | bytes 1048576 | tf_op jit(solution)/shard_map/gather_l32_cols/all_to_all | solution.py:262
  55.7 9.0 %collective-permute-start.10 = (f32[2,128,128]{2,1,0:T(8,128)S(1)}, f32[2,128,128]{2,1,0:T(8,128)S(1)}, u32[]{:S(2)}, u32[]{:S(2)}) collective-permute-start(f32[2,128,128]{2,1,0:T(8,128)S(1)} %collective-permute-done.6.refs_2_), channel_id=1, source_target_pairs={{0,14},{1,15},{2,0},{3,1},{4,2},{5,3},{6,4},{7,5},{8,6},{9,7},{10,... | collective-permute-start | bytes 393224 | tf_op jit(solution)/shard_map/gather_l32_rows/ppermute | solution.py:217
  58.3 6.5 %collective-permute-start.11 = (f32[2,128,128]{2,1,0:T(8,128)S(1)}, f32[2,128,128]{2,1,0:T(8,128)S(1)}, u32[]{:S(2)}, u32[]{:S(2)}) collective-permute-start(f32[2,128,128]{2,1,0:T(8,128)S(1)} %collective-permute-done.5.refs_6_), channel_id=1, source_target_pairs={{0,1},{1,0},{2,3},{3,2},{4,5},{5,4},{6,7},{7,6},{8,9},{9,8},{10,11... | collective-permute-start | bytes 393224 | tf_op jit(solution)/shard_map/gather_l32_rows/ppermute | solution.py:203
  58.5 8.5 %collective-permute-start.9 = (f32[2,128,128]{2,1,0:T(8,128)S(1)}, f32[2,128,128]{2,1,0:T(8,128)S(1)}, u32[]{:S(2)}, u32[]{:S(2)}) collective-permute-start(f32[2,128,128]{2,1,0:T(8,128)S(1)} %collective-permute-done.5.refs_6_), channel_id=1, source_target_pairs={{0,2},{1,3},{2,4},{3,5},{4,6},{5,7},{6,8},{7,9},{8,10},{9,11},{10,... | collective-permute-start | bytes 393224 | tf_op jit(solution)/shard_map/gather_l32_rows/ppermute | solution.py:215
  67.5 9.1 %collective-permute-start.13 = (f32[2,128,128]{2,1,0:T(8,128)S(1)}, f32[2,128,128]{2,1,0:T(8,128)S(1)}, u32[]{:S(2)}, u32[]{:S(2)}) collective-permute-start(f32[2,128,128]{2,1,0:T(8,128)S(1)} %collective-permute-done.9.refs_5_), channel_id=1, source_target_pairs={{0,2},{1,3},{2,4},{3,5},{4,6},{5,7},{6,8},{7,9},{8,10},{9,11},{10,... | collective-permute-start | bytes 393224 | tf_op jit(solution)/shard_map/gather_l32_rows/ppermute | solution.py:215
  82.6 35.1 %all-to-all-start.2 = ((f32[8,2,128,128]{3,2,1,0:T(8,128)}), f32[8,2,128,128]{3,2,1,0:T(8,128)S(1)}, u32[]{:S(2)}, u32[]{:S(2)}) async-start(f32[8,2,128,128]{3,2,1,0:T(8,128)} %copy-done.5), calls=%async_computation.2 | async-start | bytes 2097152 | tf_op jit(solution)/shard_map/gather_t_cols/all_to_all | solution.py:276
  89.7 7.1 %collective-permute-start.18 = (f32[2,128,128]{2,1,0:T(8,128)}, f32[2,128,128]{2,1,0:T(8,128)S(1)}, u32[]{:S(2)}, u32[]{:S(2)}) collective-permute-start(f32[2,128,128]{2,1,0:T(8,128)} %copy-done.24), channel_id=1, source_target_pairs={{0,14},{1,15},{2,0},{3,1},{4,2},{5,3},{6,4},{7,5},{8,6},{9,7},{10,... | collective-permute-start | bytes 393224 | tf_op jit(solution)/shard_map/gather_t_rows/ppermute | solution.py:217
  98.9 6.0 %collective-permute-start.21 = (f32[2,128,128]{2,1,0:T(8,128)S(1)}, f32[2,128,128]{2,1,0:T(8,128)}, u32[]{:S(2)}, u32[]{:S(2)}) collective-permute-start(f32[2,128,128]{2,1,0:T(8,128)S(1)} %collective-permute-done.18.refs_17_), channel_id=1, source_target_pairs={{0,14},{1,15},{2,0},{3,1},{4,2},{5,3},{6,4},{7,5},{8,6},{9,7},{10,... | collective-permute-start | bytes 393224 | tf_op jit(solution)/shard_map/gather_t_rows/ppermute | solution.py:217
  101.2 5.8 %collective-permute-start.20 = (f32[2,128,128]{2,1,0:T(8,128)S(1)}, f32[2,128,128]{2,1,0:T(8,128)}, u32[]{:S(2)}, u32[]{:S(2)}) collective-permute-start(f32[2,128,128]{2,1,0:T(8,128)S(1)} %collective-permute-done.17.refs_23_), channel_id=1, source_target_pairs={{0,2},{1,3},{2,4},{3,5},{4,6},{5,7},{6,8},{7,9},{8,10},{9,11},{10,... | collective-permute-start | bytes 393224 | tf_op jit(solution)/shard_map/gather_t_rows/ppermute | solution.py:215
  107.0 8.9 %collective-permute-start.27 = (f32[2,128,128]{2,1,0:T(8,128)}, f32[2,128,128]{2,1,0:T(8,128)}, u32[]{:S(2)}, u32[]{:S(2)}) collective-permute-start(f32[2,128,128]{2,1,0:T(8,128)} %collective-permute-done.21.refs_18_), channel_id=1, source_target_pairs={{0,1},{1,0},{2,3},{3,2},{4,5},{5,4},{6,7},{7,6},{8,9},{9,8},{10,11... | collective-permute-start | bytes 393224 | tf_op jit(solution)/shard_map/gather_t_rows/ppermute | solution.py:203
  107.0 8.9 %collective-permute-start.25 = (f32[2,128,128]{2,1,0:T(8,128)}, f32[2,128,128]{2,1,0:T(8,128)}, u32[]{:S(2)}, u32[]{:S(2)}) collective-permute-start(f32[2,128,128]{2,1,0:T(8,128)} %collective-permute-done.21.refs_18_), channel_id=1, source_target_pairs={{0,14},{1,15},{2,0},{3,1},{4,2},{5,3},{6,4},{7,5},{8,6},{9,7},{10,... | collective-permute-start | bytes 393224 | tf_op jit(solution)/shard_map/gather_t_rows/ppermute | solution.py:217
  108.5 7.4 %collective-permute-start.26 = (f32[2,128,128]{2,1,0:T(8,128)}, f32[2,128,128]{2,1,0:T(8,128)}, u32[]{:S(2)}, u32[]{:S(2)}) collective-permute-start(f32[2,128,128]{2,1,0:T(8,128)} %collective-permute-done.20.refs_22_), channel_id=1, source_target_pairs={{0,1},{1,0},{2,3},{3,2},{4,5},{5,4},{6,7},{7,6},{8,9},{9,8},{10,11... | collective-permute-start | bytes 393224 | tf_op jit(solution)/shard_map/gather_t_rows/ppermute | solution.py:203
  108.8 7.2 %collective-permute-start.24 = (f32[2,128,128]{2,1,0:T(8,128)}, f32[2,128,128]{2,1,0:T(8,128)}, u32[]{:S(2)}, u32[]{:S(2)}) collective-permute-start(f32[2,128,128]{2,1,0:T(8,128)} %collective-permute-done.20.refs_22_), channel_id=1, source_target_pairs={{0,2},{1,3},{2,4},{3,5},{4,6},{5,7},{6,8},{7,9},{8,10},{9,11},{10,... | collective-permute-start | bytes 393224 | tf_op jit(solution)/shard_map/gather_t_rows/ppermute | solution.py:215
  116.5 5.8 %collective-permute-start.28 = (f32[2,128,128]{2,1,0:T(8,128)}, f32[2,128,128]{2,1,0:T(8,128)}, u32[]{:S(2)}, u32[]{:S(2)}) collective-permute-start(f32[2,128,128]{2,1,0:T(8,128)} %collective-permute-done.24.refs_21_), channel_id=1, source_target_pairs={{0,2},{1,3},{2,4},{3,5},{4,6},{5,7},{6,8},{7,9},{8,10},{9,11},{10,... | collective-permute-start | bytes 393224 | tf_op jit(solution)/shard_map/gather_t_rows/ppermute | solution.py:215
  126.7 12.9 %collective-permute-start.33 = (f32[128,128]{1,0:T(8,128)S(1)}, f32[128,128]{1,0:T(8,128)S(1)}, u32[]{:S(2)}, u32[]{:S(2)}) collective-permute-start(f32[128,128]{1,0:T(8,128)S(1)} %get-tuple-element.117), channel_id=1, source_target_pairs={{0,16},{16,0},{32,48},{48,32},{64,80},{80,64},{96,112},{112,96},{1... | collective-permute-start | bytes 196616 | tf_op jit(solution)/shard_map/swap_y/ppermute | solution.py:292
  (56 other events, 294.0 us)
Sparse Core Ops, SparseCore 0:
  27.9 52.1 all-gather.2

commit v7 on v6

v7 whole, which is shorter than its diff:
```python
import jax
import jax.numpy as jnp
from jax import lax
from jax.experimental import pallas as pl
from jax.experimental.pallas import tpu as pltpu
from jax.sharding import PartitionSpec as P

N = 16
LAYERS = 8
TB = 128
HALF = 64
F32 = jnp.float32
BF16 = jnp.bfloat16
CORE_SWAP = [(i, i ^ 1) for i in range(N)]
ROW_SWAP = [(i, i ^ 1) for i in range(N)]
SAME_SIDE = [[p + 2 * i for i in range(N // 2)] for p in range(2)]
LAYER_UP = [(i, (i + 2) % N) for i in range(N)]
LAYER_DOWN = [(i, (i - 2) % N) for i in range(N)]


def split(x):
    high = x.astype(BF16)
    return high, (x - high.astype(F32)).astype(BF16)


def dot3(a, b):
    a_high, a_low = a
    b_high, b_low = b

    def one(x, y):
        return jnp.dot(x, y, preferred_element_type=F32)

    return one(a_high, b_high) + (one(a_high, b_low) + one(a_low, b_high))


def lanes(*tiles):
    return jnp.concatenate(tiles, axis=1)


def rows(*tiles):
    return jnp.concatenate(tiles, axis=0)


def tile(r, c):
    return pl.ds(r * 4 * TB + c, TB, stride=4)


def call(kernel, shapes, *args, scalars=1):
    smem = pl.BlockSpec(memory_space=pltpu.SMEM)
    vmem = pl.BlockSpec(memory_space=pltpu.VMEM)
    return pl.pallas_call(
        kernel,
        out_shape=[jax.ShapeDtypeStruct(s, F32) for s in shapes],
        in_specs=[smem] * scalars + [vmem] * (len(args) - scalars),
        out_specs=[vmem] * len(shapes),
        compiler_params=pltpu.CompilerParams(vmem_limit_bytes=10 * 2**20),
    )(*args)


def prepare_kernel(mask_ref, place_ref, f_ref, l32_ref, away_ref, home_ref, send_ref):
    side = lax.rem(place_ref[1], 2)

    def lower(r, c):
        return jnp.where(mask_ref[c, r] == 1, f_ref[tile(r, c), :], 0.0)

    x = lower(3, 2)
    l32_ref[...] = x
    turned = x.T
    l2 = [lower(2, s) for s in range(2)]
    l3 = [lower(3, s) for s in range(2)]
    for k in range(N):
        send_ref[k, :TB] = l2[k % 2]
        send_ref[k, TB:] = turned[k % 2 * HALF : (k % 2 + 1) * HALF]
    root, diag = f_ref[tile(3, 3), :], f_ref[tile(2, 2), :]
    away_ref[0] = home_ref[0] = root
    away_ref[1] = home_ref[1] = diag
    even = side == 0
    home_ref[2] = jnp.where(even, l2[0], l2[1])
    away_ref[2] = jnp.where(even, l2[1], l2[0])
    home_ref[3] = jnp.where(even, l3[0], l3[1])
    away_ref[3] = jnp.where(even, l3[1], l3[0])


def pack_kernel(place_ref, home_ref, got_ref, packed_ref, l3_ref):
    side = lax.rem(place_ref[1], 2)
    for i in range(3):
        packed_ref[i, side] = home_ref[i]
        packed_ref[i, 1 - side] = got_ref[i]
    l3_ref[side] = home_ref[3]
    l3_ref[1 - side] = got_ref[3]


def places(place_ref, d):
    layer, core = place_ref[0] // 2, lax.rem(place_ref[0], 2)
    k = lax.rem(layer + d, LAYERS) * 2
    return k + core, k + 1 - core


def t_kernel(place_ref, *refs):
    mine, other = refs[:LAYERS], refs[LAYERS : 2 * LAYERS]
    l2_ref, l3_ref, t_ref, send_ref, all_ref = refs[2 * LAYERS :]
    total = jnp.zeros((2 * TB, TB), F32)
    for d in range(LAYERS):
        k0, k1 = places(place_ref, d)
        a = rows(*(lanes(mine[d][i], other[d][i]) for i in range(2)))
        all_ref[d] = a
        total += dot3(split(a), split(rows(l2_ref[k0, :TB], l2_ref[k1, :TB])))
    for i in range(2):
        x = total[i * TB : (i + 1) * TB] - l3_ref[i]
        t_ref[i] = x
        for k in range(N // 2):
            send_ref[k, i] = x


def pair_rows(rows_ref, k):
    return rows(*(lanes(rows_ref[k, j], rows_ref[k + 1, j]) for j in range(2)))


def dot3_turned(a, b):
    def one(x, y):
        return lax.dot_general(x, y, (((1,), (1,)), ((), ())), preferred_element_type=F32)

    return one(a[0], b[0]) + (one(a[0], b[1]) + one(a[1], b[0]))


def uq_kernel(place_ref, root_ref, diag_ref, cols_ref, u_ref, q_ref, home_ref, away_ref):
    u = jnp.zeros((2 * TB, TB), F32)
    q = jnp.zeros((HALF, 2 * TB), F32)
    for k in range(0, N, 2):
        b = split(rows(cols_ref[k, :TB], cols_ref[k + 1, :TB]))
        u += dot3(split(pair_rows(diag_ref, k)), b)
        b = split(lanes(cols_ref[k, TB:], cols_ref[k + 1, TB:]))
        q += dot3_turned(b, split(pair_rows(root_ref, k)))
    for i in range(2):
        u_ref[i] = u[i * TB : (i + 1) * TB]
    q_ref[...] = q
    even = lax.rem(place_ref[1], 2) == 0
    home_ref[...] = jnp.where(even, q[:, :TB], q[:, TB:])
    away_ref[...] = jnp.where(even, q[:, TB:], q[:, :TB])


def y_kernel(place_ref, root_ref, t_ref, y_ref, home_ref, away_ref):
    y = jnp.zeros((2 * TB, TB), F32)
    for k in range(0, N, 2):
        b = split(rows(t_ref[k // 2, 0], t_ref[k // 2, 1]))
        y += dot3(split(pair_rows(root_ref, k)), b)
    y_ref[...] = y
    even = lax.rem(place_ref[1], 2) == 0
    home_ref[...] = jnp.where(even, y[:TB], y[TB:])
    away_ref[...] = jnp.where(even, y[TB:], y[:TB])


def sums_kernel(place_ref, *refs):
    t_mine, t_other = refs[:LAYERS], refs[LAYERS : 2 * LAYERS]
    l32_ref, y_ref, u_ref, q_ref, l2_ref, sum_ref = refs[2 * LAYERS :]
    row = place_ref[1]
    side = lax.rem(row, 2)
    y = y_ref[...].T
    u = [u_ref[i].T for i in range(2)]
    left = split(rows(y, q_ref[...]))
    yu_split = split(lanes(y, *u))
    for d in range(LAYERS):
        ks = places(place_ref, d)
        low = [lanes(t_mine[d][i], t_other[d][i]) for i in range(2)]
        low += [lanes(l2_ref[ks[0], i], l2_ref[ks[1], i]) for i in range(2)]
        x = dot3(left, split(l32_ref[d]))
        z = dot3(yu_split, split(rows(*low)))
        for i, k in enumerate(ks):
            at = slice(i * TB, (i + 1) * TB)
            sum_ref[k, :TB] = x[:TB, at]
            sum_ref[k, TB : 2 * TB] = z[:, at]
            sum_ref[k, 2 * TB :] = x[TB:, at]
    for i in range(2):
        sum_ref[row - side + i, :TB] += u[i]


def finish_kernel(
    mask_ref, place_ref, f_ref, got_ref, home_ref, away_ref, q_home_ref, q_away_ref, out_ref
):
    even = lax.rem(place_ref[1], 2) == 0

    def masked(s, r, x):
        return jnp.where(mask_ref[s, r] == 1, x, 0.0)

    def both(home, away):
        return [jnp.where(even, home, away), jnp.where(even, away, home)]

    empty = jnp.zeros((TB, TB), F32)
    for r, c in ((0, 1), (0, 2), (0, 3), (1, 0), (1, 2), (1, 3), (2, 3)):
        out_ref[tile(r, c), :] = empty
    y = both(home_ref[...], away_ref[...])
    q = rows(*both(q_home_ref[...], q_away_ref[...])).T
    parts = []
    for s in range(2):
        total = got_ref[s]
        for k in range(s + 2, N, 2):
            total += got_ref[k]
        out_ref[tile(s, s), :] = f_ref[tile(s, s), :] + total[TB : 2 * TB].T
        out_ref[tile(2, s), :] = masked(s, 2, -total[:TB].T)
        out_ref[tile(3, s), :] = masked(s, 3, y[s])
        parts.append(total[2 * TB :])
    out_ref[tile(2, 2), :] = f_ref[tile(2, 2), :] + rows(*parts).T
    out_ref[tile(3, 2), :] = masked(2, 3, -q)
    out_ref[tile(3, 3), :] = f_ref[tile(3, 3), :]


def swap_cores(x):
    return lax.ppermute(x, "col", CORE_SWAP)


def gather_layers(x, begin, ties):
    mine = {0: x}
    other = {}
    late = [0]
    up = down = x
    tied = []
    last = LAYERS // 2
    half = TB // 2
    beside = None
    for step in range(1, last + 1):
        swapped = [swap_cores(mine[d]) for d in late]
        if step == begin[0]:
            swapped, operand = lax.optimization_barrier((swapped, begin[1]))
            beside = begin[2](operand)
        if step == last:
            up, down = up[:, :half], down[:, half:]
        up = lax.ppermute(up, "col", LAYER_UP)
        down = lax.ppermute(down, "col", LAYER_DOWN)
        up, down, swapped, more = lax.optimization_barrier((up, down, swapped, ties.get(step)))
        tied.append(more)
        other.update(zip(late, swapped))
        if step < last:
            mine[LAYERS - step], mine[step] = up, down
            late = [LAYERS - step, step]
    mine[last] = jnp.concatenate([up, down], axis=1)
    other[last], beside = lax.optimization_barrier((swap_cores(mine[last]), beside))
    order = range(LAYERS)
    return [mine[d] for d in order], [other[d] for d in order], beside, *(t for t in tied if t is not None)


def body(factor, structure):
    row = lax.axis_index("row")
    col = lax.axis_index("col")
    place = jnp.stack([col, row]).astype(jnp.int32)
    mask = structure.reshape(4, 4, N)
    mask = lax.dynamic_index_in_dim(mask, row, axis=2, keepdims=False)
    flat = factor.reshape(N * TB, TB)
    square = (TB, TB)

    def to_rows(x):
        return lax.all_to_all(x, "row", 0, 0, tiled=True)

    def to_side(x):
        return lax.all_to_all(x, "row", 0, 0, tiled=True, axis_index_groups=SAME_SIDE)

    with jax.named_scope("prepare"):
        l32, away, home, send = call(
            prepare_kernel,
            [square, (4, *square), (4, *square), (N, TB + HALF, TB)],
            mask,
            place,
            flat,
            scalars=2,
        )
    with jax.named_scope("swap_l32"):
        l32_away = lax.ppermute(l32, "row", ROW_SWAP)
        even = lax.rem(row, 2) == 0
        l32_pair = jnp.stack([jnp.where(even, l32, l32_away), jnp.where(even, l32_away, l32)])
    with jax.named_scope("swap_rest"):
        l32_pair, away = lax.optimization_barrier((l32_pair, away))
        away = lax.ppermute(away, "row", ROW_SWAP)
    with jax.named_scope("gather_l"):
        l_mine, l_other, cols, away = gather_layers(l32_pair, (2, send, to_rows), {1: away})
    with jax.named_scope("pack"):
        packed, l3 = call(pack_kernel, [(3, 2, *square), (2, *square)], place, home, away)
    with jax.named_scope("gather_rows"):
        panels = lax.all_gather(packed, "col", axis=0)
        root_rows, diag_rows, l2_rows = (panels[:, i] for i in range(3))
    with jax.named_scope("term_t"):
        t, send, l32_rows = call(
            t_kernel,
            [(2, *square), (N // 2, 2, *square), (LAYERS, 2 * TB, 2 * TB)],
            place,
            *l_mine,
            *l_other,
            cols,
            l3,
        )
    with jax.named_scope("term_uq"):
        u, q, q_home, q_away = call(
            uq_kernel,
            [(2, *square), (HALF, 2 * TB), (HALF, TB), (HALF, TB)],
            place,
            root_rows,
            diag_rows,
            cols,
        )
    with jax.named_scope("gather_t"):
        t_mine, t_other, t_cols, (u, q) = gather_layers(t, (1, send, to_side), {3: (u, q)})
    with jax.named_scope("term_y"):
        y, y_home, y_away = call(
            y_kernel, [(2 * TB, TB), square, square], place, root_rows, t_cols
        )
    with jax.named_scope("swap_yq"):
        away = jnp.concatenate([y_away, q_away])
        away = lax.ppermute(away, "row", ROW_SWAP)
        y_away, q_away = away[:TB], away[TB:]
    with jax.named_scope("sums"):
        (sums,) = call(
            sums_kernel,
            [(N, 2 * TB + HALF, TB)],
            place,
            *t_mine,
            *t_other,
            l32_rows,
            y,
            u,
            q,
            l2_rows,
        )
    with jax.named_scope("scatter_sums"):
        sums, y_away, q_away = lax.optimization_barrier((sums, y_away, q_away))
        got = lax.all_to_all(sums, "row", 0, 0, tiled=True)
    with jax.named_scope("finish"):
        (out,) = call(
            finish_kernel,
            [(N * TB, TB)],
            mask,
            place,
            flat,
            got,
            y_home,
            y_away,
            q_home,
            q_away,
            scalars=2,
        )
        return out.reshape(factor.shape)


def solution(mesh):
    return jax.shard_map(
        body,
        mesh=mesh,
        in_specs=(P(None, "row", None, "col"), P()),
        out_specs=P(None, "row", None, "col"),
        check_vma=False,
    )
```

time: 198 us -> 175 us (0.88)
  waiting for transfers between devices: 55.7 us -> 42 us
  blocking collectives: 47.5 us -> 41.7 us
  local copies, waits for them, and re-layouts: 24.5 us -> 20 us
    all_to_all x3 -> x2, waiting for transfers between devices: 14.2 us -> 0.01 us  [the longest x1 0.01 us: to_rows(): return lax.all_to_all(x, 'row', 0, 0, tiled=True)]
    ppermute x8, starting transfers between devices: 3.26 us -> 17.2 us  [gather_layers(): up = lax.ppermute(up, 'col', LAYER_UP)]
    ppermute x6 -> x8, starting transfers between devices: 13 us -> 2.76 us  [gather_layers(): down = lax.ppermute(down, 'col', LAYER_DOWN)]
    unnamed x85 -> x77, local copies, waits for them, and re-layouts: 23.6 us -> 14.3 us
    ppermute x6 -> x8, waiting for transfers between devices: 11.9 us -> 18.4 us  [gather_layers(): down = lax.ppermute(down, 'col', LAYER_DOWN)]
    all_to_all x1, blocking collectives: 47.5 us -> 41.7 us  [body(): got = lax.all_to_all(sums, 'row', 0, 0, tiled=True)]
    squeeze x0 -> x1, local copies, waits for them, and re-layouts: none -> 4.82 us  [body(): root_rows, diag_rows, l2_rows = (panels[:, i] for i in range(3))]
    ppermute x2 -> x0, waiting for transfers between devices: 3.91 us -> none  [the longest x1 3.91 us: body(): q_away = lax.ppermute(q_away, 'row', ROW_SWAP)]
  transfers between devices with their start and end apart: 38 -> 38, of which waited for: 17 -> 17; matrix products, arithmetic and copies ran while one was open for 0% -> 3% of each run, Pallas kernels for 5% -> 4%
where the time goes in v7:
time: 175 us; the launch traced here: 173 us
  waiting for transfers between devices  42 us (24%)
  blocking collectives  41.7 us (24%)
  starting transfers between devices  41 us (23%)
  local copies, waits for them, and re-layouts  20 us (11%)
  between operations  13.8 us (8%)
  Pallas kernels  13.7 us (8%)
    all_to_all x1, blocking collectives, body(): got = lax.all_to_all(sums, 'row', 0, 0, tiled=True)  41.7 us
    ppermute x8, waiting for transfers between devices, gather_layers(): down = lax.ppermute(down, 'col', LAYER_DOWN)  18.4 us
    ppermute x8, starting transfers between devices, gather_layers(): up = lax.ppermute(up, 'col', LAYER_UP)  17.2 us
    ppermute x8, waiting for transfers between devices, gather_layers(): up = lax.ppermute(up, 'col', LAYER_UP)  17 us
    unnamed x77, local copies, waits for them, and re-layouts  14.3 us
    pallas_call x7, Pallas kernels, call(): pl.pallas_call(kernel, out_shape=[jax.ShapeDtypeStruct(s, F32) for s in s...  13.7 us
    all_to_all x1, starting transfers between devices, to_side(): lax.all_to_all(x, 'row', 0, 0, tiled=True, axis_index_groups=SAME_SIDE)  7.13 us
    all_to_all x1, starting transfers between devices, to_rows(): return lax.all_to_all(x, 'row', 0, 0, tiled=True)  6.74 us
  transfers between devices with their start and end apart: 38, of which 17 were waited for; matrix products, arithmetic and copies ran while one was open for 3% of the time, Pallas kernels for 4%

profile of v7, /device:TPU:32, one launch (start us, length us, event | category | flops | bytes accessed | tf_op | source)
XLA Modules:
  0.0 173.1 jit_solution(7675947144118692898)
XLA Ops:
  8.8 2.0 %prepare.1 = (f32[128,128]{1,0:T(8,128)S(1)}, f32[4,128,128]{2,1,0:T(8,128)S(1)}, f32[4,128,128]{2,1,0:T(8,128)S(1)}, f32[16,192,128]{2,1,0:T(8,128)}) custom-call(s32[4,4]{1,0:T(4,128)S(1)} %bitcast.24, s32[2]{0:T(128)S(1)} %pad_add_fusion.place_ref, f32[2048,128]{1,0:T(8,128)S(1)} %bitcast.22), custom_call_target="tpu_custom_call" | custom-call | tf_op jit(solution)/shard_map/prepare/pallas_call | solution.py:51
  12.3 2.7 %collective-permute-done = f32[128,128]{1,0:T(8,128)S(1)} collective-permute-done((f32[128,128]{1,0:T(8,128)S(1)}, f32[128,128]{1,0:T(8,128)S(1)}, u32[]{:S(2)}, u32[]{:S(2)}) %collective-permute-start) | collective-permute-done | bytes 65568 | tf_op jit(solution)/shard_map/swap_l32/ppermute | solution.py:266
  16.7 1.9 %collective-permute-start.1 = (f32[2,128,128]{2,1,0:T(8,128)S(1)}, f32[2,128,128]{2,1,0:T(8,128)S(1)}, u32[]{:S(2)}, u32[]{:S(2)}) collective-permute-start(f32[2,128,128]{2,1,0:T(8,128)S(1)} %pad_maximum_fusion.refs_0_), channel_id=1, source_target_pairs={{0,2},{1,3},{2,4},{3,5},{4,6},{5,7},{6,8},{7,9},{8,10},{9,11},{10,... | collective-permute-start | bytes 393224 | tf_op jit(solution)/shard_map/gather_l/ppermute | solution.py:227
  18.8 2.9 %collective-permute-done.1.refs_7_ = f32[2,128,128]{2,1,0:T(8,128)S(1)} collective-permute-done((f32[2,128,128]{2,1,0:T(8,128)S(1)}, f32[2,128,128]{2,1,0:T(8,128)S(1)}, u32[]{:S(2)}, u32[]{:S(2)}) %collective-permute-start.1) | collective-permute-done | bytes 131104 | tf_op jit(solution)/shard_map/gather_l/ppermute | solution.py:227
  21.7 1.9 %collective-permute-done.2.refs_1_ = f32[2,128,128]{2,1,0:T(8,128)S(1)} collective-permute-done((f32[2,128,128]{2,1,0:T(8,128)S(1)}, f32[2,128,128]{2,1,0:T(8,128)S(1)}, u32[]{:S(2)}, u32[]{:S(2)}) %collective-permute-start.2) | collective-permute-done | bytes 131104 | tf_op jit(solution)/shard_map/gather_l/ppermute | solution.py:228
  26.6 6.7 %all-to-all-start = ((f32[16,192,128]{2,1,0:T(8,128)}), f32[16,192,128]{2,1,0:T(8,128)S(1)}, u32[]{:S(2)}, u32[]{:S(2)}) async-start(f32[16,192,128]{2,1,0:T(8,128)} %get-tuple-element.87), calls=%async_computation | async-start | bytes 3145728 | tf_op jit(solution)/shard_map/gather_l/all_to_all | solution.py:251
  33.4 3.1 %collective-permute-start.5 = (f32[2,128,128]{2,1,0:T(8,128)S(1)}, f32[2,128,128]{2,1,0:T(8,128)S(1)}, u32[]{:S(2)}, u32[]{:S(2)}) collective-permute-start(f32[2,128,128]{2,1,0:T(8,128)S(1)} %collective-permute-done.1.refs_7_), channel_id=1, source_target_pairs={{0,2},{1,3},{2,4},{3,5},{4,6},{5,7},{6,8},{7,9},{8,10},{9,11},{10,... | collective-permute-start | bytes 393224 | tf_op jit(solution)/shard_map/gather_l/ppermute | solution.py:227
  36.5 4.9 %collective-permute-done.5.refs_6_ = f32[2,128,128]{2,1,0:T(8,128)S(1)} collective-permute-done((f32[2,128,128]{2,1,0:T(8,128)S(1)}, f32[2,128,128]{2,1,0:T(8,128)S(1)}, u32[]{:S(2)}, u32[]{:S(2)}) %collective-permute-start.5) | collective-permute-done | bytes 131104 | tf_op jit(solution)/shard_map/gather_l/ppermute | solution.py:227
  41.4 4.7 %collective-permute-done.6.refs_2_ = f32[2,128,128]{2,1,0:T(8,128)S(1)} collective-permute-done((f32[2,128,128]{2,1,0:T(8,128)S(1)}, f32[2,128,128]{2,1,0:T(8,128)S(1)}, u32[]{:S(2)}, u32[]{:S(2)}) %collective-permute-start.6) | collective-permute-done | bytes 131104 | tf_op jit(solution)/shard_map/gather_l/ppermute | solution.py:228
  46.6 2.1 %collective-permute-start.9 = (f32[2,128,128]{2,1,0:T(8,128)S(1)}, f32[2,128,128]{2,1,0:T(8,128)S(1)}, u32[]{:S(2)}, u32[]{:S(2)}) collective-permute-start(f32[2,128,128]{2,1,0:T(8,128)S(1)} %collective-permute-done.5.refs_6_), channel_id=1, source_target_pairs={{0,2},{1,3},{2,4},{3,5},{4,6},{5,7},{6,8},{7,9},{8,10},{9,11},{10,... | collective-permute-start | bytes 393224 | tf_op jit(solution)/shard_map/gather_l/ppermute | solution.py:227
  48.7 6.1 %collective-permute-done.10.refs_3_ = f32[2,128,128]{2,1,0:T(8,128)S(1)} collective-permute-done((f32[2,128,128]{2,1,0:T(8,128)S(1)}, f32[2,128,128]{2,1,0:T(8,128)S(1)}, u32[]{:S(2)}, u32[]{:S(2)}) %collective-permute-start.10) | collective-permute-done | bytes 131104 | tf_op jit(solution)/shard_map/gather_l/ppermute | solution.py:228
  59.4 3.8 %collective-permute-done.13 = f32[2,64,128]{2,1,0:T(8,128)S(1)} collective-permute-done((f32[2,64,128]{2,1,0:T(8,128)S(1)}, f32[2,64,128]{2,1,0:T(8,128)S(1)}, u32[]{:S(2)}, u32[]{:S(2)}) %collective-permute-start.13) | collective-permute-done | bytes 65568 | tf_op jit(solution)/shard_map/gather_l/ppermute | solution.py:227
  72.1 2.8 %collective-permute-start.18 = (f32[2,128,128]{2,1,0:T(8,128)S(1)}, f32[2,128,128]{2,1,0:T(8,128)S(1)}, u32[]{:S(2)}, u32[]{:S(2)}) collective-permute-start(f32[2,128,128]{2,1,0:T(8,128)S(1)} %get-tuple-element.96.refs_0_), channel_id=1, source_target_pairs={{0,2},{1,3},{2,4},{3,5},{4,6},{5,7},{6,8},{7,9},{8,10},{9,11},{10,... | collective-permute-start | bytes 393224 | tf_op jit(solution)/shard_map/gather_t/ppermute | solution.py:227
  76.2 2.2 %collective-permute-done.18.refs_7_ = f32[2,128,128]{2,1,0:T(8,128)S(1)} collective-permute-done((f32[2,128,128]{2,1,0:T(8,128)S(1)}, f32[2,128,128]{2,1,0:T(8,128)S(1)}, u32[]{:S(2)}, u32[]{:S(2)}) %collective-permute-start.18) | collective-permute-done | bytes 131104 | tf_op jit(solution)/shard_map/gather_t/ppermute | solution.py:227
  78.4 3.6 %collective-permute-done.19.refs_1_ = f32[2,128,128]{2,1,0:T(8,128)S(1)} collective-permute-done((f32[2,128,128]{2,1,0:T(8,128)S(1)}, f32[2,128,128]{2,1,0:T(8,128)S(1)}, u32[]{:S(2)}, u32[]{:S(2)}) %collective-permute-start.19) | collective-permute-done | bytes 131104 | tf_op jit(solution)/shard_map/gather_t/ppermute | solution.py:228
  82.0 1.7 %collective-permute-start.21 = (f32[2,128,128]{2,1,0:T(8,128)S(1)}, f32[2,128,128]{2,1,0:T(8,128)S(1)}, u32[]{:S(2)}, u32[]{:S(2)}) collective-permute-start(f32[2,128,128]{2,1,0:T(8,128)S(1)} %collective-permute-done.18.refs_7_), channel_id=1, source_target_pairs={{0,2},{1,3},{2,4},{3,5},{4,6},{5,7},{6,8},{7,9},{8,10},{9,11},{10,... | collective-permute-start | bytes 393224 | tf_op jit(solution)/shard_map/gather_t/ppermute | solution.py:227
  84.5 7.1 %all-to-all-start.1 = ((f32[8,2,128,128]{3,2,1,0:T(8,128)}), f32[8,2,128,128]{3,2,1,0:T(8,128)S(1)}, u32[]{:S(2)}, u32[]{:S(2)}) async-start(f32[8,2,128,128]{3,2,1,0:T(8,128)} %copy-done.7), calls=%async_computation.1 | async-start | bytes 2097152 | tf_op jit(solution)/shard_map/gather_t/all_to_all | solution.py:254
  95.3 4.8 %slice_bitcast_fusion = (f32[16,2,128,128]{3,2,1,0:T(8,128)}, f32[16,2,128,128]{3,2,1,0:T(8,128)S(1)}, f32[16,2,128,128]{3,2,1,0:T(8,128)S(1)}) fusion(f32[16,3,2,128,128]{4,3,2,1,0:T(8,128)} %bitcast.26), kind=kLoop, calls=%fused_computation | loop fusion | bytes 12582912 | tf_op jit(solution)/shard_map/gather_rows/squeeze | solution.py:278
  100.1 2.4 %term_uq.1 = (f32[2,128,128]{2,1,0:T(8,128)S(1)}, f32[64,256]{1,0:T(8,128)S(1)}, f32[64,128]{1,0:T(8,128)S(1)}, f32[64,128]{1,0:T(8,128)S(1)}) custom-call(s32[2]{0:T(128)S(1)} %pad_add_fusion.place_ref, f32[16,2,128,128]{3,2,1,0:T(8,128)S(1)} %get-tuple-element.133.root_ref, f32[16,2,128,128]{3,2,1,0:T(8,128)S(1)} %get-tuple-element.132.diag_ref, ...), custom_call_target="tpu_custom_call" | custom-call | tf_op jit(solution)/shard_map/term_uq/pallas_call | solution.py:51
  105.6 2.0 %collective-permute-start.29 = (f32[2,64,128]{2,1,0:T(8,128)S(1)}, f32[2,64,128]{2,1,0:T(8,128)S(1)}, u32[]{:S(2)}, u32[]{:S(2)}) collective-permute-start(f32[2,64,128]{2,1,0:T(8,128)S(1)} %slice.31), channel_id=1, source_target_pairs={{0,2},{1,3},{2,4},{3,5},{4,6},{5,7},{6,8},{7,9},{8,10},{9,11},{10,... | collective-permute-start | bytes 196616 | tf_op jit(solution)/shard_map/gather_t/ppermute | solution.py:227
  108.1 2.4 %collective-permute-done.29 = f32[2,64,128]{2,1,0:T(8,128)S(1)} collective-permute-done((f32[2,64,128]{2,1,0:T(8,128)S(1)}, f32[2,64,128]{2,1,0:T(8,128)S(1)}, u32[]{:S(2)}, u32[]{:S(2)}) %collective-permute-start.29) | collective-permute-done | bytes 65568 | tf_op jit(solution)/shard_map/gather_t/ppermute | solution.py:227
  119.5 3.1 %sums.1 = f32[16,320,128]{2,1,0:T(8,128)S(1)} custom-call(s32[2]{0:T(128)S(1)} %pad_add_fusion.place_ref, f32[2,128,128]{2,1,0:T(8,128)S(1)} %copy-done.9, f32[2,128,128]{2,1,0:T(8,128)S(1)} %copy-done.15, f32[2,128,128]{2,1,0:T(8,128)} %collective-permute-done.22.refs_2_, f32[2,128,128]{2,1,0:T(8,128)S(1)} %collective-permute-done.26.refs_3_, ...), custom_call_target="tpu_custom_call" | custom-call | tf_op jit(solution)/shard_map/sums/pallas_call | solution.py:51
  122.7 41.7 %all_to_all.15.got_ref = f32[16,320,128]{2,1,0:T(8,128)S(1)} all-to-all(f32[16,320,128]{2,1,0:T(8,128)S(1)} %sums.1), channel_id=1, replica_groups=mesh['row'=16,'col'=16] {'row'}, dimensions={0} | all-to-all | bytes 5242880 | tf_op jit(solution)/shard_map/scatter_sums/all_to_all | solution.py:323
  164.5 1.8 %finish.1 = f32[2048,128]{1,0:T(8,128)} custom-call(s32[4,4]{1,0:T(4,128)S(1)} %bitcast.25, s32[2]{0:T(128)S(1)} %pad_add_fusion.place_ref, f32[2048,128]{1,0:T(8,128)S(1)} %bitcast.23, f32[16,320,128]{2,1,0:T(8,128)S(1)} %all_to_all.15.got_ref, f32[128,128]{1,0:T(8,128)S(1)} %get-tuple-element.127.home_ref, f32[128,128]{1,0:T(8,128)S(1)} %slice.39.away_ref, ...), custom_call_target="tpu_custom_call" | custom-call | tf_op jit(solution)/shard_map/finish/pallas_call | solution.py:51
  (153 shorter events, 40.5 us)
Async XLA Ops:
  6.5 88.7 %all-gather.3.cloned.1.call-start = ((), (), s32[]{:S(2)}) async-start(), calls=%async_computation.3 | async-start | bytes 6684672 | tf_op jit(solution)/shard_map/gather_rows/all_gather | solution.py:277
  15.1 8.6 %collective-permute-start.4 = (f32[4,128,128]{2,1,0:T(8,128)S(1)}, f32[4,128,128]{2,1,0:T(8,128)S(1)}, u32[]{:S(2)}, u32[]{:S(2)}) collective-permute-start(f32[4,128,128]{2,1,0:T(8,128)S(1)} %get-tuple-element.71), channel_id=1, source_target_pairs={{0,16},{16,0},{32,48},{48,32},{64,80},{80,64},{96,112},{112,96},{1... | collective-permute-start | bytes 786440 | tf_op jit(solution)/shard_map/swap_rest/ppermute | solution.py:271
  26.6 40.4 %all-to-all-start = ((f32[16,192,128]{2,1,0:T(8,128)}), f32[16,192,128]{2,1,0:T(8,128)S(1)}, u32[]{:S(2)}, u32[]{:S(2)}) async-start(f32[16,192,128]{2,1,0:T(8,128)} %get-tuple-element.87), calls=%async_computation | async-start | bytes 3145728 | tf_op jit(solution)/shard_map/gather_l/all_to_all | solution.py:251
  33.4 8.0 %collective-permute-start.5 = (f32[2,128,128]{2,1,0:T(8,128)S(1)}, f32[2,128,128]{2,1,0:T(8,128)S(1)}, u32[]{:S(2)}, u32[]{:S(2)}) collective-permute-start(f32[2,128,128]{2,1,0:T(8,128)S(1)} %collective-permute-done.1.refs_7_), channel_id=1, source_target_pairs={{0,2},{1,3},{2,4},{3,5},{4,6},{5,7},{6,8},{7,9},{8,10},{9,11},{10,... | collective-permute-start | bytes 393224 | tf_op jit(solution)/shard_map/gather_l/ppermute | solution.py:227
  36.5 9.6 %collective-permute-start.6 = (f32[2,128,128]{2,1,0:T(8,128)S(1)}, f32[2,128,128]{2,1,0:T(8,128)S(1)}, u32[]{:S(2)}, u32[]{:S(2)}) collective-permute-start(f32[2,128,128]{2,1,0:T(8,128)S(1)} %collective-permute-done.2.refs_1_), channel_id=1, source_target_pairs={{0,14},{1,15},{2,0},{3,1},{4,2},{5,3},{6,4},{7,5},{8,6},{9,7},{10,... | collective-permute-start | bytes 393224 | tf_op jit(solution)/shard_map/gather_l/ppermute | solution.py:228
  46.1 8.8 %collective-permute-start.10 = (f32[2,128,128]{2,1,0:T(8,128)S(1)}, f32[2,128,128]{2,1,0:T(8,128)S(1)}, u32[]{:S(2)}, u32[]{:S(2)}) collective-permute-start(f32[2,128,128]{2,1,0:T(8,128)S(1)} %collective-permute-done.6.refs_2_), channel_id=1, source_target_pairs={{0,14},{1,15},{2,0},{3,1},{4,2},{5,3},{6,4},{7,5},{8,6},{9,7},{10,... | collective-permute-start | bytes 393224 | tf_op jit(solution)/shard_map/gather_l/ppermute | solution.py:228
  46.1 8.8 %collective-permute-start.11 = (f32[2,128,128]{2,1,0:T(8,128)S(1)}, f32[2,128,128]{2,1,0:T(8,128)S(1)}, u32[]{:S(2)}, u32[]{:S(2)}) collective-permute-start(f32[2,128,128]{2,1,0:T(8,128)S(1)} %collective-permute-done.5.refs_6_), channel_id=1, source_target_pairs={{0,1},{1,0},{2,3},{3,2},{4,5},{5,4},{6,7},{7,6},{8,9},{9,8},{10,11... | collective-permute-start | bytes 393224 | tf_op jit(solution)/shard_map/gather_l/ppermute | solution.py:208
  46.1 8.8 %collective-permute-start.12 = (f32[2,128,128]{2,1,0:T(8,128)S(1)}, f32[2,128,128]{2,1,0:T(8,128)S(1)}, u32[]{:S(2)}, u32[]{:S(2)}) collective-permute-start(f32[2,128,128]{2,1,0:T(8,128)S(1)} %collective-permute-done.6.refs_2_), channel_id=1, source_target_pairs={{0,1},{1,0},{2,3},{3,2},{4,5},{5,4},{6,7},{7,6},{8,9},{9,8},{10,11... | collective-permute-start | bytes 393224 | tf_op jit(solution)/shard_map/gather_l/ppermute | solution.py:208
  46.6 9.0 %collective-permute-start.9 = (f32[2,128,128]{2,1,0:T(8,128)S(1)}, f32[2,128,128]{2,1,0:T(8,128)S(1)}, u32[]{:S(2)}, u32[]{:S(2)}) collective-permute-start(f32[2,128,128]{2,1,0:T(8,128)S(1)} %collective-permute-done.5.refs_6_), channel_id=1, source_target_pairs={{0,2},{1,3},{2,4},{3,5},{4,6},{5,7},{6,8},{7,9},{8,10},{9,11},{10,... | collective-permute-start | bytes 393224 | tf_op jit(solution)/shard_map/gather_l/ppermute | solution.py:227
  55.6 8.3 %collective-permute-start.15 = (f32[2,128,128]{2,1,0:T(8,128)S(1)}, f32[2,128,128]{2,1,0:T(8,128)S(1)}, u32[]{:S(2)}, u32[]{:S(2)}) collective-permute-start(f32[2,128,128]{2,1,0:T(8,128)S(1)} %collective-permute-done.9.refs_5_), channel_id=1, source_target_pairs={{0,1},{1,0},{2,3},{3,2},{4,5},{5,4},{6,7},{7,6},{8,9},{9,8},{10,11... | collective-permute-start | bytes 393224 | tf_op jit(solution)/shard_map/gather_l/ppermute | solution.py:208
  55.6 8.3 %collective-permute-start.16 = (f32[2,128,128]{2,1,0:T(8,128)S(1)}, f32[2,128,128]{2,1,0:T(8,128)S(1)}, u32[]{:S(2)}, u32[]{:S(2)}) collective-permute-start(f32[2,128,128]{2,1,0:T(8,128)S(1)} %collective-permute-done.10.refs_3_), channel_id=1, source_target_pairs={{0,1},{1,0},{2,3},{3,2},{4,5},{5,4},{6,7},{7,6},{8,9},{9,8},{10,11... | collective-permute-start | bytes 393224 | tf_op jit(solution)/shard_map/gather_l/ppermute | solution.py:208
  56.1 7.1 %collective-permute-start.13 = (f32[2,64,128]{2,1,0:T(8,128)S(1)}, f32[2,64,128]{2,1,0:T(8,128)S(1)}, u32[]{:S(2)}, u32[]{:S(2)}) collective-permute-start(f32[2,64,128]{2,1,0:T(8,128)S(1)} %slice.27), channel_id=1, source_target_pairs={{0,2},{1,3},{2,4},{3,5},{4,6},{5,7},{6,8},{7,9},{8,10},{9,11},{10,... | collective-permute-start | bytes 196616 | tf_op jit(solution)/shard_map/gather_l/ppermute | solution.py:227
  74.9 7.1 %collective-permute-start.19 = (f32[2,128,128]{2,1,0:T(8,128)S(1)}, f32[2,128,128]{2,1,0:T(8,128)S(1)}, u32[]{:S(2)}, u32[]{:S(2)}) collective-permute-start(f32[2,128,128]{2,1,0:T(8,128)S(1)} %get-tuple-element.96.refs_0_), channel_id=1, source_target_pairs={{0,14},{1,15},{2,0},{3,1},{4,2},{5,3},{6,4},{7,5},{8,6},{9,7},{10,... | collective-permute-start | bytes 393224 | tf_op jit(solution)/shard_map/gather_t/ppermute | solution.py:228
  82.0 9.7 %collective-permute-start.21 = (f32[2,128,128]{2,1,0:T(8,128)S(1)}, f32[2,128,128]{2,1,0:T(8,128)S(1)}, u32[]{:S(2)}, u32[]{:S(2)}) collective-permute-start(f32[2,128,128]{2,1,0:T(8,128)S(1)} %collective-permute-done.18.refs_7_), channel_id=1, source_target_pairs={{0,2},{1,3},{2,4},{3,5},{4,6},{5,7},{6,8},{7,9},{8,10},{9,11},{10,... | collective-permute-start | bytes 393224 | tf_op jit(solution)/shard_map/gather_t/ppermute | solution.py:227
  83.7 7.9 %collective-permute-start.22 = (f32[2,128,128]{2,1,0:T(8,128)S(1)}, f32[2,128,128]{2,1,0:T(8,128)}, u32[]{:S(2)}, u32[]{:S(2)}) collective-permute-start(f32[2,128,128]{2,1,0:T(8,128)S(1)} %collective-permute-done.19.refs_1_), channel_id=1, source_target_pairs={{0,14},{1,15},{2,0},{3,1},{4,2},{5,3},{6,4},{7,5},{8,6},{9,7},{10,... | collective-permute-start | bytes 393224 | tf_op jit(solution)/shard_map/gather_t/ppermute | solution.py:228
  84.0 7.7 %collective-permute-start.23 = (f32[2,128,128]{2,1,0:T(8,128)S(1)}, f32[2,128,128]{2,1,0:T(8,128)S(1)}, u32[]{:S(2)}, u32[]{:S(2)}) collective-permute-start(f32[2,128,128]{2,1,0:T(8,128)S(1)} %collective-permute-done.18.refs_7_), channel_id=1, source_target_pairs={{0,1},{1,0},{2,3},{3,2},{4,5},{5,4},{6,7},{7,6},{8,9},{9,8},{10,11... | collective-permute-start | bytes 393224 | tf_op jit(solution)/shard_map/gather_t/ppermute | solution.py:208
  84.0 8.3 %collective-permute-start.24 = (f32[2,128,128]{2,1,0:T(8,128)S(1)}, f32[2,128,128]{2,1,0:T(8,128)S(1)}, u32[]{:S(2)}, u32[]{:S(2)}) collective-permute-start(f32[2,128,128]{2,1,0:T(8,128)S(1)} %collective-permute-done.19.refs_1_), channel_id=1, source_target_pairs={{0,1},{1,0},{2,3},{3,2},{4,5},{5,4},{6,7},{7,6},{8,9},{9,8},{10,11... | collective-permute-start | bytes 393224 | tf_op jit(solution)/shard_map/gather_t/ppermute | solution.py:208
  84.5 28.1 %all-to-all-start.1 = ((f32[8,2,128,128]{3,2,1,0:T(8,128)}), f32[8,2,128,128]{3,2,1,0:T(8,128)S(1)}, u32[]{:S(2)}, u32[]{:S(2)}) async-start(f32[8,2,128,128]{3,2,1,0:T(8,128)} %copy-done.7), calls=%async_computation.1 | async-start | bytes 2097152 | tf_op jit(solution)/shard_map/gather_t/all_to_all | solution.py:254
  93.0 11.9 %collective-permute-start.25 = (f32[2,128,128]{2,1,0:T(8,128)S(1)}, f32[2,128,128]{2,1,0:T(8,128)S(1)}, u32[]{:S(2)}, u32[]{:S(2)}) collective-permute-start(f32[2,128,128]{2,1,0:T(8,128)S(1)} %collective-permute-done.21.refs_6_), channel_id=1, source_target_pairs={{0,2},{1,3},{2,4},{3,5},{4,6},{5,7},{6,8},{7,9},{8,10},{9,11},{10,... | collective-permute-start | bytes 393224 | tf_op jit(solution)/shard_map/gather_t/ppermute | solution.py:227
  94.7 10.2 %collective-permute-start.27 = (f32[2,128,128]{2,1,0:T(8,128)S(1)}, f32[2,128,128]{2,1,0:T(8,128)}, u32[]{:S(2)}, u32[]{:S(2)}) collective-permute-start(f32[2,128,128]{2,1,0:T(8,128)S(1)} %collective-permute-done.21.refs_6_), channel_id=1, source_target_pairs={{0,1},{1,0},{2,3},{3,2},{4,5},{5,4},{6,7},{7,6},{8,9},{9,8},{10,11... | collective-permute-start | bytes 393224 | tf_op jit(solution)/shard_map/gather_t/ppermute | solution.py:208
  94.7 10.2 %collective-permute-start.26 = (f32[2,128,128]{2,1,0:T(8,128)}, f32[2,128,128]{2,1,0:T(8,128)S(1)}, u32[]{:S(2)}, u32[]{:S(2)}) collective-permute-start(f32[2,128,128]{2,1,0:T(8,128)} %collective-permute-done.22.refs_2_), channel_id=1, source_target_pairs={{0,14},{1,15},{2,0},{3,1},{4,2},{5,3},{6,4},{7,5},{8,6},{9,7},{10,... | collective-permute-start | bytes 393224 | tf_op jit(solution)/shard_map/gather_t/ppermute | solution.py:228
  95.0 9.9 %collective-permute-start.28 = (f32[2,128,128]{2,1,0:T(8,128)}, f32[2,128,128]{2,1,0:T(8,128)}, u32[]{:S(2)}, u32[]{:S(2)}) collective-permute-start(f32[2,128,128]{2,1,0:T(8,128)} %collective-permute-done.22.refs_2_), channel_id=1, source_target_pairs={{0,1},{1,0},{2,3},{3,2},{4,5},{5,4},{6,7},{7,6},{8,9},{9,8},{10,11... | collective-permute-start | bytes 393224 | tf_op jit(solution)/shard_map/gather_t/ppermute | solution.py:208
  104.9 6.9 %collective-permute-start.31 = (f32[2,128,128]{2,1,0:T(8,128)S(1)}, f32[2,128,128]{2,1,0:T(8,128)S(1)}, u32[]{:S(2)}, u32[]{:S(2)}) collective-permute-start(f32[2,128,128]{2,1,0:T(8,128)S(1)} %collective-permute-done.25.refs_5_), channel_id=1, source_target_pairs={{0,1},{1,0},{2,3},{3,2},{4,5},{5,4},{6,7},{7,6},{8,9},{9,8},{10,11... | collective-permute-start | bytes 393224 | tf_op jit(solution)/shard_map/gather_t/ppermute | solution.py:208
  105.3 6.6 %collective-permute-start.32 = (f32[2,128,128]{2,1,0:T(8,128)S(1)}, f32[2,128,128]{2,1,0:T(8,128)S(1)}, u32[]{:S(2)}, u32[]{:S(2)}) collective-permute-start(f32[2,128,128]{2,1,0:T(8,128)S(1)} %collective-permute-done.26.refs_3_), channel_id=1, source_target_pairs={{0,1},{1,0},{2,3},{3,2},{4,5},{5,4},{6,7},{7,6},{8,9},{9,8},{10,11... | collective-permute-start | bytes 393224 | tf_op jit(solution)/shard_map/gather_t/ppermute | solution.py:208
  (51 other events, 275.7 us)
Sparse Core Ops, SparseCore 0:
  25.1 53.4 all-gather.2

commit v8 on v7

--- a/solution.py
+++ b/solution.py
@@ -53,7 +53,7 @@
         out_shape=[jax.ShapeDtypeStruct(s, F32) for s in shapes],
         in_specs=[smem] * scalars + [vmem] * (len(args) - scalars),
         out_specs=[vmem] * len(shapes),
-        compiler_params=pltpu.CompilerParams(vmem_limit_bytes=10 * 2**20),
+        compiler_params=pltpu.CompilerParams(vmem_limit_bytes=5 * 2**20),
     )(*args)
 
 
@@ -228,6 +228,8 @@
         down = lax.ppermute(down, "col", LAYER_DOWN)
         up, down, swapped, more = lax.optimization_barrier((up, down, swapped, ties.get(step)))
         tied.append(more)
+        if step == begin[3]:
+            up, down, beside = lax.optimization_barrier((up, down, beside))
         other.update(zip(late, swapped))
         if step < last:
             mine[LAYERS - step], mine[step] = up, down
@@ -270,12 +272,15 @@
         l32_pair, away = lax.optimization_barrier((l32_pair, away))
         away = lax.ppermute(away, "row", ROW_SWAP)
     with jax.named_scope("gather_l"):
-        l_mine, l_other, cols, away = gather_layers(l32_pair, (2, send, to_rows), {1: away})
+        l_mine, l_other, cols, away = gather_layers(
+            l32_pair, (1, (send, away), lambda x: to_rows(x[0]), 4), {2: away}
+        )
     with jax.named_scope("pack"):
         packed, l3 = call(pack_kernel, [(3, 2, *square), (2, *square)], place, home, away)
     with jax.named_scope("gather_rows"):
         panels = lax.all_gather(packed, "col", axis=0)
-        root_rows, diag_rows, l2_rows = (panels[:, i] for i in range(3))
+        panels = [panels[:, i] for i in range(3)]
+        root_rows, diag_rows, l2_rows = panels
     with jax.named_scope("term_t"):
         t, send, l32_rows = call(
             t_kernel,
@@ -296,7 +301,9 @@
             cols,
         )
     with jax.named_scope("gather_t"):
-        t_mine, t_other, t_cols, (u, q) = gather_layers(t, (1, send, to_side), {3: (u, q)})
+        t_mine, t_other, t_cols, (root_rows, l2_rows), (u, q) = gather_layers(
+            t, (1, send, to_side, 5), {3: (root_rows, l2_rows), 4: (u, q)}
+        )
     with jax.named_scope("term_y"):
         y, y_home, y_away = call(
             y_kernel, [(2 * TB, TB), square, square], place, root_rows, t_cols

time: 175 us -> 169 us (0.966)
  starting transfers between devices: 41 us -> 38.7 us
  waiting for transfers between devices: 42 us -> 39.8 us
    ppermute x8, waiting for transfers between devices: 18.4 us -> 10.3 us  [gather_layers(): down = lax.ppermute(down, 'col', LAYER_DOWN)]
    all_to_all x1, waiting for transfers between devices: 0.01 us -> 4.13 us  [to_rows(): return lax.all_to_all(x, 'row', 0, 0, tiled=True)]
    ppermute x2, waiting for transfers between devices: 0.01 us -> 3.29 us  [body(): away = lax.ppermute(away, 'row', ROW_SWAP)]
    unnamed x77 -> x69, local copies, waits for them, and re-layouts: 14.3 us -> 11.9 us
    ppermute x8, starting transfers between devices: 17.2 us -> 15 us  [gather_layers(): up = lax.ppermute(up, 'col', LAYER_UP)]
  transfers between devices with their start and end apart: 38 -> 38, of which waited for: 17 -> 16; matrix products, arithmetic and copies ran while one was open for 3% -> 4% of each run, Pallas kernels for 4% -> 4%
where the time goes in v8:
time: 169 us; the launch traced here: 167 us
  blocking collectives  41.8 us (25%)
  waiting for transfers between devices  39.8 us (24%)
  starting transfers between devices  38.7 us (23%)
  local copies, waits for them, and re-layouts  18.5 us (11%)
  between operations  13.8 us (8%)
  Pallas kernels  13.7 us (8%)
    all_to_all x1, blocking collectives, body(): got = lax.all_to_all(sums, 'row', 0, 0, tiled=True)  41.8 us
    ppermute x8, waiting for transfers between devices, gather_layers(): up = lax.ppermute(up, 'col', LAYER_UP)  16.6 us
    ppermute x8, starting transfers between devices, gather_layers(): up = lax.ppermute(up, 'col', LAYER_UP)  15 us
    pallas_call x7, Pallas kernels, call(): pl.pallas_call(kernel, out_shape=[jax.ShapeDtypeStruct(s, F32) for s in s...  13.7 us
    unnamed x69, local copies, waits for them, and re-layouts  11.9 us
    ppermute x8, waiting for transfers between devices, gather_layers(): down = lax.ppermute(down, 'col', LAYER_DOWN)  10.3 us
    all_to_all x1, starting transfers between devices, to_rows(): return lax.all_to_all(x, 'row', 0, 0, tiled=True)  6.75 us
    all_to_all x1, starting transfers between devices, to_side(): lax.all_to_all(x, 'row', 0, 0, tiled=True, axis_index_groups=SAME_SIDE)  6.24 us
  transfers between devices with their start and end apart: 38, of which 16 were waited for; matrix products, arithmetic and copies ran while one was open for 4% of the time, Pallas kernels for 4%

profile of v8, /device:TPU:32, one launch (start us, length us, event | category | flops | bytes accessed | tf_op | source)
XLA Modules:
  0.0 167.0 jit_solution(6012812369620882390)
XLA Ops:
  8.8 2.0 %prepare.1 = (f32[128,128]{1,0:T(8,128)S(1)}, f32[4,128,128]{2,1,0:T(8,128)S(1)}, f32[4,128,128]{2,1,0:T(8,128)S(1)}, f32[16,192,128]{2,1,0:T(8,128)}) custom-call(s32[4,4]{1,0:T(4,128)S(1)} %bitcast.24, s32[2]{0:T(128)S(1)} %pad_add_fusion.place_ref, f32[2048,128]{1,0:T(8,128)S(1)} %bitcast.22), custom_call_target="tpu_custom_call" | custom-call | tf_op jit(solution)/shard_map/prepare/pallas_call | solution.py:51
  12.3 2.7 %collective-permute-done = f32[128,128]{1,0:T(8,128)S(1)} collective-permute-done((f32[128,128]{1,0:T(8,128)S(1)}, f32[128,128]{1,0:T(8,128)S(1)}, u32[]{:S(2)}, u32[]{:S(2)}) %collective-permute-start) | collective-permute-done | bytes 65568 | tf_op jit(solution)/shard_map/swap_l32/ppermute | solution.py:268
  16.7 1.9 %collective-permute-start.1 = (f32[2,128,128]{2,1,0:T(8,128)S(1)}, f32[2,128,128]{2,1,0:T(8,128)S(1)}, u32[]{:S(2)}, u32[]{:S(2)}) collective-permute-start(f32[2,128,128]{2,1,0:T(8,128)S(1)} %pad_maximum_fusion.refs_0_), channel_id=1, source_target_pairs={{0,2},{1,3},{2,4},{3,5},{4,6},{5,7},{6,8},{7,9},{8,10},{9,11},{10,... | collective-permute-start | bytes 393224 | tf_op jit(solution)/shard_map/gather_l/ppermute | solution.py:227
  18.8 3.3 %collective-permute-done.4.got_ref = f32[4,128,128]{2,1,0:T(8,128)S(1)} collective-permute-done((f32[4,128,128]{2,1,0:T(8,128)S(1)}, f32[4,128,128]{2,1,0:T(8,128)S(1)}, u32[]{:S(2)}, u32[]{:S(2)}) %collective-permute-start.4) | collective-permute-done | bytes 262176 | tf_op jit(solution)/shard_map/swap_rest/ppermute | solution.py:273
  22.6 1.8 %collective-permute-done.2.refs_1_ = f32[2,128,128]{2,1,0:T(8,128)S(1)} collective-permute-done((f32[2,128,128]{2,1,0:T(8,128)S(1)}, f32[2,128,128]{2,1,0:T(8,128)S(1)}, u32[]{:S(2)}, u32[]{:S(2)}) %collective-permute-start.2) | collective-permute-done | bytes 131104 | tf_op jit(solution)/shard_map/gather_l/ppermute | solution.py:228
  24.5 3.1 %collective-permute-start.5 = (f32[2,128,128]{2,1,0:T(8,128)S(1)}, f32[2,128,128]{2,1,0:T(8,128)S(1)}, u32[]{:S(2)}, u32[]{:S(2)}) collective-permute-start(f32[2,128,128]{2,1,0:T(8,128)S(1)} %collective-permute-done.1.refs_7_), channel_id=1, source_target_pairs={{0,2},{1,3},{2,4},{3,5},{4,6},{5,7},{6,8},{7,9},{8,10},{9,11},{10,... | collective-permute-start | bytes 393224 | tf_op jit(solution)/shard_map/gather_l/ppermute | solution.py:227
  28.1 2.4 %collective-permute-done.5.refs_6_ = f32[2,128,128]{2,1,0:T(8,128)S(1)} collective-permute-done((f32[2,128,128]{2,1,0:T(8,128)S(1)}, f32[2,128,128]{2,1,0:T(8,128)S(1)}, u32[]{:S(2)}, u32[]{:S(2)}) %collective-permute-start.5) | collective-permute-done | bytes 131104 | tf_op jit(solution)/shard_map/gather_l/ppermute | solution.py:227
  30.5 3.0 %collective-permute-done.6.refs_2_ = f32[2,128,128]{2,1,0:T(8,128)S(1)} collective-permute-done((f32[2,128,128]{2,1,0:T(8,128)S(1)}, f32[2,128,128]{2,1,0:T(8,128)S(1)}, u32[]{:S(2)}, u32[]{:S(2)}) %collective-permute-start.6) | collective-permute-done | bytes 131104 | tf_op jit(solution)/shard_map/gather_l/ppermute | solution.py:228
  34.9 6.8 %all-to-all-start = ((f32[16,192,128]{2,1,0:T(8,128)}), f32[16,192,128]{2,1,0:T(8,128)S(1)}, u32[]{:S(2)}, u32[]{:S(2)}) async-start(f32[16,192,128]{2,1,0:T(8,128)} %get-tuple-element.86), calls=%async_computation | async-start | bytes 3145728 | tf_op jit(solution)/shard_map/gather_l/all_to_all | solution.py:253
  42.3 2.0 %collective-permute-start.9 = (f32[2,128,128]{2,1,0:T(8,128)S(1)}, f32[2,128,128]{2,1,0:T(8,128)S(1)}, u32[]{:S(2)}, u32[]{:S(2)}) collective-permute-start(f32[2,128,128]{2,1,0:T(8,128)S(1)} %collective-permute-done.5.refs_6_), channel_id=1, source_target_pairs={{0,2},{1,3},{2,4},{3,5},{4,6},{5,7},{6,8},{7,9},{8,10},{9,11},{10,... | collective-permute-start | bytes 393224 | tf_op jit(solution)/shard_map/gather_l/ppermute | solution.py:227
  44.3 2.3 %collective-permute-done.10.refs_3_ = f32[2,128,128]{2,1,0:T(8,128)S(1)} collective-permute-done((f32[2,128,128]{2,1,0:T(8,128)S(1)}, f32[2,128,128]{2,1,0:T(8,128)S(1)}, u32[]{:S(2)}, u32[]{:S(2)}) %collective-permute-start.10) | collective-permute-done | bytes 131104 | tf_op jit(solution)/shard_map/gather_l/ppermute | solution.py:228
  46.7 4.7 %collective-permute-done.9.refs_5_ = f32[2,128,128]{2,1,0:T(8,128)S(1)} collective-permute-done((f32[2,128,128]{2,1,0:T(8,128)S(1)}, f32[2,128,128]{2,1,0:T(8,128)S(1)}, u32[]{:S(2)}, u32[]{:S(2)}) %collective-permute-start.9) | collective-permute-done | bytes 131104 | tf_op jit(solution)/shard_map/gather_l/ppermute | solution.py:227
  53.1 2.1 %collective-permute-start.14 = (f32[2,64,128]{2,1,0:T(8,128)S(1)}, f32[2,64,128]{2,1,0:T(8,128)}, u32[]{:S(2)}, u32[]{:S(2)}) collective-permute-start(f32[2,64,128]{2,1,0:T(8,128)S(1)} %slice.28), channel_id=1, source_target_pairs={{0,14},{1,15},{2,0},{3,1},{4,2},{5,3},{6,4},{7,5},{8,6},{9,7},{10,... | collective-permute-start | bytes 196616 | tf_op jit(solution)/shard_map/gather_l/ppermute | solution.py:228
  55.2 3.7 %collective-permute-done.13 = f32[2,64,128]{2,1,0:T(8,128)} collective-permute-done((f32[2,64,128]{2,1,0:T(8,128)S(1)}, f32[2,64,128]{2,1,0:T(8,128)}, u32[]{:S(2)}, u32[]{:S(2)}) %collective-permute-start.13) | collective-permute-done | bytes 65568 | tf_op jit(solution)/shard_map/gather_l/ppermute | solution.py:227
  59.3 4.1 %all-to-all-done.refs_16_.cols_ref = f32[16,192,128]{2,1,0:T(8,128)S(1)} async-done(((f32[16,192,128]{2,1,0:T(8,128)}), f32[16,192,128]{2,1,0:T(8,128)S(1)}, u32[]{:S(2)}, u32[]{:S(2)}) %all-to-all-start) | async-done | bytes 1572896 | tf_op jit(solution)/shard_map/gather_l/all_to_all | solution.py:253
  73.1 5.2 %collective-permute-done.18.refs_7_ = f32[2,128,128]{2,1,0:T(8,128)S(1)} collective-permute-done((f32[2,128,128]{2,1,0:T(8,128)S(1)}, f32[2,128,128]{2,1,0:T(8,128)S(1)}, u32[]{:S(2)}, u32[]{:S(2)}) %collective-permute-start.18) | collective-permute-done | bytes 131104 | tf_op jit(solution)/shard_map/gather_t/ppermute | solution.py:227
  78.2 2.0 %collective-permute-done.19.refs_1_ = f32[2,128,128]{2,1,0:T(8,128)S(1)} collective-permute-done((f32[2,128,128]{2,1,0:T(8,128)S(1)}, f32[2,128,128]{2,1,0:T(8,128)S(1)}, u32[]{:S(2)}, u32[]{:S(2)}) %collective-permute-start.19) | collective-permute-done | bytes 131104 | tf_op jit(solution)/shard_map/gather_t/ppermute | solution.py:228
  82.8 6.2 %all-to-all-start.1 = ((f32[8,2,128,128]{3,2,1,0:T(8,128)}), f32[8,2,128,128]{3,2,1,0:T(8,128)S(1)}, u32[]{:S(2)}, u32[]{:S(2)}) async-start(f32[8,2,128,128]{3,2,1,0:T(8,128)} %copy-done.7), calls=%async_computation.1 | async-start | bytes 2097152 | tf_op jit(solution)/shard_map/gather_t/all_to_all | solution.py:256
  90.4 1.9 %collective-permute-start.25 = (f32[2,128,128]{2,1,0:T(8,128)S(1)}, f32[2,128,128]{2,1,0:T(8,128)S(1)}, u32[]{:S(2)}, u32[]{:S(2)}) collective-permute-start(f32[2,128,128]{2,1,0:T(8,128)S(1)} %collective-permute-done.21.refs_6_), channel_id=1, source_target_pairs={{0,2},{1,3},{2,4},{3,5},{4,6},{5,7},{6,8},{7,9},{8,10},{9,11},{10,... | collective-permute-start | bytes 393224 | tf_op jit(solution)/shard_map/gather_t/ppermute | solution.py:227
  92.7 4.8 %slice_bitcast_fusion = (f32[16,2,128,128]{3,2,1,0:T(8,128)S(1)}, f32[16,2,128,128]{3,2,1,0:T(8,128)}, f32[16,2,128,128]{3,2,1,0:T(8,128)S(1)}) fusion(f32[16,3,2,128,128]{4,3,2,1,0:T(8,128)} %bitcast.26), kind=kLoop, calls=%fused_computation | loop fusion | bytes 12582912 | tf_op jit(solution)/shard_map/gather_rows/squeeze | solution.py:282
  101.0 2.4 %term_uq.1 = (f32[2,128,128]{2,1,0:T(8,128)S(1)}, f32[64,256]{1,0:T(8,128)S(1)}, f32[64,128]{1,0:T(8,128)S(1)}, f32[64,128]{1,0:T(8,128)S(1)}) custom-call(s32[2]{0:T(128)S(1)} %pad_add_fusion.place_ref, f32[16,2,128,128]{3,2,1,0:T(8,128)S(1)} %get-tuple-element.126.root_ref, f32[16,2,128,128]{3,2,1,0:T(8,128)S(1)} %get-tuple-element.139.diag_ref, ...), custom_call_target="tpu_custom_call" | custom-call | tf_op jit(solution)/shard_map/term_uq/pallas_call | solution.py:51
  113.4 3.1 %sums.1 = f32[16,320,128]{2,1,0:T(8,128)S(1)} custom-call(s32[2]{0:T(128)S(1)} %pad_add_fusion.place_ref, f32[2,128,128]{2,1,0:T(8,128)S(1)} %copy-done.9, f32[2,128,128]{2,1,0:T(8,128)S(1)} %copy-done.15, f32[2,128,128]{2,1,0:T(8,128)} %collective-permute-done.22.refs_2_, f32[2,128,128]{2,1,0:T(8,128)S(1)} %collective-permute-done.26.refs_3_, ...), custom_call_target="tpu_custom_call" | custom-call | tf_op jit(solution)/shard_map/sums/pallas_call | solution.py:51
  116.6 41.8 %all_to_all.15.got_ref = f32[16,320,128]{2,1,0:T(8,128)S(1)} all-to-all(f32[16,320,128]{2,1,0:T(8,128)S(1)} %sums.1), channel_id=1, replica_groups=mesh['row'=16,'col'=16] {'row'}, dimensions={0} | all-to-all | bytes 5242880 | tf_op jit(solution)/shard_map/scatter_sums/all_to_all | solution.py:330
  158.4 1.8 %finish.1 = f32[2048,128]{1,0:T(8,128)} custom-call(s32[4,4]{1,0:T(4,128)S(1)} %bitcast.25, s32[2]{0:T(128)S(1)} %pad_add_fusion.place_ref, f32[2048,128]{1,0:T(8,128)S(1)} %bitcast.23, f32[16,320,128]{2,1,0:T(8,128)S(1)} %all_to_all.15.got_ref, f32[128,128]{1,0:T(8,128)S(1)} %get-tuple-element.135.home_ref, f32[128,128]{1,0:T(8,128)S(1)} %slice.39.away_ref, ...), custom_call_target="tpu_custom_call" | custom-call | tf_op jit(solution)/shard_map/finish/pallas_call | solution.py:51
  (145 shorter events, 38.1 us)
Async XLA Ops:
  6.5 86.2 %all-gather.3.cloned.1.call-start = ((), (), s32[]{:S(2)}) async-start(), calls=%async_computation.3 | async-start | bytes 6684672 | tf_op jit(solution)/shard_map/gather_rows/all_gather | solution.py:281
  15.1 7.0 %collective-permute-start.4 = (f32[4,128,128]{2,1,0:T(8,128)S(1)}, f32[4,128,128]{2,1,0:T(8,128)S(1)}, u32[]{:S(2)}, u32[]{:S(2)}) collective-permute-start(f32[4,128,128]{2,1,0:T(8,128)S(1)} %get-tuple-element.76), channel_id=1, source_target_pairs={{0,16},{16,0},{32,48},{48,32},{64,80},{80,64},{96,112},{112,96},{1... | collective-permute-start | bytes 786440 | tf_op jit(solution)/shard_map/swap_rest/ppermute | solution.py:273
  24.5 6.0 %collective-permute-start.5 = (f32[2,128,128]{2,1,0:T(8,128)S(1)}, f32[2,128,128]{2,1,0:T(8,128)S(1)}, u32[]{:S(2)}, u32[]{:S(2)}) collective-permute-start(f32[2,128,128]{2,1,0:T(8,128)S(1)} %collective-permute-done.1.refs_7_), channel_id=1, source_target_pairs={{0,2},{1,3},{2,4},{3,5},{4,6},{5,7},{6,8},{7,9},{8,10},{9,11},{10,... | collective-permute-start | bytes 393224 | tf_op jit(solution)/shard_map/gather_l/ppermute | solution.py:227
  34.9 28.6 %all-to-all-start = ((f32[16,192,128]{2,1,0:T(8,128)}), f32[16,192,128]{2,1,0:T(8,128)S(1)}, u32[]{:S(2)}, u32[]{:S(2)}) async-start(f32[16,192,128]{2,1,0:T(8,128)} %get-tuple-element.86), calls=%async_computation | async-start | bytes 3145728 | tf_op jit(solution)/shard_map/gather_l/all_to_all | solution.py:253
  42.3 9.1 %collective-permute-start.9 = (f32[2,128,128]{2,1,0:T(8,128)S(1)}, f32[2,128,128]{2,1,0:T(8,128)S(1)}, u32[]{:S(2)}, u32[]{:S(2)}) collective-permute-start(f32[2,128,128]{2,1,0:T(8,128)S(1)} %collective-permute-done.5.refs_6_), channel_id=1, source_target_pairs={{0,2},{1,3},{2,4},{3,5},{4,6},{5,7},{6,8},{7,9},{8,10},{9,11},{10,... | collective-permute-start | bytes 393224 | tf_op jit(solution)/shard_map/gather_l/ppermute | solution.py:227
  51.4 8.0 %collective-permute-start.15 = (f32[2,128,128]{2,1,0:T(8,128)S(1)}, f32[2,128,128]{2,1,0:T(8,128)S(1)}, u32[]{:S(2)}, u32[]{:S(2)}) collective-permute-start(f32[2,128,128]{2,1,0:T(8,128)S(1)} %collective-permute-done.9.refs_5_), channel_id=1, source_target_pairs={{0,1},{1,0},{2,3},{3,2},{4,5},{5,4},{6,7},{7,6},{8,9},{9,8},{10,11... | collective-permute-start | bytes 393224 | tf_op jit(solution)/shard_map/gather_l/ppermute | solution.py:208
  51.4 8.0 %collective-permute-start.16 = (f32[2,128,128]{2,1,0:T(8,128)S(1)}, f32[2,128,128]{2,1,0:T(8,128)S(1)}, u32[]{:S(2)}, u32[]{:S(2)}) collective-permute-start(f32[2,128,128]{2,1,0:T(8,128)S(1)} %collective-permute-done.10.refs_3_), channel_id=1, source_target_pairs={{0,1},{1,0},{2,3},{3,2},{4,5},{5,4},{6,7},{7,6},{8,9},{9,8},{10,11... | collective-permute-start | bytes 393224 | tf_op jit(solution)/shard_map/gather_l/ppermute | solution.py:208
  51.9 7.0 %collective-permute-start.13 = (f32[2,64,128]{2,1,0:T(8,128)S(1)}, f32[2,64,128]{2,1,0:T(8,128)}, u32[]{:S(2)}, u32[]{:S(2)}) collective-permute-start(f32[2,64,128]{2,1,0:T(8,128)S(1)} %slice.27), channel_id=1, source_target_pairs={{0,2},{1,3},{2,4},{3,5},{4,6},{5,7},{6,8},{7,9},{8,10},{9,11},{10,... | collective-permute-start | bytes 196616 | tf_op jit(solution)/shard_map/gather_l/ppermute | solution.py:227
  53.1 6.2 %collective-permute-start.14 = (f32[2,64,128]{2,1,0:T(8,128)S(1)}, f32[2,64,128]{2,1,0:T(8,128)}, u32[]{:S(2)}, u32[]{:S(2)}) collective-permute-start(f32[2,64,128]{2,1,0:T(8,128)S(1)} %slice.28), channel_id=1, source_target_pairs={{0,14},{1,15},{2,0},{3,1},{4,2},{5,3},{6,4},{7,5},{8,6},{9,7},{10,... | collective-permute-start | bytes 196616 | tf_op jit(solution)/shard_map/gather_l/ppermute | solution.py:228
  69.7 8.5 %collective-permute-start.18 = (f32[2,128,128]{2,1,0:T(8,128)S(1)}, f32[2,128,128]{2,1,0:T(8,128)S(1)}, u32[]{:S(2)}, u32[]{:S(2)}) collective-permute-start(f32[2,128,128]{2,1,0:T(8,128)S(1)} %get-tuple-element.102.refs_0_), channel_id=1, source_target_pairs={{0,2},{1,3},{2,4},{3,5},{4,6},{5,7},{6,8},{7,9},{8,10},{9,11},{10,... | collective-permute-start | bytes 393224 | tf_op jit(solution)/shard_map/gather_t/ppermute | solution.py:227
  71.3 8.9 %collective-permute-start.19 = (f32[2,128,128]{2,1,0:T(8,128)S(1)}, f32[2,128,128]{2,1,0:T(8,128)S(1)}, u32[]{:S(2)}, u32[]{:S(2)}) collective-permute-start(f32[2,128,128]{2,1,0:T(8,128)S(1)} %get-tuple-element.102.refs_0_), channel_id=1, source_target_pairs={{0,14},{1,15},{2,0},{3,1},{4,2},{5,3},{6,4},{7,5},{8,6},{9,7},{10,... | collective-permute-start | bytes 393224 | tf_op jit(solution)/shard_map/gather_t/ppermute | solution.py:228
  80.2 8.8 %collective-permute-start.21 = (f32[2,128,128]{2,1,0:T(8,128)S(1)}, f32[2,128,128]{2,1,0:T(8,128)S(1)}, u32[]{:S(2)}, u32[]{:S(2)}) collective-permute-start(f32[2,128,128]{2,1,0:T(8,128)S(1)} %collective-permute-done.18.refs_7_), channel_id=1, source_target_pairs={{0,2},{1,3},{2,4},{3,5},{4,6},{5,7},{6,8},{7,9},{8,10},{9,11},{10,... | collective-permute-start | bytes 393224 | tf_op jit(solution)/shard_map/gather_t/ppermute | solution.py:227
  81.7 7.3 %collective-permute-start.22 = (f32[2,128,128]{2,1,0:T(8,128)S(1)}, f32[2,128,128]{2,1,0:T(8,128)}, u32[]{:S(2)}, u32[]{:S(2)}) collective-permute-start(f32[2,128,128]{2,1,0:T(8,128)S(1)} %collective-permute-done.19.refs_1_), channel_id=1, source_target_pairs={{0,14},{1,15},{2,0},{3,1},{4,2},{5,3},{6,4},{7,5},{8,6},{9,7},{10,... | collective-permute-start | bytes 393224 | tf_op jit(solution)/shard_map/gather_t/ppermute | solution.py:228
  82.2 6.8 %collective-permute-start.23 = (f32[2,128,128]{2,1,0:T(8,128)S(1)}, f32[2,128,128]{2,1,0:T(8,128)S(1)}, u32[]{:S(2)}, u32[]{:S(2)}) collective-permute-start(f32[2,128,128]{2,1,0:T(8,128)S(1)} %collective-permute-done.18.refs_7_), channel_id=1, source_target_pairs={{0,1},{1,0},{2,3},{3,2},{4,5},{5,4},{6,7},{7,6},{8,9},{9,8},{10,11... | collective-permute-start | bytes 393224 | tf_op jit(solution)/shard_map/gather_t/ppermute | solution.py:208
  82.3 7.5 %collective-permute-start.24 = (f32[2,128,128]{2,1,0:T(8,128)S(1)}, f32[2,128,128]{2,1,0:T(8,128)S(1)}, u32[]{:S(2)}, u32[]{:S(2)}) collective-permute-start(f32[2,128,128]{2,1,0:T(8,128)S(1)} %collective-permute-done.19.refs_1_), channel_id=1, source_target_pairs={{0,1},{1,0},{2,3},{3,2},{4,5},{5,4},{6,7},{7,6},{8,9},{9,8},{10,11... | collective-permute-start | bytes 393224 | tf_op jit(solution)/shard_map/gather_t/ppermute | solution.py:208
  82.8 23.8 %all-to-all-start.1 = ((f32[8,2,128,128]{3,2,1,0:T(8,128)}), f32[8,2,128,128]{3,2,1,0:T(8,128)S(1)}, u32[]{:S(2)}, u32[]{:S(2)}) async-start(f32[8,2,128,128]{3,2,1,0:T(8,128)} %copy-done.7), calls=%async_computation.1 | async-start | bytes 2097152 | tf_op jit(solution)/shard_map/gather_t/all_to_all | solution.py:256
  90.4 7.2 %collective-permute-start.25 = (f32[2,128,128]{2,1,0:T(8,128)S(1)}, f32[2,128,128]{2,1,0:T(8,128)S(1)}, u32[]{:S(2)}, u32[]{:S(2)}) collective-permute-start(f32[2,128,128]{2,1,0:T(8,128)S(1)} %collective-permute-done.21.refs_6_), channel_id=1, source_target_pairs={{0,2},{1,3},{2,4},{3,5},{4,6},{5,7},{6,8},{7,9},{8,10},{9,11},{10,... | collective-permute-start | bytes 393224 | tf_op jit(solution)/shard_map/gather_t/ppermute | solution.py:227
  92.2 6.1 %collective-permute-start.27 = (f32[2,128,128]{2,1,0:T(8,128)S(1)}, f32[2,128,128]{2,1,0:T(8,128)}, u32[]{:S(2)}, u32[]{:S(2)}) collective-permute-start(f32[2,128,128]{2,1,0:T(8,128)S(1)} %collective-permute-done.21.refs_6_), channel_id=1, source_target_pairs={{0,1},{1,0},{2,3},{3,2},{4,5},{5,4},{6,7},{7,6},{8,9},{9,8},{10,11... | collective-permute-start | bytes 393224 | tf_op jit(solution)/shard_map/gather_t/ppermute | solution.py:208
  92.2 6.1 %collective-permute-start.26 = (f32[2,128,128]{2,1,0:T(8,128)}, f32[2,128,128]{2,1,0:T(8,128)S(1)}, u32[]{:S(2)}, u32[]{:S(2)}) collective-permute-start(f32[2,128,128]{2,1,0:T(8,128)} %collective-permute-done.22.refs_2_), channel_id=1, source_target_pairs={{0,14},{1,15},{2,0},{3,1},{4,2},{5,3},{6,4},{7,5},{8,6},{9,7},{10,... | collective-permute-start | bytes 393224 | tf_op jit(solution)/shard_map/gather_t/ppermute | solution.py:228
  92.4 6.0 %collective-permute-start.28 = (f32[2,128,128]{2,1,0:T(8,128)}, f32[2,128,128]{2,1,0:T(8,128)}, u32[]{:S(2)}, u32[]{:S(2)}) collective-permute-start(f32[2,128,128]{2,1,0:T(8,128)} %collective-permute-done.22.refs_2_), channel_id=1, source_target_pairs={{0,1},{1,0},{2,3},{3,2},{4,5},{5,4},{6,7},{7,6},{8,9},{9,8},{10,11... | collective-permute-start | bytes 393224 | tf_op jit(solution)/shard_map/gather_t/ppermute | solution.py:208
  98.3 7.5 %collective-permute-start.31 = (f32[2,128,128]{2,1,0:T(8,128)S(1)}, f32[2,128,128]{2,1,0:T(8,128)S(1)}, u32[]{:S(2)}, u32[]{:S(2)}) collective-permute-start(f32[2,128,128]{2,1,0:T(8,128)S(1)} %collective-permute-done.25.refs_5_), channel_id=1, source_target_pairs={{0,1},{1,0},{2,3},{3,2},{4,5},{5,4},{6,7},{7,6},{8,9},{9,8},{10,11... | collective-permute-start | bytes 393224 | tf_op jit(solution)/shard_map/gather_t/ppermute | solution.py:208
  98.4 7.5 %collective-permute-start.32 = (f32[2,128,128]{2,1,0:T(8,128)S(1)}, f32[2,128,128]{2,1,0:T(8,128)S(1)}, u32[]{:S(2)}, u32[]{:S(2)}) collective-permute-start(f32[2,128,128]{2,1,0:T(8,128)S(1)} %collective-permute-done.26.refs_3_), channel_id=1, source_target_pairs={{0,1},{1,0},{2,3},{3,2},{4,5},{5,4},{6,7},{7,6},{8,9},{9,8},{10,11... | collective-permute-start | bytes 393224 | tf_op jit(solution)/shard_map/gather_t/ppermute | solution.py:208
  98.9 7.0 %collective-permute-start.29 = (f32[2,64,128]{2,1,0:T(8,128)S(1)}, f32[2,64,128]{2,1,0:T(8,128)S(1)}, u32[]{:S(2)}, u32[]{:S(2)}) collective-permute-start(f32[2,64,128]{2,1,0:T(8,128)S(1)} %slice.31), channel_id=1, source_target_pairs={{0,2},{1,3},{2,4},{3,5},{4,6},{5,7},{6,8},{7,9},{8,10},{9,11},{10,... | collective-permute-start | bytes 196616 | tf_op jit(solution)/shard_map/gather_t/ppermute | solution.py:227
  110.3 6.3 %collective-permute-start.34 = (f32[192,128]{1,0:T(8,128)S(1)}, f32[192,128]{1,0:T(8,128)S(1)}, u32[]{:S(2)}, u32[]{:S(2)}) collective-permute-start(f32[192,128]{1,0:T(8,128)S(1)} %pad_maximum_fusion.1), channel_id=1, source_target_pairs={{0,16},{16,0},{32,48},{48,32},{64,80},{80,64},{96,112},{112,96},{1... | collective-permute-start | bytes 294920 | tf_op jit(solution)/shard_map/swap_yq/ppermute | solution.py:313
  (47 other events, 279.9 us)
Sparse Core Ops, SparseCore 0:
  35.0 51.4 all-gather.2

commit v9 on v8

--- a/solution.py
+++ b/solution.py
@@ -226,7 +226,10 @@
             up, down = up[:, :half], down[:, half:]
         up = lax.ppermute(up, "col", LAYER_UP)
         down = lax.ppermute(down, "col", LAYER_DOWN)
-        up, down, swapped, more = lax.optimization_barrier((up, down, swapped, ties.get(step)))
+        more = ties.get(step)
+        if callable(more):
+            more = more(tied[-1])
+        up, down, swapped, more = lax.optimization_barrier((up, down, swapped, more))
         tied.append(more)
         if step == begin[3]:
             up, down, beside = lax.optimization_barrier((up, down, beside))
@@ -271,12 +274,13 @@
     with jax.named_scope("swap_rest"):
         l32_pair, away = lax.optimization_barrier((l32_pair, away))
         away = lax.ppermute(away, "row", ROW_SWAP)
+    def pack(away):
+        return call(pack_kernel, [(3, 2, *square), (2, *square)], place, home, away)
+
     with jax.named_scope("gather_l"):
-        l_mine, l_other, cols, away = gather_layers(
-            l32_pair, (1, (send, away), lambda x: to_rows(x[0]), 4), {2: away}
-        )
-    with jax.named_scope("pack"):
-        packed, l3 = call(pack_kernel, [(3, 2, *square), (2, *square)], place, home, away)
+        l_mine, l_other, cols, _, (packed, l3) = gather_layers(
+            l32_pair, (2, (send, away), lambda x: to_rows(x[0]), 4), {1: away, 2: pack}
+        )
     with jax.named_scope("gather_rows"):
         panels = lax.all_gather(packed, "col", axis=0)
         panels = [panels[:, i] for i in range(3)]

time: 169 us -> 171 us (1.012)
  waiting for transfers between devices: 39.8 us -> 42.1 us
  starting transfers between devices: 38.7 us -> 36.8 us
    ppermute x8, starting transfers between devices: 15 us -> 3.02 us  [gather_layers(): up = lax.ppermute(up, 'col', LAYER_UP)]
    ppermute x8, starting transfers between devices: 3.76 us -> 15.5 us  [gather_layers(): down = lax.ppermute(down, 'col', LAYER_DOWN)]
    ppermute x8, waiting for transfers between devices: 10.3 us -> 17.3 us  [gather_layers(): down = lax.ppermute(down, 'col', LAYER_DOWN)]
    ppermute x2, waiting for transfers between devices: 3.29 us -> 0.01 us  [body(): away = lax.ppermute(away, 'row', ROW_SWAP)]
    ppermute x8, waiting for transfers between devices: 16.6 us -> 14.4 us  [gather_layers(): up = lax.ppermute(up, 'col', LAYER_UP)]
    unnamed x69 -> x73, local copies, waits for them, and re-layouts: 11.9 us -> 12.5 us
  transfers between devices with their start and end apart: 38 -> 38, of which waited for: 16 -> 15; matrix products, arithmetic and copies ran while one was open for 4% -> 4% of each run, Pallas kernels for 4% -> 5%
where the time goes in v9:
time: 171 us; the launch traced here: 168 us
  waiting for transfers between devices  42.1 us (25%)
  blocking collectives  41.7 us (24%)
  starting transfers between devices  36.8 us (22%)
  local copies, waits for them, and re-layouts  19.1 us (11%)
  Pallas kernels  13.8 us (8%)
  between operations  13.8 us (8%)
    all_to_all x1, blocking collectives, body(): got = lax.all_to_all(sums, 'row', 0, 0, tiled=True)  41.7 us
    ppermute x8, waiting for transfers between devices, gather_layers(): down = lax.ppermute(down, 'col', LAYER_DOWN)  17.3 us
    ppermute x8, starting transfers between devices, gather_layers(): down = lax.ppermute(down, 'col', LAYER_DOWN)  15.5 us
    ppermute x8, waiting for transfers between devices, gather_layers(): up = lax.ppermute(up, 'col', LAYER_UP)  14.4 us
    pallas_call x7, Pallas kernels, call(): pl.pallas_call(kernel, out_shape=[jax.ShapeDtypeStruct(s, F32) for s in s...  13.8 us
    unnamed x73, local copies, waits for them, and re-layouts  12.5 us
    all_to_all x1, starting transfers between devices, to_rows(): return lax.all_to_all(x, 'row', 0, 0, tiled=True)  6.75 us
    all_to_all x1, starting transfers between devices, to_side(): lax.all_to_all(x, 'row', 0, 0, tiled=True, axis_index_groups=SAME_SIDE)  5.33 us
  transfers between devices with their start and end apart: 38, of which 15 were waited for; matrix products, arithmetic and copies ran while one was open for 4% of the time, Pallas kernels for 5%

profile of v9, /device:TPU:32, one launch (start us, length us, event | category | flops | bytes accessed | tf_op | source)
XLA Modules:
  0.0 168.1 jit_solution(11455911017726310571)
XLA Ops:
  8.8 2.0 %prepare.1 = (f32[128,128]{1,0:T(8,128)S(1)}, f32[4,128,128]{2,1,0:T(8,128)S(1)}, f32[4,128,128]{2,1,0:T(8,128)S(1)}, f32[16,192,128]{2,1,0:T(8,128)}) custom-call(s32[4,4]{1,0:T(4,128)S(1)} %bitcast.24, s32[2]{0:T(128)S(1)} %pad_add_fusion.place_ref, f32[2048,128]{1,0:T(8,128)S(1)} %bitcast.22), custom_call_target="tpu_custom_call" | custom-call | tf_op jit(solution)/shard_map/prepare/pallas_call | solution.py:51
  12.3 2.7 %collective-permute-done = f32[128,128]{1,0:T(8,128)S(1)} collective-permute-done((f32[128,128]{1,0:T(8,128)S(1)}, f32[128,128]{1,0:T(8,128)S(1)}, u32[]{:S(2)}, u32[]{:S(2)}) %collective-permute-start) | collective-permute-done | bytes 65568 | tf_op jit(solution)/shard_map/swap_l32/ppermute | solution.py:271
  15.1 1.7 collective-permute-start.4
  18.8 4.1 %collective-permute-done.2.refs_1_ = f32[2,128,128]{2,1,0:T(8,128)S(1)} collective-permute-done((f32[2,128,128]{2,1,0:T(8,128)S(1)}, f32[2,128,128]{2,1,0:T(8,128)S(1)}, u32[]{:S(2)}, u32[]{:S(2)}) %collective-permute-start.2) | collective-permute-done | bytes 131104 | tf_op jit(solution)/shard_map/gather_l/ppermute | solution.py:228
  22.8 3.8 %collective-permute-done.1.refs_7_ = f32[2,128,128]{2,1,0:T(8,128)S(1)} collective-permute-done((f32[2,128,128]{2,1,0:T(8,128)S(1)}, f32[2,128,128]{2,1,0:T(8,128)S(1)}, u32[]{:S(2)}, u32[]{:S(2)}) %collective-permute-start.1) | collective-permute-done | bytes 131104 | tf_op jit(solution)/shard_map/gather_l/ppermute | solution.py:227
  27.1 3.0 %collective-permute-start.6 = (f32[2,128,128]{2,1,0:T(8,128)S(1)}, f32[2,128,128]{2,1,0:T(8,128)S(1)}, u32[]{:S(2)}, u32[]{:S(2)}) collective-permute-start(f32[2,128,128]{2,1,0:T(8,128)S(1)} %collective-permute-done.2.refs_1_), channel_id=1, source_target_pairs={{0,14},{1,15},{2,0},{3,1},{4,2},{5,3},{6,4},{7,5},{8,6},{9,7},{10,... | collective-permute-start | bytes 393224 | tf_op jit(solution)/shard_map/gather_l/ppermute | solution.py:228
  33.0 2.2 %collective-permute-done.5.refs_6_ = f32[2,128,128]{2,1,0:T(8,128)S(1)} collective-permute-done((f32[2,128,128]{2,1,0:T(8,128)S(1)}, f32[2,128,128]{2,1,0:T(8,128)S(1)}, u32[]{:S(2)}, u32[]{:S(2)}) %collective-permute-start.5) | collective-permute-done | bytes 131104 | tf_op jit(solution)/shard_map/gather_l/ppermute | solution.py:227
  35.2 6.8 %all-to-all-start = ((f32[16,192,128]{2,1,0:T(8,128)}), f32[16,192,128]{2,1,0:T(8,128)S(1)}, u32[]{:S(2)}, u32[]{:S(2)}) async-start(f32[16,192,128]{2,1,0:T(8,128)} %get-tuple-element.94), calls=%async_computation | async-start | bytes 3145728 | tf_op jit(solution)/shard_map/gather_l/all_to_all | solution.py:256
  42.1 1.7 collective-permute-start.10
  44.3 5.6 %collective-permute-done.10.refs_3_ = f32[2,128,128]{2,1,0:T(8,128)S(1)} collective-permute-done((f32[2,128,128]{2,1,0:T(8,128)S(1)}, f32[2,128,128]{2,1,0:T(8,128)S(1)}, u32[]{:S(2)}, u32[]{:S(2)}) %collective-permute-start.10) | collective-permute-done | bytes 131104 | tf_op jit(solution)/shard_map/gather_l/ppermute | solution.py:228
  49.9 2.2 %collective-permute-done.9.refs_5_ = f32[2,128,128]{2,1,0:T(8,128)S(1)} collective-permute-done((f32[2,128,128]{2,1,0:T(8,128)S(1)}, f32[2,128,128]{2,1,0:T(8,128)S(1)}, u32[]{:S(2)}, u32[]{:S(2)}) %collective-permute-start.9) | collective-permute-done | bytes 131104 | tf_op jit(solution)/shard_map/gather_l/ppermute | solution.py:227
  54.7 3.6 %collective-permute-done.13 = f32[2,64,128]{2,1,0:T(8,128)S(1)} collective-permute-done((f32[2,64,128]{2,1,0:T(8,128)S(1)}, f32[2,64,128]{2,1,0:T(8,128)S(1)}, u32[]{:S(2)}, u32[]{:S(2)}) %collective-permute-start.13) | collective-permute-done | bytes 65568 | tf_op jit(solution)/shard_map/gather_l/ppermute | solution.py:227
  59.7 4.9 %all-to-all-done.refs_16_.cols_ref = f32[16,192,128]{2,1,0:T(8,128)S(1)} async-done(((f32[16,192,128]{2,1,0:T(8,128)}), f32[16,192,128]{2,1,0:T(8,128)S(1)}, u32[]{:S(2)}, u32[]{:S(2)}) %all-to-all-start) | async-done | bytes 1572896 | tf_op jit(solution)/shard_map/gather_l/all_to_all | solution.py:256
  70.9 1.8 %collective-permute-start.19 = (f32[2,128,128]{2,1,0:T(8,128)S(1)}, f32[2,128,128]{2,1,0:T(8,128)S(1)}, u32[]{:S(2)}, u32[]{:S(2)}) collective-permute-start(f32[2,128,128]{2,1,0:T(8,128)S(1)} %get-tuple-element.108.refs_0_), channel_id=1, source_target_pairs={{0,14},{1,15},{2,0},{3,1},{4,2},{5,3},{6,4},{7,5},{8,6},{9,7},{10,... | collective-permute-start | bytes 393224 | tf_op jit(solution)/shard_map/gather_t/ppermute | solution.py:228
  74.3 5.3 %collective-permute-done.19.refs_1_ = f32[2,128,128]{2,1,0:T(8,128)S(1)} collective-permute-done((f32[2,128,128]{2,1,0:T(8,128)S(1)}, f32[2,128,128]{2,1,0:T(8,128)S(1)}, u32[]{:S(2)}, u32[]{:S(2)}) %collective-permute-start.19) | collective-permute-done | bytes 131104 | tf_op jit(solution)/shard_map/gather_t/ppermute | solution.py:228
  81.2 2.1 %collective-permute-start.22 = (f32[2,128,128]{2,1,0:T(8,128)S(1)}, f32[2,128,128]{2,1,0:T(8,128)S(1)}, u32[]{:S(2)}, u32[]{:S(2)}) collective-permute-start(f32[2,128,128]{2,1,0:T(8,128)S(1)} %collective-permute-done.19.refs_1_), channel_id=1, source_target_pairs={{0,14},{1,15},{2,0},{3,1},{4,2},{5,3},{6,4},{7,5},{8,6},{9,7},{10,... | collective-permute-start | bytes 393224 | tf_op jit(solution)/shard_map/gather_t/ppermute | solution.py:228
  83.6 5.3 %all-to-all-start.1 = ((f32[8,2,128,128]{3,2,1,0:T(8,128)}), f32[8,2,128,128]{3,2,1,0:T(8,128)S(1)}, u32[]{:S(2)}, u32[]{:S(2)}) async-start(f32[8,2,128,128]{3,2,1,0:T(8,128)} %copy-done.7), calls=%async_computation.1 | async-start | bytes 2097152 | tf_op jit(solution)/shard_map/gather_t/all_to_all | solution.py:259
  90.3 2.0 %collective-permute-start.26 = (f32[2,128,128]{2,1,0:T(8,128)S(1)}, f32[2,128,128]{2,1,0:T(8,128)S(1)}, u32[]{:S(2)}, u32[]{:S(2)}) collective-permute-start(f32[2,128,128]{2,1,0:T(8,128)S(1)} %collective-permute-done.22.refs_2_), channel_id=1, source_target_pairs={{0,14},{1,15},{2,0},{3,1},{4,2},{5,3},{6,4},{7,5},{8,6},{9,7},{10,... | collective-permute-start | bytes 393224 | tf_op jit(solution)/shard_map/gather_t/ppermute | solution.py:228
  92.5 4.8 %slice_bitcast_fusion = (f32[16,2,128,128]{3,2,1,0:T(8,128)S(1)}, f32[16,2,128,128]{3,2,1,0:T(8,128)}, f32[16,2,128,128]{3,2,1,0:T(8,128)S(1)}) fusion(f32[16,3,2,128,128]{4,3,2,1,0:T(8,128)} %bitcast.26), kind=kLoop, calls=%fused_computation | loop fusion | bytes 12582912 | tf_op jit(solution)/shard_map/gather_rows/squeeze | solution.py:286
  99.3 2.7 %collective-permute-start.30 = (f32[2,64,128]{2,1,0:T(8,128)S(1)}, f32[2,64,128]{2,1,0:T(8,128)S(1)}, u32[]{:S(2)}, u32[]{:S(2)}) collective-permute-start(f32[2,64,128]{2,1,0:T(8,128)S(1)} %slice.32), channel_id=1, source_target_pairs={{0,14},{1,15},{2,0},{3,1},{4,2},{5,3},{6,4},{7,5},{8,6},{9,7},{10,... | collective-permute-start | bytes 196616 | tf_op jit(solution)/shard_map/gather_t/ppermute | solution.py:228
  102.0 2.4 %term_uq.1 = (f32[2,128,128]{2,1,0:T(8,128)S(1)}, f32[64,256]{1,0:T(8,128)S(1)}, f32[64,128]{1,0:T(8,128)S(1)}, f32[64,128]{1,0:T(8,128)S(1)}) custom-call(s32[2]{0:T(128)S(1)} %pad_add_fusion.place_ref, f32[16,2,128,128]{3,2,1,0:T(8,128)S(1)} %get-tuple-element.132.root_ref, f32[16,2,128,128]{3,2,1,0:T(8,128)S(1)} %get-tuple-element.145.diag_ref, ...), custom_call_target="tpu_custom_call" | custom-call | tf_op jit(solution)/shard_map/term_uq/pallas_call | solution.py:51
  114.5 3.2 %sums.1 = f32[16,320,128]{2,1,0:T(8,128)S(1)} custom-call(s32[2]{0:T(128)S(1)} %pad_add_fusion.place_ref, f32[2,128,128]{2,1,0:T(8,128)S(1)} %copy-done.9, f32[2,128,128]{2,1,0:T(8,128)S(1)} %copy-done.13, f32[2,128,128]{2,1,0:T(8,128)S(1)} %copy-done.19, f32[2,128,128]{2,1,0:T(8,128)S(1)} %collective-permute-done.26.refs_3_, ...), custom_call_target="tpu_custom_call" | custom-call | tf_op jit(solution)/shard_map/sums/pallas_call | solution.py:51
  117.8 41.7 %all_to_all.15.got_ref = f32[16,320,128]{2,1,0:T(8,128)S(1)} all-to-all(f32[16,320,128]{2,1,0:T(8,128)S(1)} %sums.1), channel_id=1, replica_groups=mesh['row'=16,'col'=16] {'row'}, dimensions={0} | all-to-all | bytes 5242880 | tf_op jit(solution)/shard_map/scatter_sums/all_to_all | solution.py:334
  159.5 1.8 %finish.1 = f32[2048,128]{1,0:T(8,128)} custom-call(s32[4,4]{1,0:T(4,128)S(1)} %bitcast.25, s32[2]{0:T(128)S(1)} %pad_add_fusion.place_ref, f32[2048,128]{1,0:T(8,128)S(1)} %bitcast.23, f32[16,320,128]{2,1,0:T(8,128)S(1)} %all_to_all.15.got_ref, f32[128,128]{1,0:T(8,128)S(1)} %get-tuple-element.141.home_ref, f32[128,128]{1,0:T(8,128)S(1)} %slice.39.away_ref, ...), custom_call_target="tpu_custom_call" | custom-call | tf_op jit(solution)/shard_map/finish/pallas_call | solution.py:51
  (149 shorter events, 37.2 us)
Async XLA Ops:
  6.5 86.0 %all-gather.3.cloned.1.call-start = ((), (), s32[]{:S(2)}) async-start(), calls=%async_computation.3 | async-start | bytes 6684672 | tf_op jit(solution)/shard_map/gather_rows/all_gather | solution.py:285
  15.1 11.5 %collective-permute-start.4 = (f32[4,128,128]{2,1,0:T(8,128)S(1)}, f32[4,128,128]{2,1,0:T(8,128)S(1)}, u32[]{:S(2)}, u32[]{:S(2)}) collective-permute-start(f32[4,128,128]{2,1,0:T(8,128)S(1)} %get-tuple-element.78), channel_id=1, source_target_pairs={{0,16},{16,0},{32,48},{48,32},{64,80},{80,64},{96,112},{112,96},{1... | collective-permute-start | bytes 786440 | tf_op jit(solution)/shard_map/swap_rest/ppermute | solution.py:276
  16.7 6.1 %collective-permute-start.2 = (f32[2,128,128]{2,1,0:T(8,128)S(1)}, f32[2,128,128]{2,1,0:T(8,128)S(1)}, u32[]{:S(2)}, u32[]{:S(2)}) collective-permute-start(f32[2,128,128]{2,1,0:T(8,128)S(1)} %pad_maximum_fusion.refs_0_), channel_id=1, source_target_pairs={{0,14},{1,15},{2,0},{3,1},{4,2},{5,3},{6,4},{7,5},{8,6},{9,7},{10,... | collective-permute-start | bytes 393224 | tf_op jit(solution)/shard_map/gather_l/ppermute | solution.py:228
  17.7 8.9 %collective-permute-start.1 = (f32[2,128,128]{2,1,0:T(8,128)S(1)}, f32[2,128,128]{2,1,0:T(8,128)S(1)}, u32[]{:S(2)}, u32[]{:S(2)}) collective-permute-start(f32[2,128,128]{2,1,0:T(8,128)S(1)} %pad_maximum_fusion.refs_0_), channel_id=1, source_target_pairs={{0,2},{1,3},{2,4},{3,5},{4,6},{5,7},{6,8},{7,9},{8,10},{9,11},{10,... | collective-permute-start | bytes 393224 | tf_op jit(solution)/shard_map/gather_l/ppermute | solution.py:227
  35.2 29.5 %all-to-all-start = ((f32[16,192,128]{2,1,0:T(8,128)}), f32[16,192,128]{2,1,0:T(8,128)S(1)}, u32[]{:S(2)}, u32[]{:S(2)}) async-start(f32[16,192,128]{2,1,0:T(8,128)} %get-tuple-element.94), calls=%async_computation | async-start | bytes 3145728 | tf_op jit(solution)/shard_map/gather_l/all_to_all | solution.py:256
  42.1 7.8 %collective-permute-start.10 = (f32[2,128,128]{2,1,0:T(8,128)S(1)}, f32[2,128,128]{2,1,0:T(8,128)S(1)}, u32[]{:S(2)}, u32[]{:S(2)}) collective-permute-start(f32[2,128,128]{2,1,0:T(8,128)S(1)} %collective-permute-done.6.refs_2_), channel_id=1, source_target_pairs={{0,14},{1,15},{2,0},{3,1},{4,2},{5,3},{6,4},{7,5},{8,6},{9,7},{10,... | collective-permute-start | bytes 393224 | tf_op jit(solution)/shard_map/gather_l/ppermute | solution.py:228
  43.7 6.2 %collective-permute-start.11 = (f32[2,128,128]{2,1,0:T(8,128)S(1)}, f32[2,128,128]{2,1,0:T(8,128)S(1)}, u32[]{:S(2)}, u32[]{:S(2)}) collective-permute-start(f32[2,128,128]{2,1,0:T(8,128)S(1)} %collective-permute-done.5.refs_6_), channel_id=1, source_target_pairs={{0,1},{1,0},{2,3},{3,2},{4,5},{5,4},{6,7},{7,6},{8,9},{9,8},{10,11... | collective-permute-start | bytes 393224 | tf_op jit(solution)/shard_map/gather_l/ppermute | solution.py:208
  43.9 8.2 %collective-permute-start.9 = (f32[2,128,128]{2,1,0:T(8,128)S(1)}, f32[2,128,128]{2,1,0:T(8,128)S(1)}, u32[]{:S(2)}, u32[]{:S(2)}) collective-permute-start(f32[2,128,128]{2,1,0:T(8,128)S(1)} %collective-permute-done.5.refs_6_), channel_id=1, source_target_pairs={{0,2},{1,3},{2,4},{3,5},{4,6},{5,7},{6,8},{7,9},{8,10},{9,11},{10,... | collective-permute-start | bytes 393224 | tf_op jit(solution)/shard_map/gather_l/ppermute | solution.py:227
  52.1 7.0 %collective-permute-start.16 = (f32[2,128,128]{2,1,0:T(8,128)S(1)}, f32[2,128,128]{2,1,0:T(8,128)S(1)}, u32[]{:S(2)}, u32[]{:S(2)}) collective-permute-start(f32[2,128,128]{2,1,0:T(8,128)S(1)} %collective-permute-done.10.refs_3_), channel_id=1, source_target_pairs={{0,1},{1,0},{2,3},{3,2},{4,5},{5,4},{6,7},{7,6},{8,9},{9,8},{10,11... | collective-permute-start | bytes 393224 | tf_op jit(solution)/shard_map/gather_l/ppermute | solution.py:208
  52.1 7.6 %collective-permute-start.15 = (f32[2,128,128]{2,1,0:T(8,128)S(1)}, f32[2,128,128]{2,1,0:T(8,128)S(1)}, u32[]{:S(2)}, u32[]{:S(2)}) collective-permute-start(f32[2,128,128]{2,1,0:T(8,128)S(1)} %collective-permute-done.9.refs_5_), channel_id=1, source_target_pairs={{0,1},{1,0},{2,3},{3,2},{4,5},{5,4},{6,7},{7,6},{8,9},{9,8},{10,11... | collective-permute-start | bytes 393224 | tf_op jit(solution)/shard_map/gather_l/ppermute | solution.py:208
  70.9 8.7 %collective-permute-start.19 = (f32[2,128,128]{2,1,0:T(8,128)S(1)}, f32[2,128,128]{2,1,0:T(8,128)S(1)}, u32[]{:S(2)}, u32[]{:S(2)}) collective-permute-start(f32[2,128,128]{2,1,0:T(8,128)S(1)} %get-tuple-element.108.refs_0_), channel_id=1, source_target_pairs={{0,14},{1,15},{2,0},{3,1},{4,2},{5,3},{6,4},{7,5},{8,6},{9,7},{10,... | collective-permute-start | bytes 393224 | tf_op jit(solution)/shard_map/gather_t/ppermute | solution.py:228
  72.7 8.5 %collective-permute-start.18 = (f32[2,128,128]{2,1,0:T(8,128)S(1)}, f32[2,128,128]{2,1,0:T(8,128)S(1)}, u32[]{:S(2)}, u32[]{:S(2)}) collective-permute-start(f32[2,128,128]{2,1,0:T(8,128)S(1)} %get-tuple-element.108.refs_0_), channel_id=1, source_target_pairs={{0,2},{1,3},{2,4},{3,5},{4,6},{5,7},{6,8},{7,9},{8,10},{9,11},{10,... | collective-permute-start | bytes 393224 | tf_op jit(solution)/shard_map/gather_t/ppermute | solution.py:227
  81.2 7.7 %collective-permute-start.24 = (f32[2,128,128]{2,1,0:T(8,128)S(1)}, f32[2,128,128]{2,1,0:T(8,128)S(1)}, u32[]{:S(2)}, u32[]{:S(2)}) collective-permute-start(f32[2,128,128]{2,1,0:T(8,128)S(1)} %collective-permute-done.19.refs_1_), channel_id=1, source_target_pairs={{0,1},{1,0},{2,3},{3,2},{4,5},{5,4},{6,7},{7,6},{8,9},{9,8},{10,11... | collective-permute-start | bytes 393224 | tf_op jit(solution)/shard_map/gather_t/ppermute | solution.py:208
  81.2 8.4 %collective-permute-start.22 = (f32[2,128,128]{2,1,0:T(8,128)S(1)}, f32[2,128,128]{2,1,0:T(8,128)S(1)}, u32[]{:S(2)}, u32[]{:S(2)}) collective-permute-start(f32[2,128,128]{2,1,0:T(8,128)S(1)} %collective-permute-done.19.refs_1_), channel_id=1, source_target_pairs={{0,14},{1,15},{2,0},{3,1},{4,2},{5,3},{6,4},{7,5},{8,6},{9,7},{10,... | collective-permute-start | bytes 393224 | tf_op jit(solution)/shard_map/gather_t/ppermute | solution.py:228
  83.4 6.2 %collective-permute-start.23 = (f32[2,128,128]{2,1,0:T(8,128)S(1)}, f32[2,128,128]{2,1,0:T(8,128)S(1)}, u32[]{:S(2)}, u32[]{:S(2)}) collective-permute-start(f32[2,128,128]{2,1,0:T(8,128)S(1)} %collective-permute-done.18.refs_7_), channel_id=1, source_target_pairs={{0,1},{1,0},{2,3},{3,2},{4,5},{5,4},{6,7},{7,6},{8,9},{9,8},{10,11... | collective-permute-start | bytes 393224 | tf_op jit(solution)/shard_map/gather_t/ppermute | solution.py:208
  83.6 6.7 %collective-permute-start.21 = (f32[2,128,128]{2,1,0:T(8,128)S(1)}, f32[2,128,128]{2,1,0:T(8,128)}, u32[]{:S(2)}, u32[]{:S(2)}) collective-permute-start(f32[2,128,128]{2,1,0:T(8,128)S(1)} %collective-permute-done.18.refs_7_), channel_id=1, source_target_pairs={{0,2},{1,3},{2,4},{3,5},{4,6},{5,7},{6,8},{7,9},{8,10},{9,11},{10,... | collective-permute-start | bytes 393224 | tf_op jit(solution)/shard_map/gather_t/ppermute | solution.py:227
  83.6 24.0 %all-to-all-start.1 = ((f32[8,2,128,128]{3,2,1,0:T(8,128)}), f32[8,2,128,128]{3,2,1,0:T(8,128)S(1)}, u32[]{:S(2)}, u32[]{:S(2)}) async-start(f32[8,2,128,128]{3,2,1,0:T(8,128)} %copy-done.7), calls=%async_computation.1 | async-start | bytes 2097152 | tf_op jit(solution)/shard_map/gather_t/all_to_all | solution.py:259
  90.3 7.1 %collective-permute-start.28 = (f32[2,128,128]{2,1,0:T(8,128)S(1)}, f32[2,128,128]{2,1,0:T(8,128)}, u32[]{:S(2)}, u32[]{:S(2)}) collective-permute-start(f32[2,128,128]{2,1,0:T(8,128)S(1)} %collective-permute-done.22.refs_2_), channel_id=1, source_target_pairs={{0,1},{1,0},{2,3},{3,2},{4,5},{5,4},{6,7},{7,6},{8,9},{9,8},{10,11... | collective-permute-start | bytes 393224 | tf_op jit(solution)/shard_map/gather_t/ppermute | solution.py:208
  90.3 7.1 %collective-permute-start.26 = (f32[2,128,128]{2,1,0:T(8,128)S(1)}, f32[2,128,128]{2,1,0:T(8,128)S(1)}, u32[]{:S(2)}, u32[]{:S(2)}) collective-permute-start(f32[2,128,128]{2,1,0:T(8,128)S(1)} %collective-permute-done.22.refs_2_), channel_id=1, source_target_pairs={{0,14},{1,15},{2,0},{3,1},{4,2},{5,3},{6,4},{7,5},{8,6},{9,7},{10,... | collective-permute-start | bytes 393224 | tf_op jit(solution)/shard_map/gather_t/ppermute | solution.py:228
  98.4 8.5 %collective-permute-start.32 = (f32[2,128,128]{2,1,0:T(8,128)S(1)}, f32[2,128,128]{2,1,0:T(8,128)S(1)}, u32[]{:S(2)}, u32[]{:S(2)}) collective-permute-start(f32[2,128,128]{2,1,0:T(8,128)S(1)} %collective-permute-done.26.refs_3_), channel_id=1, source_target_pairs={{0,1},{1,0},{2,3},{3,2},{4,5},{5,4},{6,7},{7,6},{8,9},{9,8},{10,11... | collective-permute-start | bytes 393224 | tf_op jit(solution)/shard_map/gather_t/ppermute | solution.py:208
  98.4 8.5 %collective-permute-start.31 = (f32[2,128,128]{2,1,0:T(8,128)S(1)}, f32[2,128,128]{2,1,0:T(8,128)S(1)}, u32[]{:S(2)}, u32[]{:S(2)}) collective-permute-start(f32[2,128,128]{2,1,0:T(8,128)S(1)} %collective-permute-done.25.refs_5_), channel_id=1, source_target_pairs={{0,1},{1,0},{2,3},{3,2},{4,5},{5,4},{6,7},{7,6},{8,9},{9,8},{10,11... | collective-permute-start | bytes 393224 | tf_op jit(solution)/shard_map/gather_t/ppermute | solution.py:208
  98.9 8.0 %collective-permute-start.29 = (f32[2,64,128]{2,1,0:T(8,128)S(1)}, f32[2,64,128]{2,1,0:T(8,128)S(1)}, u32[]{:S(2)}, u32[]{:S(2)}) collective-permute-start(f32[2,64,128]{2,1,0:T(8,128)S(1)} %slice.31), channel_id=1, source_target_pairs={{0,2},{1,3},{2,4},{3,5},{4,6},{5,7},{6,8},{7,9},{8,10},{9,11},{10,... | collective-permute-start | bytes 196616 | tf_op jit(solution)/shard_map/gather_t/ppermute | solution.py:227
  99.3 7.6 %collective-permute-start.30 = (f32[2,64,128]{2,1,0:T(8,128)S(1)}, f32[2,64,128]{2,1,0:T(8,128)S(1)}, u32[]{:S(2)}, u32[]{:S(2)}) collective-permute-start(f32[2,64,128]{2,1,0:T(8,128)S(1)} %slice.32), channel_id=1, source_target_pairs={{0,14},{1,15},{2,0},{3,1},{4,2},{5,3},{6,4},{7,5},{8,6},{9,7},{10,... | collective-permute-start | bytes 196616 | tf_op jit(solution)/shard_map/gather_t/ppermute | solution.py:228
  111.4 6.3 %collective-permute-start.34 = (f32[192,128]{1,0:T(8,128)S(1)}, f32[192,128]{1,0:T(8,128)S(1)}, u32[]{:S(2)}, u32[]{:S(2)}) collective-permute-start(f32[192,128]{1,0:T(8,128)S(1)} %pad_maximum_fusion.1), channel_id=1, source_target_pairs={{0,16},{16,0},{32,48},{48,32},{64,80},{80,64},{96,112},{112,96},{1... | collective-permute-start | bytes 294920 | tf_op jit(solution)/shard_map/swap_yq/ppermute | solution.py:317
  (49 other events, 274.9 us)
Sparse Core Ops, SparseCore 0:
  35.3 49.3 all-gather.2

commit v10 on v9

--- a/solution.py
+++ b/solution.py
@@ -7,6 +7,7 @@
 
 N = 16
 LAYERS = 8
+TILES = LAYERS + 1
 TB = 128
 HALF = 64
 F32 = jnp.float32
@@ -96,13 +97,25 @@
     return k + core, k + 1 - core
 
 
+def tiles_at(refs, d):
+    last = LAYERS // 2
+    if d == last:
+        return refs[last][0], refs[last + 1][0]
+    ref = refs[d + (d > last)]
+    return ref[0], ref[1]
+
+
+def both_cores(mine, other, d):
+    return [lanes(*pair) for pair in zip(tiles_at(mine, d), tiles_at(other, d))]
+
+
 def t_kernel(place_ref, *refs):
-    mine, other = refs[:LAYERS], refs[LAYERS : 2 * LAYERS]
-    l2_ref, l3_ref, t_ref, send_ref, all_ref = refs[2 * LAYERS :]
+    mine, other = refs[:TILES], refs[TILES : 2 * TILES]
+    l2_ref, l3_ref, t_ref, send_ref, all_ref = refs[2 * TILES :]
     total = jnp.zeros((2 * TB, TB), F32)
     for d in range(LAYERS):
         k0, k1 = places(place_ref, d)
-        a = rows(*(lanes(mine[d][i], other[d][i]) for i in range(2)))
+        a = rows(*both_cores(mine, other, d))
         all_ref[d] = a
         total += dot3(split(a), split(rows(l2_ref[k0, :TB], l2_ref[k1, :TB])))
     for i in range(2):
@@ -123,7 +136,7 @@
     return one(a[0], b[0]) + (one(a[0], b[1]) + one(a[1], b[0]))
 
 
-def uq_kernel(place_ref, root_ref, diag_ref, cols_ref, u_ref, q_ref, home_ref, away_ref):
+def uq_kernel(root_ref, diag_ref, cols_ref, u_ref, q_ref):
     u = jnp.zeros((2 * TB, TB), F32)
     q = jnp.zeros((HALF, 2 * TB), F32)
     for k in range(0, N, 2):
@@ -134,9 +147,6 @@
     for i in range(2):
         u_ref[i] = u[i * TB : (i + 1) * TB]
     q_ref[...] = q
-    even = lax.rem(place_ref[1], 2) == 0
-    home_ref[...] = jnp.where(even, q[:, :TB], q[:, TB:])
-    away_ref[...] = jnp.where(even, q[:, TB:], q[:, :TB])
 
 
 def y_kernel(place_ref, root_ref, t_ref, y_ref, home_ref, away_ref):
@@ -151,8 +161,8 @@
 
 
 def sums_kernel(place_ref, *refs):
-    t_mine, t_other = refs[:LAYERS], refs[LAYERS : 2 * LAYERS]
-    l32_ref, y_ref, u_ref, q_ref, l2_ref, sum_ref = refs[2 * LAYERS :]
+    t_mine, t_other = refs[:TILES], refs[TILES : 2 * TILES]
+    l32_ref, y_ref, u_ref, q_ref, l2_ref, sum_ref = refs[2 * TILES :]
     row = place_ref[1]
     side = lax.rem(row, 2)
     y = y_ref[...].T
@@ -161,7 +171,7 @@
     yu_split = split(lanes(y, *u))
     for d in range(LAYERS):
         ks = places(place_ref, d)
-        low = [lanes(t_mine[d][i], t_other[d][i]) for i in range(2)]
+        low = both_cores(t_mine, t_other, d)
         low += [lanes(l2_ref[ks[0], i], l2_ref[ks[1], i]) for i in range(2)]
         x = dot3(left, split(l32_ref[d]))
         z = dot3(yu_split, split(rows(*low)))
@@ -189,7 +199,8 @@
     for r, c in ((0, 1), (0, 2), (0, 3), (1, 0), (1, 2), (1, 3), (2, 3)):
         out_ref[tile(r, c), :] = empty
     y = both(home_ref[...], away_ref[...])
-    q = rows(*both(q_home_ref[...], q_away_ref[...])).T
+    q = rows(*both(q_home_ref[...], q_away_ref[...]))
+    q = jnp.where(even, q[:, :TB], q[:, TB:]).T
     parts = []
     for s in range(2):
         total = got_ref[s]
@@ -215,7 +226,6 @@
     up = down = x
     tied = []
     last = LAYERS // 2
-    half = TB // 2
     beside = None
     for step in range(1, last + 1):
         swapped = [swap_cores(mine[d]) for d in late]
@@ -223,7 +233,7 @@
             swapped, operand = lax.optimization_barrier((swapped, begin[1]))
             beside = begin[2](operand)
         if step == last:
-            up, down = up[:, :half], down[:, half:]
+            up, down = up[:1], down[1:]
         up = lax.ppermute(up, "col", LAYER_UP)
         down = lax.ppermute(down, "col", LAYER_DOWN)
         more = ties.get(step)
@@ -237,10 +247,11 @@
         if step < last:
             mine[LAYERS - step], mine[step] = up, down
             late = [LAYERS - step, step]
-    mine[last] = jnp.concatenate([up, down], axis=1)
-    other[last], beside = lax.optimization_barrier((swap_cores(mine[last]), beside))
-    order = range(LAYERS)
-    return [mine[d] for d in order], [other[d] for d in order], beside, *(t for t in tied if t is not None)
+    swapped, beside = lax.optimization_barrier(([swap_cores(up), swap_cores(down)], beside))
+    near, far = range(last), range(last + 1, LAYERS)
+    mine = [*(mine[d] for d in near), up, down, *(mine[d] for d in far)]
+    other = [*(other[d] for d in near), *swapped, *(other[d] for d in far)]
+    return mine, other, beside, *(t for t in tied if t is not None)
 
 
 def body(factor, structure):
@@ -296,13 +307,13 @@
             l3,
         )
     with jax.named_scope("term_uq"):
-        u, q, q_home, q_away = call(
+        u, q = call(
             uq_kernel,
-            [(2, *square), (HALF, 2 * TB), (HALF, TB), (HALF, TB)],
-            place,
+            [(2, *square), (HALF, 2 * TB)],
             root_rows,
             diag_rows,
             cols,
+            scalars=0,
         )
     with jax.named_scope("gather_t"):
         t_mine, t_other, t_cols, (root_rows, l2_rows), (u, q) = gather_layers(
@@ -313,9 +324,8 @@
             y_kernel, [(2 * TB, TB), square, square], place, root_rows, t_cols
         )
     with jax.named_scope("swap_yq"):
-        away = jnp.concatenate([y_away, q_away])
-        away = lax.ppermute(away, "row", ROW_SWAP)
-        y_away, q_away = away[:TB], away[TB:]
+        y_away = lax.ppermute(y_away, "row", ROW_SWAP)
+        q_away = lax.ppermute(q, "row", ROW_SWAP)
     with jax.named_scope("sums"):
         (sums,) = call(
             sums_kernel,
@@ -342,7 +352,7 @@
             got,
             y_home,
             y_away,
-            q_home,
+            q,
             q_away,
             scalars=2,
         )

time: 171 us -> 174 us (1.018)
  local copies, waits for them, and re-layouts: 19.1 us -> 21.9 us
  waiting for transfers between devices: 42.1 us -> 44.3 us
    unnamed x73 -> x69, local copies, waits for them, and re-layouts: 12.5 us -> 16.2 us
    ppermute x8, waiting for transfers between devices: 14.4 us -> 17.2 us  [gather_layers(): up = lax.ppermute(up, 'col', LAYER_UP)]
    all_to_all x1, starting transfers between devices: 5.33 us -> 3.56 us  [to_side(): lax.all_to_all(x, 'row', 0, 0, tiled=True, axis_index_groups=SAME_SIDE)]
    ppermute x16 -> x18, starting transfers between devices: 2.39 us -> 3.6 us  [swap_cores(): return lax.ppermute(x, 'col', CORE_SWAP)]
  transfers between devices with their start and end apart: 38 -> 41, of which waited for: 15 -> 21; matrix products, arithmetic and copies ran while one was open for 4% -> 3% of each run, Pallas kernels for 5% -> 5%
where the time goes in v10:
time: 174 us; the launch traced here: 172 us
  waiting for transfers between devices  44.3 us (25%)
  blocking collectives  41.5 us (24%)
  starting transfers between devices  37.1 us (21%)
  local copies, waits for them, and re-layouts  21.9 us (13%)
  between operations  13.7 us (8%)
  Pallas kernels  13.3 us (8%)
    all_to_all x1, blocking collectives, body(): got = lax.all_to_all(sums, 'row', 0, 0, tiled=True)  41.5 us
    ppermute x8, waiting for transfers between devices, gather_layers(): down = lax.ppermute(down, 'col', LAYER_DOWN)  17.3 us
    ppermute x8, waiting for transfers between devices, gather_layers(): up = lax.ppermute(up, 'col', LAYER_UP)  17.2 us
    unnamed x69, local copies, waits for them, and re-layouts  16.2 us
    ppermute x8, starting transfers between devices, gather_layers(): down = lax.ppermute(down, 'col', LAYER_DOWN)  14.7 us
    pallas_call x7, Pallas kernels, call(): pl.pallas_call(kernel, out_shape=[jax.ShapeDtypeStruct(s, F32) for s in s...  13.3 us
    all_to_all x1, starting transfers between devices, to_rows(): return lax.all_to_all(x, 'row', 0, 0, tiled=True)  6.75 us
    squeeze x1, local copies, waits for them, and re-layouts, body(): panels = [panels[:, i] for i in range(3)]  4.82 us
  transfers between devices with their start and end apart: 41, of which 21 were waited for; matrix products, arithmetic and copies ran while one was open for 3% of the time, Pallas kernels for 5%

profile of v10, /device:TPU:32, one launch (start us, length us, event | category | flops | bytes accessed | tf_op | source)
XLA Modules:
  0.0 171.8 jit_solution(8646219958481527117)
XLA Ops:
  8.8 2.0 %prepare.1 = (f32[128,128]{1,0:T(8,128)S(1)}, f32[4,128,128]{2,1,0:T(8,128)S(1)}, f32[4,128,128]{2,1,0:T(8,128)S(1)}, f32[16,192,128]{2,1,0:T(8,128)}) custom-call(s32[4,4]{1,0:T(4,128)S(1)} %bitcast.24, s32[2]{0:T(128)S(1)} %pad_add_fusion.place_ref, f32[2048,128]{1,0:T(8,128)S(1)} %bitcast.22), custom_call_target="tpu_custom_call" | custom-call | tf_op jit(solution)/shard_map/prepare/pallas_call | solution.py:52
  12.3 2.7 %collective-permute-done = f32[128,128]{1,0:T(8,128)S(1)} collective-permute-done((f32[128,128]{1,0:T(8,128)S(1)}, f32[128,128]{1,0:T(8,128)S(1)}, u32[]{:S(2)}, u32[]{:S(2)}) %collective-permute-start) | collective-permute-done | bytes 65568 | tf_op jit(solution)/shard_map/swap_l32/ppermute | solution.py:282
  15.1 1.7 collective-permute-start.4
  18.8 4.1 %collective-permute-done.2.refs_1_ = f32[2,128,128]{2,1,0:T(8,128)S(1)} collective-permute-done((f32[2,128,128]{2,1,0:T(8,128)S(1)}, f32[2,128,128]{2,1,0:T(8,128)S(1)}, u32[]{:S(2)}, u32[]{:S(2)}) %collective-permute-start.2) | collective-permute-done | bytes 131104 | tf_op jit(solution)/shard_map/gather_l/ppermute | solution.py:238
  22.8 3.8 %collective-permute-done.1.refs_8_ = f32[2,128,128]{2,1,0:T(8,128)S(1)} collective-permute-done((f32[2,128,128]{2,1,0:T(8,128)S(1)}, f32[2,128,128]{2,1,0:T(8,128)S(1)}, u32[]{:S(2)}, u32[]{:S(2)}) %collective-permute-start.1) | collective-permute-done | bytes 131104 | tf_op jit(solution)/shard_map/gather_l/ppermute | solution.py:237
  27.1 3.0 %collective-permute-start.6 = (f32[2,128,128]{2,1,0:T(8,128)S(1)}, f32[2,128,128]{2,1,0:T(8,128)S(1)}, u32[]{:S(2)}, u32[]{:S(2)}) collective-permute-start(f32[2,128,128]{2,1,0:T(8,128)S(1)} %collective-permute-done.2.refs_1_), channel_id=1, source_target_pairs={{0,14},{1,15},{2,0},{3,1},{4,2},{5,3},{6,4},{7,5},{8,6},{9,7},{10,... | collective-permute-start | bytes 393224 | tf_op jit(solution)/shard_map/gather_l/ppermute | solution.py:238
  33.0 2.2 %collective-permute-done.5.refs_7_ = f32[2,128,128]{2,1,0:T(8,128)S(1)} collective-permute-done((f32[2,128,128]{2,1,0:T(8,128)S(1)}, f32[2,128,128]{2,1,0:T(8,128)S(1)}, u32[]{:S(2)}, u32[]{:S(2)}) %collective-permute-start.5) | collective-permute-done | bytes 131104 | tf_op jit(solution)/shard_map/gather_l/ppermute | solution.py:237
  35.2 6.8 %all-to-all-start = ((f32[16,192,128]{2,1,0:T(8,128)}), f32[16,192,128]{2,1,0:T(8,128)S(1)}, u32[]{:S(2)}, u32[]{:S(2)}) async-start(f32[16,192,128]{2,1,0:T(8,128)} %get-tuple-element.94), calls=%async_computation | async-start | bytes 3145728 | tf_op jit(solution)/shard_map/gather_l/all_to_all | solution.py:267
  42.1 1.7 collective-permute-start.10
  44.3 5.6 %collective-permute-done.10.refs_3_ = f32[2,128,128]{2,1,0:T(8,128)S(1)} collective-permute-done((f32[2,128,128]{2,1,0:T(8,128)S(1)}, f32[2,128,128]{2,1,0:T(8,128)S(1)}, u32[]{:S(2)}, u32[]{:S(2)}) %collective-permute-start.10) | collective-permute-done | bytes 131104 | tf_op jit(solution)/shard_map/gather_l/ppermute | solution.py:238
  49.9 2.2 %collective-permute-done.9.refs_6_ = f32[2,128,128]{2,1,0:T(8,128)S(1)} collective-permute-done((f32[2,128,128]{2,1,0:T(8,128)S(1)}, f32[2,128,128]{2,1,0:T(8,128)S(1)}, u32[]{:S(2)}, u32[]{:S(2)}) %collective-permute-start.9) | collective-permute-done | bytes 131104 | tf_op jit(solution)/shard_map/gather_l/ppermute | solution.py:237
  54.7 3.6 %collective-permute-done.13.refs_4_ = f32[1,128,128]{2,1,0:T(8,128)S(1)} collective-permute-done((f32[1,128,128]{2,1,0:T(8,128)S(1)}, f32[1,128,128]{2,1,0:T(8,128)S(1)}, u32[]{:S(2)}, u32[]{:S(2)}) %collective-permute-start.13) | collective-permute-done | bytes 65568 | tf_op jit(solution)/shard_map/gather_l/ppermute | solution.py:237
  60.4 4.3 %all-to-all-done.refs_18_.cols_ref = f32[16,192,128]{2,1,0:T(8,128)S(1)} async-done(((f32[16,192,128]{2,1,0:T(8,128)}), f32[16,192,128]{2,1,0:T(8,128)S(1)}, u32[]{:S(2)}, u32[]{:S(2)}) %all-to-all-start) | async-done | bytes 1572896 | tf_op jit(solution)/shard_map/gather_l/all_to_all | solution.py:267
  74.9 3.6 %all-to-all-start.1 = ((f32[8,2,128,128]{3,2,1,0:T(8,128)}), f32[8,2,128,128]{3,2,1,0:T(8,128)S(1)}, u32[]{:S(2)}, u32[]{:S(2)}) async-start(f32[8,2,128,128]{3,2,1,0:T(8,128)} %copy-done.7), calls=%async_computation.1 | async-start | bytes 2097152 | tf_op jit(solution)/shard_map/gather_t/all_to_all | solution.py:270
  78.4 1.9 %collective-permute-start.20 = (f32[2,128,128]{2,1,0:T(8,128)S(1)}, f32[2,128,128]{2,1,0:T(8,128)S(1)}, u32[]{:S(2)}, u32[]{:S(2)}) collective-permute-start(f32[2,128,128]{2,1,0:T(8,128)S(1)} %get-tuple-element.109.refs_0_), channel_id=1, source_target_pairs={{0,14},{1,15},{2,0},{3,1},{4,2},{5,3},{6,4},{7,5},{8,6},{9,7},{10,... | collective-permute-start | bytes 393224 | tf_op jit(solution)/shard_map/gather_t/ppermute | solution.py:238
  80.5 3.7 %collective-permute-done.20.refs_1_ = f32[2,128,128]{2,1,0:T(8,128)S(1)} collective-permute-done((f32[2,128,128]{2,1,0:T(8,128)S(1)}, f32[2,128,128]{2,1,0:T(8,128)S(1)}, u32[]{:S(2)}, u32[]{:S(2)}) %collective-permute-start.20) | collective-permute-done | bytes 131104 | tf_op jit(solution)/shard_map/gather_t/ppermute | solution.py:238
  84.3 2.4 %collective-permute-done.19.refs_8_ = f32[2,128,128]{2,1,0:T(8,128)S(1)} collective-permute-done((f32[2,128,128]{2,1,0:T(8,128)S(1)}, f32[2,128,128]{2,1,0:T(8,128)S(1)}, u32[]{:S(2)}, u32[]{:S(2)}) %collective-permute-start.19) | collective-permute-done | bytes 131104 | tf_op jit(solution)/shard_map/gather_t/ppermute | solution.py:237
  86.6 3.0 %collective-permute-start.23 = (f32[2,128,128]{2,1,0:T(8,128)S(1)}, f32[2,128,128]{2,1,0:T(8,128)S(1)}, u32[]{:S(2)}, u32[]{:S(2)}) collective-permute-start(f32[2,128,128]{2,1,0:T(8,128)S(1)} %collective-permute-done.20.refs_1_), channel_id=1, source_target_pairs={{0,14},{1,15},{2,0},{3,1},{4,2},{5,3},{6,4},{7,5},{8,6},{9,7},{10,... | collective-permute-start | bytes 393224 | tf_op jit(solution)/shard_map/gather_t/ppermute | solution.py:238
  93.7 2.5 %collective-permute-done.22.refs_7_ = f32[2,128,128]{2,1,0:T(8,128)} collective-permute-done((f32[2,128,128]{2,1,0:T(8,128)S(1)}, f32[2,128,128]{2,1,0:T(8,128)}, u32[]{:S(2)}, u32[]{:S(2)}) %collective-permute-start.22) | collective-permute-done | bytes 131104 | tf_op jit(solution)/shard_map/gather_t/ppermute | solution.py:237
  98.5 4.8 %slice_bitcast_fusion = (f32[16,2,128,128]{3,2,1,0:T(8,128)S(1)}, f32[16,2,128,128]{3,2,1,0:T(8,128)}, f32[16,2,128,128]{3,2,1,0:T(8,128)S(1)}) fusion(f32[16,3,2,128,128]{4,3,2,1,0:T(8,128)} %bitcast.26), kind=kLoop, calls=%fused_computation | loop fusion | bytes 12582912 | tf_op jit(solution)/shard_map/gather_rows/squeeze | solution.py:297
  106.5 1.8 %term_uq.1 = (f32[2,128,128]{2,1,0:T(8,128)S(1)}, f32[64,256]{1,0:T(8,128)S(1)}) custom-call(f32[16,2,128,128]{3,2,1,0:T(8,128)S(1)} %get-tuple-element.134.root_ref, f32[16,2,128,128]{3,2,1,0:T(8,128)S(1)} %get-tuple-element.145.diag_ref, f32[16,192,128]{2,1,0:T(8,128)S(1)} %copy-done.1), custom_call_target="tpu_custom_call" | custom-call | tf_op jit(solution)/shard_map/term_uq/pallas_call | solution.py:52
  118.4 3.0 %sums.1 = f32[16,320,128]{2,1,0:T(8,128)S(1)} custom-call(s32[2]{0:T(128)S(1)} %pad_add_fusion.place_ref, f32[2,128,128]{2,1,0:T(8,128)S(1)} %copy-done.9, f32[2,128,128]{2,1,0:T(8,128)S(1)} %copy-done.13, f32[2,128,128]{2,1,0:T(8,128)S(1)} %copy-done.19, f32[2,128,128]{2,1,0:T(8,128)S(1)} %collective-permute-done.27.refs_3_, ...), custom_call_target="tpu_custom_call" | custom-call | tf_op jit(solution)/shard_map/sums/pallas_call | solution.py:52
  121.4 41.5 %all_to_all.15.got_ref = f32[16,320,128]{2,1,0:T(8,128)S(1)} all-to-all(f32[16,320,128]{2,1,0:T(8,128)S(1)} %sums.1), channel_id=1, replica_groups=mesh['row'=16,'col'=16] {'row'}, dimensions={0} | all-to-all | bytes 5242880 | tf_op jit(solution)/shard_map/scatter_sums/all_to_all | solution.py:344
  162.9 2.1 %finish.1 = f32[2048,128]{1,0:T(8,128)} custom-call(s32[4,4]{1,0:T(4,128)S(1)} %bitcast.25, s32[2]{0:T(128)S(1)} %pad_add_fusion.place_ref, f32[2048,128]{1,0:T(8,128)S(1)} %bitcast.23, f32[16,320,128]{2,1,0:T(8,128)S(1)} %all_to_all.15.got_ref, f32[128,128]{1,0:T(8,128)S(1)} %get-tuple-element.142.home_ref, ...), custom_call_target="tpu_custom_call" | custom-call | tf_op jit(solution)/shard_map/finish/pallas_call | solution.py:52
  (146 shorter events, 44.5 us)
Async XLA Ops:
  6.5 91.9 %all-gather.3.cloned.1.call-start = ((), (), s32[]{:S(2)}) async-start(), calls=%async_computation.3 | async-start | bytes 6684672 | tf_op jit(solution)/shard_map/gather_rows/all_gather | solution.py:296
  15.1 11.5 %collective-permute-start.4 = (f32[4,128,128]{2,1,0:T(8,128)S(1)}, f32[4,128,128]{2,1,0:T(8,128)S(1)}, u32[]{:S(2)}, u32[]{:S(2)}) collective-permute-start(f32[4,128,128]{2,1,0:T(8,128)S(1)} %get-tuple-element.78), channel_id=1, source_target_pairs={{0,16},{16,0},{32,48},{48,32},{64,80},{80,64},{96,112},{112,96},{1... | collective-permute-start | bytes 786440 | tf_op jit(solution)/shard_map/swap_rest/ppermute | solution.py:287
  16.7 6.1 %collective-permute-start.2 = (f32[2,128,128]{2,1,0:T(8,128)S(1)}, f32[2,128,128]{2,1,0:T(8,128)S(1)}, u32[]{:S(2)}, u32[]{:S(2)}) collective-permute-start(f32[2,128,128]{2,1,0:T(8,128)S(1)} %pad_maximum_fusion.refs_0_), channel_id=1, source_target_pairs={{0,14},{1,15},{2,0},{3,1},{4,2},{5,3},{6,4},{7,5},{8,6},{9,7},{10,... | collective-permute-start | bytes 393224 | tf_op jit(solution)/shard_map/gather_l/ppermute | solution.py:238
  17.7 8.9 %collective-permute-start.1 = (f32[2,128,128]{2,1,0:T(8,128)S(1)}, f32[2,128,128]{2,1,0:T(8,128)S(1)}, u32[]{:S(2)}, u32[]{:S(2)}) collective-permute-start(f32[2,128,128]{2,1,0:T(8,128)S(1)} %pad_maximum_fusion.refs_0_), channel_id=1, source_target_pairs={{0,2},{1,3},{2,4},{3,5},{4,6},{5,7},{6,8},{7,9},{8,10},{9,11},{10,... | collective-permute-start | bytes 393224 | tf_op jit(solution)/shard_map/gather_l/ppermute | solution.py:237
  27.1 5.9 %collective-permute-start.6 = (f32[2,128,128]{2,1,0:T(8,128)S(1)}, f32[2,128,128]{2,1,0:T(8,128)S(1)}, u32[]{:S(2)}, u32[]{:S(2)}) collective-permute-start(f32[2,128,128]{2,1,0:T(8,128)S(1)} %collective-permute-done.2.refs_1_), channel_id=1, source_target_pairs={{0,14},{1,15},{2,0},{3,1},{4,2},{5,3},{6,4},{7,5},{8,6},{9,7},{10,... | collective-permute-start | bytes 393224 | tf_op jit(solution)/shard_map/gather_l/ppermute | solution.py:238
  35.2 29.5 %all-to-all-start = ((f32[16,192,128]{2,1,0:T(8,128)}), f32[16,192,128]{2,1,0:T(8,128)S(1)}, u32[]{:S(2)}, u32[]{:S(2)}) async-start(f32[16,192,128]{2,1,0:T(8,128)} %get-tuple-element.94), calls=%async_computation | async-start | bytes 3145728 | tf_op jit(solution)/shard_map/gather_l/all_to_all | solution.py:267
  42.1 7.8 %collective-permute-start.10 = (f32[2,128,128]{2,1,0:T(8,128)S(1)}, f32[2,128,128]{2,1,0:T(8,128)S(1)}, u32[]{:S(2)}, u32[]{:S(2)}) collective-permute-start(f32[2,128,128]{2,1,0:T(8,128)S(1)} %collective-permute-done.6.refs_2_), channel_id=1, source_target_pairs={{0,14},{1,15},{2,0},{3,1},{4,2},{5,3},{6,4},{7,5},{8,6},{9,7},{10,... | collective-permute-start | bytes 393224 | tf_op jit(solution)/shard_map/gather_l/ppermute | solution.py:238
  43.7 6.2 %collective-permute-start.11 = (f32[2,128,128]{2,1,0:T(8,128)S(1)}, f32[2,128,128]{2,1,0:T(8,128)S(1)}, u32[]{:S(2)}, u32[]{:S(2)}) collective-permute-start(f32[2,128,128]{2,1,0:T(8,128)S(1)} %collective-permute-done.5.refs_7_), channel_id=1, source_target_pairs={{0,1},{1,0},{2,3},{3,2},{4,5},{5,4},{6,7},{7,6},{8,9},{9,8},{10,11... | collective-permute-start | bytes 393224 | tf_op jit(solution)/shard_map/gather_l/ppermute | solution.py:219
  43.9 8.2 %collective-permute-start.9 = (f32[2,128,128]{2,1,0:T(8,128)S(1)}, f32[2,128,128]{2,1,0:T(8,128)S(1)}, u32[]{:S(2)}, u32[]{:S(2)}) collective-permute-start(f32[2,128,128]{2,1,0:T(8,128)S(1)} %collective-permute-done.5.refs_7_), channel_id=1, source_target_pairs={{0,2},{1,3},{2,4},{3,5},{4,6},{5,7},{6,8},{7,9},{8,10},{9,11},{10,... | collective-permute-start | bytes 393224 | tf_op jit(solution)/shard_map/gather_l/ppermute | solution.py:237
  52.1 7.0 %collective-permute-start.16 = (f32[2,128,128]{2,1,0:T(8,128)S(1)}, f32[2,128,128]{2,1,0:T(8,128)S(1)}, u32[]{:S(2)}, u32[]{:S(2)}) collective-permute-start(f32[2,128,128]{2,1,0:T(8,128)S(1)} %collective-permute-done.10.refs_3_), channel_id=1, source_target_pairs={{0,1},{1,0},{2,3},{3,2},{4,5},{5,4},{6,7},{7,6},{8,9},{9,8},{10,11... | collective-permute-start | bytes 393224 | tf_op jit(solution)/shard_map/gather_l/ppermute | solution.py:219
  52.1 7.6 %collective-permute-start.15 = (f32[2,128,128]{2,1,0:T(8,128)S(1)}, f32[2,128,128]{2,1,0:T(8,128)S(1)}, u32[]{:S(2)}, u32[]{:S(2)}) collective-permute-start(f32[2,128,128]{2,1,0:T(8,128)S(1)} %collective-permute-done.9.refs_6_), channel_id=1, source_target_pairs={{0,1},{1,0},{2,3},{3,2},{4,5},{5,4},{6,7},{7,6},{8,9},{9,8},{10,11... | collective-permute-start | bytes 393224 | tf_op jit(solution)/shard_map/gather_l/ppermute | solution.py:219
  52.6 5.7 %collective-permute-start.13 = (f32[1,128,128]{2,1,0:T(8,128)S(1)}, f32[1,128,128]{2,1,0:T(8,128)S(1)}, u32[]{:S(2)}, u32[]{:S(2)}) collective-permute-start(f32[1,128,128]{2,1,0:T(8,128)S(1)} %slice.21), channel_id=1, source_target_pairs={{0,2},{1,3},{2,4},{3,5},{4,6},{5,7},{6,8},{7,9},{8,10},{9,11},{10,... | collective-permute-start | bytes 196616 | tf_op jit(solution)/shard_map/gather_l/ppermute | solution.py:237
  53.5 5.6 %collective-permute-start.14 = (f32[1,128,128]{2,1,0:T(8,128)S(1)}, f32[1,128,128]{2,1,0:T(8,128)S(1)}, u32[]{:S(2)}, u32[]{:S(2)}) collective-permute-start(f32[1,128,128]{2,1,0:T(8,128)S(1)} %slice.22), channel_id=1, source_target_pairs={{0,14},{1,15},{2,0},{3,1},{4,2},{5,3},{6,4},{7,5},{8,6},{9,7},{10,... | collective-permute-start | bytes 196616 | tf_op jit(solution)/shard_map/gather_l/ppermute | solution.py:238
  74.9 36.9 %all-to-all-start.1 = ((f32[8,2,128,128]{3,2,1,0:T(8,128)}), f32[8,2,128,128]{3,2,1,0:T(8,128)S(1)}, u32[]{:S(2)}, u32[]{:S(2)}) async-start(f32[8,2,128,128]{3,2,1,0:T(8,128)} %copy-done.7), calls=%async_computation.1 | async-start | bytes 2097152 | tf_op jit(solution)/shard_map/gather_t/all_to_all | solution.py:270
  78.4 5.8 %collective-permute-start.20 = (f32[2,128,128]{2,1,0:T(8,128)S(1)}, f32[2,128,128]{2,1,0:T(8,128)S(1)}, u32[]{:S(2)}, u32[]{:S(2)}) collective-permute-start(f32[2,128,128]{2,1,0:T(8,128)S(1)} %get-tuple-element.109.refs_0_), channel_id=1, source_target_pairs={{0,14},{1,15},{2,0},{3,1},{4,2},{5,3},{6,4},{7,5},{8,6},{9,7},{10,... | collective-permute-start | bytes 393224 | tf_op jit(solution)/shard_map/gather_t/ppermute | solution.py:238
  80.4 6.3 %collective-permute-start.19 = (f32[2,128,128]{2,1,0:T(8,128)S(1)}, f32[2,128,128]{2,1,0:T(8,128)S(1)}, u32[]{:S(2)}, u32[]{:S(2)}) collective-permute-start(f32[2,128,128]{2,1,0:T(8,128)S(1)} %get-tuple-element.109.refs_0_), channel_id=1, source_target_pairs={{0,2},{1,3},{2,4},{3,5},{4,6},{5,7},{6,8},{7,9},{8,10},{9,11},{10,... | collective-permute-start | bytes 393224 | tf_op jit(solution)/shard_map/gather_t/ppermute | solution.py:237
  86.6 6.4 %collective-permute-start.23 = (f32[2,128,128]{2,1,0:T(8,128)S(1)}, f32[2,128,128]{2,1,0:T(8,128)S(1)}, u32[]{:S(2)}, u32[]{:S(2)}) collective-permute-start(f32[2,128,128]{2,1,0:T(8,128)S(1)} %collective-permute-done.20.refs_1_), channel_id=1, source_target_pairs={{0,14},{1,15},{2,0},{3,1},{4,2},{5,3},{6,4},{7,5},{8,6},{9,7},{10,... | collective-permute-start | bytes 393224 | tf_op jit(solution)/shard_map/gather_t/ppermute | solution.py:238
  90.4 5.8 %collective-permute-start.22 = (f32[2,128,128]{2,1,0:T(8,128)S(1)}, f32[2,128,128]{2,1,0:T(8,128)}, u32[]{:S(2)}, u32[]{:S(2)}) collective-permute-start(f32[2,128,128]{2,1,0:T(8,128)S(1)} %collective-permute-done.19.refs_8_), channel_id=1, source_target_pairs={{0,2},{1,3},{2,4},{3,5},{4,6},{5,7},{6,8},{7,9},{8,10},{9,11},{10,... | collective-permute-start | bytes 393224 | tf_op jit(solution)/shard_map/gather_t/ppermute | solution.py:237
  96.2 7.1 %collective-permute-start.29 = (f32[2,128,128]{2,1,0:T(8,128)S(1)}, f32[2,128,128]{2,1,0:T(8,128)}, u32[]{:S(2)}, u32[]{:S(2)}) collective-permute-start(f32[2,128,128]{2,1,0:T(8,128)S(1)} %collective-permute-done.23.refs_2_), channel_id=1, source_target_pairs={{0,1},{1,0},{2,3},{3,2},{4,5},{5,4},{6,7},{7,6},{8,9},{9,8},{10,11... | collective-permute-start | bytes 393224 | tf_op jit(solution)/shard_map/gather_t/ppermute | solution.py:219
  96.2 7.1 %collective-permute-start.27 = (f32[2,128,128]{2,1,0:T(8,128)S(1)}, f32[2,128,128]{2,1,0:T(8,128)S(1)}, u32[]{:S(2)}, u32[]{:S(2)}) collective-permute-start(f32[2,128,128]{2,1,0:T(8,128)S(1)} %collective-permute-done.23.refs_2_), channel_id=1, source_target_pairs={{0,14},{1,15},{2,0},{3,1},{4,2},{5,3},{6,4},{7,5},{8,6},{9,7},{10,... | collective-permute-start | bytes 393224 | tf_op jit(solution)/shard_map/gather_t/ppermute | solution.py:238
  97.9 5.9 %collective-permute-start.26 = (f32[2,128,128]{2,1,0:T(8,128)}, f32[2,128,128]{2,1,0:T(8,128)S(1)}, u32[]{:S(2)}, u32[]{:S(2)}) collective-permute-start(f32[2,128,128]{2,1,0:T(8,128)} %collective-permute-done.22.refs_7_), channel_id=1, source_target_pairs={{0,2},{1,3},{2,4},{3,5},{4,6},{5,7},{6,8},{7,9},{8,10},{9,11},{10,... | collective-permute-start | bytes 393224 | tf_op jit(solution)/shard_map/gather_t/ppermute | solution.py:237
  103.8 6.2 %collective-permute-start.32 = (f32[2,128,128]{2,1,0:T(8,128)S(1)}, f32[2,128,128]{2,1,0:T(8,128)S(1)}, u32[]{:S(2)}, u32[]{:S(2)}) collective-permute-start(f32[2,128,128]{2,1,0:T(8,128)S(1)} %collective-permute-done.26.refs_6_), channel_id=1, source_target_pairs={{0,1},{1,0},{2,3},{3,2},{4,5},{5,4},{6,7},{7,6},{8,9},{9,8},{10,11... | collective-permute-start | bytes 393224 | tf_op jit(solution)/shard_map/gather_t/ppermute | solution.py:219
  111.2 10.2 %collective-permute-start.37 = (f32[64,256]{1,0:T(8,128)S(1)}, f32[64,256]{1,0:T(8,128)}, u32[]{:S(2)}, u32[]{:S(2)}) collective-permute-start(f32[64,256]{1,0:T(8,128)S(1)} %get-tuple-element.138.refs_21_.q_home_ref), channel_id=1, source_target_pairs={{0,16},{16,0},{32,48},{48,32},{64,80},{80,64},{96,112},{112,96},{1... | collective-permute-start | bytes 196616 | tf_op jit(solution)/shard_map/swap_yq/ppermute | solution.py:328
  113.9 7.5 %collective-permute-start.36 = (f32[128,128]{1,0:T(8,128)S(1)}, f32[128,128]{1,0:T(8,128)S(1)}, u32[]{:S(2)}, u32[]{:S(2)}) collective-permute-start(f32[128,128]{1,0:T(8,128)S(1)} %get-tuple-element.140), channel_id=1, source_target_pairs={{0,16},{16,0},{32,48},{48,32},{64,80},{80,64},{96,112},{112,96},{1... | collective-permute-start | bytes 196616 | tf_op jit(solution)/shard_map/swap_yq/ppermute | solution.py:327
  (51 other events, 199.4 us)
Sparse Core Ops, SparseCore 0:
  35.3 46.5 all-gather.2

commit v11 on v10

--- a/solution.py
+++ b/solution.py
@@ -15,8 +15,6 @@
 CORE_SWAP = [(i, i ^ 1) for i in range(N)]
 ROW_SWAP = [(i, i ^ 1) for i in range(N)]
 SAME_SIDE = [[p + 2 * i for i in range(N // 2)] for p in range(2)]
-LAYER_UP = [(i, (i + 2) % N) for i in range(N)]
-LAYER_DOWN = [(i, (i - 2) % N) for i in range(N)]
 
 
 def split(x):
@@ -219,39 +217,25 @@
     return lax.ppermute(x, "col", CORE_SWAP)
 
 
+def shift(x, layers):
+    return lax.ppermute(x, "col", [(i, (i + 2 * layers) % N) for i in range(N)])
+
+
 def gather_layers(x, begin, ties):
-    mine = {0: x}
-    other = {}
-    late = [0]
-    up = down = x
-    tied = []
-    last = LAYERS // 2
-    beside = None
-    for step in range(1, last + 1):
-        swapped = [swap_cores(mine[d]) for d in late]
-        if step == begin[0]:
-            swapped, operand = lax.optimization_barrier((swapped, begin[1]))
-            beside = begin[2](operand)
-        if step == last:
-            up, down = up[:1], down[1:]
-        up = lax.ppermute(up, "col", LAYER_UP)
-        down = lax.ppermute(down, "col", LAYER_DOWN)
-        more = ties.get(step)
+    def tie(values, more, before):
         if callable(more):
-            more = more(tied[-1])
-        up, down, swapped, more = lax.optimization_barrier((up, down, swapped, more))
-        tied.append(more)
-        if step == begin[3]:
-            up, down, beside = lax.optimization_barrier((up, down, beside))
-        other.update(zip(late, swapped))
-        if step < last:
-            mine[LAYERS - step], mine[step] = up, down
-            late = [LAYERS - step, step]
-    swapped, beside = lax.optimization_barrier(([swap_cores(up), swap_cores(down)], beside))
-    near, far = range(last), range(last + 1, LAYERS)
-    mine = [*(mine[d] for d in near), up, down, *(mine[d] for d in far)]
-    other = [*(other[d] for d in near), *swapped, *(other[d] for d in far)]
-    return mine, other, beside, *(t for t in tied if t is not None)
+            more = more(before)
+        return lax.optimization_barrier((values, more))
+
+    near = [shift(x, -1), shift(x, -2), shift(x, 2), shift(x, 1)]
+    (near, own), first = tie((near, swap_cores(x)), ties[0], None)
+    far = [shift(near[0], -2), shift(near[2][:1], 2), shift(near[1][1:], -2), shift(near[3], 2)]
+    beside = begin[1](begin[0])
+    (far, near_swapped), second = tie((far, [swap_cores(t) for t in near]), ties[1], first)
+    far_swapped, beside = lax.optimization_barrier(([swap_cores(t) for t in far], beside))
+    mine = [x, *near[:2], *far, *near[2:]]
+    other = [own, *near_swapped[:2], *far_swapped, *near_swapped[2:]]
+    return mine, other, beside, first, second
 
 
 def body(factor, structure):
@@ -289,9 +273,10 @@
         return call(pack_kernel, [(3, 2, *square), (2, *square)], place, home, away)
 
     with jax.named_scope("gather_l"):
-        l_mine, l_other, cols, _, (packed, l3) = gather_layers(
-            l32_pair, (2, (send, away), lambda x: to_rows(x[0]), 4), {1: away, 2: pack}
-        )
+        send, away = lax.optimization_barrier((send, away))
+        l_mine, l_other, cols, away, _ = gather_layers(l32_pair, (send, to_rows), (away, None))
+    with jax.named_scope("pack"):
+        packed, l3 = pack(away)
     with jax.named_scope("gather_rows"):
         panels = lax.all_gather(packed, "col", axis=0)
         panels = [panels[:, i] for i in range(3)]
@@ -316,8 +301,8 @@
             scalars=0,
         )
     with jax.named_scope("gather_t"):
-        t_mine, t_other, t_cols, (root_rows, l2_rows), (u, q) = gather_layers(
-            t, (1, send, to_side, 5), {3: (root_rows, l2_rows), 4: (u, q)}
+        t_mine, t_other, t_cols, _, (root_rows, l2_rows, u, q) = gather_layers(
+            t, (send, to_side), (None, lambda _: (root_rows, l2_rows, u, q))
         )
     with jax.named_scope("term_y"):
         y, y_home, y_away = call(

time: 174 us -> 183 us (1.052); the launches traced: 172 us -> 183 us
  starting transfers between devices: 37.1 us -> 52.7 us
  local copies, waits for them, and re-layouts: 21.9 us -> 19.2 us
  waiting for transfers between devices: 44.3 us -> 42.4 us
    ppermute x16, starting transfers between devices: 18.4 us -> 29.9 us  [shift(): return lax.ppermute(x, 'col', [(i, (i + 2 * layers) % N) for i in range(N)])]
    all_to_all x1, starting transfers between devices: 3.56 us -> 7.89 us  [to_side(): lax.all_to_all(x, 'row', 0, 0, tiled=True, axis_index_groups=SAME_SIDE)]
    all_to_all x1, waiting for transfers between devices: 4.28 us -> 0.01 us  [to_rows(): return lax.all_to_all(x, 'row', 0, 0, tiled=True)]
    ppermute x16, waiting for transfers between devices: 34.5 us -> 38.7 us  [shift(): return lax.ppermute(x, 'col', [(i, (i + 2 * layers) % N) for i in range(N)])]
    unnamed x69 -> x49, local copies, waits for them, and re-layouts: 16.2 us -> 13.5 us
    ppermute x18, waiting for transfers between devices: 2.76 us -> 0.92 us  [swap_cores(): return lax.ppermute(x, 'col', CORE_SWAP)]
  transfers between devices with their start and end apart: 41 -> 41, of which waited for: 21 -> 14; matrix products, arithmetic and copies ran while one was open for 3% -> 3% of each run, Pallas kernels for 5% -> 4%
where the time goes in v11:
time: 183 us
  starting transfers between devices  52.7 us (29%)
  waiting for transfers between devices  42.4 us (23%)
  blocking collectives  41.1 us (22%)
  local copies, waits for them, and re-layouts  19.2 us (10%)
  between operations  13.6 us (7%)
  Pallas kernels  13.5 us (7%)
    all_to_all x1, blocking collectives, body(): got = lax.all_to_all(sums, 'row', 0, 0, tiled=True)  41.1 us
    ppermute x16, waiting for transfers between devices, shift(): return lax.ppermute(x, 'col', [(i, (i + 2 * layers) % N) for i in range(N)])  38.7 us
    ppermute x16, starting transfers between devices, shift(): return lax.ppermute(x, 'col', [(i, (i + 2 * layers) % N) for i in range(N)])  29.9 us
    pallas_call x7, Pallas kernels, call(): pl.pallas_call(kernel, out_shape=[jax.ShapeDtypeStruct(s, F32) for s in s...  13.5 us
    unnamed x49, local copies, waits for them, and re-layouts  13.5 us
    all_to_all x1, starting transfers between devices, to_side(): lax.all_to_all(x, 'row', 0, 0, tiled=True, axis_index_groups=SAME_SIDE)  7.89 us
    all_to_all x1, starting transfers between devices, to_rows(): return lax.all_to_all(x, 'row', 0, 0, tiled=True)  6.75 us
    squeeze x1, local copies, waits for them, and re-layouts, body(): panels = [panels[:, i] for i in range(3)]  4.82 us
  transfers between devices with their start and end apart: 41, of which 14 were waited for; matrix products, arithmetic and copies ran while one was open for 3% of the time, Pallas kernels for 4%

profile of v11, /device:TPU:32, one launch (start us, length us, event | category | flops | bytes accessed | tf_op | source)
XLA Modules:
  0.0 182.7 jit_solution(3707414795336286211)
XLA Ops:
  8.8 2.0 %prepare.1 = (f32[128,128]{1,0:T(8,128)S(1)}, f32[4,128,128]{2,1,0:T(8,128)S(1)}, f32[4,128,128]{2,1,0:T(8,128)S(1)}, f32[16,192,128]{2,1,0:T(8,128)}) custom-call(s32[4,4]{1,0:T(4,128)S(1)} %bitcast.24, s32[2]{0:T(128)S(1)} %pad_add_fusion.place_ref, f32[2048,128]{1,0:T(8,128)S(1)} %bitcast.22), custom_call_target="tpu_custom_call" | custom-call | tf_op jit(solution)/shard_map/prepare/pallas_call | solution.py:50
  12.4 2.7 %collective-permute-done = f32[128,128]{1,0:T(8,128)S(1)} collective-permute-done((f32[128,128]{1,0:T(8,128)S(1)}, f32[128,128]{1,0:T(8,128)S(1)}, u32[]{:S(2)}, u32[]{:S(2)}) %collective-permute-start) | collective-permute-done | bytes 65568 | tf_op jit(solution)/shard_map/swap_l32/ppermute | solution.py:266
  17.6 5.6 %collective-permute-start.2 = (f32[2,128,128]{2,1,0:T(8,128)S(1)}, f32[2,128,128]{2,1,0:T(8,128)S(1)}, u32[]{:S(2)}, u32[]{:S(2)}) collective-permute-start(f32[2,128,128]{2,1,0:T(8,128)S(1)} %pad_maximum_fusion.refs_0_), channel_id=1, source_target_pairs={{0,12},{1,13},{2,14},{3,15},{4,0},{5,1},{6,2},{7,3},{8,4},{9,5},{1... | collective-permute-start | bytes 393224 | tf_op jit(solution)/shard_map/gather_l/ppermute | solution.py:221
  24.2 2.9 %collective-permute-done.2.refs_2_ = f32[2,128,128]{2,1,0:T(8,128)S(1)} collective-permute-done((f32[2,128,128]{2,1,0:T(8,128)S(1)}, f32[2,128,128]{2,1,0:T(8,128)S(1)}, u32[]{:S(2)}, u32[]{:S(2)}) %collective-permute-start.2) | collective-permute-done | bytes 131104 | tf_op jit(solution)/shard_map/gather_l/ppermute | solution.py:221
  27.1 5.2 %collective-permute-done.3.refs_7_ = f32[2,128,128]{2,1,0:T(8,128)S(1)} collective-permute-done((f32[2,128,128]{2,1,0:T(8,128)S(1)}, f32[2,128,128]{2,1,0:T(8,128)S(1)}, u32[]{:S(2)}, u32[]{:S(2)}) %collective-permute-start.3) | collective-permute-done | bytes 131104 | tf_op jit(solution)/shard_map/gather_l/ppermute | solution.py:221
  33.9 6.8 %all-to-all-start = ((f32[16,192,128]{2,1,0:T(8,128)}), f32[16,192,128]{2,1,0:T(8,128)S(1)}, u32[]{:S(2)}, u32[]{:S(2)}) async-start(f32[16,192,128]{2,1,0:T(8,128)} %get-tuple-element.84), calls=%async_computation | async-start | bytes 3145728 | tf_op jit(solution)/shard_map/gather_l/all_to_all | solution.py:251
  40.9 1.9 %collective-permute-start.8 = (f32[1,128,128]{2,1,0:T(8,128)S(1)}, f32[1,128,128]{2,1,0:T(8,128)S(1)}, u32[]{:S(2)}, u32[]{:S(2)}) collective-permute-start(f32[1,128,128]{2,1,0:T(8,128)S(1)} %slice.21), channel_id=1, source_target_pairs={{0,4},{1,5},{2,6},{3,7},{4,8},{5,9},{6,10},{7,11},{8,12},{9,13},{1... | collective-permute-start | bytes 196616 | tf_op jit(solution)/shard_map/gather_l/ppermute | solution.py:221
  42.9 2.2 %collective-permute-start.9 = (f32[1,128,128]{2,1,0:T(8,128)S(1)}, f32[1,128,128]{2,1,0:T(8,128)S(1)}, u32[]{:S(2)}, u32[]{:S(2)}) collective-permute-start(f32[1,128,128]{2,1,0:T(8,128)S(1)} %slice.22), channel_id=1, source_target_pairs={{0,12},{1,13},{2,14},{3,15},{4,0},{5,1},{6,2},{7,3},{8,4},{9,5},{1... | collective-permute-start | bytes 196616 | tf_op jit(solution)/shard_map/gather_l/ppermute | solution.py:221
  45.6 8.5 %collective-permute-done.8.refs_4_ = f32[1,128,128]{2,1,0:T(8,128)S(1)} collective-permute-done((f32[1,128,128]{2,1,0:T(8,128)S(1)}, f32[1,128,128]{2,1,0:T(8,128)S(1)}, u32[]{:S(2)}, u32[]{:S(2)}) %collective-permute-start.8) | collective-permute-done | bytes 65568 | tf_op jit(solution)/shard_map/gather_l/ppermute | solution.py:221
  56.3 10.1 %collective-permute-done.7.refs_3_ = f32[2,128,128]{2,1,0:T(8,128)S(1)} collective-permute-done((f32[2,128,128]{2,1,0:T(8,128)S(1)}, f32[2,128,128]{2,1,0:T(8,128)S(1)}, u32[]{:S(2)}, u32[]{:S(2)}) %collective-permute-start.7) | collective-permute-done | bytes 131104 | tf_op jit(solution)/shard_map/gather_l/ppermute | solution.py:221
  78.9 7.9 %all-to-all-start.1 = ((f32[8,2,128,128]{3,2,1,0:T(8,128)}), f32[8,2,128,128]{3,2,1,0:T(8,128)S(1)}, u32[]{:S(2)}, u32[]{:S(2)}) async-start(f32[8,2,128,128]{3,2,1,0:T(8,128)} %copy-done.7), calls=%async_computation.1 | async-start | bytes 2097152 | tf_op jit(solution)/shard_map/gather_t/all_to_all | solution.py:254
  86.8 2.3 %collective-permute-start.19 = (f32[2,128,128]{2,1,0:T(8,128)S(1)}, f32[2,128,128]{2,1,0:T(8,128)}, u32[]{:S(2)}, u32[]{:S(2)}) collective-permute-start(f32[2,128,128]{2,1,0:T(8,128)S(1)} %get-tuple-element.95.refs_0_), channel_id=1, source_target_pairs={{0,14},{1,15},{2,0},{3,1},{4,2},{5,3},{6,4},{7,5},{8,6},{9,7},{10,... | collective-permute-start | bytes 393224 | tf_op jit(solution)/shard_map/gather_t/ppermute | solution.py:221
  92.9 2.9 %collective-permute-done.19.refs_1_ = f32[2,128,128]{2,1,0:T(8,128)} collective-permute-done((f32[2,128,128]{2,1,0:T(8,128)S(1)}, f32[2,128,128]{2,1,0:T(8,128)}, u32[]{:S(2)}, u32[]{:S(2)}) %collective-permute-start.19) | collective-permute-done | bytes 131104 | tf_op jit(solution)/shard_map/gather_t/ppermute | solution.py:221
  97.3 3.2 %collective-permute-done.21.refs_7_ = f32[2,128,128]{2,1,0:T(8,128)S(1)} collective-permute-done((f32[2,128,128]{2,1,0:T(8,128)S(1)}, f32[2,128,128]{2,1,0:T(8,128)S(1)}, u32[]{:S(2)}, u32[]{:S(2)}) %collective-permute-start.21) | collective-permute-done | bytes 131104 | tf_op jit(solution)/shard_map/gather_t/ppermute | solution.py:221
  100.6 1.8 collective-permute-start.24
  103.6 3.0 %collective-permute-start.26 = (f32[1,128,128]{2,1,0:T(8,128)S(1)}, f32[1,128,128]{2,1,0:T(8,128)}, u32[]{:S(2)}, u32[]{:S(2)}) collective-permute-start(f32[1,128,128]{2,1,0:T(8,128)S(1)} %slice.24), channel_id=1, source_target_pairs={{0,12},{1,13},{2,14},{3,15},{4,0},{5,1},{6,2},{7,3},{8,4},{9,5},{1... | collective-permute-start | bytes 196616 | tf_op jit(solution)/shard_map/gather_t/ppermute | solution.py:221
  107.1 1.9 %collective-permute-done.25.refs_4_ = f32[1,128,128]{2,1,0:T(8,128)S(1)} collective-permute-done((f32[1,128,128]{2,1,0:T(8,128)S(1)}, f32[1,128,128]{2,1,0:T(8,128)S(1)}, u32[]{:S(2)}, u32[]{:S(2)}) %collective-permute-start.25) | collective-permute-done | bytes 65568 | tf_op jit(solution)/shard_map/gather_t/ppermute | solution.py:221
  109.0 2.2 %collective-permute-done.26.refs_5_ = f32[1,128,128]{2,1,0:T(8,128)} collective-permute-done((f32[1,128,128]{2,1,0:T(8,128)S(1)}, f32[1,128,128]{2,1,0:T(8,128)}, u32[]{:S(2)}, u32[]{:S(2)}) %collective-permute-start.26) | collective-permute-done | bytes 65568 | tf_op jit(solution)/shard_map/gather_t/ppermute | solution.py:221
  111.2 4.3 %collective-permute-start.27 = (f32[2,128,128]{2,1,0:T(8,128)}, f32[2,128,128]{2,1,0:T(8,128)}, u32[]{:S(2)}, u32[]{:S(2)}) collective-permute-start(f32[2,128,128]{2,1,0:T(8,128)} %collective-permute-done.22.refs_8_), channel_id=1, source_target_pairs={{0,4},{1,5},{2,6},{3,7},{4,8},{5,9},{6,10},{7,11},{8,12},{9,13},{1... | collective-permute-start | bytes 393224 | tf_op jit(solution)/shard_map/gather_t/ppermute | solution.py:221
  115.6 4.8 %slice_bitcast_fusion = (f32[16,2,128,128]{3,2,1,0:T(8,128)S(1)}, f32[16,2,128,128]{3,2,1,0:T(8,128)}, f32[16,2,128,128]{3,2,1,0:T(8,128)S(1)}) fusion(f32[16,3,2,128,128]{4,3,2,1,0:T(8,128)} %bitcast.26), kind=kLoop, calls=%fused_computation | loop fusion | bytes 12582912 | tf_op jit(solution)/shard_map/gather_rows/squeeze | solution.py:282
  120.4 1.8 term_uq.1
  129.4 3.2 %sums.1 = f32[16,320,128]{2,1,0:T(8,128)S(1)} custom-call(s32[2]{0:T(128)S(1)} %pad_add_fusion.place_ref, f32[2,128,128]{2,1,0:T(8,128)S(1)} %copy-done.9, f32[2,128,128]{2,1,0:T(8,128)} %collective-permute-done.19.refs_1_, f32[2,128,128]{2,1,0:T(8,128)S(1)} %collective-permute-done.20.refs_2_, f32[2,128,128]{2,1,0:T(8,128)} %collective-permute-done.24.refs_3_, ...), custom_call_target="tpu_custom_call" | custom-call | tf_op jit(solution)/shard_map/sums/pallas_call | solution.py:50
  132.7 41.1 %all_to_all.15.got_ref = f32[16,320,128]{2,1,0:T(8,128)S(1)} all-to-all(f32[16,320,128]{2,1,0:T(8,128)S(1)} %sums.1), channel_id=1, replica_groups=mesh['row'=16,'col'=16] {'row'}, dimensions={0} | all-to-all | bytes 5242880 | tf_op jit(solution)/shard_map/scatter_sums/all_to_all | solution.py:329
  173.8 2.1 %finish.1 = f32[2048,128]{1,0:T(8,128)} custom-call(s32[4,4]{1,0:T(4,128)S(1)} %bitcast.25, s32[2]{0:T(128)S(1)} %pad_add_fusion.place_ref, f32[2048,128]{1,0:T(8,128)S(1)} %bitcast.23, f32[16,320,128]{2,1,0:T(8,128)S(1)} %all_to_all.15.got_ref, f32[128,128]{1,0:T(8,128)S(1)} %get-tuple-element.126.home_ref, ...), custom_call_target="tpu_custom_call" | custom-call | tf_op jit(solution)/shard_map/finish/pallas_call | solution.py:50
  (126 shorter events, 38.9 us)
Async XLA Ops:
  6.5 109.0 %all-gather.3.cloned.1.call-start = ((), (), s32[]{:S(2)}) async-start(), calls=%async_computation.3 | async-start | bytes 6684672 | tf_op jit(solution)/shard_map/gather_rows/all_gather | solution.py:281
  15.1 9.1 %collective-permute-start.6 = (f32[4,128,128]{2,1,0:T(8,128)S(1)}, f32[4,128,128]{2,1,0:T(8,128)S(1)}, u32[]{:S(2)}, u32[]{:S(2)}) collective-permute-start(f32[4,128,128]{2,1,0:T(8,128)S(1)} %get-tuple-element.71), channel_id=1, source_target_pairs={{0,16},{16,0},{32,48},{48,32},{64,80},{80,64},{96,112},{112,96},{1... | collective-permute-start | bytes 786440 | tf_op jit(solution)/shard_map/swap_rest/ppermute | solution.py:271
  17.6 9.5 %collective-permute-start.2 = (f32[2,128,128]{2,1,0:T(8,128)S(1)}, f32[2,128,128]{2,1,0:T(8,128)S(1)}, u32[]{:S(2)}, u32[]{:S(2)}) collective-permute-start(f32[2,128,128]{2,1,0:T(8,128)S(1)} %pad_maximum_fusion.refs_0_), channel_id=1, source_target_pairs={{0,12},{1,13},{2,14},{3,15},{4,0},{5,1},{6,2},{7,3},{8,4},{9,5},{1... | collective-permute-start | bytes 393224 | tf_op jit(solution)/shard_map/gather_l/ppermute | solution.py:221
  23.1 9.1 %collective-permute-start.3 = (f32[2,128,128]{2,1,0:T(8,128)S(1)}, f32[2,128,128]{2,1,0:T(8,128)S(1)}, u32[]{:S(2)}, u32[]{:S(2)}) collective-permute-start(f32[2,128,128]{2,1,0:T(8,128)S(1)} %pad_maximum_fusion.refs_0_), channel_id=1, source_target_pairs={{0,4},{1,5},{2,6},{3,7},{4,8},{5,9},{6,10},{7,11},{8,12},{9,13},{1... | collective-permute-start | bytes 393224 | tf_op jit(solution)/shard_map/gather_l/ppermute | solution.py:221
  23.2 9.4 %collective-permute-start.4 = (f32[2,128,128]{2,1,0:T(8,128)S(1)}, f32[2,128,128]{2,1,0:T(8,128)S(1)}, u32[]{:S(2)}, u32[]{:S(2)}) collective-permute-start(f32[2,128,128]{2,1,0:T(8,128)S(1)} %pad_maximum_fusion.refs_0_), channel_id=1, source_target_pairs={{0,2},{1,3},{2,4},{3,5},{4,6},{5,7},{6,8},{7,9},{8,10},{9,11},{10,... | collective-permute-start | bytes 393224 | tf_op jit(solution)/shard_map/gather_l/ppermute | solution.py:221
  24.2 8.3 %collective-permute-start.5 = (f32[2,128,128]{2,1,0:T(8,128)S(1)}, f32[2,128,128]{2,1,0:T(8,128)S(1)}, u32[]{:S(2)}, u32[]{:S(2)}) collective-permute-start(f32[2,128,128]{2,1,0:T(8,128)S(1)} %pad_maximum_fusion.refs_0_), channel_id=1, source_target_pairs={{0,1},{1,0},{2,3},{3,2},{4,5},{5,4},{6,7},{7,6},{8,9},{9,8},{10,11... | collective-permute-start | bytes 393224 | tf_op jit(solution)/shard_map/gather_l/ppermute | solution.py:217
  33.9 36.6 %all-to-all-start = ((f32[16,192,128]{2,1,0:T(8,128)}), f32[16,192,128]{2,1,0:T(8,128)S(1)}, u32[]{:S(2)}, u32[]{:S(2)}) async-start(f32[16,192,128]{2,1,0:T(8,128)} %get-tuple-element.84), calls=%async_computation | async-start | bytes 3145728 | tf_op jit(solution)/shard_map/gather_l/all_to_all | solution.py:251
  40.6 14.0 %collective-permute-start.10 = (f32[2,128,128]{2,1,0:T(8,128)S(1)}, f32[2,128,128]{2,1,0:T(8,128)S(1)}, u32[]{:S(2)}, u32[]{:S(2)}) collective-permute-start(f32[2,128,128]{2,1,0:T(8,128)S(1)} %collective-permute-done.4.refs_8_), channel_id=1, source_target_pairs={{0,4},{1,5},{2,6},{3,7},{4,8},{5,9},{6,10},{7,11},{8,12},{9,13},{1... | collective-permute-start | bytes 393224 | tf_op jit(solution)/shard_map/gather_l/ppermute | solution.py:221
  40.9 13.2 %collective-permute-start.8 = (f32[1,128,128]{2,1,0:T(8,128)S(1)}, f32[1,128,128]{2,1,0:T(8,128)S(1)}, u32[]{:S(2)}, u32[]{:S(2)}) collective-permute-start(f32[1,128,128]{2,1,0:T(8,128)S(1)} %slice.21), channel_id=1, source_target_pairs={{0,4},{1,5},{2,6},{3,7},{4,8},{5,9},{6,10},{7,11},{8,12},{9,13},{1... | collective-permute-start | bytes 196616 | tf_op jit(solution)/shard_map/gather_l/ppermute | solution.py:221
  42.9 11.3 %collective-permute-start.9 = (f32[1,128,128]{2,1,0:T(8,128)S(1)}, f32[1,128,128]{2,1,0:T(8,128)S(1)}, u32[]{:S(2)}, u32[]{:S(2)}) collective-permute-start(f32[1,128,128]{2,1,0:T(8,128)S(1)} %slice.22), channel_id=1, source_target_pairs={{0,12},{1,13},{2,14},{3,15},{4,0},{5,1},{6,2},{7,3},{8,4},{9,5},{1... | collective-permute-start | bytes 196616 | tf_op jit(solution)/shard_map/gather_l/ppermute | solution.py:221
  45.1 11.2 %collective-permute-start.12 = (f32[2,128,128]{2,1,0:T(8,128)S(1)}, f32[2,128,128]{2,1,0:T(8,128)S(1)}, u32[]{:S(2)}, u32[]{:S(2)}) collective-permute-start(f32[2,128,128]{2,1,0:T(8,128)S(1)} %collective-permute-done.2.refs_2_), channel_id=1, source_target_pairs={{0,1},{1,0},{2,3},{3,2},{4,5},{5,4},{6,7},{7,6},{8,9},{9,8},{10,11... | collective-permute-start | bytes 393224 | tf_op jit(solution)/shard_map/gather_l/ppermute | solution.py:217
  45.1 11.2 %collective-permute-start.13 = (f32[2,128,128]{2,1,0:T(8,128)S(1)}, f32[2,128,128]{2,1,0:T(8,128)S(1)}, u32[]{:S(2)}, u32[]{:S(2)}) collective-permute-start(f32[2,128,128]{2,1,0:T(8,128)S(1)} %collective-permute-done.3.refs_7_), channel_id=1, source_target_pairs={{0,1},{1,0},{2,3},{3,2},{4,5},{5,4},{6,7},{7,6},{8,9},{9,8},{10,11... | collective-permute-start | bytes 393224 | tf_op jit(solution)/shard_map/gather_l/ppermute | solution.py:217
  54.6 11.7 %collective-permute-start.7 = (f32[2,128,128]{2,1,0:T(8,128)S(1)}, f32[2,128,128]{2,1,0:T(8,128)S(1)}, u32[]{:S(2)}, u32[]{:S(2)}) collective-permute-start(f32[2,128,128]{2,1,0:T(8,128)S(1)} %collective-permute-done.1.refs_1_), channel_id=1, source_target_pairs={{0,12},{1,13},{2,14},{3,15},{4,0},{5,1},{6,2},{7,3},{8,4},{9,5},{1... | collective-permute-start | bytes 393224 | tf_op jit(solution)/shard_map/gather_l/ppermute | solution.py:221
  78.9 45.8 %all-to-all-start.1 = ((f32[8,2,128,128]{3,2,1,0:T(8,128)}), f32[8,2,128,128]{3,2,1,0:T(8,128)S(1)}, u32[]{:S(2)}, u32[]{:S(2)}) async-start(f32[8,2,128,128]{3,2,1,0:T(8,128)} %copy-done.7), calls=%async_computation.1 | async-start | bytes 2097152 | tf_op jit(solution)/shard_map/gather_t/all_to_all | solution.py:254
  86.8 9.0 %collective-permute-start.19 = (f32[2,128,128]{2,1,0:T(8,128)S(1)}, f32[2,128,128]{2,1,0:T(8,128)}, u32[]{:S(2)}, u32[]{:S(2)}) collective-permute-start(f32[2,128,128]{2,1,0:T(8,128)S(1)} %get-tuple-element.95.refs_0_), channel_id=1, source_target_pairs={{0,14},{1,15},{2,0},{3,1},{4,2},{5,3},{6,4},{7,5},{8,6},{9,7},{10,... | collective-permute-start | bytes 393224 | tf_op jit(solution)/shard_map/gather_t/ppermute | solution.py:221
  89.1 8.3 %collective-permute-start.20 = (f32[2,128,128]{2,1,0:T(8,128)S(1)}, f32[2,128,128]{2,1,0:T(8,128)S(1)}, u32[]{:S(2)}, u32[]{:S(2)}) collective-permute-start(f32[2,128,128]{2,1,0:T(8,128)S(1)} %get-tuple-element.95.refs_0_), channel_id=1, source_target_pairs={{0,12},{1,13},{2,14},{3,15},{4,0},{5,1},{6,2},{7,3},{8,4},{9,5},{1... | collective-permute-start | bytes 393224 | tf_op jit(solution)/shard_map/gather_t/ppermute | solution.py:221
  90.4 10.1 %collective-permute-start.21 = (f32[2,128,128]{2,1,0:T(8,128)S(1)}, f32[2,128,128]{2,1,0:T(8,128)S(1)}, u32[]{:S(2)}, u32[]{:S(2)}) collective-permute-start(f32[2,128,128]{2,1,0:T(8,128)S(1)} %get-tuple-element.95.refs_0_), channel_id=1, source_target_pairs={{0,4},{1,5},{2,6},{3,7},{4,8},{5,9},{6,10},{7,11},{8,12},{9,13},{1... | collective-permute-start | bytes 393224 | tf_op jit(solution)/shard_map/gather_t/ppermute | solution.py:221
  92.0 8.6 %collective-permute-start.22 = (f32[2,128,128]{2,1,0:T(8,128)S(1)}, f32[2,128,128]{2,1,0:T(8,128)}, u32[]{:S(2)}, u32[]{:S(2)}) collective-permute-start(f32[2,128,128]{2,1,0:T(8,128)S(1)} %get-tuple-element.95.refs_0_), channel_id=1, source_target_pairs={{0,2},{1,3},{2,4},{3,5},{4,6},{5,7},{6,8},{7,9},{8,10},{9,11},{10,... | collective-permute-start | bytes 393224 | tf_op jit(solution)/shard_map/gather_t/ppermute | solution.py:221
  100.6 14.9 %collective-permute-start.24 = (f32[2,128,128]{2,1,0:T(8,128)}, f32[2,128,128]{2,1,0:T(8,128)}, u32[]{:S(2)}, u32[]{:S(2)}) collective-permute-start(f32[2,128,128]{2,1,0:T(8,128)} %collective-permute-done.19.refs_1_), channel_id=1, source_target_pairs={{0,12},{1,13},{2,14},{3,15},{4,0},{5,1},{6,2},{7,3},{8,4},{9,5},{1... | collective-permute-start | bytes 393224 | tf_op jit(solution)/shard_map/gather_t/ppermute | solution.py:221
  106.6 16.3 %collective-permute-start.28 = (f32[2,128,128]{2,1,0:T(8,128)}, f32[2,128,128]{2,1,0:T(8,128)}, u32[]{:S(2)}, u32[]{:S(2)}) collective-permute-start(f32[2,128,128]{2,1,0:T(8,128)} %collective-permute-done.19.refs_1_), channel_id=1, source_target_pairs={{0,1},{1,0},{2,3},{3,2},{4,5},{5,4},{6,7},{7,6},{8,9},{9,8},{10,11... | collective-permute-start | bytes 393224 | tf_op jit(solution)/shard_map/gather_t/ppermute | solution.py:217
  106.6 16.3 %collective-permute-start.29 = (f32[2,128,128]{2,1,0:T(8,128)S(1)}, f32[2,128,128]{2,1,0:T(8,128)}, u32[]{:S(2)}, u32[]{:S(2)}) collective-permute-start(f32[2,128,128]{2,1,0:T(8,128)S(1)} %collective-permute-done.20.refs_2_), channel_id=1, source_target_pairs={{0,1},{1,0},{2,3},{3,2},{4,5},{5,4},{6,7},{7,6},{8,9},{9,8},{10,11... | collective-permute-start | bytes 393224 | tf_op jit(solution)/shard_map/gather_t/ppermute | solution.py:217
  109.0 13.9 %collective-permute-start.30 = (f32[2,128,128]{2,1,0:T(8,128)S(1)}, f32[2,128,128]{2,1,0:T(8,128)}, u32[]{:S(2)}, u32[]{:S(2)}) collective-permute-start(f32[2,128,128]{2,1,0:T(8,128)S(1)} %collective-permute-done.21.refs_7_), channel_id=1, source_target_pairs={{0,1},{1,0},{2,3},{3,2},{4,5},{5,4},{6,7},{7,6},{8,9},{9,8},{10,11... | collective-permute-start | bytes 393224 | tf_op jit(solution)/shard_map/gather_t/ppermute | solution.py:217
  111.2 11.7 %collective-permute-start.27 = (f32[2,128,128]{2,1,0:T(8,128)}, f32[2,128,128]{2,1,0:T(8,128)}, u32[]{:S(2)}, u32[]{:S(2)}) collective-permute-start(f32[2,128,128]{2,1,0:T(8,128)} %collective-permute-done.22.refs_8_), channel_id=1, source_target_pairs={{0,4},{1,5},{2,6},{3,7},{4,8},{5,9},{6,10},{7,11},{8,12},{9,13},{1... | collective-permute-start | bytes 393224 | tf_op jit(solution)/shard_map/gather_t/ppermute | solution.py:221
  124.1 8.6 %collective-permute-start.37 = (f32[64,256]{1,0:T(8,128)S(1)}, f32[64,256]{1,0:T(8,128)}, u32[]{:S(2)}, u32[]{:S(2)}) collective-permute-start(f32[64,256]{1,0:T(8,128)S(1)} %get-tuple-element.122.refs_21_.q_home_ref), channel_id=1, source_target_pairs={{0,16},{16,0},{32,48},{48,32},{64,80},{80,64},{96,112},{112,96},{1... | collective-permute-start | bytes 196616 | tf_op jit(solution)/shard_map/swap_yq/ppermute | solution.py:313
  (41 other events, 200.9 us)
Sparse Core Ops, SparseCore 0:
  34.0 51.8 all-gather.2

commit v12 on v8

--- a/solution.py
+++ b/solution.py
@@ -123,7 +123,7 @@
     return one(a[0], b[0]) + (one(a[0], b[1]) + one(a[1], b[0]))
 
 
-def uq_kernel(place_ref, root_ref, diag_ref, cols_ref, u_ref, q_ref, home_ref, away_ref):
+def uq_kernel(root_ref, diag_ref, cols_ref, u_ref, q_ref):
     u = jnp.zeros((2 * TB, TB), F32)
     q = jnp.zeros((HALF, 2 * TB), F32)
     for k in range(0, N, 2):
@@ -134,9 +134,6 @@
     for i in range(2):
         u_ref[i] = u[i * TB : (i + 1) * TB]
     q_ref[...] = q
-    even = lax.rem(place_ref[1], 2) == 0
-    home_ref[...] = jnp.where(even, q[:, :TB], q[:, TB:])
-    away_ref[...] = jnp.where(even, q[:, TB:], q[:, :TB])
 
 
 def y_kernel(place_ref, root_ref, t_ref, y_ref, home_ref, away_ref):
@@ -189,7 +186,8 @@
     for r, c in ((0, 1), (0, 2), (0, 3), (1, 0), (1, 2), (1, 3), (2, 3)):
         out_ref[tile(r, c), :] = empty
     y = both(home_ref[...], away_ref[...])
-    q = rows(*both(q_home_ref[...], q_away_ref[...])).T
+    q = rows(*both(q_home_ref[...], q_away_ref[...]))
+    q = jnp.where(even, q[:, :TB], q[:, TB:]).T
     parts = []
     for s in range(2):
         total = got_ref[s]
@@ -292,13 +290,13 @@
             l3,
         )
     with jax.named_scope("term_uq"):
-        u, q, q_home, q_away = call(
+        u, q = call(
             uq_kernel,
-            [(2, *square), (HALF, 2 * TB), (HALF, TB), (HALF, TB)],
-            place,
+            [(2, *square), (HALF, 2 * TB)],
             root_rows,
             diag_rows,
             cols,
+            scalars=0,
         )
     with jax.named_scope("gather_t"):
         t_mine, t_other, t_cols, (root_rows, l2_rows), (u, q) = gather_layers(
@@ -309,9 +307,8 @@
             y_kernel, [(2 * TB, TB), square, square], place, root_rows, t_cols
         )
     with jax.named_scope("swap_yq"):
-        away = jnp.concatenate([y_away, q_away])
-        away = lax.ppermute(away, "row", ROW_SWAP)
-        y_away, q_away = away[:TB], away[TB:]
+        y_away = lax.ppermute(y_away, "row", ROW_SWAP)
+        q_away = lax.ppermute(q, "row", ROW_SWAP)
     with jax.named_scope("sums"):
         (sums,) = call(
             sums_kernel,
@@ -338,7 +335,7 @@
             got,
             y_home,
             y_away,
-            q_home,
+            q,
             q_away,
             scalars=2,
         )

time: 169 us -> 168 us (level)
  starting transfers between devices: 38.7 us -> 40.6 us
    ppermute x0 -> x2, starting transfers between devices: none -> 1.84 us  [the longest x1 1.28 us: body(): y_away = lax.ppermute(y_away, 'row', ROW_SWAP)]
    unnamed x69 -> x63, local copies, waits for them, and re-layouts: 11.9 us -> 11.5 us
  transfers between devices with their start and end apart: 38 -> 39, of which waited for: 16 -> 17; matrix products, arithmetic and copies ran while one was open for 4% -> 4% of each run, Pallas kernels for 4% -> 5%
where the time goes in v12:
time: 168 us; the launch traced here: 167 us
  blocking collectives  41.1 us (24%)
  starting transfers between devices  40.6 us (24%)
  waiting for transfers between devices  39.5 us (24%)
  local copies, waits for them, and re-layouts  18.1 us (11%)
  Pallas kernels  14.2 us (8%)
  between operations  13.7 us (8%)
    all_to_all x1, blocking collectives, body(): got = lax.all_to_all(sums, 'row', 0, 0, tiled=True)  41.1 us
    ppermute x8, waiting for transfers between devices, gather_layers(): up = lax.ppermute(up, 'col', LAYER_UP)  16.5 us
    ppermute x8, starting transfers between devices, gather_layers(): up = lax.ppermute(up, 'col', LAYER_UP)  14.7 us
    pallas_call x7, Pallas kernels, call(): pl.pallas_call(kernel, out_shape=[jax.ShapeDtypeStruct(s, F32) for s in s...  14.2 us
    ppermute x8, waiting for transfers between devices, gather_layers(): down = lax.ppermute(down, 'col', LAYER_DOWN)  11.7 us
    unnamed x63, local copies, waits for them, and re-layouts  11.5 us
    all_to_all x1, starting transfers between devices, to_side(): lax.all_to_all(x, 'row', 0, 0, tiled=True, axis_index_groups=SAME_SIDE)  6.92 us
    all_to_all x1, starting transfers between devices, to_rows(): return lax.all_to_all(x, 'row', 0, 0, tiled=True)  6.75 us
  transfers between devices with their start and end apart: 39, of which 17 were waited for; matrix products, arithmetic and copies ran while one was open for 4% of the time, Pallas kernels for 5%

profile of v12, /device:TPU:32, one launch (start us, length us, event | category | flops | bytes accessed | tf_op | source)
XLA Modules:
  0.0 167.3 jit_solution(6209728643440021171)
XLA Ops:
  8.8 2.0 %prepare.1 = (f32[128,128]{1,0:T(8,128)S(1)}, f32[4,128,128]{2,1,0:T(8,128)S(1)}, f32[4,128,128]{2,1,0:T(8,128)S(1)}, f32[16,192,128]{2,1,0:T(8,128)}) custom-call(s32[4,4]{1,0:T(4,128)S(1)} %bitcast.24, s32[2]{0:T(128)S(1)} %pad_add_fusion.place_ref, f32[2048,128]{1,0:T(8,128)S(1)} %bitcast.22), custom_call_target="tpu_custom_call" | custom-call | tf_op jit(solution)/shard_map/prepare/pallas_call | solution.py:51
  12.4 2.7 %collective-permute-done = f32[128,128]{1,0:T(8,128)S(1)} collective-permute-done((f32[128,128]{1,0:T(8,128)S(1)}, f32[128,128]{1,0:T(8,128)S(1)}, u32[]{:S(2)}, u32[]{:S(2)}) %collective-permute-start) | collective-permute-done | bytes 65568 | tf_op jit(solution)/shard_map/swap_l32/ppermute | solution.py:266
  16.7 1.9 %collective-permute-start.1 = (f32[2,128,128]{2,1,0:T(8,128)S(1)}, f32[2,128,128]{2,1,0:T(8,128)S(1)}, u32[]{:S(2)}, u32[]{:S(2)}) collective-permute-start(f32[2,128,128]{2,1,0:T(8,128)S(1)} %pad_maximum_fusion.refs_0_), channel_id=1, source_target_pairs={{0,2},{1,3},{2,4},{3,5},{4,6},{5,7},{6,8},{7,9},{8,10},{9,11},{10,... | collective-permute-start | bytes 393224 | tf_op jit(solution)/shard_map/gather_l/ppermute | solution.py:225
  18.8 3.3 %collective-permute-done.4.got_ref = f32[4,128,128]{2,1,0:T(8,128)S(1)} collective-permute-done((f32[4,128,128]{2,1,0:T(8,128)S(1)}, f32[4,128,128]{2,1,0:T(8,128)S(1)}, u32[]{:S(2)}, u32[]{:S(2)}) %collective-permute-start.4) | collective-permute-done | bytes 262176 | tf_op jit(solution)/shard_map/swap_rest/ppermute | solution.py:271
  22.7 1.8 %collective-permute-done.2.refs_1_ = f32[2,128,128]{2,1,0:T(8,128)S(1)} collective-permute-done((f32[2,128,128]{2,1,0:T(8,128)S(1)}, f32[2,128,128]{2,1,0:T(8,128)S(1)}, u32[]{:S(2)}, u32[]{:S(2)}) %collective-permute-start.2) | collective-permute-done | bytes 131104 | tf_op jit(solution)/shard_map/gather_l/ppermute | solution.py:226
  24.5 3.1 %collective-permute-start.5 = (f32[2,128,128]{2,1,0:T(8,128)S(1)}, f32[2,128,128]{2,1,0:T(8,128)S(1)}, u32[]{:S(2)}, u32[]{:S(2)}) collective-permute-start(f32[2,128,128]{2,1,0:T(8,128)S(1)} %collective-permute-done.1.refs_7_), channel_id=1, source_target_pairs={{0,2},{1,3},{2,4},{3,5},{4,6},{5,7},{6,8},{7,9},{8,10},{9,11},{10,... | collective-permute-start | bytes 393224 | tf_op jit(solution)/shard_map/gather_l/ppermute | solution.py:225
  28.1 2.4 %collective-permute-done.5.refs_6_ = f32[2,128,128]{2,1,0:T(8,128)S(1)} collective-permute-done((f32[2,128,128]{2,1,0:T(8,128)S(1)}, f32[2,128,128]{2,1,0:T(8,128)S(1)}, u32[]{:S(2)}, u32[]{:S(2)}) %collective-permute-start.5) | collective-permute-done | bytes 131104 | tf_op jit(solution)/shard_map/gather_l/ppermute | solution.py:225
  30.5 3.0 %collective-permute-done.6.refs_2_ = f32[2,128,128]{2,1,0:T(8,128)S(1)} collective-permute-done((f32[2,128,128]{2,1,0:T(8,128)S(1)}, f32[2,128,128]{2,1,0:T(8,128)S(1)}, u32[]{:S(2)}, u32[]{:S(2)}) %collective-permute-start.6) | collective-permute-done | bytes 131104 | tf_op jit(solution)/shard_map/gather_l/ppermute | solution.py:226
  34.9 6.8 %all-to-all-start = ((f32[16,192,128]{2,1,0:T(8,128)}), f32[16,192,128]{2,1,0:T(8,128)S(1)}, u32[]{:S(2)}, u32[]{:S(2)}) async-start(f32[16,192,128]{2,1,0:T(8,128)} %get-tuple-element.84), calls=%async_computation | async-start | bytes 3145728 | tf_op jit(solution)/shard_map/gather_l/all_to_all | solution.py:251
  42.3 2.0 %collective-permute-start.9 = (f32[2,128,128]{2,1,0:T(8,128)S(1)}, f32[2,128,128]{2,1,0:T(8,128)S(1)}, u32[]{:S(2)}, u32[]{:S(2)}) collective-permute-start(f32[2,128,128]{2,1,0:T(8,128)S(1)} %collective-permute-done.5.refs_6_), channel_id=1, source_target_pairs={{0,2},{1,3},{2,4},{3,5},{4,6},{5,7},{6,8},{7,9},{8,10},{9,11},{10,... | collective-permute-start | bytes 393224 | tf_op jit(solution)/shard_map/gather_l/ppermute | solution.py:225
  44.3 2.3 %collective-permute-done.10.refs_3_ = f32[2,128,128]{2,1,0:T(8,128)S(1)} collective-permute-done((f32[2,128,128]{2,1,0:T(8,128)S(1)}, f32[2,128,128]{2,1,0:T(8,128)S(1)}, u32[]{:S(2)}, u32[]{:S(2)}) %collective-permute-start.10) | collective-permute-done | bytes 131104 | tf_op jit(solution)/shard_map/gather_l/ppermute | solution.py:226
  46.7 4.7 %collective-permute-done.9.refs_5_ = f32[2,128,128]{2,1,0:T(8,128)S(1)} collective-permute-done((f32[2,128,128]{2,1,0:T(8,128)S(1)}, f32[2,128,128]{2,1,0:T(8,128)S(1)}, u32[]{:S(2)}, u32[]{:S(2)}) %collective-permute-start.9) | collective-permute-done | bytes 131104 | tf_op jit(solution)/shard_map/gather_l/ppermute | solution.py:225
  53.1 2.1 %collective-permute-start.14 = (f32[2,64,128]{2,1,0:T(8,128)S(1)}, f32[2,64,128]{2,1,0:T(8,128)S(1)}, u32[]{:S(2)}, u32[]{:S(2)}) collective-permute-start(f32[2,64,128]{2,1,0:T(8,128)S(1)} %slice.22), channel_id=1, source_target_pairs={{0,14},{1,15},{2,0},{3,1},{4,2},{5,3},{6,4},{7,5},{8,6},{9,7},{10,... | collective-permute-start | bytes 196616 | tf_op jit(solution)/shard_map/gather_l/ppermute | solution.py:226
  55.2 3.6 %collective-permute-done.13 = f32[2,64,128]{2,1,0:T(8,128)S(1)} collective-permute-done((f32[2,64,128]{2,1,0:T(8,128)S(1)}, f32[2,64,128]{2,1,0:T(8,128)S(1)}, u32[]{:S(2)}, u32[]{:S(2)}) %collective-permute-start.13) | collective-permute-done | bytes 65568 | tf_op jit(solution)/shard_map/gather_l/ppermute | solution.py:225
  59.9 3.6 %all-to-all-done.refs_16_.cols_ref = f32[16,192,128]{2,1,0:T(8,128)S(1)} async-done(((f32[16,192,128]{2,1,0:T(8,128)}), f32[16,192,128]{2,1,0:T(8,128)S(1)}, u32[]{:S(2)}, u32[]{:S(2)}) %all-to-all-start) | async-done | bytes 1572896 | tf_op jit(solution)/shard_map/gather_l/all_to_all | solution.py:251
  73.1 5.2 %collective-permute-done.18.refs_7_ = f32[2,128,128]{2,1,0:T(8,128)S(1)} collective-permute-done((f32[2,128,128]{2,1,0:T(8,128)S(1)}, f32[2,128,128]{2,1,0:T(8,128)S(1)}, u32[]{:S(2)}, u32[]{:S(2)}) %collective-permute-start.18) | collective-permute-done | bytes 131104 | tf_op jit(solution)/shard_map/gather_t/ppermute | solution.py:225
  78.3 2.0 %collective-permute-done.19.refs_1_ = f32[2,128,128]{2,1,0:T(8,128)S(1)} collective-permute-done((f32[2,128,128]{2,1,0:T(8,128)S(1)}, f32[2,128,128]{2,1,0:T(8,128)S(1)}, u32[]{:S(2)}, u32[]{:S(2)}) %collective-permute-start.19) | collective-permute-done | bytes 131104 | tf_op jit(solution)/shard_map/gather_t/ppermute | solution.py:226
  82.8 6.9 %all-to-all-start.1 = ((f32[8,2,128,128]{3,2,1,0:T(8,128)}), f32[8,2,128,128]{3,2,1,0:T(8,128)S(1)}, u32[]{:S(2)}, u32[]{:S(2)}) async-start(f32[8,2,128,128]{3,2,1,0:T(8,128)} %copy-done.7), calls=%async_computation.1 | async-start | bytes 2097152 | tf_op jit(solution)/shard_map/gather_t/all_to_all | solution.py:254
  91.1 1.7 collective-permute-start.25
  93.4 4.8 %slice_bitcast_fusion = (f32[16,2,128,128]{3,2,1,0:T(8,128)S(1)}, f32[16,2,128,128]{3,2,1,0:T(8,128)}, f32[16,2,128,128]{3,2,1,0:T(8,128)S(1)}) fusion(f32[16,3,2,128,128]{4,3,2,1,0:T(8,128)} %bitcast.26), kind=kLoop, calls=%fused_computation | loop fusion | bytes 12582912 | tf_op jit(solution)/shard_map/gather_rows/squeeze | solution.py:280
  101.5 2.5 %term_uq.1 = (f32[2,128,128]{2,1,0:T(8,128)S(1)}, f32[64,256]{1,0:T(8,128)}) custom-call(f32[16,2,128,128]{3,2,1,0:T(8,128)S(1)} %get-tuple-element.124.root_ref, f32[16,2,128,128]{3,2,1,0:T(8,128)S(1)} %get-tuple-element.135.diag_ref, f32[16,192,128]{2,1,0:T(8,128)S(1)} %copy-done.1), custom_call_target="tpu_custom_call" | custom-call | tf_op jit(solution)/shard_map/term_uq/pallas_call | solution.py:51
  114.0 3.2 %sums.1 = f32[16,320,128]{2,1,0:T(8,128)S(1)} custom-call(s32[2]{0:T(128)S(1)} %pad_add_fusion.place_ref, f32[2,128,128]{2,1,0:T(8,128)S(1)} %copy-done.9, f32[2,128,128]{2,1,0:T(8,128)S(1)} %copy-done.15, f32[2,128,128]{2,1,0:T(8,128)} %collective-permute-done.22.refs_2_, f32[2,128,128]{2,1,0:T(8,128)S(1)} %collective-permute-done.26.refs_3_, ...), custom_call_target="tpu_custom_call" | custom-call | tf_op jit(solution)/shard_map/sums/pallas_call | solution.py:51
  117.3 41.1 %all_to_all.15.got_ref = f32[16,320,128]{2,1,0:T(8,128)S(1)} all-to-all(f32[16,320,128]{2,1,0:T(8,128)S(1)} %sums.1), channel_id=1, replica_groups=mesh['row'=16,'col'=16] {'row'}, dimensions={0} | all-to-all | bytes 5242880 | tf_op jit(solution)/shard_map/scatter_sums/all_to_all | solution.py:327
  158.4 2.1 %finish.1 = f32[2048,128]{1,0:T(8,128)} custom-call(s32[4,4]{1,0:T(4,128)S(1)} %bitcast.25, s32[2]{0:T(128)S(1)} %pad_add_fusion.place_ref, f32[2048,128]{1,0:T(8,128)S(1)} %bitcast.23, f32[16,320,128]{2,1,0:T(8,128)S(1)} %all_to_all.15.got_ref, f32[128,128]{1,0:T(8,128)S(1)} %get-tuple-element.132.home_ref, ...), custom_call_target="tpu_custom_call" | custom-call | tf_op jit(solution)/shard_map/finish/pallas_call | solution.py:51
  (138 shorter events, 38.8 us)
Async XLA Ops:
  6.5 86.8 %all-gather.3.cloned.1.call-start = ((), (), s32[]{:S(2)}) async-start(), calls=%async_computation.3 | async-start | bytes 6684672 | tf_op jit(solution)/shard_map/gather_rows/all_gather | solution.py:279
  15.1 7.0 %collective-permute-start.4 = (f32[4,128,128]{2,1,0:T(8,128)S(1)}, f32[4,128,128]{2,1,0:T(8,128)S(1)}, u32[]{:S(2)}, u32[]{:S(2)}) collective-permute-start(f32[4,128,128]{2,1,0:T(8,128)S(1)} %get-tuple-element.74), channel_id=1, source_target_pairs={{0,16},{16,0},{32,48},{48,32},{64,80},{80,64},{96,112},{112,96},{1... | collective-permute-start | bytes 786440 | tf_op jit(solution)/shard_map/swap_rest/ppermute | solution.py:271
  16.7 5.9 %collective-permute-start.1 = (f32[2,128,128]{2,1,0:T(8,128)S(1)}, f32[2,128,128]{2,1,0:T(8,128)S(1)}, u32[]{:S(2)}, u32[]{:S(2)}) collective-permute-start(f32[2,128,128]{2,1,0:T(8,128)S(1)} %pad_maximum_fusion.refs_0_), channel_id=1, source_target_pairs={{0,2},{1,3},{2,4},{3,5},{4,6},{5,7},{6,8},{7,9},{8,10},{9,11},{10,... | collective-permute-start | bytes 393224 | tf_op jit(solution)/shard_map/gather_l/ppermute | solution.py:225
  24.5 6.0 %collective-permute-start.5 = (f32[2,128,128]{2,1,0:T(8,128)S(1)}, f32[2,128,128]{2,1,0:T(8,128)S(1)}, u32[]{:S(2)}, u32[]{:S(2)}) collective-permute-start(f32[2,128,128]{2,1,0:T(8,128)S(1)} %collective-permute-done.1.refs_7_), channel_id=1, source_target_pairs={{0,2},{1,3},{2,4},{3,5},{4,6},{5,7},{6,8},{7,9},{8,10},{9,11},{10,... | collective-permute-start | bytes 393224 | tf_op jit(solution)/shard_map/gather_l/ppermute | solution.py:225
  34.9 28.6 %all-to-all-start = ((f32[16,192,128]{2,1,0:T(8,128)}), f32[16,192,128]{2,1,0:T(8,128)S(1)}, u32[]{:S(2)}, u32[]{:S(2)}) async-start(f32[16,192,128]{2,1,0:T(8,128)} %get-tuple-element.84), calls=%async_computation | async-start | bytes 3145728 | tf_op jit(solution)/shard_map/gather_l/all_to_all | solution.py:251
  42.3 9.1 %collective-permute-start.9 = (f32[2,128,128]{2,1,0:T(8,128)S(1)}, f32[2,128,128]{2,1,0:T(8,128)S(1)}, u32[]{:S(2)}, u32[]{:S(2)}) collective-permute-start(f32[2,128,128]{2,1,0:T(8,128)S(1)} %collective-permute-done.5.refs_6_), channel_id=1, source_target_pairs={{0,2},{1,3},{2,4},{3,5},{4,6},{5,7},{6,8},{7,9},{8,10},{9,11},{10,... | collective-permute-start | bytes 393224 | tf_op jit(solution)/shard_map/gather_l/ppermute | solution.py:225
  51.4 7.8 %collective-permute-start.15 = (f32[2,128,128]{2,1,0:T(8,128)S(1)}, f32[2,128,128]{2,1,0:T(8,128)S(1)}, u32[]{:S(2)}, u32[]{:S(2)}) collective-permute-start(f32[2,128,128]{2,1,0:T(8,128)S(1)} %collective-permute-done.9.refs_5_), channel_id=1, source_target_pairs={{0,1},{1,0},{2,3},{3,2},{4,5},{5,4},{6,7},{7,6},{8,9},{9,8},{10,11... | collective-permute-start | bytes 393224 | tf_op jit(solution)/shard_map/gather_l/ppermute | solution.py:206
  51.4 8.5 %collective-permute-start.16 = (f32[2,128,128]{2,1,0:T(8,128)S(1)}, f32[2,128,128]{2,1,0:T(8,128)S(1)}, u32[]{:S(2)}, u32[]{:S(2)}) collective-permute-start(f32[2,128,128]{2,1,0:T(8,128)S(1)} %collective-permute-done.10.refs_3_), channel_id=1, source_target_pairs={{0,1},{1,0},{2,3},{3,2},{4,5},{5,4},{6,7},{7,6},{8,9},{9,8},{10,11... | collective-permute-start | bytes 393224 | tf_op jit(solution)/shard_map/gather_l/ppermute | solution.py:206
  51.9 6.9 %collective-permute-start.13 = (f32[2,64,128]{2,1,0:T(8,128)S(1)}, f32[2,64,128]{2,1,0:T(8,128)S(1)}, u32[]{:S(2)}, u32[]{:S(2)}) collective-permute-start(f32[2,64,128]{2,1,0:T(8,128)S(1)} %slice.21), channel_id=1, source_target_pairs={{0,2},{1,3},{2,4},{3,5},{4,6},{5,7},{6,8},{7,9},{8,10},{9,11},{10,... | collective-permute-start | bytes 196616 | tf_op jit(solution)/shard_map/gather_l/ppermute | solution.py:225
  53.1 6.1 %collective-permute-start.14 = (f32[2,64,128]{2,1,0:T(8,128)S(1)}, f32[2,64,128]{2,1,0:T(8,128)S(1)}, u32[]{:S(2)}, u32[]{:S(2)}) collective-permute-start(f32[2,64,128]{2,1,0:T(8,128)S(1)} %slice.22), channel_id=1, source_target_pairs={{0,14},{1,15},{2,0},{3,1},{4,2},{5,3},{6,4},{7,5},{8,6},{9,7},{10,... | collective-permute-start | bytes 196616 | tf_op jit(solution)/shard_map/gather_l/ppermute | solution.py:226
  69.7 8.5 %collective-permute-start.18 = (f32[2,128,128]{2,1,0:T(8,128)S(1)}, f32[2,128,128]{2,1,0:T(8,128)S(1)}, u32[]{:S(2)}, u32[]{:S(2)}) collective-permute-start(f32[2,128,128]{2,1,0:T(8,128)S(1)} %get-tuple-element.100.refs_0_), channel_id=1, source_target_pairs={{0,2},{1,3},{2,4},{3,5},{4,6},{5,7},{6,8},{7,9},{8,10},{9,11},{10,... | collective-permute-start | bytes 393224 | tf_op jit(solution)/shard_map/gather_t/ppermute | solution.py:225
  71.4 8.9 %collective-permute-start.19 = (f32[2,128,128]{2,1,0:T(8,128)S(1)}, f32[2,128,128]{2,1,0:T(8,128)S(1)}, u32[]{:S(2)}, u32[]{:S(2)}) collective-permute-start(f32[2,128,128]{2,1,0:T(8,128)S(1)} %get-tuple-element.100.refs_0_), channel_id=1, source_target_pairs={{0,14},{1,15},{2,0},{3,1},{4,2},{5,3},{6,4},{7,5},{8,6},{9,7},{10,... | collective-permute-start | bytes 393224 | tf_op jit(solution)/shard_map/gather_t/ppermute | solution.py:226
  80.3 9.5 %collective-permute-start.21 = (f32[2,128,128]{2,1,0:T(8,128)S(1)}, f32[2,128,128]{2,1,0:T(8,128)S(1)}, u32[]{:S(2)}, u32[]{:S(2)}) collective-permute-start(f32[2,128,128]{2,1,0:T(8,128)S(1)} %collective-permute-done.18.refs_7_), channel_id=1, source_target_pairs={{0,2},{1,3},{2,4},{3,5},{4,6},{5,7},{6,8},{7,9},{8,10},{9,11},{10,... | collective-permute-start | bytes 393224 | tf_op jit(solution)/shard_map/gather_t/ppermute | solution.py:225
  81.8 7.9 %collective-permute-start.22 = (f32[2,128,128]{2,1,0:T(8,128)S(1)}, f32[2,128,128]{2,1,0:T(8,128)}, u32[]{:S(2)}, u32[]{:S(2)}) collective-permute-start(f32[2,128,128]{2,1,0:T(8,128)S(1)} %collective-permute-done.19.refs_1_), channel_id=1, source_target_pairs={{0,14},{1,15},{2,0},{3,1},{4,2},{5,3},{6,4},{7,5},{8,6},{9,7},{10,... | collective-permute-start | bytes 393224 | tf_op jit(solution)/shard_map/gather_t/ppermute | solution.py:226
  82.3 7.5 %collective-permute-start.23 = (f32[2,128,128]{2,1,0:T(8,128)S(1)}, f32[2,128,128]{2,1,0:T(8,128)S(1)}, u32[]{:S(2)}, u32[]{:S(2)}) collective-permute-start(f32[2,128,128]{2,1,0:T(8,128)S(1)} %collective-permute-done.18.refs_7_), channel_id=1, source_target_pairs={{0,1},{1,0},{2,3},{3,2},{4,5},{5,4},{6,7},{7,6},{8,9},{9,8},{10,11... | collective-permute-start | bytes 393224 | tf_op jit(solution)/shard_map/gather_t/ppermute | solution.py:206
  82.3 8.1 %collective-permute-start.24 = (f32[2,128,128]{2,1,0:T(8,128)S(1)}, f32[2,128,128]{2,1,0:T(8,128)S(1)}, u32[]{:S(2)}, u32[]{:S(2)}) collective-permute-start(f32[2,128,128]{2,1,0:T(8,128)S(1)} %collective-permute-done.19.refs_1_), channel_id=1, source_target_pairs={{0,1},{1,0},{2,3},{3,2},{4,5},{5,4},{6,7},{7,6},{8,9},{9,8},{10,11... | collective-permute-start | bytes 393224 | tf_op jit(solution)/shard_map/gather_t/ppermute | solution.py:206
  82.8 24.6 %all-to-all-start.1 = ((f32[8,2,128,128]{3,2,1,0:T(8,128)}), f32[8,2,128,128]{3,2,1,0:T(8,128)S(1)}, u32[]{:S(2)}, u32[]{:S(2)}) async-start(f32[8,2,128,128]{3,2,1,0:T(8,128)} %copy-done.7), calls=%async_computation.1 | async-start | bytes 2097152 | tf_op jit(solution)/shard_map/gather_t/all_to_all | solution.py:254
  91.1 7.1 %collective-permute-start.25 = (f32[2,128,128]{2,1,0:T(8,128)S(1)}, f32[2,128,128]{2,1,0:T(8,128)S(1)}, u32[]{:S(2)}, u32[]{:S(2)}) collective-permute-start(f32[2,128,128]{2,1,0:T(8,128)S(1)} %collective-permute-done.21.refs_6_), channel_id=1, source_target_pairs={{0,2},{1,3},{2,4},{3,5},{4,6},{5,7},{6,8},{7,9},{8,10},{9,11},{10,... | collective-permute-start | bytes 393224 | tf_op jit(solution)/shard_map/gather_t/ppermute | solution.py:225
  92.8 6.1 %collective-permute-start.27 = (f32[2,128,128]{2,1,0:T(8,128)S(1)}, f32[2,128,128]{2,1,0:T(8,128)}, u32[]{:S(2)}, u32[]{:S(2)}) collective-permute-start(f32[2,128,128]{2,1,0:T(8,128)S(1)} %collective-permute-done.21.refs_6_), channel_id=1, source_target_pairs={{0,1},{1,0},{2,3},{3,2},{4,5},{5,4},{6,7},{7,6},{8,9},{9,8},{10,11... | collective-permute-start | bytes 393224 | tf_op jit(solution)/shard_map/gather_t/ppermute | solution.py:206
  92.8 6.1 %collective-permute-start.26 = (f32[2,128,128]{2,1,0:T(8,128)}, f32[2,128,128]{2,1,0:T(8,128)S(1)}, u32[]{:S(2)}, u32[]{:S(2)}) collective-permute-start(f32[2,128,128]{2,1,0:T(8,128)} %collective-permute-done.22.refs_2_), channel_id=1, source_target_pairs={{0,14},{1,15},{2,0},{3,1},{4,2},{5,3},{6,4},{7,5},{8,6},{9,7},{10,... | collective-permute-start | bytes 393224 | tf_op jit(solution)/shard_map/gather_t/ppermute | solution.py:226
  98.9 7.2 %collective-permute-start.31 = (f32[2,128,128]{2,1,0:T(8,128)S(1)}, f32[2,128,128]{2,1,0:T(8,128)S(1)}, u32[]{:S(2)}, u32[]{:S(2)}) collective-permute-start(f32[2,128,128]{2,1,0:T(8,128)S(1)} %collective-permute-done.25.refs_5_), channel_id=1, source_target_pairs={{0,1},{1,0},{2,3},{3,2},{4,5},{5,4},{6,7},{7,6},{8,9},{9,8},{10,11... | collective-permute-start | bytes 393224 | tf_op jit(solution)/shard_map/gather_t/ppermute | solution.py:206
  98.9 7.2 %collective-permute-start.32 = (f32[2,128,128]{2,1,0:T(8,128)S(1)}, f32[2,128,128]{2,1,0:T(8,128)S(1)}, u32[]{:S(2)}, u32[]{:S(2)}) collective-permute-start(f32[2,128,128]{2,1,0:T(8,128)S(1)} %collective-permute-done.26.refs_3_), channel_id=1, source_target_pairs={{0,1},{1,0},{2,3},{3,2},{4,5},{5,4},{6,7},{7,6},{8,9},{9,8},{10,11... | collective-permute-start | bytes 393224 | tf_op jit(solution)/shard_map/gather_t/ppermute | solution.py:206
  106.8 10.4 %collective-permute-start.35 = (f32[64,256]{1,0:T(8,128)}, f32[64,256]{1,0:T(8,128)}, u32[]{:S(2)}, u32[]{:S(2)}) collective-permute-start(f32[64,256]{1,0:T(8,128)} %get-tuple-element.128.refs_19_.q_home_ref), channel_id=1, source_target_pairs={{0,16},{16,0},{32,48},{48,32},{64,80},{80,64},{96,112},{112,96},{1... | collective-permute-start | bytes 196616 | tf_op jit(solution)/shard_map/swap_yq/ppermute | solution.py:311
  109.3 8.0 %collective-permute-start.34 = (f32[128,128]{1,0:T(8,128)S(1)}, f32[128,128]{1,0:T(8,128)S(1)}, u32[]{:S(2)}, u32[]{:S(2)}) collective-permute-start(f32[128,128]{1,0:T(8,128)S(1)} %get-tuple-element.130), channel_id=1, source_target_pairs={{0,16},{16,0},{32,48},{48,32},{64,80},{80,64},{96,112},{112,96},{1... | collective-permute-start | bytes 196616 | tf_op jit(solution)/shard_map/swap_yq/ppermute | solution.py:310
  (45 other events, 225.0 us)
Sparse Core Ops, SparseCore 0:
  35.0 51.4 all-gather.2

commit v13 on v12

--- a/solution.py
+++ b/solution.py
@@ -224,7 +224,10 @@
             up, down = up[:, :half], down[:, half:]
         up = lax.ppermute(up, "col", LAYER_UP)
         down = lax.ppermute(down, "col", LAYER_DOWN)
-        up, down, swapped, more = lax.optimization_barrier((up, down, swapped, ties.get(step)))
+        more = ties.get(step)
+        if callable(more):
+            more = more(tied[-1])
+        up, down, swapped, more = lax.optimization_barrier((up, down, swapped, more))
         tied.append(more)
         if step == begin[3]:
             up, down, beside = lax.optimization_barrier((up, down, beside))
@@ -269,12 +272,13 @@
     with jax.named_scope("swap_rest"):
         l32_pair, away = lax.optimization_barrier((l32_pair, away))
         away = lax.ppermute(away, "row", ROW_SWAP)
+    def pack(away):
+        return call(pack_kernel, [(3, 2, *square), (2, *square)], place, home, away)
+
     with jax.named_scope("gather_l"):
-        l_mine, l_other, cols, away = gather_layers(
-            l32_pair, (1, (send, away), lambda x: to_rows(x[0]), 4), {2: away}
-        )
-    with jax.named_scope("pack"):
-        packed, l3 = call(pack_kernel, [(3, 2, *square), (2, *square)], place, home, away)
+        l_mine, l_other, cols, _, (packed, l3) = gather_layers(
+            l32_pair, (2, (send, away), lambda x: to_rows(x[0]), 4), {1: away, 2: pack}
+        )
     with jax.named_scope("gather_rows"):
         panels = lax.all_gather(packed, "col", axis=0)
         panels = [panels[:, i] for i in range(3)]

time: 168 us -> 169 us (level); the launches traced: 167 us -> 166 us
  starting transfers between devices: 40.6 us -> 38.1 us
    ppermute x8, starting transfers between devices: 14.7 us -> 3.01 us  [gather_layers(): up = lax.ppermute(up, 'col', LAYER_UP)]
    ppermute x8, starting transfers between devices: 4.04 us -> 15.5 us  [gather_layers(): down = lax.ppermute(down, 'col', LAYER_DOWN)]
    ppermute x8, waiting for transfers between devices: 11.7 us -> 17.3 us  [gather_layers(): down = lax.ppermute(down, 'col', LAYER_DOWN)]
    ppermute x1, waiting for transfers between devices: 3.29 us -> 0.01 us  [body(): away = lax.ppermute(away, 'row', ROW_SWAP)]
    ppermute x8, waiting for transfers between devices: 16.5 us -> 14.4 us  [gather_layers(): up = lax.ppermute(up, 'col', LAYER_UP)]
  transfers between devices with their start and end apart: 39 -> 39, of which waited for: 17 -> 15; matrix products, arithmetic and copies ran while one was open for 4% -> 4% of each run, Pallas kernels for 5% -> 6%
where the time goes in v13:
time: 169 us; the launch traced here: 166 us
  blocking collectives  41.1 us (24%)
  waiting for transfers between devices  41 us (24%)
  starting transfers between devices  38.1 us (23%)
  local copies, waits for them, and re-layouts  18 us (11%)
  Pallas kernels  14.2 us (8%)
  between operations  13.7 us (8%)
    all_to_all x1, blocking collectives, body(): got = lax.all_to_all(sums, 'row', 0, 0, tiled=True)  41.1 us
    ppermute x8, waiting for transfers between devices, gather_layers(): down = lax.ppermute(down, 'col', LAYER_DOWN)  17.3 us
    ppermute x8, starting transfers between devices, gather_layers(): down = lax.ppermute(down, 'col', LAYER_DOWN)  15.5 us
    ppermute x8, waiting for transfers between devices, gather_layers(): up = lax.ppermute(up, 'col', LAYER_UP)  14.4 us
    pallas_call x7, Pallas kernels, call(): pl.pallas_call(kernel, out_shape=[jax.ShapeDtypeStruct(s, F32) for s in s...  14.2 us
    unnamed x63, local copies, waits for them, and re-layouts  11.5 us
    all_to_all x1, starting transfers between devices, to_rows(): return lax.all_to_all(x, 'row', 0, 0, tiled=True)  6.75 us
    all_to_all x1, starting transfers between devices, to_side(): lax.all_to_all(x, 'row', 0, 0, tiled=True, axis_index_groups=SAME_SIDE)  5.33 us
  transfers between devices with their start and end apart: 39, of which 15 were waited for; matrix products, arithmetic and copies ran while one was open for 4% of the time, Pallas kernels for 6%

profile of v13, /device:TPU:32, one launch (start us, length us, event | category | flops | bytes accessed | tf_op | source)
XLA Modules:
  0.0 166.4 jit_solution(16823865186602394842)
XLA Ops:
  8.8 2.0 %prepare.1 = (f32[128,128]{1,0:T(8,128)S(1)}, f32[4,128,128]{2,1,0:T(8,128)S(1)}, f32[4,128,128]{2,1,0:T(8,128)S(1)}, f32[16,192,128]{2,1,0:T(8,128)}) custom-call(s32[4,4]{1,0:T(4,128)S(1)} %bitcast.24, s32[2]{0:T(128)S(1)} %pad_add_fusion.place_ref, f32[2048,128]{1,0:T(8,128)S(1)} %bitcast.22), custom_call_target="tpu_custom_call" | custom-call | tf_op jit(solution)/shard_map/prepare/pallas_call | solution.py:51
  12.4 2.7 %collective-permute-done = f32[128,128]{1,0:T(8,128)S(1)} collective-permute-done((f32[128,128]{1,0:T(8,128)S(1)}, f32[128,128]{1,0:T(8,128)S(1)}, u32[]{:S(2)}, u32[]{:S(2)}) %collective-permute-start) | collective-permute-done | bytes 65568 | tf_op jit(solution)/shard_map/swap_l32/ppermute | solution.py:269
  15.1 1.7 collective-permute-start.4
  18.8 4.1 %collective-permute-done.2.refs_1_ = f32[2,128,128]{2,1,0:T(8,128)S(1)} collective-permute-done((f32[2,128,128]{2,1,0:T(8,128)S(1)}, f32[2,128,128]{2,1,0:T(8,128)S(1)}, u32[]{:S(2)}, u32[]{:S(2)}) %collective-permute-start.2) | collective-permute-done | bytes 131104 | tf_op jit(solution)/shard_map/gather_l/ppermute | solution.py:226
  22.8 3.8 %collective-permute-done.1.refs_7_ = f32[2,128,128]{2,1,0:T(8,128)S(1)} collective-permute-done((f32[2,128,128]{2,1,0:T(8,128)S(1)}, f32[2,128,128]{2,1,0:T(8,128)S(1)}, u32[]{:S(2)}, u32[]{:S(2)}) %collective-permute-start.1) | collective-permute-done | bytes 131104 | tf_op jit(solution)/shard_map/gather_l/ppermute | solution.py:225
  27.1 3.0 %collective-permute-start.6 = (f32[2,128,128]{2,1,0:T(8,128)S(1)}, f32[2,128,128]{2,1,0:T(8,128)S(1)}, u32[]{:S(2)}, u32[]{:S(2)}) collective-permute-start(f32[2,128,128]{2,1,0:T(8,128)S(1)} %collective-permute-done.2.refs_1_), channel_id=1, source_target_pairs={{0,14},{1,15},{2,0},{3,1},{4,2},{5,3},{6,4},{7,5},{8,6},{9,7},{10,... | collective-permute-start | bytes 393224 | tf_op jit(solution)/shard_map/gather_l/ppermute | solution.py:226
  33.0 2.2 %collective-permute-done.5.refs_6_ = f32[2,128,128]{2,1,0:T(8,128)S(1)} collective-permute-done((f32[2,128,128]{2,1,0:T(8,128)S(1)}, f32[2,128,128]{2,1,0:T(8,128)S(1)}, u32[]{:S(2)}, u32[]{:S(2)}) %collective-permute-start.5) | collective-permute-done | bytes 131104 | tf_op jit(solution)/shard_map/gather_l/ppermute | solution.py:225
  35.2 6.8 %all-to-all-start = ((f32[16,192,128]{2,1,0:T(8,128)}), f32[16,192,128]{2,1,0:T(8,128)S(1)}, u32[]{:S(2)}, u32[]{:S(2)}) async-start(f32[16,192,128]{2,1,0:T(8,128)} %get-tuple-element.92), calls=%async_computation | async-start | bytes 3145728 | tf_op jit(solution)/shard_map/gather_l/all_to_all | solution.py:254
  42.1 1.7 collective-permute-start.10
  44.3 5.6 %collective-permute-done.10.refs_3_ = f32[2,128,128]{2,1,0:T(8,128)S(1)} collective-permute-done((f32[2,128,128]{2,1,0:T(8,128)S(1)}, f32[2,128,128]{2,1,0:T(8,128)S(1)}, u32[]{:S(2)}, u32[]{:S(2)}) %collective-permute-start.10) | collective-permute-done | bytes 131104 | tf_op jit(solution)/shard_map/gather_l/ppermute | solution.py:226
  49.9 2.2 %collective-permute-done.9.refs_5_ = f32[2,128,128]{2,1,0:T(8,128)S(1)} collective-permute-done((f32[2,128,128]{2,1,0:T(8,128)S(1)}, f32[2,128,128]{2,1,0:T(8,128)S(1)}, u32[]{:S(2)}, u32[]{:S(2)}) %collective-permute-start.9) | collective-permute-done | bytes 131104 | tf_op jit(solution)/shard_map/gather_l/ppermute | solution.py:225
  54.7 3.6 %collective-permute-done.13 = f32[2,64,128]{2,1,0:T(8,128)S(1)} collective-permute-done((f32[2,64,128]{2,1,0:T(8,128)S(1)}, f32[2,64,128]{2,1,0:T(8,128)S(1)}, u32[]{:S(2)}, u32[]{:S(2)}) %collective-permute-start.13) | collective-permute-done | bytes 65568 | tf_op jit(solution)/shard_map/gather_l/ppermute | solution.py:225
  59.7 4.9 %all-to-all-done.refs_16_.cols_ref = f32[16,192,128]{2,1,0:T(8,128)S(1)} async-done(((f32[16,192,128]{2,1,0:T(8,128)}), f32[16,192,128]{2,1,0:T(8,128)S(1)}, u32[]{:S(2)}, u32[]{:S(2)}) %all-to-all-start) | async-done | bytes 1572896 | tf_op jit(solution)/shard_map/gather_l/all_to_all | solution.py:254
  70.9 1.8 %collective-permute-start.19 = (f32[2,128,128]{2,1,0:T(8,128)S(1)}, f32[2,128,128]{2,1,0:T(8,128)S(1)}, u32[]{:S(2)}, u32[]{:S(2)}) collective-permute-start(f32[2,128,128]{2,1,0:T(8,128)S(1)} %get-tuple-element.106.refs_0_), channel_id=1, source_target_pairs={{0,14},{1,15},{2,0},{3,1},{4,2},{5,3},{6,4},{7,5},{8,6},{9,7},{10,... | collective-permute-start | bytes 393224 | tf_op jit(solution)/shard_map/gather_t/ppermute | solution.py:226
  74.3 5.3 %collective-permute-done.19.refs_1_ = f32[2,128,128]{2,1,0:T(8,128)S(1)} collective-permute-done((f32[2,128,128]{2,1,0:T(8,128)S(1)}, f32[2,128,128]{2,1,0:T(8,128)S(1)}, u32[]{:S(2)}, u32[]{:S(2)}) %collective-permute-start.19) | collective-permute-done | bytes 131104 | tf_op jit(solution)/shard_map/gather_t/ppermute | solution.py:226
  81.2 2.1 %collective-permute-start.22 = (f32[2,128,128]{2,1,0:T(8,128)S(1)}, f32[2,128,128]{2,1,0:T(8,128)S(1)}, u32[]{:S(2)}, u32[]{:S(2)}) collective-permute-start(f32[2,128,128]{2,1,0:T(8,128)S(1)} %collective-permute-done.19.refs_1_), channel_id=1, source_target_pairs={{0,14},{1,15},{2,0},{3,1},{4,2},{5,3},{6,4},{7,5},{8,6},{9,7},{10,... | collective-permute-start | bytes 393224 | tf_op jit(solution)/shard_map/gather_t/ppermute | solution.py:226
  83.6 5.3 %all-to-all-start.1 = ((f32[8,2,128,128]{3,2,1,0:T(8,128)}), f32[8,2,128,128]{3,2,1,0:T(8,128)S(1)}, u32[]{:S(2)}, u32[]{:S(2)}) async-start(f32[8,2,128,128]{3,2,1,0:T(8,128)} %copy-done.7), calls=%async_computation.1 | async-start | bytes 2097152 | tf_op jit(solution)/shard_map/gather_t/all_to_all | solution.py:257
  90.3 2.0 %collective-permute-start.26 = (f32[2,128,128]{2,1,0:T(8,128)S(1)}, f32[2,128,128]{2,1,0:T(8,128)S(1)}, u32[]{:S(2)}, u32[]{:S(2)}) collective-permute-start(f32[2,128,128]{2,1,0:T(8,128)S(1)} %collective-permute-done.22.refs_2_), channel_id=1, source_target_pairs={{0,14},{1,15},{2,0},{3,1},{4,2},{5,3},{6,4},{7,5},{8,6},{9,7},{10,... | collective-permute-start | bytes 393224 | tf_op jit(solution)/shard_map/gather_t/ppermute | solution.py:226
  92.6 4.8 %slice_bitcast_fusion = (f32[16,2,128,128]{3,2,1,0:T(8,128)S(1)}, f32[16,2,128,128]{3,2,1,0:T(8,128)}, f32[16,2,128,128]{3,2,1,0:T(8,128)S(1)}) fusion(f32[16,3,2,128,128]{4,3,2,1,0:T(8,128)} %bitcast.26), kind=kLoop, calls=%fused_computation | loop fusion | bytes 12582912 | tf_op jit(solution)/shard_map/gather_rows/squeeze | solution.py:284
  99.3 2.7 %collective-permute-start.30 = (f32[2,64,128]{2,1,0:T(8,128)S(1)}, f32[2,64,128]{2,1,0:T(8,128)S(1)}, u32[]{:S(2)}, u32[]{:S(2)}) collective-permute-start(f32[2,64,128]{2,1,0:T(8,128)S(1)} %slice.26), channel_id=1, source_target_pairs={{0,14},{1,15},{2,0},{3,1},{4,2},{5,3},{6,4},{7,5},{8,6},{9,7},{10,... | collective-permute-start | bytes 196616 | tf_op jit(solution)/shard_map/gather_t/ppermute | solution.py:226
  102.0 2.5 %term_uq.1 = (f32[2,128,128]{2,1,0:T(8,128)S(1)}, f32[64,256]{1,0:T(8,128)}) custom-call(f32[16,2,128,128]{3,2,1,0:T(8,128)S(1)} %get-tuple-element.130.root_ref, f32[16,2,128,128]{3,2,1,0:T(8,128)S(1)} %get-tuple-element.141.diag_ref, f32[16,192,128]{2,1,0:T(8,128)S(1)} %copy-done.1), custom_call_target="tpu_custom_call" | custom-call | tf_op jit(solution)/shard_map/term_uq/pallas_call | solution.py:51
  113.1 3.2 %sums.1 = f32[16,320,128]{2,1,0:T(8,128)S(1)} custom-call(s32[2]{0:T(128)S(1)} %pad_add_fusion.place_ref, f32[2,128,128]{2,1,0:T(8,128)S(1)} %copy-done.9, f32[2,128,128]{2,1,0:T(8,128)S(1)} %copy-done.13, f32[2,128,128]{2,1,0:T(8,128)S(1)} %copy-done.19, f32[2,128,128]{2,1,0:T(8,128)S(1)} %collective-permute-done.26.refs_3_, ...), custom_call_target="tpu_custom_call" | custom-call | tf_op jit(solution)/shard_map/sums/pallas_call | solution.py:51
  116.3 41.1 %all_to_all.15.got_ref = f32[16,320,128]{2,1,0:T(8,128)S(1)} all-to-all(f32[16,320,128]{2,1,0:T(8,128)S(1)} %sums.1), channel_id=1, replica_groups=mesh['row'=16,'col'=16] {'row'}, dimensions={0} | all-to-all | bytes 5242880 | tf_op jit(solution)/shard_map/scatter_sums/all_to_all | solution.py:331
  157.4 2.1 %finish.1 = f32[2048,128]{1,0:T(8,128)} custom-call(s32[4,4]{1,0:T(4,128)S(1)} %bitcast.25, s32[2]{0:T(128)S(1)} %pad_add_fusion.place_ref, f32[2048,128]{1,0:T(8,128)S(1)} %bitcast.23, f32[16,320,128]{2,1,0:T(8,128)S(1)} %all_to_all.15.got_ref, f32[128,128]{1,0:T(8,128)S(1)} %get-tuple-element.138.home_ref, ...), custom_call_target="tpu_custom_call" | custom-call | tf_op jit(solution)/shard_map/finish/pallas_call | solution.py:51
  (138 shorter events, 35.7 us)
Async XLA Ops:
  6.5 86.0 %all-gather.3.cloned.1.call-start = ((), (), s32[]{:S(2)}) async-start(), calls=%async_computation.3 | async-start | bytes 6684672 | tf_op jit(solution)/shard_map/gather_rows/all_gather | solution.py:283
  15.1 11.5 %collective-permute-start.4 = (f32[4,128,128]{2,1,0:T(8,128)S(1)}, f32[4,128,128]{2,1,0:T(8,128)S(1)}, u32[]{:S(2)}, u32[]{:S(2)}) collective-permute-start(f32[4,128,128]{2,1,0:T(8,128)S(1)} %get-tuple-element.76), channel_id=1, source_target_pairs={{0,16},{16,0},{32,48},{48,32},{64,80},{80,64},{96,112},{112,96},{1... | collective-permute-start | bytes 786440 | tf_op jit(solution)/shard_map/swap_rest/ppermute | solution.py:274
  16.7 6.1 %collective-permute-start.2 = (f32[2,128,128]{2,1,0:T(8,128)S(1)}, f32[2,128,128]{2,1,0:T(8,128)S(1)}, u32[]{:S(2)}, u32[]{:S(2)}) collective-permute-start(f32[2,128,128]{2,1,0:T(8,128)S(1)} %pad_maximum_fusion.refs_0_), channel_id=1, source_target_pairs={{0,14},{1,15},{2,0},{3,1},{4,2},{5,3},{6,4},{7,5},{8,6},{9,7},{10,... | collective-permute-start | bytes 393224 | tf_op jit(solution)/shard_map/gather_l/ppermute | solution.py:226
  17.7 8.9 %collective-permute-start.1 = (f32[2,128,128]{2,1,0:T(8,128)S(1)}, f32[2,128,128]{2,1,0:T(8,128)S(1)}, u32[]{:S(2)}, u32[]{:S(2)}) collective-permute-start(f32[2,128,128]{2,1,0:T(8,128)S(1)} %pad_maximum_fusion.refs_0_), channel_id=1, source_target_pairs={{0,2},{1,3},{2,4},{3,5},{4,6},{5,7},{6,8},{7,9},{8,10},{9,11},{10,... | collective-permute-start | bytes 393224 | tf_op jit(solution)/shard_map/gather_l/ppermute | solution.py:225
  35.2 29.5 %all-to-all-start = ((f32[16,192,128]{2,1,0:T(8,128)}), f32[16,192,128]{2,1,0:T(8,128)S(1)}, u32[]{:S(2)}, u32[]{:S(2)}) async-start(f32[16,192,128]{2,1,0:T(8,128)} %get-tuple-element.92), calls=%async_computation | async-start | bytes 3145728 | tf_op jit(solution)/shard_map/gather_l/all_to_all | solution.py:254
  42.1 7.8 %collective-permute-start.10 = (f32[2,128,128]{2,1,0:T(8,128)S(1)}, f32[2,128,128]{2,1,0:T(8,128)S(1)}, u32[]{:S(2)}, u32[]{:S(2)}) collective-permute-start(f32[2,128,128]{2,1,0:T(8,128)S(1)} %collective-permute-done.6.refs_2_), channel_id=1, source_target_pairs={{0,14},{1,15},{2,0},{3,1},{4,2},{5,3},{6,4},{7,5},{8,6},{9,7},{10,... | collective-permute-start | bytes 393224 | tf_op jit(solution)/shard_map/gather_l/ppermute | solution.py:226
  43.7 6.2 %collective-permute-start.11 = (f32[2,128,128]{2,1,0:T(8,128)S(1)}, f32[2,128,128]{2,1,0:T(8,128)S(1)}, u32[]{:S(2)}, u32[]{:S(2)}) collective-permute-start(f32[2,128,128]{2,1,0:T(8,128)S(1)} %collective-permute-done.5.refs_6_), channel_id=1, source_target_pairs={{0,1},{1,0},{2,3},{3,2},{4,5},{5,4},{6,7},{7,6},{8,9},{9,8},{10,11... | collective-permute-start | bytes 393224 | tf_op jit(solution)/shard_map/gather_l/ppermute | solution.py:206
  43.9 8.2 %collective-permute-start.9 = (f32[2,128,128]{2,1,0:T(8,128)S(1)}, f32[2,128,128]{2,1,0:T(8,128)S(1)}, u32[]{:S(2)}, u32[]{:S(2)}) collective-permute-start(f32[2,128,128]{2,1,0:T(8,128)S(1)} %collective-permute-done.5.refs_6_), channel_id=1, source_target_pairs={{0,2},{1,3},{2,4},{3,5},{4,6},{5,7},{6,8},{7,9},{8,10},{9,11},{10,... | collective-permute-start | bytes 393224 | tf_op jit(solution)/shard_map/gather_l/ppermute | solution.py:225
  52.1 7.0 %collective-permute-start.16 = (f32[2,128,128]{2,1,0:T(8,128)S(1)}, f32[2,128,128]{2,1,0:T(8,128)S(1)}, u32[]{:S(2)}, u32[]{:S(2)}) collective-permute-start(f32[2,128,128]{2,1,0:T(8,128)S(1)} %collective-permute-done.10.refs_3_), channel_id=1, source_target_pairs={{0,1},{1,0},{2,3},{3,2},{4,5},{5,4},{6,7},{7,6},{8,9},{9,8},{10,11... | collective-permute-start | bytes 393224 | tf_op jit(solution)/shard_map/gather_l/ppermute | solution.py:206
  52.1 7.6 %collective-permute-start.15 = (f32[2,128,128]{2,1,0:T(8,128)S(1)}, f32[2,128,128]{2,1,0:T(8,128)S(1)}, u32[]{:S(2)}, u32[]{:S(2)}) collective-permute-start(f32[2,128,128]{2,1,0:T(8,128)S(1)} %collective-permute-done.9.refs_5_), channel_id=1, source_target_pairs={{0,1},{1,0},{2,3},{3,2},{4,5},{5,4},{6,7},{7,6},{8,9},{9,8},{10,11... | collective-permute-start | bytes 393224 | tf_op jit(solution)/shard_map/gather_l/ppermute | solution.py:206
  70.9 8.7 %collective-permute-start.19 = (f32[2,128,128]{2,1,0:T(8,128)S(1)}, f32[2,128,128]{2,1,0:T(8,128)S(1)}, u32[]{:S(2)}, u32[]{:S(2)}) collective-permute-start(f32[2,128,128]{2,1,0:T(8,128)S(1)} %get-tuple-element.106.refs_0_), channel_id=1, source_target_pairs={{0,14},{1,15},{2,0},{3,1},{4,2},{5,3},{6,4},{7,5},{8,6},{9,7},{10,... | collective-permute-start | bytes 393224 | tf_op jit(solution)/shard_map/gather_t/ppermute | solution.py:226
  72.7 8.5 %collective-permute-start.18 = (f32[2,128,128]{2,1,0:T(8,128)S(1)}, f32[2,128,128]{2,1,0:T(8,128)S(1)}, u32[]{:S(2)}, u32[]{:S(2)}) collective-permute-start(f32[2,128,128]{2,1,0:T(8,128)S(1)} %get-tuple-element.106.refs_0_), channel_id=1, source_target_pairs={{0,2},{1,3},{2,4},{3,5},{4,6},{5,7},{6,8},{7,9},{8,10},{9,11},{10,... | collective-permute-start | bytes 393224 | tf_op jit(solution)/shard_map/gather_t/ppermute | solution.py:225
  81.2 7.7 %collective-permute-start.24 = (f32[2,128,128]{2,1,0:T(8,128)S(1)}, f32[2,128,128]{2,1,0:T(8,128)S(1)}, u32[]{:S(2)}, u32[]{:S(2)}) collective-permute-start(f32[2,128,128]{2,1,0:T(8,128)S(1)} %collective-permute-done.19.refs_1_), channel_id=1, source_target_pairs={{0,1},{1,0},{2,3},{3,2},{4,5},{5,4},{6,7},{7,6},{8,9},{9,8},{10,11... | collective-permute-start | bytes 393224 | tf_op jit(solution)/shard_map/gather_t/ppermute | solution.py:206
  81.2 8.4 %collective-permute-start.22 = (f32[2,128,128]{2,1,0:T(8,128)S(1)}, f32[2,128,128]{2,1,0:T(8,128)S(1)}, u32[]{:S(2)}, u32[]{:S(2)}) collective-permute-start(f32[2,128,128]{2,1,0:T(8,128)S(1)} %collective-permute-done.19.refs_1_), channel_id=1, source_target_pairs={{0,14},{1,15},{2,0},{3,1},{4,2},{5,3},{6,4},{7,5},{8,6},{9,7},{10,... | collective-permute-start | bytes 393224 | tf_op jit(solution)/shard_map/gather_t/ppermute | solution.py:226
  83.4 6.2 %collective-permute-start.23 = (f32[2,128,128]{2,1,0:T(8,128)S(1)}, f32[2,128,128]{2,1,0:T(8,128)S(1)}, u32[]{:S(2)}, u32[]{:S(2)}) collective-permute-start(f32[2,128,128]{2,1,0:T(8,128)S(1)} %collective-permute-done.18.refs_7_), channel_id=1, source_target_pairs={{0,1},{1,0},{2,3},{3,2},{4,5},{5,4},{6,7},{7,6},{8,9},{9,8},{10,11... | collective-permute-start | bytes 393224 | tf_op jit(solution)/shard_map/gather_t/ppermute | solution.py:206
  83.6 6.7 %collective-permute-start.21 = (f32[2,128,128]{2,1,0:T(8,128)S(1)}, f32[2,128,128]{2,1,0:T(8,128)}, u32[]{:S(2)}, u32[]{:S(2)}) collective-permute-start(f32[2,128,128]{2,1,0:T(8,128)S(1)} %collective-permute-done.18.refs_7_), channel_id=1, source_target_pairs={{0,2},{1,3},{2,4},{3,5},{4,6},{5,7},{6,8},{7,9},{8,10},{9,11},{10,... | collective-permute-start | bytes 393224 | tf_op jit(solution)/shard_map/gather_t/ppermute | solution.py:225
  83.6 22.8 %all-to-all-start.1 = ((f32[8,2,128,128]{3,2,1,0:T(8,128)}), f32[8,2,128,128]{3,2,1,0:T(8,128)S(1)}, u32[]{:S(2)}, u32[]{:S(2)}) async-start(f32[8,2,128,128]{3,2,1,0:T(8,128)} %copy-done.7), calls=%async_computation.1 | async-start | bytes 2097152 | tf_op jit(solution)/shard_map/gather_t/all_to_all | solution.py:257
  90.3 7.1 %collective-permute-start.28 = (f32[2,128,128]{2,1,0:T(8,128)S(1)}, f32[2,128,128]{2,1,0:T(8,128)}, u32[]{:S(2)}, u32[]{:S(2)}) collective-permute-start(f32[2,128,128]{2,1,0:T(8,128)S(1)} %collective-permute-done.22.refs_2_), channel_id=1, source_target_pairs={{0,1},{1,0},{2,3},{3,2},{4,5},{5,4},{6,7},{7,6},{8,9},{9,8},{10,11... | collective-permute-start | bytes 393224 | tf_op jit(solution)/shard_map/gather_t/ppermute | solution.py:206
  90.3 7.1 %collective-permute-start.26 = (f32[2,128,128]{2,1,0:T(8,128)S(1)}, f32[2,128,128]{2,1,0:T(8,128)S(1)}, u32[]{:S(2)}, u32[]{:S(2)}) collective-permute-start(f32[2,128,128]{2,1,0:T(8,128)S(1)} %collective-permute-done.22.refs_2_), channel_id=1, source_target_pairs={{0,14},{1,15},{2,0},{3,1},{4,2},{5,3},{6,4},{7,5},{8,6},{9,7},{10,... | collective-permute-start | bytes 393224 | tf_op jit(solution)/shard_map/gather_t/ppermute | solution.py:226
  98.4 6.7 %collective-permute-start.32 = (f32[2,128,128]{2,1,0:T(8,128)S(1)}, f32[2,128,128]{2,1,0:T(8,128)S(1)}, u32[]{:S(2)}, u32[]{:S(2)}) collective-permute-start(f32[2,128,128]{2,1,0:T(8,128)S(1)} %collective-permute-done.26.refs_3_), channel_id=1, source_target_pairs={{0,1},{1,0},{2,3},{3,2},{4,5},{5,4},{6,7},{7,6},{8,9},{9,8},{10,11... | collective-permute-start | bytes 393224 | tf_op jit(solution)/shard_map/gather_t/ppermute | solution.py:206
  98.4 6.8 %collective-permute-start.31 = (f32[2,128,128]{2,1,0:T(8,128)S(1)}, f32[2,128,128]{2,1,0:T(8,128)S(1)}, u32[]{:S(2)}, u32[]{:S(2)}) collective-permute-start(f32[2,128,128]{2,1,0:T(8,128)S(1)} %collective-permute-done.25.refs_5_), channel_id=1, source_target_pairs={{0,1},{1,0},{2,3},{3,2},{4,5},{5,4},{6,7},{7,6},{8,9},{9,8},{10,11... | collective-permute-start | bytes 393224 | tf_op jit(solution)/shard_map/gather_t/ppermute | solution.py:206
  98.9 6.2 %collective-permute-start.29 = (f32[2,64,128]{2,1,0:T(8,128)S(1)}, f32[2,64,128]{2,1,0:T(8,128)S(1)}, u32[]{:S(2)}, u32[]{:S(2)}) collective-permute-start(f32[2,64,128]{2,1,0:T(8,128)S(1)} %slice.25), channel_id=1, source_target_pairs={{0,2},{1,3},{2,4},{3,5},{4,6},{5,7},{6,8},{7,9},{8,10},{9,11},{10,... | collective-permute-start | bytes 196616 | tf_op jit(solution)/shard_map/gather_t/ppermute | solution.py:225
  105.9 10.4 %collective-permute-start.35 = (f32[64,256]{1,0:T(8,128)}, f32[64,256]{1,0:T(8,128)}, u32[]{:S(2)}, u32[]{:S(2)}) collective-permute-start(f32[64,256]{1,0:T(8,128)} %get-tuple-element.134.refs_19_.q_home_ref), channel_id=1, source_target_pairs={{0,16},{16,0},{32,48},{48,32},{64,80},{80,64},{96,112},{112,96},{1... | collective-permute-start | bytes 196616 | tf_op jit(solution)/shard_map/swap_yq/ppermute | solution.py:315
  108.4 7.9 %collective-permute-start.34 = (f32[128,128]{1,0:T(8,128)S(1)}, f32[128,128]{1,0:T(8,128)S(1)}, u32[]{:S(2)}, u32[]{:S(2)}) collective-permute-start(f32[128,128]{1,0:T(8,128)S(1)} %get-tuple-element.136), channel_id=1, source_target_pairs={{0,16},{16,0},{32,48},{48,32},{64,80},{80,64},{96,112},{112,96},{1... | collective-permute-start | bytes 196616 | tf_op jit(solution)/shard_map/swap_yq/ppermute | solution.py:314
  (45 other events, 218.5 us)
Sparse Core Ops, SparseCore 0:
  35.3 49.3 all-gather.2
